TPU v7x, 32 devices: a whole 2x2x4 slice. The times are simulated.
32 devices in a mesh: gz: 8 (over y, x, core), gy: 4 (over z).
Axes of the slice: x: 2, y: 2, z: 4, core: 2. Of those that a mesh axis runs over, the one named last changes fastest.
Arguments:
- fields: bfloat16 [6, 64, 128, 256], P(None, 'gz', 'gy'), may hold values from -13 to 13
- target: bfloat16 [128, 32, 64, 128], P(None, 'gz', 'gy'), may hold values from -6 to 6
- conv_weight: bfloat16 [64, 162], replicated, may hold values from -0.5 to 0.5
- conv_bias: float32 [64], replicated, may hold values from -3 to 3
- down_weight: bfloat16 [128, 512], replicated, may hold values from -0.25 to 0.25
- down_bias: float32 [128], replicated, may hold values from -3 to 3
Outputs:
- out_field: bfloat16 [128, 32, 64, 128], P(None, 'gz', 'gy')
- sensitivity: float32 [6, 64, 128, 256], P(None, 'gz', 'gy')
- grad_conv: float32 [64, 162], replicated
- grad_conv_bias: float32 [64], replicated
- grad_down: float32 [128, 512], P('gz')
- grad_down_bias: float32 [128], replicated
- loss: float32 [], replicated
All inputs are finite; a program needn't handle non-finite values.
Results may differ from a plain program's by a relative error of at most 0.0046.
Values may be sent and summed in bfloat16 or wider, within the bound.
No kernel may reach another device: no remote copies, remote signals or barrier semaphores. Data moves between devices by JAX's collectives and lax.ppermute only.
A program may use at most 192 MiB of HBM per device.

v0:
```python
import functools

import jax
import jax.numpy as jnp
import numpy as np
from jax import lax
from jax.experimental import pallas as pl
from jax.experimental.pallas import tpu as pltpu
from jax.sharding import PartitionSpec as P

gelu_scale = 0.7978845608028654
gelu_cubic = 0.044715
lanes = 128
bf16 = jnp.bfloat16
f32 = jnp.float32


def shifted(value, axis, by):
    count = lax.axis_size(axis)
    return lax.ppermute(value, axis, [(i, (i + by) % count) for i in range(count)])


def exchanged(value, axis, bit):
    count = lax.axis_size(axis)
    return lax.ppermute(value, axis, [(i, i ^ bit) for i in range(count)])


def column_spread(half_cols):
    spread = np.zeros((2 * half_cols, 4 * half_cols), np.float32)
    for step in range(2):
        for par in range(2):
            for col in range(half_cols):
                source = (2 * ((col + step) % half_cols) + par - 1) % (2 * half_cols)
                spread[source, (2 * step + par) * half_cols + col] = 1
    return spread


def column_merge(half_cols):
    merge = np.zeros((2 * half_cols, 2 * half_cols), np.float32)
    for par in range(2):
        for col in range(half_cols):
            merge[par * half_cols + col, (2 * col + par - 1) % (2 * half_cols)] = 1
    return merge


def row_spread(channels, pair_rows, row_pad):
    spread = np.zeros((pair_rows * 4 * channels, 2 * channels * row_pad), np.float32)
    for row in range(pair_rows):
        for par_z in range(2):
            for par_y in range(2):
                for ch in range(channels):
                    target = ((row * 2 + par_z) * 2 + par_y) * channels + ch
                    spread[target, (par_z * channels + ch) * row_pad + 2 * row + par_y] = 1
    return spread


def tap_spread(channels):
    spread = np.zeros((8, channels * 27, 64 * channels), np.float32)
    for cls in range(8):
        par_z, par_y, par_x = cls // 4, cls // 2 % 2, cls % 2
        for ch in range(channels):
            for off_z in range(3):
                for off_y in range(3):
                    for off_x in range(3):
                        at_z, at_y, at_x = par_z + off_z, par_y + off_y, par_x + off_x
                        place = (at_z // 2 * 2 + at_y // 2) * 2 + at_x // 2
                        place = ((place * 2 + at_x % 2) * 2 + at_z % 2) * 2 + at_y % 2
                        spread[cls, ch * 27 + 9 * off_z + 3 * off_y + off_x, place * channels + ch] = 1
    return spread


def dot(a, b):
    return jnp.dot(a, b, preferred_element_type=f32)


def dot_rows(a, b):
    return lax.dot_general(a, b, (((1,), (1,)), ((), ())), preferred_element_type=f32)


def split_two(value):
    high = value.astype(bf16)
    return high, (value - high.astype(f32)).astype(bf16)


def block_kernel(
    sizes,
    field_ref,
    target_ref,
    conv_ref,
    conv_t_ref,
    cbias_ref,
    down_ref,
    down_t_ref,
    dbias_ref,
    col_ref,
    merge_ref,
    row_ref,
    row_t_ref,
    tap_ref,
    out_ref,
    acc_ref,
    gdown_ref,
    small_ref,
    split_ref,
    spread_ref,
    hid_ref,
    slope_ref,
    gpre_ref,
    gconv_ref,
    gcb_ref,
    gdb_ref,
    sq_ref,
):
    channels, pairs, pair_rows, row_pad, width, hidden, tile = sizes
    group = 4 * channels
    span = 4 * group
    step_z, step_y = pl.program_id(0), pl.program_id(1)
    last = (step_z == pairs - 1) & (step_y == pl.num_programs(1) - 1)

    @pl.when((step_z == 0) & (step_y == 0))
    def _():
        gdown_ref[...] = jnp.zeros_like(gdown_ref)
        gconv_ref[...] = jnp.zeros_like(gconv_ref)
        gcb_ref[...] = jnp.zeros_like(gcb_ref)
        gdb_ref[...] = jnp.zeros_like(gdb_ref)
        sq_ref[...] = jnp.zeros_like(sq_ref)
        spread_ref[...] = jnp.zeros_like(spread_ref)

        @pl.loop(0, pairs + 1)
        def _(slot):
            planes = [field_ref[ch, 2 * slot + par] for par in range(2) for ch in range(channels)]
            rows = jnp.concatenate(planes, axis=0)
            rows = dot(rows, col_ref[...]).astype(bf16)
            rows = dot(row_ref[...], rows)
            for row in range(pair_rows):
                piece = [
                    rows[row * group : (row + 1) * group, v * lanes : (v + 1) * lanes]
                    for v in range(4)
                ]
                split_ref[slot, :, row * lanes : (row + 1) * lanes] = jnp.concatenate(
                    piece, axis=0
                ).astype(bf16)

    for part in range(width // tile):
        here = slice(part * tile, (part + 1) * tile)
        base = step_y * width + part * tile

        def cells(dy):
            return pl.ds(pl.multiple_of(base + dy * lanes, lanes), tile)

        window = jnp.concatenate(
            [split_ref[step_z + dz, :, cells(dy)] for dz in range(2) for dy in range(2)], axis=0
        )
        pre = dot(conv_ref[...], window)
        pre = pre + jnp.concatenate([cbias_ref[...]] * (tile // lanes), axis=1)
        square = pre * pre
        tangent = jnp.tanh(pre * (square * (gelu_scale * gelu_cubic) + gelu_scale))
        half = 0.5 * tangent + 0.5
        hid = (pre * half).astype(bf16)
        bend = pre * (square * (6.0 * gelu_scale * gelu_cubic) + 2.0 * gelu_scale)
        slope = half * (bend * (1.0 - half)) + half
        output = dot(down_ref[...], hid)
        output = output + jnp.concatenate([dbias_ref[...]] * (tile // lanes), axis=1)
        diff = output - target_ref[0, :, here].astype(f32)
        out_ref[0, :, here] = output.astype(bf16)
        grad_out = diff.astype(bf16)
        gdown_ref[...] += dot_rows(grad_out, hid)
        for k in range(tile // lanes):
            piece = diff[:, k * lanes : (k + 1) * lanes]
            gdb_ref[...] += piece
            sq_ref[...] += piece * piece
        back = dot(down_t_ref[...], grad_out)
        grad_pre = (back * slope).astype(bf16)
        for k in range(tile // lanes):
            gcb_ref[...] += grad_pre[:, k * lanes : (k + 1) * lanes].astype(f32)
        gconv_ref[...] += dot_rows(grad_pre, window)
        spread = dot(conv_t_ref[...], grad_pre)
        for dz in range(2):
            for dy in range(2):
                at = (2 * dz + dy) * span
                spread_ref[step_z + dz, :, cells(dy)] += spread[at : at + span]

    @pl.when(last)
    def _():
        @pl.loop(0, pairs + 1)
        def _(slot):
            rows = []
            for row in range(pair_rows):
                piece = spread_ref[slot, :, row * lanes : (row + 1) * lanes]
                rows.append(
                    jnp.concatenate(
                        [
                            piece[par * group : (par + 1) * group]
                            + pltpu.roll(piece[(2 + par) * group : (3 + par) * group], 1, 1)
                            for par in range(2)
                        ],
                        axis=1,
                    )
                )
            total = 0.0
            for value in split_two(jnp.concatenate(rows, axis=0)):
                moved = dot(row_t_ref[...], value).astype(bf16)
                total = total + dot(moved, merge_ref[...])
            for par in range(2):
                for ch in range(channels):
                    at = (par * channels + ch) * row_pad
                    acc_ref[ch, 2 * slot + par] = total[at : at + row_pad]

        taps = channels * 27
        folded = jnp.zeros((hidden, taps), f32)
        cb = jnp.zeros((hidden, lanes), f32)
        for cls in range(8):
            rows = gconv_ref[cls * hidden : (cls + 1) * hidden]
            high, rest = split_two(rows)
            low, least = split_two(rows - high.astype(f32))
            tap = tap_ref[cls]
            folded = folded + (dot_rows(high, tap) + dot_rows(low, tap) + dot_rows(least, tap))
            cb = cb + gcb_ref[cls * hidden : (cls + 1) * hidden]
        small_ref[:, :taps] = folded
        columns = [jnp.sum(cb, axis=1, keepdims=True)]
        for ref in (gdb_ref, sq_ref):
            whole = jnp.sum(ref[...], axis=1, keepdims=True)
            columns += [whole[:hidden], whole[hidden:]]
        columns.append(jnp.zeros((hidden, small_ref.shape[1] - taps - 5), f32))
        small_ref[:, taps:] = jnp.concatenate(columns, axis=1)


def on_device(fields, target, conv_weight, conv_bias, down_weight, down_bias):
    channels, depth, row_count, col_count = fields.shape
    hidden = conv_weight.shape[0]
    out_count = down_weight.shape[0]
    pairs, half_rows, half_cols = depth // 2, row_count // 2, col_count // 2
    pair_rows = half_rows + 1
    row_pad = -(-(row_count + 2) // 16) * 16
    taps = channels * 27
    big = 8 * hidden
    win = 64 * channels
    cells = half_rows * half_cols
    cell_total = pairs * cells * lax.axis_size("gz") * lax.axis_size("gy")
    width, tile = 1024, 256

    before = shifted(fields[:, :, row_count - 1 :], "gy", 1)
    after = shifted(fields[:, :, :1], "gy", -1)
    blank = jnp.zeros((channels, depth, row_pad - row_count - 2, col_count), bf16)
    rows = jnp.concatenate([before, fields, after, blank], axis=2)
    below = shifted(rows[:, depth - 1 :], "gz", 1)
    above = shifted(rows[:, :1], "gz", -1)
    padded = jnp.concatenate([below, rows, above], axis=1)

    col = jnp.asarray(column_spread(half_cols), bf16)
    merge = jnp.asarray(column_merge(half_cols), bf16)
    row_np = row_spread(channels, pair_rows, row_pad)
    row = jnp.asarray(row_np, bf16)
    row_t = jnp.asarray(row_np.T, bf16)
    tap = jnp.asarray(tap_spread(channels), bf16)
    conv_big = jnp.concatenate([dot(conv_weight, tap[cls]) for cls in range(8)], axis=0).astype(bf16)
    conv_big_t = conv_big.T
    cbias = jnp.broadcast_to(jnp.tile(conv_bias, 8)[:, None], (big, lanes))
    dbias = jnp.broadcast_to(down_bias[:, None], (out_count, lanes))
    down = down_weight.reshape(out_count, hidden, 8).transpose(0, 2, 1).reshape(out_count, big)
    down_t = down.T
    wanted = target.transpose(1, 0, 2, 3).reshape(pairs, out_count, cells)

    sizes = (channels, pairs, pair_rows, row_pad, width, hidden, tile)
    whole = lambda *shape: pl.BlockSpec(shape, lambda z, y: (0,) * len(shape))
    out, accum, grad_down, small = pl.pallas_call(
        functools.partial(block_kernel, sizes),
        grid=(pairs, cells // width),
        in_specs=[
            whole(channels, depth + 2, row_pad, col_count),
            pl.BlockSpec((1, out_count, width), lambda z, y: (z, 0, y)),
            whole(big, win),
            whole(win, big),
            whole(big, lanes),
            whole(out_count, big),
            whole(big, out_count),
            whole(out_count, lanes),
            whole(*col.shape),
            whole(*merge.shape),
            whole(*row.shape),
            whole(*row_t.shape),
            whole(*tap.shape),
        ],
        out_specs=[
            pl.BlockSpec((1, out_count, width), lambda z, y: (z, 0, y)),
            whole(channels, depth + 2, row_pad, col_count),
            whole(out_count, big),
            whole(hidden, 256),
        ],
        out_shape=[
            jax.ShapeDtypeStruct((pairs, out_count, cells), bf16),
            jax.ShapeDtypeStruct((channels, depth + 2, row_pad, col_count), f32),
            jax.ShapeDtypeStruct((out_count, big), f32),
            jax.ShapeDtypeStruct((hidden, 256), f32),
        ],
        scratch_shapes=[
            pltpu.VMEM((pairs + 1, 16 * channels, pair_rows * lanes), bf16),
            pltpu.VMEM((pairs + 1, 16 * channels, pair_rows * lanes), f32),
            pltpu.VMEM((big, width), bf16),
            pltpu.VMEM((big, width), f32),
            pltpu.VMEM((big, width), bf16),
            pltpu.VMEM((big, win), f32),
            pltpu.VMEM((big, lanes), f32),
            pltpu.VMEM((out_count, lanes), f32),
            pltpu.VMEM((out_count, lanes), f32),
        ],
        compiler_params=pltpu.CompilerParams(vmem_limit_bytes=56 * 1024 * 1024),
        name="down_block",
    )(padded, wanted, conv_big, conv_big_t, cbias, down, down_t, dbias, col, merge, row, row_t, tap)
    out_field = out.reshape(pairs, out_count, half_rows, half_cols).transpose(1, 0, 2, 3)

    from_above = shifted(accum[:, 0].astype(bf16), "gz", -1).astype(f32)
    from_below = shifted(accum[:, depth + 1].astype(bf16), "gz", 1).astype(f32)
    core = accum[:, 1 : depth + 1]
    core = core.at[:, depth - 1].add(from_above)
    core = core.at[:, 0].add(from_below)
    from_right = shifted(core[:, :, 0].astype(bf16), "gy", -1).astype(f32)
    from_left = shifted(core[:, :, row_count + 1].astype(bf16), "gy", 1).astype(f32)
    sensitivity = core[:, :, 1 : row_count + 1]
    sensitivity = sensitivity.at[:, :, row_count - 1].add(from_right)
    sensitivity = sensitivity.at[:, :, 0].add(from_left)

    def beside(value, count):
        return jnp.concatenate(jnp.split(value, value.shape[0] // count, axis=0), axis=1)

    me = lax.axis_index("gz")
    own = grad_down
    bit = lax.axis_size("gz")
    bits = []
    while bit > 1:
        bit //= 2
        bits.append(bit)
    for bit in bits:
        count = own.shape[0] // 2
        upper = (me // bit) % 2
        keep = lax.dynamic_slice_in_dim(own, upper * count, count, 0)
        give = lax.dynamic_slice_in_dim(own, (1 - upper) * count, count, 0)
        packed = jnp.concatenate([give, beside(small, count) if count < hidden else small], axis=1)
        got = exchanged(packed, "gz", bit)
        own = keep + got[:, :big]
        small = small + jnp.concatenate(
            jnp.split(got[:, big:], hidden // count, axis=1), axis=0
        )
    bit = 1
    count = own.shape[0]
    packed = jnp.concatenate([own, beside(small, count)], axis=1)
    while bit < lax.axis_size("gy"):
        packed = packed + exchanged(packed, "gy", bit)
        bit *= 2
    own = packed[:, :big]
    small = jnp.concatenate(jnp.split(packed[:, big:], hidden // count, axis=1), axis=0)
    down_rows = own.reshape(count, 8, hidden).transpose(0, 2, 1).reshape(count, big)
    return (
        out_field,
        sensitivity,
        small[:, :taps] / cell_total,
        small[:, taps] / cell_total,
        down_rows / cell_total,
        jnp.concatenate([small[:, taps + 1], small[:, taps + 2]]) / cell_total,
        jnp.sum(small[:, taps + 3 : taps + 5]) / (out_count * cell_total),
    )


def solution(mesh):
    in_specs = (P(None, "gz", "gy", None), P(None, "gz", "gy", None), P(), P(), P(), P())
    out_specs = (
        P(None, "gz", "gy", None),
        P(None, "gz", "gy", None),
        P(),
        P(),
        P("gz", None),
        P(),
        P(),
    )
    return jax.shard_map(
        on_device, mesh=mesh, in_specs=in_specs, out_specs=out_specs, check_vma=False
    )
```

profile of v0, /device:TPU:0, one launch (start us, length us, event | category | flops | bytes accessed | tf_op | source)
XLA Modules:
  0.0 120.7 jit_solution(14102941587937008706)
XLA Ops:
  0.6 1.7 %fusion.5 = (bf16[6,8,1,256]{3,2,1,0:T(2,128)(2,1)S(1)}, bf16[6,8,1,256]{3,2,1,0:T(2,128)(2,1)}) fusion(bf16[6,8,32,256]{3,2,1,0:T(8,128)(2,1)} %param.19), kind=kLoop, calls=%fused_computation.56 | loop fusion | bytes 98304 | tf_op jit(solution)/shard_map/slice | solution.py:242
  2.4 5.0 %collective-permute-start.1 = (bf16[6,8,1,256]{3,2,1,0:T(2,128)(2,1)}, bf16[6,8,1,256]{3,2,1,0:T(2,128)(2,1)S(1)}, u32[]{:S(2)}, u32[]{:S(2)}) collective-permute-start(bf16[6,8,1,256]{3,2,1,0:T(2,128)(2,1)} %get-tuple-element.108), channel_id=1, source_target_pairs={{0,3},{1,0},{2,1},{3,2},{4,7},{5,4},{6,5},{7,6},{8,11},{9,8},{10,9... | collective-permute-start | bytes 73736 | tf_op jit(solution)/shard_map/ppermute | solution.py:20
  7.4 1.1 convolution_convert_fusion.7
  8.5 1.1 convolution_convert_fusion.6
  9.6 1.1 convolution_convert_fusion.5
  10.6 1.1 convolution_convert_fusion.4
  11.7 1.1 convolution_convert_fusion.3
  12.8 1.1 convolution_convert_fusion.2
  13.8 1.1 convolution_convert_fusion.1
  15.0 2.5 %reshape.198 = bf16[4,128,2048]{2,0,1:T(4,128)(2,1)S(1)} reshape(bf16[4,128,16,128]{3,2,0,1:T(8,128)(2,1)} %bitcast.75) | data formatting | bytes 4194304 | tf_op jit(solution)/shard_map/reshape | solution.py:262
  17.5 2.5 %copy.135.target_ref = bf16[4,128,2048]{2,1,0:T(8,128)(2,1)} copy(bf16[4,128,2048]{2,0,1:T(4,128)(2,1)S(1)} %reshape.198) | data formatting | bytes 4194304 | tf_op jit(solution)/shard_map/reshape | solution.py:262
  21.1 1.7 %collective-permute-start.3 = (bf16[6,1,48,256]{3,2,1,0:T(8,128)(2,1)S(1)}, bf16[6,1,48,256]{3,2,1,0:T(8,128)(2,1)S(1)}, u32[]{:S(2)}, u32[]{:S(2)}) collective-permute-start(bf16[6,1,48,256]{3,2,1,0:T(8,128)(2,1)S(1)} %get-tuple-element.104), channel_id=1, source_target_pairs={{0,28},{4,0},{8,4},{12,8},{16,12},{20,16},{24,20},{28,24},{1,29},{... | collective-permute-start | bytes 442376 | tf_op jit(solution)/shard_map/ppermute | solution.py:20
  22.8 0.2 convolution_convert_fusion
  23.1 0.4 concatenate.44
  23.5 0.9 copy.122.conv_ref
  24.7 0.8 copy.123.down_ref
  25.5 0.9 collective-permute-done.3
  26.4 1.9 %collective-permute-done.2 = bf16[6,1,48,256]{3,2,1,0:T(8,128)(2,1)S(1)} collective-permute-done((bf16[6,1,48,256]{3,2,1,0:T(8,128)(2,1)S(1)}, bf16[6,1,48,256]{3,2,1,0:T(8,128)(2,1)S(1)}, u32[]{:S(2)}, u32[]{:S(2)}) %collective-permute-start.2) | collective-permute-done | bytes 147488 | tf_op jit(solution)/shard_map/ppermute | solution.py:20
  28.3 1.9 %pad_maximum_fusion.field_ref = bf16[6,10,48,256]{3,2,1,0:T(8,128)(2,1)} fusion(bf16[6,1,48,256]{3,2,1,0:T(8,128)(2,1)S(1)} %collective-permute-done.3, bf16[6,8,14,256]{3,2,1,0:T(8,128)(2,1)S(1)} %broadcast_in_dim.16, bf16[6,8,1,256]{3,2,1,0:T(2,128)(2,1)S(1)} %collective-permute-done.1, bf16[6,8,32,256]{3,2,1,0:T(8,128)(2,1)S(1)} %copy-done.2, ...), kind=kLoop, calls=%fused_computation.1 | loop fusion | flops 8847360 | bytes 2949120 | tf_op jit(solution)/shard_map/concatenate | solution.py:248
  30.2 0.8 broadcast_in_dim.18.cbias_ref
  31.1 0.7 broadcast_in_dim.19.dbias_ref
  31.8 46.5 %down_block.1 = (bf16[4,128,2048]{2,1,0:T(8,128)(2,1)}, f32[6,10,48,256]{3,2,1,0:T(8,128)}, f32[128,512]{1,0:T(8,128)}, f32[64,256]{1,0:T(8,128)}) custom-call(bf16[6,10,48,256]{3,2,1,0:T(8,128)(2,1)} %pad_maximum_fusion.field_ref, bf16[4,128,2048]{2,1,0:T(8,128)(2,1)} %copy.135.target_ref, bf16[512,384]{1,0:T(8,128)(2,1)} %copy.122.conv_ref, ...), custom_call_target="tpu_custom_call" | custom-call | tf_op jit(solution)/shard_map/down_block/pallas_call | solution.py:266
  78.3 2.3 %copy.125 = f32[6,10,48,256]{3,2,0,1:T(8,128)S(1)} copy(f32[6,10,48,256]{3,2,1,0:T(8,128)} %get-tuple-element.60) | data formatting | bytes 5898240 | tf_op jit(solution)/shard_map/down_block/pallas_call | solution.py:266
  80.5 0.5 copy-done.1
  81.0 0.2 convert.52
  81.2 1.4 %copy-done.4 = bf16[4,128,2048]{2,1,0:T(8,128)(2,1)S(1)} copy-done((bf16[4,128,2048]{2,1,0:T(8,128)(2,1)S(1)}, bf16[4,128,2048]{2,1,0:T(8,128)(2,1)}, u32[]{:S(2)}) %copy-start.4) | copy-done | bytes 2097176
  82.6 0.6 copy.137
  83.2 2.0 %copy_bitcast_fusion = bf16[128,4,16,128]{3,2,1,0:T(8,128)(2,1)} fusion(bf16[4,128,16,128]{3,2,1,0:T(8,128)(2,1)S(1)} %bitcast.73), kind=kLoop, calls=%fused_computation | loop fusion | bytes 4194304 | tf_op jit(solution)/shard_map/transpose | solution.py:310
  85.4 0.9 collective-permute-start.4
  86.4 0.9 collective-permute-start.8
  87.3 2.3 %collective-permute-done.4 = bf16[6,48,256]{2,1,0:T(8,128)(2,1)S(1)} collective-permute-done((bf16[6,48,256]{2,1,0:T(8,128)(2,1)S(1)}, bf16[6,48,256]{2,1,0:T(8,128)(2,1)S(1)}, u32[]{:S(2)}, u32[]{:S(2)}) %collective-permute-start.4) | collective-permute-done | bytes 147488 | tf_op jit(solution)/shard_map/ppermute | solution.py:20
  89.6 2.3 %collective-permute-done.5 = bf16[6,48,256]{2,1,0:T(8,128)(2,1)S(1)} collective-permute-done((bf16[6,48,256]{2,1,0:T(8,128)(2,1)S(1)}, bf16[6,48,256]{2,1,0:T(8,128)(2,1)S(1)}, u32[]{:S(2)}, u32[]{:S(2)}) %collective-permute-start.5) | collective-permute-done | bytes 147488 | tf_op jit(solution)/shard_map/ppermute | solution.py:20
  92.0 0.2 slice.248
  92.4 3.9 %collective-permute-start.6 = (bf16[6,8,256]{2,1,0:T(8,128)(2,1)S(1)}, bf16[6,8,256]{2,1,0:T(8,128)(2,1)S(1)}, u32[]{:S(2)}, u32[]{:S(2)}) collective-permute-start(bf16[6,8,256]{2,1,0:T(8,128)(2,1)S(1)} %bitcast.90), channel_id=1, source_target_pairs={{0,3},{1,0},{2,1},{3,2},{4,7},{5,4},{6,5},{7,6},{8,11},{9,8},{10,9... | collective-permute-start | bytes 73736 | tf_op jit(solution)/shard_map/ppermute | solution.py:20
  96.5 1.3 %collective-permute-done.6 = bf16[6,8,256]{2,1,0:T(8,128)(2,1)S(1)} collective-permute-done((bf16[6,8,256]{2,1,0:T(8,128)(2,1)S(1)}, bf16[6,8,256]{2,1,0:T(8,128)(2,1)S(1)}, u32[]{:S(2)}, u32[]{:S(2)}) %collective-permute-start.6) | collective-permute-done | bytes 24608 | tf_op jit(solution)/shard_map/ppermute | solution.py:20
  97.8 3.6 %collective-permute-done.9 = f32[32,1024]{1,0:T(8,128)S(1)} collective-permute-done((f32[32,1024]{1,0:T(8,128)S(1)}, f32[32,1024]{1,0:T(8,128)S(1)}, u32[]{:S(2)}, u32[]{:S(2)}) %collective-permute-start.9) | collective-permute-done | bytes 131104 | tf_op jit(solution)/shard_map/ppermute | solution.py:25
  101.7 1.2 collective-permute-done.10
  103.1 2.1 %scatter-add.16 = f32[6,8,32,256]{3,2,0,1:T(8,128)S(1)} dynamic-update-slice(f32[6,8,32,256]{3,2,0,1:T(8,128)S(1)} %slice.248, f32[6,8,1,256]{3,2,0,1:T(1,128)S(1)} %slice_add_fusion.6, s32[]{:T(128)} %constant.183.clone.1, s32[]{:T(128)} %constant.183.clone.1, s32[]{:T(128)} %constant.185.clone.1, s32[]{:T(128)} %constant.183.clone.1) | dynamic-update-slice | bytes 98308 | tf_op jit(solution)/shard_map/scatter-add | solution.py:320
  105.2 2.7 %collective-permute-done.11 = f32[16,1536]{1,0:T(8,128)S(1)} collective-permute-done((f32[16,1536]{1,0:T(8,128)S(1)}, f32[16,1536]{1,0:T(8,128)S(1)}, u32[]{:S(2)}, u32[]{:S(2)}) %collective-permute-start.11) | collective-permute-done | bytes 98336 | tf_op jit(solution)/shard_map/ppermute | solution.py:25
  107.9 2.7 %collective-permute-start.12 = (f32[16,1536]{1,0:T(8,128)S(1)}, f32[16,1536]{1,0:T(8,128)S(1)}, u32[]{:S(2)}, u32[]{:S(2)}) collective-permute-start(f32[16,1536]{1,0:T(8,128)S(1)} %add.102), channel_id=1, source_target_pairs={{0,2},{1,3},{2,0},{3,1},{4,6},{5,7},{6,4},{7,5},{8,10},{9,11},{10,... | collective-permute-start | bytes 294920 | tf_op jit(solution)/shard_map/ppermute | solution.py:25
  110.7 2.1 %scatter-add.19 = f32[6,8,32,256]{3,2,0,1:T(8,128)S(1)} dynamic-update-slice(f32[6,8,32,256]{3,2,0,1:T(8,128)S(1)} %scatter-add.16, f32[6,8,1,256]{3,2,0,1:T(1,128)S(1)} %slice_add_fusion.5, s32[]{:T(128)} %constant.183.clone.1, s32[]{:T(128)} %constant.183.clone.1, s32[]{:T(128)} %constant.183.clone.1, s32[]{:T(128)} %constant.183.clone.1) | dynamic-update-slice | bytes 98308 | tf_op jit(solution)/shard_map/scatter-add | solution.py:321
  112.8 1.3 %copy.133 = f32[6,8,32,256]{3,2,1,0:T(8,128)} copy(f32[6,8,32,256]{3,2,0,1:T(8,128)S(1)} %scatter-add.19) | data formatting | bytes 3145728
  114.0 1.3 %collective-permute-done.12 = f32[16,1536]{1,0:T(8,128)S(1)} collective-permute-done((f32[16,1536]{1,0:T(8,128)S(1)}, f32[16,1536]{1,0:T(8,128)S(1)}, u32[]{:S(2)}, u32[]{:S(2)}) %collective-permute-start.12) | collective-permute-done | bytes 98336 | tf_op jit(solution)/shard_map/ppermute | solution.py:25
  115.4 0.6 slice_multiply_fusion
  116.0 0.7 slice_reduce_fusion.2
  116.7 0.7 slice_reduce_fusion
  117.6 0.7 copy.134
  118.4 0.6 maximum_multiply_fusion
  (88 shorter events, 2.8 us)
Async XLA Ops:
  0.6 6.8 %copy-start = (bf16[64,162]{1,0:T(8,128)(2,1)S(1)}, bf16[64,162]{1,0:T(8,128)(2,1)}, u32[]{:S(2)}) copy-start(bf16[64,162]{1,0:T(8,128)(2,1)} %param.21) | copy-start | bytes 62212
  2.4 18.5 %collective-permute-start.1 = (bf16[6,8,1,256]{3,2,1,0:T(2,128)(2,1)}, bf16[6,8,1,256]{3,2,1,0:T(2,128)(2,1)S(1)}, u32[]{:S(2)}, u32[]{:S(2)}) collective-permute-start(bf16[6,8,1,256]{3,2,1,0:T(2,128)(2,1)} %get-tuple-element.108), channel_id=1, source_target_pairs={{0,3},{1,0},{2,1},{3,2},{4,7},{5,4},{6,5},{7,6},{8,11},{9,8},{10,9... | collective-permute-start | bytes 73736 | tf_op jit(solution)/shard_map/ppermute | solution.py:20
  7.4 13.5 %collective-permute-start = (bf16[6,8,1,256]{3,2,1,0:T(2,128)(2,1)S(1)}, bf16[6,8,1,256]{3,2,1,0:T(2,128)(2,1)S(1)}, u32[]{:S(2)}, u32[]{:S(2)}) collective-permute-start(bf16[6,8,1,256]{3,2,1,0:T(2,128)(2,1)S(1)} %get-tuple-element.107), channel_id=1, source_target_pairs={{0,1},{1,2},{2,3},{3,0},{4,5},{5,6},{6,7},{7,4},{8,9},{9,10},{10,1... | collective-permute-start | bytes 73736 | tf_op jit(solution)/shard_map/ppermute | solution.py:20
  17.5 3.5 %copy-start.2 = (bf16[6,8,32,256]{3,2,1,0:T(8,128)(2,1)S(1)}, bf16[6,8,32,256]{3,2,1,0:T(8,128)(2,1)}, u32[]{:S(2)}) copy-start(bf16[6,8,32,256]{3,2,1,0:T(8,128)(2,1)} %param.19) | copy-start | bytes 2359300
  20.0 2.8 %copy-start.9 = (bf16[162,384]{1,0:T(8,128)(2,1)S(1)}, bf16[162,384]{1,0:T(8,128)(2,1)}, u32[]{:S(2)}) copy-start(bf16[162,384]{1,0:T(8,128)(2,1)} %constant.220) | copy-start | bytes 373252
  20.5 4.0 %copy-start.11 = (f32[64]{0:T(128)S(1)}, f32[64]{0:T(128)}, u32[]{:S(2)}) copy-start(f32[64]{0:T(128)} %param.22) | copy-start | bytes 772
  20.5 4.0 %copy-start.8 = (bf16[128,512]{1,0:T(8,128)(2,1)S(1)}, bf16[128,512]{1,0:T(8,128)(2,1)}, u32[]{:S(2)}) copy-start(bf16[128,512]{1,0:T(8,128)(2,1)} %param.23) | copy-start | bytes 393220
  21.1 5.3 %collective-permute-start.3 = (bf16[6,1,48,256]{3,2,1,0:T(8,128)(2,1)S(1)}, bf16[6,1,48,256]{3,2,1,0:T(8,128)(2,1)S(1)}, u32[]{:S(2)}, u32[]{:S(2)}) collective-permute-start(bf16[6,1,48,256]{3,2,1,0:T(8,128)(2,1)S(1)} %get-tuple-element.104), channel_id=1, source_target_pairs={{0,28},{4,0},{8,4},{12,8},{16,12},{20,16},{24,20},{28,24},{1,29},{... | collective-permute-start | bytes 442376 | tf_op jit(solution)/shard_map/ppermute | solution.py:20
  22.8 5.5 %collective-permute-start.2 = (bf16[6,1,48,256]{3,2,1,0:T(8,128)(2,1)S(1)}, bf16[6,1,48,256]{3,2,1,0:T(8,128)(2,1)S(1)}, u32[]{:S(2)}, u32[]{:S(2)}) collective-permute-start(bf16[6,1,48,256]{3,2,1,0:T(8,128)(2,1)S(1)} %get-tuple-element.103), channel_id=1, source_target_pairs={{0,4},{4,8},{8,12},{12,16},{16,20},{20,24},{24,28},{28,0},{1,5},{5... | collective-permute-start | bytes 442376 | tf_op jit(solution)/shard_map/ppermute | solution.py:20
  23.5 7.6 %copy-start.3 = (bf16[512,384]{0,1:T(8,128)(2,1)}, bf16[512,384]{0,1:T(8,128)(2,1)S(1)}, u32[]{:S(2)}) copy-start(bf16[512,384]{0,1:T(8,128)(2,1)S(1)} %concatenate.44) | copy-start | bytes 1179652
  23.5 7.5 %copy-start.10 = (f32[128]{0:T(128)S(1)}, f32[128]{0:T(128)}, u32[]{:S(2)}) copy-start(f32[128]{0:T(128)} %param.24) | copy-start | bytes 1540
  24.7 7.1 %copy-start.5 = (bf16[128,8,64]{0,2,1:T(8,128)(2,1)}, bf16[128,8,64]{0,2,1:T(8,128)(2,1)S(1)}, u32[]{:S(2)}) copy-start(bf16[128,8,64]{0,2,1:T(8,128)(2,1)S(1)} %copy.121) | copy-start | bytes 393220
  78.3 2.7 %copy-start.1 = (f32[6,10,48,256]{3,2,1,0:T(8,128)S(1)}, f32[6,10,48,256]{3,2,1,0:T(8,128)}, u32[]{:S(2)}) copy-start(f32[6,10,48,256]{3,2,1,0:T(8,128)} %get-tuple-element.60) | copy-start | bytes 8847364
  81.0 1.6 %copy-start.4 = (bf16[4,128,2048]{2,1,0:T(8,128)(2,1)S(1)}, bf16[4,128,2048]{2,1,0:T(8,128)(2,1)}, u32[]{:S(2)}) copy-start(bf16[4,128,2048]{2,1,0:T(8,128)(2,1)} %get-tuple-element.59) | copy-start | bytes 6291460
  85.2 1.1 copy-start.6
  85.2 1.1 copy-start.7
  85.4 4.2 %collective-permute-start.4 = (bf16[6,48,256]{2,1,0:T(8,128)(2,1)S(1)}, bf16[6,48,256]{2,1,0:T(8,128)(2,1)S(1)}, u32[]{:S(2)}, u32[]{:S(2)}) collective-permute-start(bf16[6,48,256]{2,1,0:T(8,128)(2,1)S(1)} %get-tuple-element.102), channel_id=1, source_target_pairs={{0,28},{4,0},{8,4},{12,8},{16,12},{20,16},{24,20},{28,24},{1,29},{... | collective-permute-start | bytes 442376 | tf_op jit(solution)/shard_map/ppermute | solution.py:20
  86.3 5.6 %collective-permute-start.5 = (bf16[6,48,256]{2,1,0:T(8,128)(2,1)S(1)}, bf16[6,48,256]{2,1,0:T(8,128)(2,1)S(1)}, u32[]{:S(2)}, u32[]{:S(2)}) collective-permute-start(bf16[6,48,256]{2,1,0:T(8,128)(2,1)S(1)} %get-tuple-element.101), channel_id=1, source_target_pairs={{0,4},{4,8},{8,12},{12,16},{16,20},{20,24},{24,28},{28,0},{1,5},{5... | collective-permute-start | bytes 442376 | tf_op jit(solution)/shard_map/ppermute | solution.py:20
  86.4 9.9 %collective-permute-start.8 = (f32[64,768]{1,0:T(8,128)S(1)}, f32[64,768]{1,0:T(8,128)S(1)}, u32[]{:S(2)}, u32[]{:S(2)}) collective-permute-start(f32[64,768]{1,0:T(8,128)S(1)} %pad_maximum_fusion.1), channel_id=1, source_target_pairs={{0,16},{4,20},{8,24},{12,28},{16,0},{20,4},{24,8},{28,12},{1,17},{... | collective-permute-start | bytes 589832 | tf_op jit(solution)/shard_map/ppermute | solution.py:25
  92.4 5.4 %collective-permute-start.6 = (bf16[6,8,256]{2,1,0:T(8,128)(2,1)S(1)}, bf16[6,8,256]{2,1,0:T(8,128)(2,1)S(1)}, u32[]{:S(2)}, u32[]{:S(2)}) collective-permute-start(bf16[6,8,256]{2,1,0:T(8,128)(2,1)S(1)} %bitcast.90), channel_id=1, source_target_pairs={{0,3},{1,0},{2,1},{3,2},{4,7},{5,4},{6,5},{7,6},{8,11},{9,8},{10,9... | collective-permute-start | bytes 73736 | tf_op jit(solution)/shard_map/ppermute | solution.py:20
  96.3 6.8 %collective-permute-start.7 = (bf16[6,8,256]{2,1,0:T(8,128)(2,1)S(1)}, bf16[6,8,256]{2,1,0:T(8,128)(2,1)S(1)}, u32[]{:S(2)}, u32[]{:S(2)}) collective-permute-start(bf16[6,8,256]{2,1,0:T(8,128)(2,1)S(1)} %bitcast.89), channel_id=1, source_target_pairs={{0,1},{1,2},{2,3},{3,0},{4,5},{5,6},{6,7},{7,4},{8,9},{9,10},{10,1... | collective-permute-start | bytes 73736 | tf_op jit(solution)/shard_map/ppermute | solution.py:20
  96.4 5.0 %collective-permute-start.9 = (f32[32,1024]{1,0:T(8,128)S(1)}, f32[32,1024]{1,0:T(8,128)S(1)}, u32[]{:S(2)}, u32[]{:S(2)}) collective-permute-start(f32[32,1024]{1,0:T(8,128)S(1)} %pad_maximum_fusion.6), channel_id=1, source_target_pairs={{0,8},{4,12},{8,0},{12,4},{16,24},{20,28},{24,16},{28,20},{1,9},{5... | collective-permute-start | bytes 393224 | tf_op jit(solution)/shard_map/ppermute | solution.py:25
  101.5 1.4 %collective-permute-start.10 = (f32[16,1536]{1,0:T(8,128)S(1)}, f32[16,1536]{1,0:T(8,128)S(1)}, u32[]{:S(2)}, u32[]{:S(2)}) collective-permute-start(f32[16,1536]{1,0:T(8,128)S(1)} %constant_dynamic-update-slice_fusion), channel_id=1, source_target_pairs={{0,4},{4,0},{8,12},{12,8},{16,20},{20,16},{24,28},{28,24},{1,5},{5... | collective-permute-start | bytes 294920 | tf_op jit(solution)/shard_map/ppermute | solution.py:25
  103.0 4.9 %collective-permute-start.11 = (f32[16,1536]{1,0:T(8,128)S(1)}, f32[16,1536]{1,0:T(8,128)S(1)}, u32[]{:S(2)}, u32[]{:S(2)}) collective-permute-start(f32[16,1536]{1,0:T(8,128)S(1)} %constant_dynamic-update-slice_fusion.4), channel_id=1, source_target_pairs={{0,1},{1,0},{2,3},{3,2},{4,5},{5,4},{6,7},{7,6},{8,9},{9,8},{10,11... | collective-permute-start | bytes 294920 | tf_op jit(solution)/shard_map/ppermute | solution.py:25
  107.9 7.4 %collective-permute-start.12 = (f32[16,1536]{1,0:T(8,128)S(1)}, f32[16,1536]{1,0:T(8,128)S(1)}, u32[]{:S(2)}, u32[]{:S(2)}) collective-permute-start(f32[16,1536]{1,0:T(8,128)S(1)} %add.102), channel_id=1, source_target_pairs={{0,2},{1,3},{2,0},{3,1},{4,6},{5,7},{6,4},{7,5},{8,10},{9,11},{10,... | collective-permute-start | bytes 294920 | tf_op jit(solution)/shard_map/ppermute | solution.py:25
where the time goes:
time: 121 us
  Pallas kernels  46.5 us (38%)
  local copies, waits for them, and re-layouts  25.3 us (21%)
  waiting for transfers between devices  17.6 us (15%)
  starting transfers between devices  15.3 us (13%)
  matrix products  7.61 us (6%)
  other arithmetic  5.34 us (4%)
  between operations  3.02 us (2%)
    pallas_call x1, Pallas kernels, on_device(): pl.pallas_call(functools.partial(block_kernel, sizes), grid=(pairs, cells...  46.5 us
    ppermute x8, starting transfers between devices, shifted(): lax.ppermute(value, axis, [(i, (i + by) % count) for i in range(count)])  11.5 us
    ppermute x5, waiting for transfers between devices, exchanged(): return lax.ppermute(value, axis, [(i, i ^ bit) for i in range(count)])  8.85 us
    ppermute x8, waiting for transfers between devices, shifted(): lax.ppermute(value, axis, [(i, (i + by) % count) for i in range(count)])  8.76 us
    dot_general x8, matrix products, dot(): return jnp.dot(a, b, preferred_element_type=f32)  7.61 us
    reshape x2, local copies, waits for them, and re-layouts, on_device(): wanted = target.transpose(1, 0, 2, 3).reshape(pairs, out_count, cells)  5.02 us
    unnamed x35, local copies, waits for them, and re-layouts  4.66 us
    ppermute x5, starting transfers between devices, exchanged(): return lax.ppermute(value, axis, [(i, i ^ bit) for i in range(count)])  3.8 us
  transfers between devices with their start and end apart: 13, of which 9 were waited for; matrix products, arithmetic and copies ran while one was open for 18% of the time, Pallas kernels for 0%

commit v1 on v0

v1 whole, which is shorter than its diff:
```python
import functools

import jax
import jax.numpy as jnp
import numpy as np
from jax import lax
from jax.experimental import pallas as pl
from jax.experimental.pallas import tpu as pltpu
from jax.sharding import PartitionSpec as P

gelu_scale = 0.7978845608028654
gelu_cubic = 0.044715
lanes = 128
bf16 = jnp.bfloat16
f32 = jnp.float32


def shifted(value, axis, by):
    count = lax.axis_size(axis)
    return lax.ppermute(value, axis, [(i, (i + by) % count) for i in range(count)])


def exchanged(value, axis, bit):
    count = lax.axis_size(axis)
    return lax.ppermute(value, axis, [(i, i ^ bit) for i in range(count)])


def column_spread(half_cols):
    spread = np.zeros((2 * half_cols, 4 * half_cols), np.float32)
    for step in range(2):
        for par in range(2):
            for col in range(half_cols):
                source = (2 * ((col + step) % half_cols) + par - 1) % (2 * half_cols)
                spread[source, (2 * step + par) * half_cols + col] = 1
    return spread


def column_merge(half_cols):
    merge = np.zeros((2 * half_cols, 2 * half_cols), np.float32)
    for par in range(2):
        for col in range(half_cols):
            merge[par * half_cols + col, (2 * col + par - 1) % (2 * half_cols)] = 1
    return merge


def row_spread(channels, row_count):
    pair_rows = row_count // 2 + 1
    core = np.zeros((pair_rows * 4 * channels, 2 * channels * row_count), np.float32)
    edge = np.zeros((8 * channels, 32), np.float32)
    for par_z in range(2):
        for ch in range(channels):
            for at in range(1, row_count + 1):
                target = ((at // 2 * 2 + par_z) * 2 + at % 2) * channels + ch
                core[target, (par_z * channels + ch) * row_count + at - 1] = 1
            edge[(par_z * 2) * channels + ch, par_z * 16 + ch] = 1
            edge[((2 + par_z) * 2 + 1) * channels + ch, par_z * 16 + 8 + ch] = 1
    return core, edge


def tap_spread(channels):
    spread = np.zeros((8, channels * 27, 64 * channels), np.float32)
    for cls in range(8):
        par_z, par_y, par_x = cls // 4, cls // 2 % 2, cls % 2
        for ch in range(channels):
            for off_z in range(3):
                for off_y in range(3):
                    for off_x in range(3):
                        at_z, at_y, at_x = par_z + off_z, par_y + off_y, par_x + off_x
                        place = (at_z // 2 * 2 + at_y // 2) * 2 + at_x // 2
                        place = ((place * 2 + at_x % 2) * 2 + at_z % 2) * 2 + at_y % 2
                        spread[cls, ch * 27 + 9 * off_z + 3 * off_y + off_x, place * channels + ch] = 1
    return spread


def class_order(hidden):
    order = np.zeros((8 * hidden, 8 * hidden), np.float32)
    for ch in range(hidden):
        for cls in range(8):
            order[ch * 8 + cls, cls * hidden + ch] = 1
    return order


def dot(a, b):
    return jnp.dot(a, b, preferred_element_type=f32)


def dot_rows(a, b):
    return lax.dot_general(a, b, (((1,), (1,)), ((), ())), preferred_element_type=f32)


def split_two(value):
    high = value.astype(bf16)
    return high, (value - high.astype(f32)).astype(bf16)


def split_three(value):
    high = value.astype(bf16)
    return (high,) + split_two(value - high.astype(f32))


def conv_rows(conv_ref, tap_ref):
    return jnp.concatenate([dot(conv_ref[...], tap_ref[cls]) for cls in range(8)], axis=0)


def row_of(ref, count):
    return jnp.transpose(jnp.broadcast_to(ref[...], (lanes, count)))


def forward_kernel(
    sizes,
    field_ref,
    below_ref,
    above_ref,
    before_ref,
    after_ref,
    target_ref,
    conv_weight_ref,
    conv_bias_ref,
    down_weight_ref,
    down_bias_ref,
    tap_ref,
    order_ref,
    col_ref,
    row_ref,
    edge_ref,
    out_ref,
    gpre_ref,
    gdown_ref,
    small_ref,
    split_ref,
    conv_ref,
    down_ref,
    down_t_ref,
    gconv_ref,
    gcb_ref,
    gdb_ref,
    sq_ref,
):
    channels, pairs, half_rows, hidden, out_count, tile = sizes
    group = 4 * channels
    cells = half_rows * lanes
    step = pl.program_id(0)

    @pl.when(step == 0)
    def _():
        gdown_ref[...] = jnp.zeros_like(gdown_ref)
        gconv_ref[...] = jnp.zeros_like(gconv_ref)
        gcb_ref[...] = jnp.zeros_like(gcb_ref)
        gdb_ref[...] = jnp.zeros_like(gdb_ref)
        sq_ref[...] = jnp.zeros_like(sq_ref)
        conv_ref[...] = conv_rows(conv_weight_ref, tap_ref).astype(bf16)
        down = dot(down_weight_ref[...], order_ref[...])
        down_ref[...] = down.astype(bf16)
        down_t_ref[...] = jnp.transpose(down).astype(bf16)
        for slot in range(pairs + 1):
            lower = below_ref if slot == 0 else field_ref.at[:, 2 * slot - 1]
            upper = above_ref if slot == pairs else field_ref.at[:, 2 * slot]
            rows = [ref[ch] for ref in (lower, upper) for ch in range(channels)]
            rows = dot(jnp.concatenate(rows, axis=0), col_ref[...]).astype(bf16)
            rows = dot(row_ref[...], rows)
            sides = [ref[2 * slot + par].astype(f32) for par in range(2) for ref in (before_ref, after_ref)]
            sides = jnp.concatenate(sides, axis=0).astype(bf16)
            sides = dot(edge_ref[...], dot(sides, col_ref[...]).astype(bf16))
            for row in range(half_rows + 1):
                piece = rows[row * group : (row + 1) * group]
                if row == 0:
                    piece = piece + sides[:group]
                if row == half_rows:
                    piece = piece + sides[group:]
                piece = [piece[:, v * lanes : (v + 1) * lanes] for v in range(4)]
                split_ref[slot, :, row * lanes : (row + 1) * lanes] = jnp.concatenate(
                    piece, axis=0
                ).astype(bf16)

    conv_bias = row_of(conv_bias_ref, hidden)
    conv_bias = jnp.concatenate([conv_bias] * 8, axis=0)
    conv_bias = jnp.concatenate([conv_bias] * (tile // lanes), axis=1)
    down_bias = row_of(down_bias_ref, out_count)
    down_bias = jnp.concatenate([down_bias] * (tile // lanes), axis=1)
    wanted = jnp.swapaxes(target_ref[:, 0].astype(f32), 0, 1)
    outputs = []
    for part in range(cells // tile):
        here = slice(part * tile, (part + 1) * tile)
        window = jnp.concatenate(
            [
                split_ref[step + dz, :, part * tile + dy * lanes : (part + 1) * tile + dy * lanes]
                for dz in range(2)
                for dy in range(2)
            ],
            axis=0,
        )
        pre = dot(conv_ref[...], window) + conv_bias
        square = pre * pre
        tangent = jnp.tanh(pre * (square * (gelu_scale * gelu_cubic) + gelu_scale))
        half = 0.5 * tangent + 0.5
        hid = (pre * half).astype(bf16)
        bend = pre * (square * (6.0 * gelu_scale * gelu_cubic) + 2.0 * gelu_scale)
        slope = half * (bend * (1.0 - half)) + half
        output = dot(down_ref[...], hid) + down_bias
        outputs += [output[:, k * lanes : (k + 1) * lanes] for k in range(tile // lanes)]
        first = part * tile // lanes
        diff = output - jnp.concatenate([wanted[first + k] for k in range(tile // lanes)], axis=1)
        grad_out = diff.astype(bf16)
        gdown_ref[...] += dot_rows(grad_out, hid)
        for k in range(tile // lanes):
            piece = diff[:, k * lanes : (k + 1) * lanes]
            gdb_ref[...] += piece
            sq_ref[...] += piece * piece
        back = dot(down_t_ref[...], grad_out)
        grad_pre = (back * slope).astype(bf16)
        gpre_ref[0, :, here] = grad_pre
        for k in range(tile // lanes):
            gcb_ref[...] += grad_pre[:, k * lanes : (k + 1) * lanes].astype(f32)
        gconv_ref[...] += dot_rows(grad_pre, window)
    out_ref[:, 0] = jnp.swapaxes(jnp.stack(outputs, axis=0), 0, 1).astype(bf16)

    @pl.when(step == pairs - 1)
    def _():
        taps = channels * 27
        folded = jnp.zeros((hidden, taps), f32)
        cb = jnp.zeros((hidden, lanes), f32)
        for cls in range(8):
            tap = tap_ref[cls]
            for piece in split_three(gconv_ref[cls * hidden : (cls + 1) * hidden]):
                folded = folded + dot_rows(piece, tap)
            cb = cb + gcb_ref[cls * hidden : (cls + 1) * hidden]
        small_ref[:, :taps] = folded
        columns = [jnp.sum(cb, axis=1, keepdims=True)]
        for ref in (gdb_ref, sq_ref):
            whole = jnp.sum(ref[...], axis=1, keepdims=True)
            columns += [whole[:hidden], whole[hidden:]]
        columns.append(jnp.zeros((hidden, small_ref.shape[1] - taps - 5), f32))
        small_ref[:, taps:] = jnp.concatenate(columns, axis=1)


def spread_kernel(
    sizes,
    gpre_ref,
    conv_weight_ref,
    tap_ref,
    merge_ref,
    row_t_ref,
    edge_t_ref,
    sens_ref,
    below_ref,
    above_ref,
    before_ref,
    after_ref,
    spread_ref,
    conv_t_ref,
):
    channels, pairs, half_rows, tile = sizes
    group = 4 * channels
    span = 4 * group
    row_count = 2 * half_rows
    cells = half_rows * lanes
    step = pl.program_id(0)

    @pl.when(step == 0)
    def _():
        spread_ref[...] = jnp.zeros_like(spread_ref)
        conv_t_ref[...] = jnp.transpose(conv_rows(conv_weight_ref, tap_ref)).astype(bf16)

    for part in range(cells // tile):
        spread = dot(conv_t_ref[...], gpre_ref[0, :, part * tile : (part + 1) * tile])
        for dz in range(2):
            for dy in range(2):
                at = (2 * dz + dy) * span
                here = slice(part * tile + dy * lanes, (part + 1) * tile + dy * lanes)
                spread_ref[step + dz, :, here] += spread[at : at + span]

    def finish(slot, store):
        rows = []
        for row in range(half_rows + 1):
            piece = spread_ref[slot, :, row * lanes : (row + 1) * lanes]
            halves = [
                piece[par * group : (par + 1) * group]
                + pltpu.roll(piece[(2 + par) * group : (3 + par) * group], 1, 1)
                for par in range(2)
            ]
            rows.append(jnp.concatenate(halves, axis=1))
        core, sides = 0.0, 0.0
        outer = jnp.concatenate([rows[0], rows[half_rows]], axis=0)
        for value in split_two(jnp.concatenate(rows, axis=0)):
            core = core + dot(dot(row_t_ref[...], value).astype(bf16), merge_ref[...])
        for value in split_two(outer):
            sides = sides + dot(dot(edge_t_ref[...], value).astype(bf16), merge_ref[...])
        for par in range(2):
            before_ref[2 * slot + par] = sides[par * 16 : par * 16 + 8].astype(bf16)
            after_ref[2 * slot + par] = sides[par * 16 + 8 : par * 16 + 16].astype(bf16)
            for ch in range(channels):
                at = (par * channels + ch) * row_count
                store(2 * slot + par, ch, core[at : at + row_count])

    def store_first(at, ch, value):
        if at == 0:
            below_ref[ch] = value.astype(bf16)
        else:
            sens_ref[ch, at - 1] = value

    def store_middle(at, ch, value):
        sens_ref[ch, at - 1] = value

    def store_last(at, ch, value):
        if at == 2 * pairs + 1:
            above_ref[ch] = value.astype(bf16)
        else:
            sens_ref[ch, at - 1] = value

    @pl.when(step == 0)
    def _():
        finish(0, store_first)

    @pl.when(step > 0)
    def _():
        finish(step, store_middle)

    @pl.when(step == pairs - 1)
    def _():
        finish(pairs, store_last)


def join_kernel(sizes, sens_ref, below_ref, above_ref, before_ref, after_ref, out_ref):
    channels, depth, row_count = sizes
    out_ref[...] = sens_ref[...]
    for ch in range(channels):
        for z in range(depth):
            out_ref[ch, z, 0:1] += after_ref[z + 1, ch : ch + 1].astype(f32)
            out_ref[ch, z, row_count - 1 : row_count] += before_ref[z + 1, ch : ch + 1].astype(f32)
        out_ref[ch, 0] += above_ref[ch].astype(f32)
        out_ref[ch, depth - 1] += below_ref[ch].astype(f32)


def last_kernel(sizes, small_ref, down_ref, order_ref, conv_out, cbias_out, down_out, dbias_out, loss_out):
    hidden, taps, cell_total, out_count = sizes
    scale = 1.0 / cell_total
    small = small_ref[...]
    conv_out[...] = small[:, :taps] * scale
    turned = jnp.transpose(small[:, lanes : 2 * lanes])
    at = taps - lanes
    cbias_out[...] = turned[at : at + 1] * scale
    dbias_out[...] = jnp.concatenate([turned[at + 1 : at + 2], turned[at + 2 : at + 3]], axis=1) * scale
    squares = jnp.sum(turned[at + 3 : at + 4] + turned[at + 4 : at + 5], axis=1, keepdims=True)
    loss_out[...] = squares * (scale / out_count)
    rows = 0.0
    for piece in split_three(down_ref[...]):
        rows = rows + dot_rows(piece, order_ref[...])
    down_out[...] = rows * scale


def call(kernel, sizes, out_shape, *args, grid=None, in_specs=None, out_specs=None, scratch=(), flops=0, name):
    if grid is None:
        in_specs = [pl.BlockSpec(memory_space=pltpu.VMEM)] * len(args)
        out_specs = [pl.BlockSpec(memory_space=pltpu.VMEM)] * len(out_shape)
    return pl.pallas_call(
        functools.partial(kernel, sizes),
        out_shape=out_shape,
        in_specs=in_specs,
        out_specs=out_specs,
        scratch_shapes=scratch,
        compiler_params=pltpu.CompilerParams(vmem_limit_bytes=56 * 1024 * 1024),
        cost_estimate=pl.CostEstimate(
            flops=flops,
            bytes_accessed=sum(a.size * a.dtype.itemsize for a in (*args, *out_shape)),
            transcendentals=0,
        ),
        name=name,
        **({} if grid is None else {"grid": grid}),
    )(*args)


def whole(shape):
    return pl.BlockSpec(tuple(shape), lambda z: (0,) * len(shape))


def constants(channels, row_count, half_cols, hidden):
    core, edge = row_spread(channels, row_count)
    names = {
        "col": column_spread(half_cols),
        "merge": column_merge(half_cols),
        "row": core,
        "row_t": core.T,
        "edge": edge,
        "edge_t": edge.T,
        "tap": tap_spread(channels),
        "order": class_order(hidden),
    }
    return {name: jnp.asarray(value, bf16) for name, value in names.items()}


def forward(fields, below, above, before, after, target, conv_weight, conv_bias, down_weight, down_bias, fixed):
    channels, depth, row_count, col_count = fields.shape
    hidden, out_count = conv_weight.shape[0], down_weight.shape[0]
    pairs, half_rows, half_cols = depth // 2, row_count // 2, col_count // 2
    cells = half_rows * half_cols
    big, win = 8 * hidden, 64 * channels
    args = (
        fields, below, above, before, after, target,
        conv_weight, conv_bias[None], down_weight, down_bias[None],
        fixed["tap"], fixed["order"], fixed["col"], fixed["row"], fixed["edge"],
    )
    slab = pl.BlockSpec((out_count, 1, half_rows, half_cols), lambda z: (0, z, 0, 0))
    return call(
        forward_kernel,
        (channels, pairs, half_rows, hidden, out_count, forward_tile),
        [
            jax.ShapeDtypeStruct(target.shape, bf16),
            jax.ShapeDtypeStruct((pairs, big, cells), bf16),
            jax.ShapeDtypeStruct((out_count, big), f32),
            jax.ShapeDtypeStruct((hidden, 2 * lanes), f32),
        ],
        *args,
        grid=(pairs,),
        in_specs=[slab if i == 5 else whole(a.shape) for i, a in enumerate(args)],
        out_specs=[
            slab,
            pl.BlockSpec((1, big, cells), lambda z: (z, 0, 0)),
            whole((out_count, big)),
            whole((hidden, 2 * lanes)),
        ],
        scratch=[
            pltpu.VMEM((pairs + 1, 16 * channels, cells + lanes), bf16),
            pltpu.VMEM((big, win), bf16),
            pltpu.VMEM((out_count, big), bf16),
            pltpu.VMEM((big, out_count), bf16),
            pltpu.VMEM((big, win), f32),
            pltpu.VMEM((big, lanes), f32),
            pltpu.VMEM((out_count, lanes), f32),
            pltpu.VMEM((out_count, lanes), f32),
        ],
        flops=4 * pairs * cells * big * (win + out_count),
        name="forward",
    )


def backward(grad_pre, conv_weight, fixed, channels, depth, row_count, col_count):
    pairs, big, cells = grad_pre.shape
    half_rows = row_count // 2
    win = 64 * channels
    args = (grad_pre, conv_weight, fixed["tap"], fixed["merge"], fixed["row_t"], fixed["edge_t"])
    outs = [
        jax.ShapeDtypeStruct((channels, depth, row_count, col_count), f32),
        jax.ShapeDtypeStruct((channels, row_count, col_count), bf16),
        jax.ShapeDtypeStruct((channels, row_count, col_count), bf16),
        jax.ShapeDtypeStruct((depth + 2, 8, col_count), bf16),
        jax.ShapeDtypeStruct((depth + 2, 8, col_count), bf16),
    ]
    return call(
        spread_kernel,
        (channels, pairs, half_rows, spread_tile),
        outs,
        *args,
        grid=(pairs,),
        in_specs=[pl.BlockSpec((1, big, cells), lambda z: (z, 0, 0))] + [whole(a.shape) for a in args[1:]],
        out_specs=[whole(o.shape) for o in outs],
        scratch=[
            pltpu.VMEM((pairs + 1, 16 * channels, cells + lanes), f32),
            pltpu.VMEM((win, big), bf16),
        ],
        flops=2 * pairs * cells * big * win,
        name="spread",
    )


forward_tile = 1024
spread_tile = 1024


def on_device(fields, target, conv_weight, conv_bias, down_weight, down_bias):
    channels, depth, row_count, col_count = fields.shape
    hidden = conv_weight.shape[0]
    out_count = down_weight.shape[0]
    taps = channels * 27
    big = 8 * hidden
    cell_total = fields.size // channels // 8 * lax.axis_size("gz") * lax.axis_size("gy")
    fixed = constants(channels, row_count, col_count // 2, hidden)

    below = shifted(fields[:, depth - 1], "gz", 1)
    above = shifted(fields[:, 0], "gz", -1)

    def side(row):
        rows = [below[:, row][:, None], fields[:, :, row], above[:, row][:, None]]
        rows = jnp.concatenate(rows, axis=1).transpose(1, 0, 2)
        return jnp.pad(rows, ((0, 0), (0, 8 - channels), (0, 0)))

    before = shifted(side(row_count - 1), "gy", 1)
    after = shifted(side(0), "gy", -1)
    out_field, grad_pre, grad_down, small = forward(
        fields, below, above, before, after, target, conv_weight, conv_bias, down_weight, down_bias, fixed
    )

    def beside(value, count):
        return jnp.concatenate(jnp.split(value, value.shape[0] // count, axis=0), axis=1)

    me = lax.axis_index("gz")
    own = grad_down
    bit = lax.axis_size("gz")
    while bit > 1:
        bit //= 2
        count = own.shape[0] // 2
        upper = (me // bit) % 2
        keep = lax.dynamic_slice_in_dim(own, upper * count, count, 0)
        give = lax.dynamic_slice_in_dim(own, (1 - upper) * count, count, 0)
        packed = jnp.concatenate([give, beside(small, min(count, hidden))], axis=1)
        got = exchanged(packed, "gz", bit)
        own = keep + got[:, :big]
        parts = jnp.split(got[:, big:], hidden // count, axis=1)
        small = small + jnp.concatenate(parts, axis=0)
    count = own.shape[0]
    packed = jnp.concatenate([own, beside(small, count)], axis=1)
    bit = 1
    while bit < lax.axis_size("gy"):
        packed = packed + exchanged(packed, "gy", bit)
        bit *= 2
    own = packed[:, :big]
    small = jnp.concatenate(jnp.split(packed[:, big:], hidden // count, axis=1), axis=0)

    sens, to_below, to_above, to_before, to_after = backward(
        grad_pre, conv_weight, fixed, channels, depth, row_count, col_count
    )
    from_before = shifted(to_after, "gy", 1)
    from_after = shifted(to_before, "gy", -1)

    def plane(value, at):
        low = from_before[at, :channels, None].astype(f32)
        high = from_after[at, :channels, None].astype(f32)
        gap = jnp.zeros((channels, row_count - 2, col_count), f32)
        return (value.astype(f32) + jnp.concatenate([low, gap, high], axis=1)).astype(bf16)

    from_below = shifted(plane(to_above, depth + 1), "gz", 1)
    from_above = shifted(plane(to_below, 0), "gz", -1)
    (sensitivity,) = call(
        join_kernel,
        (channels, depth, row_count),
        [jax.ShapeDtypeStruct(sens.shape, f32)],
        sens, from_above, from_below, from_after, from_before,
        name="join",
    )
    conv, cbias, down, dbias, loss = call(
        last_kernel,
        (hidden, taps, cell_total, out_count),
        [
            jax.ShapeDtypeStruct((hidden, taps), f32),
            jax.ShapeDtypeStruct((1, hidden), f32),
            jax.ShapeDtypeStruct((count, big), f32),
            jax.ShapeDtypeStruct((1, out_count), f32),
            jax.ShapeDtypeStruct((1, 1), f32),
        ],
        small, own, fixed["order"],
        name="last",
    )
    return out_field, sensitivity, conv, cbias[0], down, dbias[0], loss[0, 0]


def solution(mesh):
    in_specs = (P(None, "gz", "gy", None), P(None, "gz", "gy", None), P(), P(), P(), P())
    out_specs = (
        P(None, "gz", "gy", None),
        P(None, "gz", "gy", None),
        P(),
        P(),
        P("gz", None),
        P(),
        P(),
    )
    return jax.shard_map(
        on_device, mesh=mesh, in_specs=in_specs, out_specs=out_specs, check_vma=False
    )
```

time: 121 us -> 91.7 us (0.76)
  local copies, waits for them, and re-layouts: 25.3 us -> 6.53 us
  matrix products: 7.61 us -> 0 us
  other arithmetic: 5.34 us -> 1.77 us
  waiting for transfers between devices: 17.6 us -> 19.7 us
  between operations: 3.02 us -> 1.08 us
  Pallas kernels: 46.5 us -> 47.9 us
    dot_general x8 -> x0, matrix products: 7.61 us -> none  [dot(): return jnp.dot(a, b, preferred_element_type=f32)]
    reshape x3 -> x0, local copies, waits for them, and re-layouts: 5.78 us -> none  [the longest x2 5.02 us: on_device(): wanted = target.transpose(1, 0, 2, 3).reshape(pairs, out_count, cells)]
    scatter-add x2 -> x0, local copies, waits for them, and re-layouts: 4.18 us -> none  [the longest x1 2.09 us: on_device(): sensitivity = sensitivity.at[:, :, 0].add(from_left)]
    unnamed x35 -> x29, local copies, waits for them, and re-layouts: 4.66 us -> 1.42 us
    pallas_call x1 -> x0, local copies, waits for them, and re-layouts: 2.25 us -> none  [on_device(): pl.pallas_call(functools.partial(block_kernel, sizes), grid=(pairs, cells...]
    ppermute x5, waiting for transfers between devices: 8.85 us -> 10.9 us  [exchanged(): return lax.ppermute(value, axis, [(i, i ^ bit) for i in range(count)])]
    transpose x2 -> x0, local copies, waits for them, and re-layouts: 2.01 us -> none  [the longest x1 1.99 us: on_device(): out.reshape(pairs, out_count, half_rows, half_cols).transpose(1, 0, 2, 3)]
    broadcast_in_dim x4 -> x0, local copies, waits for them, and re-layouts: 1.65 us -> none  [the longest x2 0.91 us: on_device(): cbias = jnp.broadcast_to(jnp.tile(conv_bias, 8)[:, None], (big, lanes))]
  transfers between devices with their start and end apart: 13 -> 13, of which waited for: 9 -> 10; matrix products, arithmetic and copies ran while one was open for 18% -> 3% of each run, Pallas kernels for 0% -> 16%
where the time goes in v1:
time: 91.7 us; the launch traced here: 91.4 us
  Pallas kernels  47.9 us (52%)
  waiting for transfers between devices  19.7 us (21%)
  starting transfers between devices  14.4 us (16%)
  local copies, waits for them, and re-layouts  6.53 us (7%)
  other arithmetic  1.77 us (2%)
  between operations  1.08 us (1%)
    pallas_call x4, Pallas kernels, call(): pl.pallas_call(functools.partial(kernel, sizes), out_shape=out_shape, in_...  47.9 us
    ppermute x8, starting transfers between devices, shifted(): lax.ppermute(value, axis, [(i, (i + by) % count) for i in range(count)])  12.2 us
    ppermute x5, waiting for transfers between devices, exchanged(): return lax.ppermute(value, axis, [(i, i ^ bit) for i in range(count)])  10.9 us
    ppermute x8, waiting for transfers between devices, shifted(): lax.ppermute(value, axis, [(i, (i + by) % count) for i in range(count)])  8.84 us
    ppermute x5, starting transfers between devices, exchanged(): return lax.ppermute(value, axis, [(i, i ^ bit) for i in range(count)])  2.22 us
  transfers between devices with their start and end apart: 13, of which 10 were waited for; matrix products, arithmetic and copies ran while one was open for 3% of the time, Pallas kernels for 16%

profile of v1, /device:TPU:0, one launch (start us, length us, event | category | flops | bytes accessed | tf_op | source)
XLA Modules:
  0.0 91.4 jit_solution(5681883781566600026)
XLA Ops:
  0.6 1.0 %fusion.8 = (bf16[6,1,32,256]{3,2,1,0:T(8,128)(2,1)S(1)}, bf16[6,1,32,256]{3,2,1,0:T(8,128)(2,1)S(1)}) fusion(bf16[6,8,32,256]{3,2,1,0:T(8,128)(2,1)} %field_ref.1), kind=kLoop, calls=%fused_computation.40 | loop fusion | bytes 393216 | tf_op jit(solution)/shard_map/slice | solution.py:479
  1.6 0.1 copy.40
  1.7 0.5 collective-permute-start
  2.2 0.1 copy.39
  2.2 3.0 %collective-permute-start.1 = (bf16[6,32,256]{2,0,1:T(8,128)(2,1)S(1)}, bf16[6,32,256]{2,0,1:T(8,128)(2,1)S(1)}, u32[]{:S(2)}, u32[]{:S(2)}) collective-permute-start(bf16[6,32,256]{2,0,1:T(8,128)(2,1)S(1)} %bitcast.40), channel_id=1, source_target_pairs={{0,28},{4,0},{8,4},{12,8},{16,12},{20,16},{24,20},{28,24},{1,29},{... | collective-permute-start | bytes 294920 | tf_op jit(solution)/shard_map/ppermute | solution.py:20
  5.2 1.1 %fusion.7 = (bf16[6,8,1,256]{3,2,1,0:T(2,128)(2,1)S(1)}, bf16[6,8,1,256]{3,2,1,0:T(2,128)(2,1)S(1)}) fusion(bf16[6,8,32,256]{3,2,1,0:T(8,128)(2,1)} %field_ref.1), kind=kLoop, calls=%fused_computation.39 | loop fusion | bytes 98304 | tf_op jit(solution)/shard_map/slice | solution.py:482
  6.3 1.4 %collective-permute-done = bf16[6,32,256]{2,0,1:T(8,128)(2,1)S(1)} collective-permute-done((bf16[6,32,256]{2,0,1:T(8,128)(2,1)S(1)}, bf16[6,32,256]{2,0,1:T(8,128)(2,1)S(1)}, u32[]{:S(2)}, u32[]{:S(2)}) %collective-permute-start) | collective-permute-done | bytes 98336 | tf_op jit(solution)/shard_map/ppermute | solution.py:20
  7.7 0.3 collective-permute-done.1
  8.0 4.1 %collective-permute-start.3 = (bf16[10,8,256]{2,1,0:T(8,128)(2,1)S(1)}, bf16[10,8,256]{2,1,0:T(8,128)(2,1)S(1)}, u32[]{:S(2)}, u32[]{:S(2)}) collective-permute-start(bf16[10,8,256]{2,1,0:T(8,128)(2,1)S(1)} %pad.8), channel_id=1, source_target_pairs={{0,3},{1,0},{2,1},{3,2},{4,7},{5,4},{6,5},{7,6},{8,11},{9,8},{10,9... | collective-permute-start | bytes 122888 | tf_op jit(solution)/shard_map/ppermute | solution.py:20
  12.2 0.1 collective-permute-start.2
  12.4 0.1 pad.28.clone
  12.4 0.7 copy.25.below_ref
  13.1 0.7 copy.26.above_ref
  13.7 0.1 collective-permute-done.3.after_ref
  13.8 4.6 %collective-permute-done.2.before_ref = bf16[10,8,256]{2,1,0:T(8,128)(2,1)S(1)} collective-permute-done((bf16[10,8,256]{2,1,0:T(8,128)(2,1)S(1)}, bf16[10,8,256]{2,1,0:T(8,128)(2,1)S(1)}, u32[]{:S(2)}, u32[]{:S(2)}) %collective-permute-start.2) | collective-permute-done | bytes 40992 | tf_op jit(solution)/shard_map/ppermute | solution.py:20
  18.5 0.0 copy-done.8
  18.5 0.6 copy-done.9
  19.1 31.1 %forward.1 = (bf16[128,4,16,128]{3,2,1,0:T(8,128)(2,1)}, bf16[4,512,2048]{2,1,0:T(8,128)(2,1)}, f32[128,512]{1,0:T(8,128)}, f32[64,256]{1,0:T(8,128)}) custom-call(bf16[6,8,32,256]{3,2,1,0:T(8,128)(2,1)} %field_ref.1, bf16[6,32,256]{2,1,0:T(8,128)(2,1)} %copy.25.below_ref, bf16[6,32,256]{2,1,0:T(8,128)(2,1)} %copy.26.above_ref, ...), custom_call_target="tpu_custom_call" | custom-call | flops 8589934592 | bytes 16226304 | tf_op jit(solution)/shard_map/forward/pallas_call | solution.py:355
  50.2 0.9 %constant_dynamic-slice_fusion.1 = f32[64,512]{1,0:T(8,128)S(1)} fusion(f32[128,512]{1,0:T(8,128)} %get-tuple-element.28, s32[]{:T(128)S(6)} %select_n.44), kind=kLoop, calls=%fused_computation.38 | loop fusion | bytes 262148 | tf_op jit(solution)/shard_map/dynamic_slice | solution.py:503
  51.1 0.9 pad_maximum_fusion
  52.0 1.6 %collective-permute-start.8 = (f32[64,768]{1,0:T(8,128)S(1)}, f32[64,768]{1,0:T(8,128)S(1)}, u32[]{:S(2)}, u32[]{:S(2)}) collective-permute-start(f32[64,768]{1,0:T(8,128)S(1)} %pad_maximum_fusion), channel_id=1, source_target_pairs={{0,16},{4,20},{8,24},{12,28},{16,0},{20,4},{24,8},{28,12},{1,17},{... | collective-permute-start | bytes 589832 | tf_op jit(solution)/shard_map/ppermute | solution.py:25
  53.6 11.7 %spread.1 = (f32[6,8,32,256]{3,2,1,0:T(8,128)}, bf16[6,32,256]{2,1,0:T(8,128)(2,1)}, bf16[6,32,256]{2,1,0:T(8,128)(2,1)}, bf16[10,8,256]{2,1,0:T(8,128)(2,1)}, bf16[10,8,256]{2,1,0:T(8,128)(2,1)}) custom-call(bf16[4,512,2048]{2,1,0:T(8,128)(2,1)} %get-tuple-element.22.gpre_ref, bf16[64,162]{1,0:T(8,128)(2,1)} %conv_weight_ref.3, ...), custom_call_target="tpu_custom_call" | custom-call | flops 3221225472 | bytes 11703552 | tf_op jit(solution)/shard_map/spread/pallas_call | solution.py:355
  65.3 0.1 collective-permute-start.4
  65.3 3.8 %collective-permute-start.5 = (bf16[10,8,256]{2,1,0:T(8,128)(2,1)}, bf16[10,8,256]{2,1,0:T(8,128)(2,1)S(1)}, u32[]{:S(2)}, u32[]{:S(2)}) collective-permute-start(bf16[10,8,256]{2,1,0:T(8,128)(2,1)} %get-tuple-element.26), channel_id=1, source_target_pairs={{0,3},{1,0},{2,1},{3,2},{4,7},{5,4},{6,5},{7,6},{8,11},{9,8},{10,9... | collective-permute-start | bytes 122888 | tf_op jit(solution)/shard_map/ppermute | solution.py:20
  69.1 0.0 collective-permute-done.8
  69.1 0.0 copy-done.1
  69.2 0.0 copy-done
  69.2 0.4 collective-permute-start.9
  69.6 1.7 %collective-permute-done.4.after_ref = bf16[10,8,256]{2,1,0:T(8,128)(2,1)S(1)} collective-permute-done((bf16[10,8,256]{2,1,0:T(8,128)(2,1)}, bf16[10,8,256]{2,1,0:T(8,128)(2,1)S(1)}, u32[]{:S(2)}, u32[]{:S(2)}) %collective-permute-start.4) | collective-permute-done | bytes 40992 | tf_op jit(solution)/shard_map/ppermute | solution.py:20
  71.3 3.0 %collective-permute-done.9 = f32[32,1024]{1,0:T(8,128)S(1)} collective-permute-done((f32[32,1024]{1,0:T(8,128)S(1)}, f32[32,1024]{1,0:T(8,128)S(1)}, u32[]{:S(2)}, u32[]{:S(2)}) %collective-permute-start.9) | collective-permute-done | bytes 131104 | tf_op jit(solution)/shard_map/ppermute | solution.py:25
  74.4 0.1 collective-permute-start.10
  74.5 0.0 collective-permute-done.5.before_ref
  74.5 0.0 copy-start.7
  74.6 1.2 %collective-permute-done.10 = f32[16,1536]{1,0:T(8,128)S(1)} collective-permute-done((f32[16,1536]{1,0:T(8,128)S(1)}, f32[16,1536]{1,0:T(8,128)S(1)}, u32[]{:S(2)}, u32[]{:S(2)}) %collective-permute-start.10) | collective-permute-done | bytes 98336 | tf_op jit(solution)/shard_map/ppermute | solution.py:25
  75.8 0.1 collective-permute-start.11
  75.9 0.1 fusion.1
  76.1 0.6 collective-permute-start.6
  76.7 0.0 collective-permute-start.7
  76.7 4.0 %collective-permute-done.11 = f32[16,1536]{1,0:T(8,128)S(1)} collective-permute-done((f32[16,1536]{1,0:T(8,128)S(1)}, f32[16,1536]{1,0:T(8,128)S(1)}, u32[]{:S(2)}, u32[]{:S(2)}) %collective-permute-start.11) | collective-permute-done | bytes 98336 | tf_op jit(solution)/shard_map/ppermute | solution.py:25
  80.8 0.1 collective-permute-start.12
  80.9 0.0 collective-permute-done.6.below_ref
  80.9 0.8 collective-permute-done.7.above_ref
  81.7 0.6 copy-done.5
  82.3 2.9 %join.1 = f32[6,8,32,256]{3,2,1,0:T(8,128)} custom-call(f32[6,8,32,256]{3,2,1,0:T(8,128)} %get-tuple-element.23.sens_ref, bf16[6,32,256]{2,1,0:T(8,128)(2,1)} %copy-done.4, bf16[6,32,256]{2,1,0:T(8,128)(2,1)} %copy-done.5, bf16[10,8,256]{2,1,0:T(8,128)(2,1)} %copy-done.7, bf16[10,8,256]{2,1,0:T(8,128)(2,1)} %copy-done.6), custom_call_target="tpu_custom_call" | custom-call | bytes 3424256 | tf_op jit(solution)/shard_map/join/pallas_call | solution.py:355
  85.1 2.7 %collective-permute-done.12 = f32[16,1536]{1,0:T(8,128)S(1)} collective-permute-done((f32[16,1536]{1,0:T(8,128)S(1)}, f32[16,1536]{1,0:T(8,128)S(1)}, u32[]{:S(2)}, u32[]{:S(2)}) %collective-permute-start.12) | collective-permute-done | bytes 98336 | tf_op jit(solution)/shard_map/ppermute | solution.py:25
  87.9 0.6 slice.93.down_ref
  88.5 0.6 pad_maximum_fusion.2.small_ref
  89.1 2.2 %last.1 = (f32[64,162]{1,0:T(8,128)}, f32[1,64]{1,0:T(1,128)}, f32[16,512]{1,0:T(8,128)}, f32[1,128]{1,0:T(1,128)}, f32[1,1]{1,0:T(1,128)}) custom-call(f32[64,256]{1,0:T(8,128)} %pad_maximum_fusion.2.small_ref, f32[16,512]{1,0:T(8,128)} %slice.93.down_ref, bf16[512,512]{1,0:T(8,128)(2,1)} %constant.93.clone.order_ref), custom_call_target="tpu_custom_call" | custom-call | bytes 697604 | tf_op jit(solution)/shard_map/last/pallas_call | solution.py:355
  (51 shorter events, 0.4 us)
Async XLA Ops:
  1.7 6.0 %collective-permute-start = (bf16[6,32,256]{2,0,1:T(8,128)(2,1)S(1)}, bf16[6,32,256]{2,0,1:T(8,128)(2,1)S(1)}, u32[]{:S(2)}, u32[]{:S(2)}) collective-permute-start(bf16[6,32,256]{2,0,1:T(8,128)(2,1)S(1)} %bitcast.39), channel_id=1, source_target_pairs={{0,4},{4,8},{8,12},{12,16},{16,20},{20,24},{24,28},{28,0},{1,5},{5... | collective-permute-start | bytes 294920 | tf_op jit(solution)/shard_map/ppermute | solution.py:20
  2.2 5.7 %collective-permute-start.1 = (bf16[6,32,256]{2,0,1:T(8,128)(2,1)S(1)}, bf16[6,32,256]{2,0,1:T(8,128)(2,1)S(1)}, u32[]{:S(2)}, u32[]{:S(2)}) collective-permute-start(bf16[6,32,256]{2,0,1:T(8,128)(2,1)S(1)} %bitcast.40), channel_id=1, source_target_pairs={{0,28},{4,0},{8,4},{12,8},{16,12},{20,16},{24,20},{28,24},{1,29},{... | collective-permute-start | bytes 294920 | tf_op jit(solution)/shard_map/ppermute | solution.py:20
  8.0 5.8 %collective-permute-start.3 = (bf16[10,8,256]{2,1,0:T(8,128)(2,1)S(1)}, bf16[10,8,256]{2,1,0:T(8,128)(2,1)S(1)}, u32[]{:S(2)}, u32[]{:S(2)}) collective-permute-start(bf16[10,8,256]{2,1,0:T(8,128)(2,1)S(1)} %pad.8), channel_id=1, source_target_pairs={{0,3},{1,0},{2,1},{3,2},{4,7},{5,4},{6,5},{7,6},{8,11},{9,8},{10,9... | collective-permute-start | bytes 122888 | tf_op jit(solution)/shard_map/ppermute | solution.py:20
  12.2 6.3 %collective-permute-start.2 = (bf16[10,8,256]{2,1,0:T(8,128)(2,1)S(1)}, bf16[10,8,256]{2,1,0:T(8,128)(2,1)S(1)}, u32[]{:S(2)}, u32[]{:S(2)}) collective-permute-start(bf16[10,8,256]{2,1,0:T(8,128)(2,1)S(1)} %pad.7), channel_id=1, source_target_pairs={{0,1},{1,2},{2,3},{3,0},{4,5},{5,6},{6,7},{7,4},{8,9},{9,10},{10,1... | collective-permute-start | bytes 122888 | tf_op jit(solution)/shard_map/ppermute | solution.py:20
  13.8 4.6 %copy-start.8 = (bf16[10,8,256]{2,1,0:T(8,128)(2,1)}, bf16[10,8,256]{2,1,0:T(8,128)(2,1)S(1)}, u32[]{:S(2)}) copy-start(bf16[10,8,256]{2,1,0:T(8,128)(2,1)S(1)} %collective-permute-done.3.after_ref) | copy-start | bytes 122884
  18.5 0.6 copy-start.9
  52.0 17.2 %collective-permute-start.8 = (f32[64,768]{1,0:T(8,128)S(1)}, f32[64,768]{1,0:T(8,128)S(1)}, u32[]{:S(2)}, u32[]{:S(2)}) collective-permute-start(f32[64,768]{1,0:T(8,128)S(1)} %pad_maximum_fusion), channel_id=1, source_target_pairs={{0,16},{4,20},{8,24},{12,28},{16,0},{20,4},{24,8},{28,12},{1,17},{... | collective-permute-start | bytes 589832 | tf_op jit(solution)/shard_map/ppermute | solution.py:25
  53.6 15.5 %copy-start.1 = (f32[64,256]{1,0:T(8,128)S(1)}, f32[64,256]{1,0:T(8,128)}, u32[]{:S(2)}) copy-start(f32[64,256]{1,0:T(8,128)} %get-tuple-element.29) | copy-start | bytes 196612
  53.6 15.6 %copy-start = (f32[128,512]{1,0:T(8,128)S(1)}, f32[128,512]{1,0:T(8,128)}, u32[]{:S(2)}) copy-start(f32[128,512]{1,0:T(8,128)} %get-tuple-element.28) | copy-start | bytes 786436
  65.3 10.7 %copy-start.2 = (bf16[6,32,256]{2,1,0:T(8,128)(2,1)S(1)}, bf16[6,32,256]{2,1,0:T(8,128)(2,1)}, u32[]{:S(2)}) copy-start(bf16[6,32,256]{2,1,0:T(8,128)(2,1)} %get-tuple-element.24) | copy-start | bytes 294916
  65.3 10.7 %copy-start.3 = (bf16[6,32,256]{2,1,0:T(8,128)(2,1)S(1)}, bf16[6,32,256]{2,1,0:T(8,128)(2,1)}, u32[]{:S(2)}) copy-start(bf16[6,32,256]{2,1,0:T(8,128)(2,1)} %get-tuple-element.27) | copy-start | bytes 294916
  65.3 6.1 %collective-permute-start.4 = (bf16[10,8,256]{2,1,0:T(8,128)(2,1)}, bf16[10,8,256]{2,1,0:T(8,128)(2,1)S(1)}, u32[]{:S(2)}, u32[]{:S(2)}) collective-permute-start(bf16[10,8,256]{2,1,0:T(8,128)(2,1)} %get-tuple-element.25), channel_id=1, source_target_pairs={{0,1},{1,2},{2,3},{3,0},{4,5},{5,6},{6,7},{7,4},{8,9},{9,10},{10,1... | collective-permute-start | bytes 122888 | tf_op jit(solution)/shard_map/ppermute | solution.py:20
  65.3 9.1 %collective-permute-start.5 = (bf16[10,8,256]{2,1,0:T(8,128)(2,1)}, bf16[10,8,256]{2,1,0:T(8,128)(2,1)S(1)}, u32[]{:S(2)}, u32[]{:S(2)}) collective-permute-start(bf16[10,8,256]{2,1,0:T(8,128)(2,1)} %get-tuple-element.26), channel_id=1, source_target_pairs={{0,3},{1,0},{2,1},{3,2},{4,7},{5,4},{6,5},{7,6},{8,11},{9,8},{10,9... | collective-permute-start | bytes 122888 | tf_op jit(solution)/shard_map/ppermute | solution.py:20
  69.2 5.0 %collective-permute-start.9 = (f32[32,1024]{1,0:T(8,128)S(1)}, f32[32,1024]{1,0:T(8,128)S(1)}, u32[]{:S(2)}, u32[]{:S(2)}) collective-permute-start(f32[32,1024]{1,0:T(8,128)S(1)} %pad_maximum_fusion.1), channel_id=1, source_target_pairs={{0,8},{4,12},{8,0},{12,4},{16,24},{20,28},{24,16},{28,20},{1,9},{5... | collective-permute-start | bytes 393224 | tf_op jit(solution)/shard_map/ppermute | solution.py:25
  71.3 10.4 %copy-start.6 = (bf16[10,8,256]{2,1,0:T(8,128)(2,1)}, bf16[10,8,256]{2,1,0:T(8,128)(2,1)S(1)}, u32[]{:S(2)}) copy-start(bf16[10,8,256]{2,1,0:T(8,128)(2,1)S(1)} %collective-permute-done.4.after_ref) | copy-start | bytes 122884
  74.4 1.4 %collective-permute-start.10 = (f32[16,1536]{1,0:T(8,128)S(1)}, f32[16,1536]{1,0:T(8,128)S(1)}, u32[]{:S(2)}, u32[]{:S(2)}) collective-permute-start(f32[16,1536]{1,0:T(8,128)S(1)} %constant_dynamic-update-slice_fusion), channel_id=1, source_target_pairs={{0,4},{4,0},{8,12},{12,8},{16,20},{20,16},{24,28},{28,24},{1,5},{5... | collective-permute-start | bytes 294920 | tf_op jit(solution)/shard_map/ppermute | solution.py:25
  74.5 7.2 %copy-start.7 = (bf16[10,8,256]{2,1,0:T(8,128)(2,1)}, bf16[10,8,256]{2,1,0:T(8,128)(2,1)S(1)}, u32[]{:S(2)}) copy-start(bf16[10,8,256]{2,1,0:T(8,128)(2,1)S(1)} %collective-permute-done.5.before_ref) | copy-start | bytes 122884
  75.8 4.9 %collective-permute-start.11 = (f32[16,1536]{1,0:T(8,128)S(1)}, f32[16,1536]{1,0:T(8,128)S(1)}, u32[]{:S(2)}, u32[]{:S(2)}) collective-permute-start(f32[16,1536]{1,0:T(8,128)S(1)} %constant_dynamic-update-slice_fusion.4), channel_id=1, source_target_pairs={{0,1},{1,0},{2,3},{3,2},{4,5},{5,4},{6,7},{7,6},{8,9},{9,8},{10,11... | collective-permute-start | bytes 294920 | tf_op jit(solution)/shard_map/ppermute | solution.py:25
  76.1 4.8 %collective-permute-start.6 = (bf16[6,32,256]{2,1,0:T(8,128)(2,1)S(1)}, bf16[6,32,256]{2,1,0:T(8,128)(2,1)S(1)}, u32[]{:S(2)}, u32[]{:S(2)}) collective-permute-start(bf16[6,32,256]{2,1,0:T(8,128)(2,1)S(1)} %get-tuple-element.60), channel_id=1, source_target_pairs={{0,28},{4,0},{8,4},{12,8},{16,12},{20,16},{24,20},{28,24},{1,29},{... | collective-permute-start | bytes 294920 | tf_op jit(solution)/shard_map/ppermute | solution.py:20
  76.7 4.9 %collective-permute-start.7 = (bf16[6,32,256]{2,1,0:T(8,128)(2,1)S(1)}, bf16[6,32,256]{2,1,0:T(8,128)(2,1)S(1)}, u32[]{:S(2)}, u32[]{:S(2)}) collective-permute-start(bf16[6,32,256]{2,1,0:T(8,128)(2,1)S(1)} %get-tuple-element.59), channel_id=1, source_target_pairs={{0,4},{4,8},{8,12},{12,16},{16,20},{20,24},{24,28},{28,0},{1,5},{5... | collective-permute-start | bytes 294920 | tf_op jit(solution)/shard_map/ppermute | solution.py:20
  80.8 7.1 %collective-permute-start.12 = (f32[16,1536]{1,0:T(8,128)S(1)}, f32[16,1536]{1,0:T(8,128)S(1)}, u32[]{:S(2)}, u32[]{:S(2)}) collective-permute-start(f32[16,1536]{1,0:T(8,128)S(1)} %add.82), channel_id=1, source_target_pairs={{0,2},{1,3},{2,0},{3,1},{4,6},{5,7},{6,4},{7,5},{8,10},{9,11},{10,... | collective-permute-start | bytes 294920 | tf_op jit(solution)/shard_map/ppermute | solution.py:25
  80.9 0.8 copy-start.4
  81.7 0.6 copy-start.5

commit v2 on v1

v2 whole, which is shorter than its diff:
```python
import functools

import jax
import jax.numpy as jnp
import numpy as np
from jax import lax
from jax.experimental import pallas as pl
from jax.experimental.pallas import tpu as pltpu
from jax.sharding import PartitionSpec as P

gelu_scale = 0.7978845608028654
gelu_cubic = 0.044715
lanes = 128
bf16 = jnp.bfloat16
f32 = jnp.float32


def shifted(value, axis, by):
    count = lax.axis_size(axis)
    return lax.ppermute(value, axis, [(i, (i + by) % count) for i in range(count)])


def exchanged(value, axis, bit):
    count = lax.axis_size(axis)
    return lax.ppermute(value, axis, [(i, i ^ bit) for i in range(count)])


def column_merge(half_cols):
    merge = np.zeros((2 * half_cols, 2 * half_cols), np.float32)
    for par in range(2):
        for col in range(half_cols):
            merge[par * half_cols + col, (2 * col + par - 1) % (2 * half_cols)] = 1
    return merge


def row_spread(channels, row_count):
    pair_rows = row_count // 2 + 1
    core = np.zeros((pair_rows * 4 * channels, 2 * channels * row_count), np.float32)
    edge = np.zeros((8 * channels, 32), np.float32)
    for par_z in range(2):
        for ch in range(channels):
            for at in range(1, row_count + 1):
                target = ((at // 2 * 2 + par_z) * 2 + at % 2) * channels + ch
                core[target, (par_z * channels + ch) * row_count + at - 1] = 1
            edge[(par_z * 2) * channels + ch, par_z * 16 + ch] = 1
            edge[((2 + par_z) * 2 + 1) * channels + ch, par_z * 16 + 8 + ch] = 1
    return core, edge


def tap_spread(channels):
    spread = np.zeros((8, channels * 27, 64 * channels), np.float32)
    for cls in range(8):
        par_z, par_y, par_x = cls // 4, cls // 2 % 2, cls % 2
        for ch in range(channels):
            for off_z in range(3):
                for off_y in range(3):
                    for off_x in range(3):
                        at_z, at_y, at_x = par_z + off_z, par_y + off_y, par_x + off_x
                        place = (at_z // 2 * 2 + at_y // 2) * 2 + at_x // 2
                        place = ((place * 2 + at_x % 2) * 2 + at_z % 2) * 2 + at_y % 2
                        spread[cls, ch * 27 + 9 * off_z + 3 * off_y + off_x, place * channels + ch] = 1
    return spread


def class_order(hidden):
    order = np.zeros((8 * hidden, 8 * hidden), np.float32)
    for ch in range(hidden):
        for cls in range(8):
            order[ch * 8 + cls, cls * hidden + ch] = 1
    return order


def dot(a, b):
    return jnp.dot(a, b, preferred_element_type=f32)


def dot_rows(a, b):
    return lax.dot_general(a, b, (((1,), (1,)), ((), ())), preferred_element_type=f32)


def split_two(value):
    high = value.astype(bf16)
    return high, (value - high.astype(f32)).astype(bf16)


def split_three(value):
    high = value.astype(bf16)
    return (high,) + split_two(value - high.astype(f32))


def conv_rows(conv_ref, tap_ref):
    return jnp.concatenate([dot(conv_ref[...], tap_ref[cls]) for cls in range(8)], axis=0)


def row_of(ref, count):
    return jnp.transpose(jnp.broadcast_to(ref[...], (lanes, count)))


def forward_kernel(
    sizes,
    field_ref,
    below_ref,
    above_ref,
    before_ref,
    after_ref,
    target_ref,
    conv_weight_ref,
    conv_bias_ref,
    down_weight_ref,
    down_bias_ref,
    tap_ref,
    order_ref,
    col_ref,
    row_ref,
    edge_ref,
    out_ref,
    gpre_ref,
    keep_ref,
    give_ref,
    split_ref,
    conv_ref,
    down_ref,
    down_t_ref,
    gdown_t_ref,
    gconv_t_ref,
    gdb_ref,
    sq_ref,
    hid_ref,
    slope_ref,
    whole_ref,
):
    channels, pairs, half_rows, hidden, out_count, tile, cell_total = sizes
    group = 4 * channels
    cells = half_rows * lanes
    step = pl.program_id(0)

    @pl.when(step == 0)
    def _():
        gdown_t_ref[...] = jnp.zeros_like(gdown_t_ref)
        gconv_t_ref[...] = jnp.zeros_like(gconv_t_ref)
        gdb_ref[...] = jnp.zeros_like(gdb_ref)
        sq_ref[...] = jnp.zeros_like(sq_ref)
        conv_ref[:, : 16 * group] = (0.5 * conv_rows(conv_weight_ref, tap_ref)).astype(bf16)
        bias = 0.5 * row_of(conv_bias_ref, hidden)
        at = lax.broadcasted_iota(jnp.int32, bias.shape, 1)
        columns = jnp.zeros_like(bias)
        for k, piece in enumerate(split_three(bias)):
            columns = jnp.where(at == k, piece.astype(f32), columns)
        columns = jnp.concatenate([columns[:, :16]] * 8, axis=0)
        conv_ref[:, 16 * group :] = columns.astype(bf16)
        down = dot(down_weight_ref[...], order_ref[...])
        down_ref[...] = down.astype(bf16)
        down_t_ref[...] = jnp.transpose(down).astype(bf16)
        for slot in range(pairs + 1):
            lower = below_ref if slot == 0 else field_ref.at[:, 2 * slot - 1]
            upper = above_ref if slot == pairs else field_ref.at[:, 2 * slot]
            rows = [ref[ch] for ref in (lower, upper) for ch in range(channels)]
            rows = dot(row_ref[...], jnp.concatenate(rows, axis=0)).astype(bf16)
            rows = dot(rows, col_ref[...])
            sides = [ref[2 * slot + par].astype(f32) for par in range(2) for ref in (before_ref, after_ref)]
            sides = jnp.concatenate(sides, axis=0).astype(bf16)
            sides = dot(dot(edge_ref[...], sides).astype(bf16), col_ref[...])
            for row in range(half_rows + 1):
                piece = rows[row * group : (row + 1) * group]
                if row == 0:
                    piece = piece + sides[:group]
                if row == half_rows:
                    piece = piece + sides[group:]
                piece = jnp.concatenate([piece[:, :lanes], piece[:, lanes:]], axis=0)
                piece = jnp.concatenate([piece, pltpu.roll(piece, lanes - 1, 1)], axis=0)
                split_ref[slot, :, row * lanes : (row + 1) * lanes] = piece.astype(bf16)

    ones = jnp.ones((16, tile), bf16)
    down_bias = row_of(down_bias_ref, out_count)
    down_bias = jnp.concatenate([down_bias] * (tile // lanes), axis=1)
    wanted = jnp.swapaxes(target_ref[:, 0].astype(f32), 0, 1)
    parts = cells // tile
    count = tile // lanes

    def window_of(part):
        start, stop = part * tile, (part + 1) * tile
        return jnp.concatenate(
            [
                split_ref[step + dz, :, start + dy * lanes : stop + dy * lanes]
                for dz in range(2)
                for dy in range(2)
            ]
            + [ones],
            axis=0,
        )

    outputs, diffs = {}, {}

    def activate(part, rows):
        pre = dot(conv_ref[rows], window_of(part))
        square = pre * pre
        tangent = jnp.tanh(pre * (square * (8.0 * gelu_scale * gelu_cubic) + 2.0 * gelu_scale))
        above = 1.0 + tangent
        bend = pre * (square * (12.0 * gelu_scale * gelu_cubic) + gelu_scale)
        hid_ref[part % 2, rows] = (pre * above).astype(bf16)
        slope_ref[part % 2, rows] = above * ((1.0 - tangent) * bend + 0.5)

    def compare(part):
        output = dot(down_ref[...], hid_ref[part % 2]) + down_bias
        first = part * count
        diff = output - jnp.concatenate([wanted[first + k] for k in range(count)], axis=1)
        outputs[part] = [output[:, k * lanes : (k + 1) * lanes] for k in range(count)]
        for k in range(count):
            piece = diff[:, k * lanes : (k + 1) * lanes]
            gdb_ref[...] += piece
            sq_ref[...] += piece * piece
        diffs[part] = diff.astype(bf16)

    def weigh_down(part):
        gdown_t_ref[...] += dot_rows(hid_ref[part % 2], diffs[part])

    def back(part, rows):
        value = dot(down_t_ref[rows], diffs[part]) * slope_ref[part % 2, rows]
        gpre_ref[0, rows, part * tile : (part + 1) * tile] = value.astype(bf16)

    def weigh_conv(part):
        gconv_t_ref[...] += dot_rows(window_of(part), gpre_ref[0, :, part * tile : (part + 1) * tile])

    big = 8 * hidden
    blocks = [slice(0, big)]
    for part in range(parts + 1):
        first = [functools.partial(activate, part, rows) for rows in blocks] if part < parts else []
        second = []
        if part > 0:
            done = part - 1
            second = [functools.partial(compare, done), functools.partial(weigh_down, done)]
            second += [functools.partial(back, done, rows) for rows in blocks]
            second += [functools.partial(weigh_conv, done)]
        for k in range(max(len(first), len(second))):
            if k < len(second):
                second[k]()
            if k < len(first):
                first[k]()
    outputs = [value for part in range(parts) for value in outputs[part]]
    out_ref[:, 0] = jnp.swapaxes(jnp.stack(outputs, axis=0), 0, 1).astype(bf16)

    @pl.when(step == pairs - 1)
    def _():
        taps = channels * 27
        folded = 0.0
        cb = jnp.zeros((hidden, 1), f32)
        gconv = jnp.transpose(gconv_t_ref[...])
        for cls in range(8):
            rows = gconv[cls * hidden : (cls + 1) * hidden]
            cb = cb + rows[:, 16 * group : 16 * group + 1]
            rows = jnp.concatenate(split_three(rows[:, : 16 * group]), axis=0)
            folded = folded + dot_rows(rows, tap_ref[cls])
        folded = folded[:hidden] + (folded[hidden : 2 * hidden] + folded[2 * hidden :])
        columns = [folded, cb]
        for ref, share in ((gdb_ref, 1.0), (sq_ref, 1.0 / out_count)):
            total = share * jnp.sum(ref[...], axis=1, keepdims=True)
            columns += [total[:hidden], total[hidden:]]
        columns.append(jnp.zeros((hidden, 2 * lanes - taps - 5), f32))
        small = jnp.concatenate(columns, axis=1) / cell_total
        pieces = jnp.concatenate(split_three(jnp.transpose(gdown_t_ref[...])), axis=0)
        pieces = dot_rows(pieces, order_ref[...])
        grad_down = pieces[:out_count] + (pieces[out_count : 2 * out_count] + pieces[2 * out_count :])
        rows = out_count // 2
        upper = lax.axis_index("gz") // (lax.axis_size("gz") // 2)
        whole_ref[...] = grad_down / cell_total
        keep_ref[...] = whole_ref[pl.ds(pl.multiple_of(upper * rows, rows), rows)]
        give_ref[:, : 8 * hidden] = whole_ref[pl.ds(pl.multiple_of((1 - upper) * rows, rows), rows)]
        give_ref[:, 8 * hidden :] = small


def spread_kernel(sizes, *refs):
    channels, count, half_rows, tile, opening = sizes
    refs = list(refs)
    gpre_ref, conv_weight_ref, tap_ref, merge_ref, row_t_ref, edge_t_ref = refs[:6]
    if opening:
        core_ref, before_ref, after_ref, open_ref, spread_ref, conv_t_ref = refs[6:]
        at = 0
    else:
        open_ref, early_before_ref, early_after_ref = refs[6:9]
        core_ref, before_ref, after_ref, spread_ref, conv_t_ref = refs[9:]
        at = early_before_ref.shape[0]
    group = 4 * channels
    span = 4 * group
    row_count = 2 * half_rows
    cells = half_rows * lanes
    step = pl.program_id(0)

    def spread_out(pair):
        for part in range(cells // tile):
            spread = dot(conv_t_ref[...], gpre_ref[0, :, part * tile : (part + 1) * tile])
            for dz in range(2):
                for dy in range(2):
                    first = (2 * dz + dy) * span
                    here = slice(part * tile + dy * lanes, (part + 1) * tile + dy * lanes)
                    spread_ref[pair + dz, :, here] += spread[first : first + span]

    def finish(slot):
        rows = []
        for row in range(half_rows + 1):
            piece = spread_ref[slot, :, row * lanes : (row + 1) * lanes]
            halves = [
                piece[par * group : (par + 1) * group]
                + pltpu.roll(piece[(2 + par) * group : (3 + par) * group], 1, 1)
                for par in range(2)
            ]
            rows.append(jnp.concatenate(halves, axis=1))
        core, sides = 0.0, 0.0
        outer = jnp.concatenate([rows[0], rows[half_rows]], axis=0)
        for value in split_two(jnp.concatenate(rows, axis=0)):
            core = core + dot(dot(row_t_ref[...], value).astype(bf16), merge_ref[...])
        for value in split_two(outer):
            sides = sides + dot(dot(edge_t_ref[...], value).astype(bf16), merge_ref[...])
        for par in range(2):
            before_ref[at + 2 * slot + par] = sides[par * 16 : par * 16 + 8].astype(bf16)
            after_ref[at + 2 * slot + par] = sides[par * 16 + 8 : par * 16 + 16].astype(bf16)
            for ch in range(channels):
                first = (par * channels + ch) * row_count
                core_ref[2 * slot + par, ch] = core[first : first + row_count]

    for pair in range(count):

        @pl.when(step == pair)
        def _():
            if pair == 0:
                spread_ref[...] = jnp.zeros_like(spread_ref)
                conv_t_ref[...] = jnp.transpose(conv_rows(conv_weight_ref, tap_ref)).astype(bf16)
                if not opening:
                    spread_ref[0] = open_ref[...]
                    before_ref[:at] = early_before_ref[...]
                    after_ref[:at] = early_after_ref[...]
            else:
                finish(pair - 1)
            spread_out(pair)
            if pair == count - 1:
                finish(pair)
                if opening:
                    open_ref[...] = spread_ref[count]
                else:
                    finish(count)


def join_kernel(
    sizes, early_ref, late_ref, below_ref, above_ref, before_ref, after_ref, out_ref
):
    channels, depth, row_count = sizes
    early = early_ref.shape[0]
    for z in range(depth):
        plane_ref = early_ref.at[z + 1] if z + 1 < early else late_ref.at[z + 1 - early]
        for ch in range(channels):
            value = plane_ref[ch]
            if z == 0:
                value = value + above_ref[ch].astype(f32)
            if z == depth - 1:
                value = value + below_ref[ch].astype(f32)
            out_ref[ch, z] = value
            out_ref[ch, z, 0:1] += after_ref[z + 1, ch : ch + 1].astype(f32)
            out_ref[ch, z, row_count - 1 : row_count] += before_ref[z + 1, ch : ch + 1].astype(f32)


def last_kernel(sizes, mine_ref, theirs_ref, conv_out, cbias_out, down_out, dbias_out, loss_out):
    hidden, taps, big = sizes
    total = mine_ref[...] + theirs_ref[...]
    down_out[...] = total[:, :big]
    small = jnp.concatenate(
        [total[:, at : at + 2 * lanes] for at in range(big, total.shape[1], 2 * lanes)], axis=0
    )
    conv_out[...] = small[:, :taps]
    turned = jnp.transpose(small[:, lanes:])
    at = taps - lanes
    cbias_out[...] = turned[at : at + 1]
    dbias_out[...] = jnp.concatenate([turned[at + 1 : at + 2], turned[at + 2 : at + 3]], axis=1)
    loss_out[...] = jnp.sum(turned[at + 3 : at + 4] + turned[at + 4 : at + 5], axis=1, keepdims=True)


def call(kernel, sizes, out_shape, *args, grid=None, in_specs=None, out_specs=None, scratch=(), flops=0, name):
    if grid is None:
        in_specs = [pl.BlockSpec(memory_space=pltpu.VMEM)] * len(args)
        out_specs = [pl.BlockSpec(memory_space=pltpu.VMEM)] * len(out_shape)
    return pl.pallas_call(
        functools.partial(kernel, sizes),
        out_shape=out_shape,
        in_specs=in_specs,
        out_specs=out_specs,
        scratch_shapes=scratch,
        compiler_params=pltpu.CompilerParams(vmem_limit_bytes=56 * 1024 * 1024),
        cost_estimate=pl.CostEstimate(
            flops=flops,
            bytes_accessed=sum(a.size * a.dtype.itemsize for a in (*args, *out_shape)),
            transcendentals=0,
        ),
        name=name,
        **({} if grid is None else {"grid": grid}),
    )(*args)


def whole(shape):
    return pl.BlockSpec(tuple(shape), lambda z: (0,) * len(shape))


def constants(channels, row_count, half_cols, hidden):
    core, edge = row_spread(channels, row_count)
    names = {
        "col": column_merge(half_cols).T,
        "merge": column_merge(half_cols),
        "row": core,
        "row_t": core.T,
        "edge": edge,
        "edge_t": edge.T,
        "tap": tap_spread(channels),
        "order": class_order(hidden),
    }
    return {name: jnp.asarray(value, bf16) for name, value in names.items()}


def forward(fields, below, above, before, after, target, conv_weight, conv_bias, down_weight, down_bias, fixed, cell_total):
    channels, depth, row_count, col_count = fields.shape
    hidden, out_count = conv_weight.shape[0], down_weight.shape[0]
    pairs, half_rows, half_cols = depth // 2, row_count // 2, col_count // 2
    cells = half_rows * half_cols
    big, win = 8 * hidden, 64 * channels
    args = (
        fields, below, above, before, after, target,
        conv_weight, conv_bias[None], down_weight, down_bias[None],
        fixed["tap"], fixed["order"], fixed["col"], fixed["row"], fixed["edge"],
    )
    slab = pl.BlockSpec((out_count, 1, half_rows, half_cols), lambda z: (0, z, 0, 0))
    return call(
        forward_kernel,
        (channels, pairs, half_rows, hidden, out_count, forward_tile, cell_total),
        [
            jax.ShapeDtypeStruct(target.shape, bf16),
            jax.ShapeDtypeStruct((pairs, big, cells), bf16),
            jax.ShapeDtypeStruct((out_count // 2, big), f32),
            jax.ShapeDtypeStruct((out_count // 2, big + 2 * lanes), f32),
        ],
        *args,
        grid=(pairs,),
        in_specs=[slab if i == 5 else whole(a.shape) for i, a in enumerate(args)],
        out_specs=[
            slab,
            pl.BlockSpec((1, big, cells), lambda z: (z, 0, 0)),
            whole((out_count // 2, big)),
            whole((out_count // 2, big + 2 * lanes)),
        ],
        scratch=[
            pltpu.VMEM((pairs + 1, 16 * channels, cells + lanes), bf16),
            pltpu.VMEM((big, win + 16), bf16),
            pltpu.VMEM((out_count, big), bf16),
            pltpu.VMEM((big, out_count), bf16),
            pltpu.VMEM((big, out_count), f32),
            pltpu.VMEM((win + 16, big), f32),
            pltpu.VMEM((out_count, lanes), f32),
            pltpu.VMEM((out_count, lanes), f32),
            pltpu.VMEM((2, big, forward_tile), bf16),
            pltpu.VMEM((2, big, forward_tile), f32),
            pltpu.VMEM((out_count, big), f32),
        ],
        flops=4 * pairs * cells * big * (win + out_count),
        name="forward",
    )


def backward(grad_pre, first, count, conv_weight, fixed, shape, open_slot=None, early=()):
    channels, depth, row_count, col_count = shape
    _, big, cells = grad_pre.shape
    half_rows = row_count // 2
    win = 64 * channels
    opening = open_slot is None
    args = (grad_pre, conv_weight, fixed["tap"], fixed["merge"], fixed["row_t"], fixed["edge_t"])
    if not opening:
        args += (open_slot, *early)
    slots = count if opening else count + 1
    sides = jax.ShapeDtypeStruct((2 * (first + slots), 8, col_count), bf16)
    outs = [jax.ShapeDtypeStruct((2 * slots, channels, row_count, col_count), f32), sides, sides]
    if opening:
        outs.append(jax.ShapeDtypeStruct((16 * channels, cells + lanes), f32))
    return call(
        spread_kernel,
        (channels, count, half_rows, spread_tile, opening),
        outs,
        *args,
        grid=(count,),
        in_specs=[pl.BlockSpec((1, big, cells), lambda z: (first + z, 0, 0))] + [whole(a.shape) for a in args[1:]],
        out_specs=[whole(o.shape) for o in outs],
        scratch=[
            pltpu.VMEM((count + 1, 16 * channels, cells + lanes), f32),
            pltpu.VMEM((win, big), bf16),
        ],
        flops=2 * count * cells * big * win,
        name="spread",
    )


forward_tile = 1024
spread_tile = 1024


def on_device(fields, target, conv_weight, conv_bias, down_weight, down_bias):
    channels, depth, row_count, col_count = fields.shape
    hidden = conv_weight.shape[0]
    out_count = down_weight.shape[0]
    taps = channels * 27
    big = 8 * hidden
    cell_total = fields.size // channels // 8 * lax.axis_size("gz") * lax.axis_size("gy")
    fixed = constants(channels, row_count, col_count // 2, hidden)

    below = shifted(fields[:, depth - 1], "gz", 1)
    above = shifted(fields[:, 0], "gz", -1)

    def side(row):
        rows = [below[:, row][:, None], fields[:, :, row], above[:, row][:, None]]
        rows = jnp.concatenate(rows, axis=1).transpose(1, 0, 2)
        return jnp.pad(rows, ((0, 0), (0, 8 - channels), (0, 0)))

    before = shifted(side(row_count - 1), "gy", 1)
    after = shifted(side(0), "gy", -1)
    out_field, grad_pre, own, packed = forward(
        fields, below, above, before, after, target,
        conv_weight, conv_bias, down_weight, down_bias, fixed, cell_total,
    )

    def beside(value, count):
        return jnp.concatenate(jnp.split(value, value.shape[0] // count, axis=0), axis=1)

    me = lax.axis_index("gz")
    bit = lax.axis_size("gz") // 2
    small = packed[:, big:]
    parts, open_slot, early, core = 2, None, (), []
    pairs = depth // 2
    while True:
        got = exchanged(packed, "gz", bit)
        if len(core) < parts:
            count = pairs // parts
            found = backward(
                grad_pre, len(core) * count, count, conv_weight, fixed, fields.shape, open_slot, early
            )
            core.append(found[0])
            early = found[1:3]
            open_slot = found[3] if len(core) < parts else None
        count = own.shape[0]
        own = own + got[:, :big]
        pieces = jnp.split(got[:, big:], hidden // count, axis=1)
        small = small + jnp.concatenate(pieces, axis=0)
        if bit == 1:
            break
        bit //= 2
        count //= 2
        upper = (me // bit) % 2
        give = lax.dynamic_slice_in_dim(own, (1 - upper) * count, count, 0)
        own = lax.dynamic_slice_in_dim(own, upper * count, count, 0)
        packed = jnp.concatenate([give, beside(small, count)], axis=1)
        if len(core) < parts:
            packed, open_slot = lax.optimization_barrier((packed, open_slot))
    packed = jnp.concatenate([own, beside(small, own.shape[0])], axis=1)
    count = own.shape[0]
    to_before, to_after = early

    from_before = shifted(to_after, "gy", 1)
    from_after = shifted(to_before, "gy", -1)

    def plane(value, at):
        low = from_before[at, :channels, None].astype(f32)
        high = from_after[at, :channels, None].astype(f32)
        gap = jnp.zeros((channels, row_count - 2, col_count), f32)
        return (value + jnp.concatenate([low, gap, high], axis=1)).astype(bf16)

    from_below = shifted(plane(core[-1][-1], depth + 1), "gz", 1)
    from_above = shifted(plane(core[0][0], 0), "gz", -1)

    bit = 1
    while 2 * bit < lax.axis_size("gy"):
        packed = packed + exchanged(packed, "gy", bit)
        bit *= 2
    got = exchanged(packed, "gy", bit)
    (sensitivity,) = call(
        join_kernel,
        (channels, depth, row_count),
        [jax.ShapeDtypeStruct(fields.shape, f32)],
        *core, from_above, from_below, from_after, from_before,
        name="join",
    )
    conv, cbias, down, dbias, loss = call(
        last_kernel,
        (hidden, taps, big),
        [
            jax.ShapeDtypeStruct((hidden, taps), f32),
            jax.ShapeDtypeStruct((1, hidden), f32),
            jax.ShapeDtypeStruct((count, big), f32),
            jax.ShapeDtypeStruct((1, out_count), f32),
            jax.ShapeDtypeStruct((1, 1), f32),
        ],
        packed, got,
        name="last",
    )
    return out_field, sensitivity, conv, cbias[0], down, dbias[0], loss[0, 0]


def solution(mesh):
    in_specs = (P(None, "gz", "gy", None), P(None, "gz", "gy", None), P(), P(), P(), P())
    out_specs = (
        P(None, "gz", "gy", None),
        P(None, "gz", "gy", None),
        P(),
        P(),
        P("gz", None),
        P(),
        P(),
    )
    return jax.shard_map(
        on_device, mesh=mesh, in_specs=in_specs, out_specs=out_specs, check_vma=False
    )
```

time: 91.7 us -> 83.2 us (0.907)
  waiting for transfers between devices: 19.7 us -> 14.1 us
  Pallas kernels: 47.9 us -> 43.8 us
  starting transfers between devices: 14.4 us -> 15.9 us
    ppermute x5, waiting for transfers between devices: 10.9 us -> 5.53 us  [exchanged(): return lax.ppermute(value, axis, [(i, i ^ bit) for i in range(count)])]
    pallas_call x4 -> x5, Pallas kernels: 47.9 us -> 43.8 us  [call(): pl.pallas_call(functools.partial(kernel, sizes), out_shape=out_shape, in_...]
    ppermute x5, starting transfers between devices: 2.22 us -> 3.81 us  [exchanged(): return lax.ppermute(value, axis, [(i, i ^ bit) for i in range(count)])]
    concatenate x3 -> x1, other arithmetic: 1.49 us -> 0.01 us  [on_device(): packed = jnp.concatenate([give, beside(small, count)], axis=1)]
    unnamed x29 -> x27, local copies, waits for them, and re-layouts: 1.42 us -> 2.44 us
    convert_element_type x1, other arithmetic: 0.13 us -> 1.13 us  [plane(): return (value + jnp.concatenate([low, gap, high], axis=1)).astype(bf16)]
    dynamic_slice x2 -> x1, local copies, waits for them, and re-layouts: 0.93 us -> 0.01 us  [on_device(): give = lax.dynamic_slice_in_dim(own, (1 - upper) * count, count, 0)]
  transfers between devices with their start and end apart: 13 -> 13, of which waited for: 10 -> 9; matrix products, arithmetic and copies ran while one was open for 3% -> 5% of each run, Pallas kernels for 16% -> 11%
where the time goes in v2:
time: 83.2 us; the launch traced here: 82.9 us
  Pallas kernels  43.8 us (53%)
  starting transfers between devices  15.9 us (19%)
  waiting for transfers between devices  14.1 us (17%)
  local copies, waits for them, and re-layouts  6.03 us (7%)
  other arithmetic  2.11 us (3%)
  between operations  0.98 us (1%)
    pallas_call x5, Pallas kernels, call(): pl.pallas_call(functools.partial(kernel, sizes), out_shape=out_shape, in_...  43.8 us
    ppermute x8, starting transfers between devices, shifted(): lax.ppermute(value, axis, [(i, (i + by) % count) for i in range(count)])  12 us
    ppermute x8, waiting for transfers between devices, shifted(): lax.ppermute(value, axis, [(i, (i + by) % count) for i in range(count)])  8.6 us
    ppermute x5, waiting for transfers between devices, exchanged(): return lax.ppermute(value, axis, [(i, i ^ bit) for i in range(count)])  5.53 us
    ppermute x5, starting transfers between devices, exchanged(): return lax.ppermute(value, axis, [(i, i ^ bit) for i in range(count)])  3.81 us
    unnamed x27, local copies, waits for them, and re-layouts  2.44 us
  transfers between devices with their start and end apart: 13, of which 9 were waited for; matrix products, arithmetic and copies ran while one was open for 5% of the time, Pallas kernels for 11%

profile of v2, /device:TPU:0, one launch (start us, length us, event | category | flops | bytes accessed | tf_op | source)
XLA Modules:
  0.0 82.9 jit_solution(18219032052495671024)
XLA Ops:
  0.6 1.0 %fusion.8 = (bf16[6,1,32,256]{3,2,1,0:T(8,128)(2,1)S(1)}, bf16[6,1,32,256]{3,2,1,0:T(8,128)(2,1)S(1)}) fusion(bf16[6,8,32,256]{3,2,1,0:T(8,128)(2,1)} %field_ref.1), kind=kLoop, calls=%fused_computation.37 | loop fusion | bytes 393216 | tf_op jit(solution)/shard_map/slice | solution.py:508
  1.6 0.1 copy.40
  1.7 0.5 collective-permute-start
  2.2 0.1 copy.39
  2.2 3.0 %collective-permute-start.1 = (bf16[6,32,256]{2,0,1:T(8,128)(2,1)S(1)}, bf16[6,32,256]{2,0,1:T(8,128)(2,1)S(1)}, u32[]{:S(2)}, u32[]{:S(2)}) collective-permute-start(bf16[6,32,256]{2,0,1:T(8,128)(2,1)S(1)} %bitcast.44), channel_id=1, source_target_pairs={{0,28},{4,0},{8,4},{12,8},{16,12},{20,16},{24,20},{28,24},{1,29},{... | collective-permute-start | bytes 294920 | tf_op jit(solution)/shard_map/ppermute | solution.py:20
  5.2 1.1 %fusion.7 = (bf16[6,8,1,256]{3,2,1,0:T(2,128)(2,1)S(1)}, bf16[6,8,1,256]{3,2,1,0:T(2,128)(2,1)S(1)}) fusion(bf16[6,8,32,256]{3,2,1,0:T(8,128)(2,1)} %field_ref.1), kind=kLoop, calls=%fused_computation.36 | loop fusion | bytes 98304 | tf_op jit(solution)/shard_map/slice | solution.py:511
  6.3 1.4 %collective-permute-done = bf16[6,32,256]{2,0,1:T(8,128)(2,1)S(1)} collective-permute-done((bf16[6,32,256]{2,0,1:T(8,128)(2,1)S(1)}, bf16[6,32,256]{2,0,1:T(8,128)(2,1)S(1)}, u32[]{:S(2)}, u32[]{:S(2)}) %collective-permute-start) | collective-permute-done | bytes 98336 | tf_op jit(solution)/shard_map/ppermute | solution.py:20
  7.7 0.3 collective-permute-done.1
  8.0 4.1 %collective-permute-start.3 = (bf16[10,8,256]{2,1,0:T(8,128)(2,1)S(1)}, bf16[10,8,256]{2,1,0:T(8,128)(2,1)S(1)}, u32[]{:S(2)}, u32[]{:S(2)}) collective-permute-start(bf16[10,8,256]{2,1,0:T(8,128)(2,1)S(1)} %pad.8), channel_id=1, source_target_pairs={{0,3},{1,0},{2,1},{3,2},{4,7},{5,4},{6,5},{7,6},{8,11},{9,8},{10,9... | collective-permute-start | bytes 122888 | tf_op jit(solution)/shard_map/ppermute | solution.py:20
  12.2 0.1 collective-permute-start.2
  12.3 0.7 copy.25.below_ref
  12.9 0.7 copy.26.above_ref
  13.6 0.3 collective-permute-done.3.after_ref
  13.8 4.6 %collective-permute-done.2.before_ref = bf16[10,8,256]{2,1,0:T(8,128)(2,1)S(1)} collective-permute-done((bf16[10,8,256]{2,1,0:T(8,128)(2,1)S(1)}, bf16[10,8,256]{2,1,0:T(8,128)(2,1)S(1)}, u32[]{:S(2)}, u32[]{:S(2)}) %collective-permute-start.2) | collective-permute-done | bytes 40992 | tf_op jit(solution)/shard_map/ppermute | solution.py:20
  18.5 0.0 copy-done.7
  18.5 0.6 copy-done.8
  19.1 25.5 %forward.1 = (bf16[128,4,16,128]{3,2,1,0:T(8,128)(2,1)}, bf16[4,512,2048]{2,1,0:T(8,128)(2,1)}, f32[64,512]{1,0:T(8,128)}, f32[64,768]{1,0:T(8,128)}) custom-call(bf16[6,8,32,256]{3,2,1,0:T(8,128)(2,1)} %field_ref.1, bf16[6,32,256]{2,1,0:T(8,128)(2,1)} %copy.25.below_ref, bf16[6,32,256]{2,1,0:T(8,128)(2,1)} %copy.26.above_ref, ...), custom_call_target="tpu_custom_call" | custom-call | flops 8589934592 | bytes 16095232 | tf_op jit(solution)/shard_map/forward/pallas_call | solution.py:379
  44.6 1.7 %collective-permute-start.4 = (f32[64,768]{1,0:T(8,128)}, f32[64,768]{1,0:T(8,128)S(1)}, u32[]{:S(2)}, u32[]{:S(2)}) collective-permute-start(f32[64,768]{1,0:T(8,128)} %get-tuple-element.29), channel_id=1, source_target_pairs={{0,16},{4,20},{8,24},{12,28},{16,0},{20,4},{24,8},{28,12},{1,17},{... | collective-permute-start | bytes 589832 | tf_op jit(solution)/shard_map/ppermute | solution.py:25
  46.2 6.5 %spread.2 = (f32[4,6,32,256]{3,2,1,0:T(8,128)}, bf16[4,8,256]{2,1,0:T(8,128)(2,1)}, bf16[4,8,256]{2,1,0:T(8,128)(2,1)}, f32[96,2176]{1,0:T(8,128)}) custom-call(bf16[4,512,2048]{2,1,0:T(8,128)(2,1)} %get-tuple-element.26.refs_0_, bf16[64,162]{1,0:T(8,128)(2,1)} %refs_1_.3, bf16[8,162,384]{2,1,0:T(8,128)(2,1)} %constant.76.clone.tap_ref.refs_2_, ...), custom_call_target="tpu_custom_call" | custom-call | flops 1610612736 | bytes 11506944 | tf_op jit(solution)/shard_map/spread/pallas_call | solution.py:379
  52.7 0.0 collective-permute-done.4
  52.8 0.8 %slice_add_fusion.2 = f32[64,256]{1,0:T(8,128)S(1)} fusion(f32[64,768]{1,0:T(8,128)S(1)} %collective-permute-done.4, f32[64,768]{1,0:T(8,128)} %get-tuple-element.29), kind=kLoop, calls=%fused_computation.9 | loop fusion | flops 16384 | bytes 196608 | tf_op jit(solution)/shard_map/add | solution.py:543
  53.6 0.0 copy-done.1
  53.7 7.3 %spread.3 = (f32[6,6,32,256]{3,2,1,0:T(8,128)}, bf16[10,8,256]{2,1,0:T(8,128)(2,1)}, bf16[10,8,256]{2,1,0:T(8,128)(2,1)}) custom-call(bf16[4,512,2048]{2,1,0:T(8,128)(2,1)} %get-tuple-element.26.refs_0_, bf16[64,162]{1,0:T(8,128)(2,1)} %refs_1_.3, bf16[8,162,384]{2,1,0:T(8,128)(2,1)} %constant.76.clone.tap_ref.refs_2_, ...), custom_call_target="tpu_custom_call" | custom-call | flops 1610612736 | bytes 11982080 | tf_op jit(solution)/shard_map/spread/pallas_call | solution.py:379
  61.0 0.0 collective-permute-start.5
  61.1 0.1 pad.19.clone
  61.1 0.3 collective-permute-start.9
  61.4 3.8 %collective-permute-start.6 = (bf16[10,8,256]{2,1,0:T(8,128)(2,1)}, bf16[10,8,256]{2,1,0:T(8,128)(2,1)S(1)}, u32[]{:S(2)}, u32[]{:S(2)}) collective-permute-start(bf16[10,8,256]{2,1,0:T(8,128)(2,1)} %get-tuple-element.36), channel_id=1, source_target_pairs={{0,3},{1,0},{2,1},{3,2},{4,7},{5,4},{6,5},{7,6},{8,11},{9,8},{10,9... | collective-permute-start | bytes 122888 | tf_op jit(solution)/shard_map/ppermute | solution.py:20
  65.2 1.8 %collective-permute-done.5.after_ref = bf16[10,8,256]{2,1,0:T(8,128)(2,1)S(1)} collective-permute-done((bf16[10,8,256]{2,1,0:T(8,128)(2,1)}, bf16[10,8,256]{2,1,0:T(8,128)(2,1)S(1)}, u32[]{:S(2)}, u32[]{:S(2)}) %collective-permute-start.5) | collective-permute-done | bytes 40992 | tf_op jit(solution)/shard_map/ppermute | solution.py:20
  67.0 0.0 collective-permute-done.9
  67.2 0.1 collective-permute-start.10
  67.2 0.0 collective-permute-done.6.before_ref
  67.2 0.0 copy-start.6
  67.3 1.2 %collective-permute-done.10 = f32[16,1536]{1,0:T(8,128)S(1)} collective-permute-done((f32[16,1536]{1,0:T(8,128)S(1)}, f32[16,1536]{1,0:T(8,128)S(1)}, u32[]{:S(2)}, u32[]{:S(2)}) %collective-permute-start.10) | collective-permute-done | bytes 98336 | tf_op jit(solution)/shard_map/ppermute | solution.py:25
  68.6 0.1 collective-permute-start.11
  68.7 1.1 %fusion.1 = (bf16[6,32,256]{2,1,0:T(8,128)(2,1)S(1)}, bf16[6,32,256]{2,1,0:T(8,128)(2,1)S(1)}) fusion(f32[6,1,256]{2,1,0:T(1,128)S(1)} %copy.30, f32[6,1,256]{2,1,0:T(1,128)S(1)} %copy.29, f32[6,6,32,256]{3,2,1,0:T(8,128)} %get-tuple-element.34.late_ref, f32[32]{0:T(128)S(1)} %pad.19.clone, f32[6,1,256]{2,1,0:T(1,128)S(1)} %copy.28, ...), kind=kLoop, calls=%fused_computation.3 | loop fusion | flops 393216 | bytes 614528 | tf_op jit(solution)/shard_map/convert_element_type | solution.py:565
  69.8 0.6 collective-permute-start.7
  70.4 0.0 collective-permute-start.8
  70.4 3.1 %collective-permute-done.11 = f32[16,1536]{1,0:T(8,128)S(1)} collective-permute-done((f32[16,1536]{1,0:T(8,128)S(1)}, f32[16,1536]{1,0:T(8,128)S(1)}, u32[]{:S(2)}, u32[]{:S(2)}) %collective-permute-start.11) | collective-permute-done | bytes 98336 | tf_op jit(solution)/shard_map/ppermute | solution.py:25
  73.5 0.0 copy-start
  73.6 1.7 %collective-permute-start.12 = (f32[16,1536]{1,0:T(8,128)S(1)}, f32[16,1536]{1,0:T(8,128)S(1)}, u32[]{:S(2)}, u32[]{:S(2)}) collective-permute-start(f32[16,1536]{1,0:T(8,128)S(1)} %add.66.mine_ref), channel_id=1, source_target_pairs={{0,2},{1,3},{2,0},{3,1},{4,6},{5,7},{6,4},{7,5},{8,10},{9,11},{10,... | collective-permute-start | bytes 294920 | tf_op jit(solution)/shard_map/ppermute | solution.py:25
  75.3 0.0 collective-permute-done.7.below_ref
  75.3 0.3 collective-permute-done.8.above_ref
  75.5 0.4 copy-done.3
  75.9 0.6 copy-done.4
  76.6 2.9 %join.1 = f32[6,8,32,256]{3,2,1,0:T(8,128)} custom-call(f32[4,6,32,256]{3,2,1,0:T(8,128)} %get-tuple-element.27.early_ref, f32[6,6,32,256]{3,2,1,0:T(8,128)} %get-tuple-element.34.late_ref, bf16[6,32,256]{2,1,0:T(8,128)(2,1)} %copy-done.3, bf16[6,32,256]{2,1,0:T(8,128)(2,1)} %copy-done.4, bf16[10,8,256]{2,1,0:T(8,128)(2,1)} %copy-done.6, ...), custom_call_target="tpu_custom_call" | custom-call | bytes 3817472 | tf_op jit(solution)/shard_map/join/pallas_call | solution.py:379
  79.4 1.2 %collective-permute-done.12.theirs_ref = f32[16,1536]{1,0:T(8,128)S(1)} collective-permute-done((f32[16,1536]{1,0:T(8,128)S(1)}, f32[16,1536]{1,0:T(8,128)S(1)}, u32[]{:S(2)}, u32[]{:S(2)}) %collective-permute-start.12) | collective-permute-done | bytes 98336 | tf_op jit(solution)/shard_map/ppermute | solution.py:25
  80.7 0.6 copy-done.2
  81.3 1.6 %last.1 = (f32[64,162]{1,0:T(8,128)}, f32[1,64]{1,0:T(1,128)}, f32[16,512]{1,0:T(8,128)}, f32[1,128]{1,0:T(1,128)}, f32[1,1]{1,0:T(1,128)}) custom-call(f32[16,1536]{1,0:T(8,128)} %copy-done, f32[16,1536]{1,0:T(8,128)} %copy-done.2), custom_call_target="tpu_custom_call" | custom-call | bytes 271620 | tf_op jit(solution)/shard_map/last/pallas_call | solution.py:379
  (44 shorter events, 0.3 us)
Async XLA Ops:
  1.7 6.0 %collective-permute-start = (bf16[6,32,256]{2,0,1:T(8,128)(2,1)S(1)}, bf16[6,32,256]{2,0,1:T(8,128)(2,1)S(1)}, u32[]{:S(2)}, u32[]{:S(2)}) collective-permute-start(bf16[6,32,256]{2,0,1:T(8,128)(2,1)S(1)} %bitcast.43), channel_id=1, source_target_pairs={{0,4},{4,8},{8,12},{12,16},{16,20},{20,24},{24,28},{28,0},{1,5},{5... | collective-permute-start | bytes 294920 | tf_op jit(solution)/shard_map/ppermute | solution.py:20
  2.2 5.7 %collective-permute-start.1 = (bf16[6,32,256]{2,0,1:T(8,128)(2,1)S(1)}, bf16[6,32,256]{2,0,1:T(8,128)(2,1)S(1)}, u32[]{:S(2)}, u32[]{:S(2)}) collective-permute-start(bf16[6,32,256]{2,0,1:T(8,128)(2,1)S(1)} %bitcast.44), channel_id=1, source_target_pairs={{0,28},{4,0},{8,4},{12,8},{16,12},{20,16},{24,20},{28,24},{1,29},{... | collective-permute-start | bytes 294920 | tf_op jit(solution)/shard_map/ppermute | solution.py:20
  8.0 5.8 %collective-permute-start.3 = (bf16[10,8,256]{2,1,0:T(8,128)(2,1)S(1)}, bf16[10,8,256]{2,1,0:T(8,128)(2,1)S(1)}, u32[]{:S(2)}, u32[]{:S(2)}) collective-permute-start(bf16[10,8,256]{2,1,0:T(8,128)(2,1)S(1)} %pad.8), channel_id=1, source_target_pairs={{0,3},{1,0},{2,1},{3,2},{4,7},{5,4},{6,5},{7,6},{8,11},{9,8},{10,9... | collective-permute-start | bytes 122888 | tf_op jit(solution)/shard_map/ppermute | solution.py:20
  12.2 6.3 %collective-permute-start.2 = (bf16[10,8,256]{2,1,0:T(8,128)(2,1)S(1)}, bf16[10,8,256]{2,1,0:T(8,128)(2,1)S(1)}, u32[]{:S(2)}, u32[]{:S(2)}) collective-permute-start(bf16[10,8,256]{2,1,0:T(8,128)(2,1)S(1)} %pad.7), channel_id=1, source_target_pairs={{0,1},{1,2},{2,3},{3,0},{4,5},{5,6},{6,7},{7,4},{8,9},{9,10},{10,1... | collective-permute-start | bytes 122888 | tf_op jit(solution)/shard_map/ppermute | solution.py:20
  13.8 4.6 %copy-start.7 = (bf16[10,8,256]{2,1,0:T(8,128)(2,1)}, bf16[10,8,256]{2,1,0:T(8,128)(2,1)S(1)}, u32[]{:S(2)}) copy-start(bf16[10,8,256]{2,1,0:T(8,128)(2,1)S(1)} %collective-permute-done.3.after_ref) | copy-start | bytes 122884
  18.5 0.6 copy-start.8
  44.6 8.2 %collective-permute-start.4 = (f32[64,768]{1,0:T(8,128)}, f32[64,768]{1,0:T(8,128)S(1)}, u32[]{:S(2)}, u32[]{:S(2)}) collective-permute-start(f32[64,768]{1,0:T(8,128)} %get-tuple-element.29), channel_id=1, source_target_pairs={{0,16},{4,20},{8,24},{12,28},{16,0},{20,4},{24,8},{28,12},{1,17},{... | collective-permute-start | bytes 589832 | tf_op jit(solution)/shard_map/ppermute | solution.py:25
  46.2 7.4 %copy-start.1 = (f32[64,512]{1,0:T(8,128)S(1)}, f32[64,512]{1,0:T(8,128)}, u32[]{:S(2)}) copy-start(f32[64,512]{1,0:T(8,128)} %get-tuple-element.28) | copy-start | bytes 393220
  61.0 6.0 %collective-permute-start.5 = (bf16[10,8,256]{2,1,0:T(8,128)(2,1)}, bf16[10,8,256]{2,1,0:T(8,128)(2,1)S(1)}, u32[]{:S(2)}, u32[]{:S(2)}) collective-permute-start(bf16[10,8,256]{2,1,0:T(8,128)(2,1)} %get-tuple-element.35), channel_id=1, source_target_pairs={{0,1},{1,2},{2,3},{3,0},{4,5},{5,6},{6,7},{7,4},{8,9},{9,10},{10,1... | collective-permute-start | bytes 122888 | tf_op jit(solution)/shard_map/ppermute | solution.py:20
  61.1 5.9 %collective-permute-start.9 = (f32[32,1024]{1,0:T(8,128)S(1)}, f32[32,1024]{1,0:T(8,128)S(1)}, u32[]{:S(2)}, u32[]{:S(2)}) collective-permute-start(f32[32,1024]{1,0:T(8,128)S(1)} %pad_maximum_fusion), channel_id=1, source_target_pairs={{0,8},{4,12},{8,0},{12,4},{16,24},{20,28},{24,16},{28,20},{1,9},{5... | collective-permute-start | bytes 393224 | tf_op jit(solution)/shard_map/ppermute | solution.py:25
  61.4 5.8 %collective-permute-start.6 = (bf16[10,8,256]{2,1,0:T(8,128)(2,1)}, bf16[10,8,256]{2,1,0:T(8,128)(2,1)S(1)}, u32[]{:S(2)}, u32[]{:S(2)}) collective-permute-start(bf16[10,8,256]{2,1,0:T(8,128)(2,1)} %get-tuple-element.36), channel_id=1, source_target_pairs={{0,3},{1,0},{2,1},{3,2},{4,7},{5,4},{6,5},{7,6},{8,11},{9,8},{10,9... | collective-permute-start | bytes 122888 | tf_op jit(solution)/shard_map/ppermute | solution.py:20
  67.0 8.5 %copy-start.5 = (bf16[10,8,256]{2,1,0:T(8,128)(2,1)}, bf16[10,8,256]{2,1,0:T(8,128)(2,1)S(1)}, u32[]{:S(2)}) copy-start(bf16[10,8,256]{2,1,0:T(8,128)(2,1)S(1)} %collective-permute-done.5.after_ref) | copy-start | bytes 122884
  67.2 1.4 %collective-permute-start.10 = (f32[16,1536]{1,0:T(8,128)S(1)}, f32[16,1536]{1,0:T(8,128)S(1)}, u32[]{:S(2)}, u32[]{:S(2)}) collective-permute-start(f32[16,1536]{1,0:T(8,128)S(1)} %constant_dynamic-update-slice_fusion), channel_id=1, source_target_pairs={{0,4},{4,0},{8,12},{12,8},{16,20},{20,16},{24,28},{28,24},{1,5},{5... | collective-permute-start | bytes 294920 | tf_op jit(solution)/shard_map/ppermute | solution.py:25
  67.2 8.3 %copy-start.6 = (bf16[10,8,256]{2,1,0:T(8,128)(2,1)}, bf16[10,8,256]{2,1,0:T(8,128)(2,1)S(1)}, u32[]{:S(2)}) copy-start(bf16[10,8,256]{2,1,0:T(8,128)(2,1)S(1)} %collective-permute-done.6.before_ref) | copy-start | bytes 122884
  68.6 4.9 %collective-permute-start.11 = (f32[16,1536]{1,0:T(8,128)S(1)}, f32[16,1536]{1,0:T(8,128)S(1)}, u32[]{:S(2)}, u32[]{:S(2)}) collective-permute-start(f32[16,1536]{1,0:T(8,128)S(1)} %constant_dynamic-update-slice_fusion.4), channel_id=1, source_target_pairs={{0,1},{1,0},{2,3},{3,2},{4,5},{5,4},{6,7},{7,6},{8,9},{9,8},{10,11... | collective-permute-start | bytes 294920 | tf_op jit(solution)/shard_map/ppermute | solution.py:25
  69.8 5.5 %collective-permute-start.7 = (bf16[6,32,256]{2,1,0:T(8,128)(2,1)S(1)}, bf16[6,32,256]{2,1,0:T(8,128)(2,1)S(1)}, u32[]{:S(2)}, u32[]{:S(2)}) collective-permute-start(bf16[6,32,256]{2,1,0:T(8,128)(2,1)S(1)} %get-tuple-element.64), channel_id=1, source_target_pairs={{0,28},{4,0},{8,4},{12,8},{16,12},{20,16},{24,20},{28,24},{1,29},{... | collective-permute-start | bytes 294920 | tf_op jit(solution)/shard_map/ppermute | solution.py:20
  70.4 5.1 %collective-permute-start.8 = (bf16[6,32,256]{2,1,0:T(8,128)(2,1)S(1)}, bf16[6,32,256]{2,1,0:T(8,128)(2,1)S(1)}, u32[]{:S(2)}, u32[]{:S(2)}) collective-permute-start(bf16[6,32,256]{2,1,0:T(8,128)(2,1)S(1)} %get-tuple-element.63), channel_id=1, source_target_pairs={{0,4},{4,8},{8,12},{12,16},{16,20},{20,24},{24,28},{28,0},{1,5},{5... | collective-permute-start | bytes 294920 | tf_op jit(solution)/shard_map/ppermute | solution.py:20
  73.5 7.1 %copy-start = (f32[16,1536]{1,0:T(8,128)}, f32[16,1536]{1,0:T(8,128)S(1)}, u32[]{:S(2)}) copy-start(f32[16,1536]{1,0:T(8,128)S(1)} %add.66.mine_ref) | copy-start | bytes 294916
  73.6 7.1 %collective-permute-start.12 = (f32[16,1536]{1,0:T(8,128)S(1)}, f32[16,1536]{1,0:T(8,128)S(1)}, u32[]{:S(2)}, u32[]{:S(2)}) collective-permute-start(f32[16,1536]{1,0:T(8,128)S(1)} %add.66.mine_ref), channel_id=1, source_target_pairs={{0,2},{1,3},{2,0},{3,1},{4,6},{5,7},{6,4},{7,5},{8,10},{9,11},{10,... | collective-permute-start | bytes 294920 | tf_op jit(solution)/shard_map/ppermute | solution.py:25
  75.3 0.6 copy-start.3
  75.9 0.6 copy-start.4
  80.7 0.6 copy-start.2

commit v3 on v2

--- a/solution.py
+++ b/solution.py
@@ -541,6 +541,9 @@
         own = own + got[:, :big]
         pieces = jnp.split(got[:, big:], hidden // count, axis=1)
         small = small + jnp.concatenate(pieces, axis=0)
+        if len(core) == parts and early:
+            own, small, to_before, to_after = lax.optimization_barrier((own, small, *early))
+            early = ()
         if bit == 1:
             break
         bit //= 2
@@ -553,7 +556,6 @@
             packed, open_slot = lax.optimization_barrier((packed, open_slot))
     packed = jnp.concatenate([own, beside(small, own.shape[0])], axis=1)
     count = own.shape[0]
-    to_before, to_after = early
 
     from_before = shifted(to_after, "gy", 1)
     from_after = shifted(to_before, "gy", -1)

time: 83.2 us -> 82.9 us (level)
    ppermute x5, waiting for transfers between devices: 5.53 us -> 4.36 us  [exchanged(): return lax.ppermute(value, axis, [(i, i ^ bit) for i in range(count)])]
  transfers between devices with their start and end apart: 13 -> 13, of which waited for: 9 -> 7; matrix products, arithmetic and copies ran while one was open for 5% -> 5% of each run, Pallas kernels for 11% -> 20%
where the time goes in v3:
time: 82.9 us; the launch traced here: 82.6 us
  Pallas kernels  43.6 us (53%)
  starting transfers between devices  16.3 us (20%)
  waiting for transfers between devices  13.3 us (16%)
  local copies, waits for them, and re-layouts  6.27 us (8%)
  other arithmetic  2.11 us (3%)
  between operations  0.98 us (1%)
    pallas_call x5, Pallas kernels, call(): pl.pallas_call(functools.partial(kernel, sizes), out_shape=out_shape, in_...  43.6 us
    ppermute x8, starting transfers between devices, shifted(): lax.ppermute(value, axis, [(i, (i + by) % count) for i in range(count)])  12 us
    ppermute x8, waiting for transfers between devices, shifted(): lax.ppermute(value, axis, [(i, (i + by) % count) for i in range(count)])  8.97 us
    ppermute x5, waiting for transfers between devices, exchanged(): return lax.ppermute(value, axis, [(i, i ^ bit) for i in range(count)])  4.36 us
    ppermute x5, starting transfers between devices, exchanged(): return lax.ppermute(value, axis, [(i, i ^ bit) for i in range(count)])  4.28 us
    unnamed x27, local copies, waits for them, and re-layouts  2.68 us
  transfers between devices with their start and end apart: 13, of which 7 were waited for; matrix products, arithmetic and copies ran while one was open for 5% of the time, Pallas kernels for 20%

profile of v3, /device:TPU:0, one launch (start us, length us, event | category | flops | bytes accessed | tf_op | source)
XLA Modules:
  0.0 82.6 jit_solution(4986161383409271045)
XLA Ops:
  0.6 1.0 %fusion.8 = (bf16[6,1,32,256]{3,2,1,0:T(8,128)(2,1)S(1)}, bf16[6,1,32,256]{3,2,1,0:T(8,128)(2,1)S(1)}) fusion(bf16[6,8,32,256]{3,2,1,0:T(8,128)(2,1)} %field_ref.1), kind=kLoop, calls=%fused_computation.37 | loop fusion | bytes 393216 | tf_op jit(solution)/shard_map/slice | solution.py:508
  1.6 0.1 copy.40
  1.7 0.5 collective-permute-start
  2.2 0.1 copy.39
  2.2 3.0 %collective-permute-start.1 = (bf16[6,32,256]{2,0,1:T(8,128)(2,1)S(1)}, bf16[6,32,256]{2,0,1:T(8,128)(2,1)S(1)}, u32[]{:S(2)}, u32[]{:S(2)}) collective-permute-start(bf16[6,32,256]{2,0,1:T(8,128)(2,1)S(1)} %bitcast.44), channel_id=1, source_target_pairs={{0,28},{4,0},{8,4},{12,8},{16,12},{20,16},{24,20},{28,24},{1,29},{... | collective-permute-start | bytes 294920 | tf_op jit(solution)/shard_map/ppermute | solution.py:20
  5.2 1.1 %fusion.7 = (bf16[6,8,1,256]{3,2,1,0:T(2,128)(2,1)S(1)}, bf16[6,8,1,256]{3,2,1,0:T(2,128)(2,1)S(1)}) fusion(bf16[6,8,32,256]{3,2,1,0:T(8,128)(2,1)} %field_ref.1), kind=kLoop, calls=%fused_computation.36 | loop fusion | bytes 98304 | tf_op jit(solution)/shard_map/slice | solution.py:511
  6.3 1.4 %collective-permute-done = bf16[6,32,256]{2,0,1:T(8,128)(2,1)S(1)} collective-permute-done((bf16[6,32,256]{2,0,1:T(8,128)(2,1)S(1)}, bf16[6,32,256]{2,0,1:T(8,128)(2,1)S(1)}, u32[]{:S(2)}, u32[]{:S(2)}) %collective-permute-start) | collective-permute-done | bytes 98336 | tf_op jit(solution)/shard_map/ppermute | solution.py:20
  7.7 0.3 collective-permute-done.1
  8.0 4.1 %collective-permute-start.3 = (bf16[10,8,256]{2,1,0:T(8,128)(2,1)S(1)}, bf16[10,8,256]{2,1,0:T(8,128)(2,1)S(1)}, u32[]{:S(2)}, u32[]{:S(2)}) collective-permute-start(bf16[10,8,256]{2,1,0:T(8,128)(2,1)S(1)} %pad.8), channel_id=1, source_target_pairs={{0,3},{1,0},{2,1},{3,2},{4,7},{5,4},{6,5},{7,6},{8,11},{9,8},{10,9... | collective-permute-start | bytes 122888 | tf_op jit(solution)/shard_map/ppermute | solution.py:20
  12.2 0.1 collective-permute-start.2
  12.3 0.7 copy.25.below_ref
  12.9 0.7 copy.26.above_ref
  13.6 0.3 collective-permute-done.3.after_ref
  13.8 4.6 %collective-permute-done.2.before_ref = bf16[10,8,256]{2,1,0:T(8,128)(2,1)S(1)} collective-permute-done((bf16[10,8,256]{2,1,0:T(8,128)(2,1)S(1)}, bf16[10,8,256]{2,1,0:T(8,128)(2,1)S(1)}, u32[]{:S(2)}, u32[]{:S(2)}) %collective-permute-start.2) | collective-permute-done | bytes 40992 | tf_op jit(solution)/shard_map/ppermute | solution.py:20
  18.5 0.0 copy-done.7
  18.5 0.6 copy-done.8
  19.1 25.5 %forward.1 = (bf16[128,4,16,128]{3,2,1,0:T(8,128)(2,1)}, bf16[4,512,2048]{2,1,0:T(8,128)(2,1)}, f32[64,512]{1,0:T(8,128)}, f32[64,768]{1,0:T(8,128)}) custom-call(bf16[6,8,32,256]{3,2,1,0:T(8,128)(2,1)} %field_ref.1, bf16[6,32,256]{2,1,0:T(8,128)(2,1)} %copy.25.below_ref, bf16[6,32,256]{2,1,0:T(8,128)(2,1)} %copy.26.above_ref, ...), custom_call_target="tpu_custom_call" | custom-call | flops 8589934592 | bytes 16095232 | tf_op jit(solution)/shard_map/forward/pallas_call | solution.py:379
  44.6 1.7 %collective-permute-start.4 = (f32[64,768]{1,0:T(8,128)}, f32[64,768]{1,0:T(8,128)S(1)}, u32[]{:S(2)}, u32[]{:S(2)}) collective-permute-start(f32[64,768]{1,0:T(8,128)} %get-tuple-element.33), channel_id=1, source_target_pairs={{0,16},{4,20},{8,24},{12,28},{16,0},{20,4},{24,8},{28,12},{1,17},{... | collective-permute-start | bytes 589832 | tf_op jit(solution)/shard_map/ppermute | solution.py:25
  46.2 0.1 pad.17.clone
  46.3 6.5 %spread.2 = (f32[4,6,32,256]{3,2,1,0:T(8,128)}, bf16[4,8,256]{2,1,0:T(8,128)(2,1)}, bf16[4,8,256]{2,1,0:T(8,128)(2,1)}, f32[96,2176]{1,0:T(8,128)}) custom-call(bf16[4,512,2048]{2,1,0:T(8,128)(2,1)} %get-tuple-element.30.refs_0_, bf16[64,162]{1,0:T(8,128)(2,1)} %refs_1_.3, bf16[8,162,384]{2,1,0:T(8,128)(2,1)} %constant.76.clone.tap_ref.refs_2_, ...), custom_call_target="tpu_custom_call" | custom-call | flops 1610612736 | bytes 11506944 | tf_op jit(solution)/shard_map/spread/pallas_call | solution.py:379
  52.8 0.0 collective-permute-done.4
  52.8 0.8 %slice_add_fusion.2 = f32[64,256]{1,0:T(8,128)S(1)} fusion(f32[64,768]{1,0:T(8,128)S(1)} %collective-permute-done.4, f32[64,768]{1,0:T(8,128)} %get-tuple-element.33), kind=kLoop, calls=%fused_computation.9 | loop fusion | flops 16384 | bytes 196608 | tf_op jit(solution)/shard_map/add | solution.py:543
  53.7 0.0 copy-done.1
  53.8 0.3 collective-permute-start.5
  54.1 7.1 %spread.3 = (f32[6,6,32,256]{3,2,1,0:T(8,128)}, bf16[10,8,256]{2,1,0:T(8,128)(2,1)}, bf16[10,8,256]{2,1,0:T(8,128)(2,1)}) custom-call(bf16[4,512,2048]{2,1,0:T(8,128)(2,1)} %get-tuple-element.30.refs_0_, bf16[64,162]{1,0:T(8,128)(2,1)} %refs_1_.3, bf16[8,162,384]{2,1,0:T(8,128)(2,1)} %constant.76.clone.tap_ref.refs_2_, ...), custom_call_target="tpu_custom_call" | custom-call | flops 1610612736 | bytes 11982080 | tf_op jit(solution)/shard_map/spread/pallas_call | solution.py:379
  61.2 0.0 collective-permute-done.5
  61.3 0.1 collective-permute-start.6
  61.4 0.1 collective-permute-start.10
  61.5 3.7 %collective-permute-start.7 = (bf16[10,8,256]{2,1,0:T(8,128)(2,1)}, bf16[10,8,256]{2,1,0:T(8,128)(2,1)S(1)}, u32[]{:S(2)}, u32[]{:S(2)}) collective-permute-start(bf16[10,8,256]{2,1,0:T(8,128)(2,1)} %get-tuple-element.43), channel_id=1, source_target_pairs={{0,3},{1,0},{2,1},{3,2},{4,7},{5,4},{6,5},{7,6},{8,11},{9,8},{10,9... | collective-permute-start | bytes 122888 | tf_op jit(solution)/shard_map/ppermute | solution.py:20
  65.2 2.4 %collective-permute-done.6.after_ref = bf16[10,8,256]{2,1,0:T(8,128)(2,1)S(1)} collective-permute-done((bf16[10,8,256]{2,1,0:T(8,128)(2,1)}, bf16[10,8,256]{2,1,0:T(8,128)(2,1)S(1)}, u32[]{:S(2)}, u32[]{:S(2)}) %collective-permute-start.6) | collective-permute-done | bytes 40992 | tf_op jit(solution)/shard_map/ppermute | solution.py:20
  67.7 0.0 collective-permute-done.7.before_ref
  67.7 0.0 copy-start.6
  67.8 0.0 collective-permute-done.10
  67.9 0.1 collective-permute-start.11
  68.0 1.1 %fusion.1 = (bf16[6,32,256]{2,1,0:T(8,128)(2,1)S(1)}, bf16[6,32,256]{2,1,0:T(8,128)(2,1)S(1)}) fusion(f32[6,1,256]{2,1,0:T(1,128)S(1)} %copy.30, f32[6,1,256]{2,1,0:T(1,128)S(1)} %copy.29, f32[6,6,32,256]{3,2,1,0:T(8,128)} %get-tuple-element.38.late_ref, f32[32]{0:T(128)S(1)} %pad.17.clone, f32[6,1,256]{2,1,0:T(1,128)S(1)} %copy.28, ...), kind=kLoop, calls=%fused_computation.3 | loop fusion | flops 393216 | bytes 614528 | tf_op jit(solution)/shard_map/convert_element_type | solution.py:567
  69.1 0.4 collective-permute-start.8
  69.5 0.1 collective-permute-start.9
  69.7 2.9 %collective-permute-done.11 = f32[16,1536]{1,0:T(8,128)S(1)} collective-permute-done((f32[16,1536]{1,0:T(8,128)S(1)}, f32[16,1536]{1,0:T(8,128)S(1)}, u32[]{:S(2)}, u32[]{:S(2)}) %collective-permute-start.11) | collective-permute-done | bytes 98336 | tf_op jit(solution)/shard_map/ppermute | solution.py:25
  72.6 0.0 copy-start
  72.6 2.1 %collective-permute-start.12 = (f32[16,1536]{1,0:T(8,128)S(1)}, f32[16,1536]{1,0:T(8,128)S(1)}, u32[]{:S(2)}, u32[]{:S(2)}) collective-permute-start(f32[16,1536]{1,0:T(8,128)S(1)} %add.66.mine_ref), channel_id=1, source_target_pairs={{0,2},{1,3},{2,0},{3,1},{4,6},{5,7},{6,4},{7,5},{8,10},{9,11},{10,... | collective-permute-start | bytes 294920 | tf_op jit(solution)/shard_map/ppermute | solution.py:25
  74.7 0.0 collective-permute-done.8.below_ref
  74.7 0.0 collective-permute-done.9.above_ref
  74.8 0.6 copy-done.3
  75.4 0.6 copy-done.4
  76.0 2.9 %join.1 = f32[6,8,32,256]{3,2,1,0:T(8,128)} custom-call(f32[4,6,32,256]{3,2,1,0:T(8,128)} %get-tuple-element.31.early_ref, f32[6,6,32,256]{3,2,1,0:T(8,128)} %get-tuple-element.38.late_ref, bf16[6,32,256]{2,1,0:T(8,128)(2,1)} %copy-done.3, bf16[6,32,256]{2,1,0:T(8,128)(2,1)} %copy-done.4, bf16[10,8,256]{2,1,0:T(8,128)(2,1)} %copy-done.6, ...), custom_call_target="tpu_custom_call" | custom-call | bytes 3817472 | tf_op jit(solution)/shard_map/join/pallas_call | solution.py:379
  78.9 1.4 %collective-permute-done.12.theirs_ref = f32[16,1536]{1,0:T(8,128)S(1)} collective-permute-done((f32[16,1536]{1,0:T(8,128)S(1)}, f32[16,1536]{1,0:T(8,128)S(1)}, u32[]{:S(2)}, u32[]{:S(2)}) %collective-permute-start.12) | collective-permute-done | bytes 98336 | tf_op jit(solution)/shard_map/ppermute | solution.py:25
  80.3 0.6 copy-done.2
  80.9 1.6 %last.1 = (f32[64,162]{1,0:T(8,128)}, f32[1,64]{1,0:T(1,128)}, f32[16,512]{1,0:T(8,128)}, f32[1,128]{1,0:T(1,128)}, f32[1,1]{1,0:T(1,128)}) custom-call(f32[16,1536]{1,0:T(8,128)} %copy-done, f32[16,1536]{1,0:T(8,128)} %copy-done.2), custom_call_target="tpu_custom_call" | custom-call | bytes 271620 | tf_op jit(solution)/shard_map/last/pallas_call | solution.py:379
  (44 shorter events, 0.3 us)
Async XLA Ops:
  1.7 6.0 %collective-permute-start = (bf16[6,32,256]{2,0,1:T(8,128)(2,1)S(1)}, bf16[6,32,256]{2,0,1:T(8,128)(2,1)S(1)}, u32[]{:S(2)}, u32[]{:S(2)}) collective-permute-start(bf16[6,32,256]{2,0,1:T(8,128)(2,1)S(1)} %bitcast.43), channel_id=1, source_target_pairs={{0,4},{4,8},{8,12},{12,16},{16,20},{20,24},{24,28},{28,0},{1,5},{5... | collective-permute-start | bytes 294920 | tf_op jit(solution)/shard_map/ppermute | solution.py:20
  2.2 5.7 %collective-permute-start.1 = (bf16[6,32,256]{2,0,1:T(8,128)(2,1)S(1)}, bf16[6,32,256]{2,0,1:T(8,128)(2,1)S(1)}, u32[]{:S(2)}, u32[]{:S(2)}) collective-permute-start(bf16[6,32,256]{2,0,1:T(8,128)(2,1)S(1)} %bitcast.44), channel_id=1, source_target_pairs={{0,28},{4,0},{8,4},{12,8},{16,12},{20,16},{24,20},{28,24},{1,29},{... | collective-permute-start | bytes 294920 | tf_op jit(solution)/shard_map/ppermute | solution.py:20
  8.0 5.8 %collective-permute-start.3 = (bf16[10,8,256]{2,1,0:T(8,128)(2,1)S(1)}, bf16[10,8,256]{2,1,0:T(8,128)(2,1)S(1)}, u32[]{:S(2)}, u32[]{:S(2)}) collective-permute-start(bf16[10,8,256]{2,1,0:T(8,128)(2,1)S(1)} %pad.8), channel_id=1, source_target_pairs={{0,3},{1,0},{2,1},{3,2},{4,7},{5,4},{6,5},{7,6},{8,11},{9,8},{10,9... | collective-permute-start | bytes 122888 | tf_op jit(solution)/shard_map/ppermute | solution.py:20
  12.2 6.3 %collective-permute-start.2 = (bf16[10,8,256]{2,1,0:T(8,128)(2,1)S(1)}, bf16[10,8,256]{2,1,0:T(8,128)(2,1)S(1)}, u32[]{:S(2)}, u32[]{:S(2)}) collective-permute-start(bf16[10,8,256]{2,1,0:T(8,128)(2,1)S(1)} %pad.7), channel_id=1, source_target_pairs={{0,1},{1,2},{2,3},{3,0},{4,5},{5,6},{6,7},{7,4},{8,9},{9,10},{10,1... | collective-permute-start | bytes 122888 | tf_op jit(solution)/shard_map/ppermute | solution.py:20
  13.8 4.6 %copy-start.7 = (bf16[10,8,256]{2,1,0:T(8,128)(2,1)}, bf16[10,8,256]{2,1,0:T(8,128)(2,1)S(1)}, u32[]{:S(2)}) copy-start(bf16[10,8,256]{2,1,0:T(8,128)(2,1)S(1)} %collective-permute-done.3.after_ref) | copy-start | bytes 122884
  18.5 0.6 copy-start.8
  44.6 8.3 %collective-permute-start.4 = (f32[64,768]{1,0:T(8,128)}, f32[64,768]{1,0:T(8,128)S(1)}, u32[]{:S(2)}, u32[]{:S(2)}) collective-permute-start(f32[64,768]{1,0:T(8,128)} %get-tuple-element.33), channel_id=1, source_target_pairs={{0,16},{4,20},{8,24},{12,28},{16,0},{20,4},{24,8},{28,12},{1,17},{... | collective-permute-start | bytes 589832 | tf_op jit(solution)/shard_map/ppermute | solution.py:25
  46.3 7.4 %copy-start.1 = (f32[64,512]{1,0:T(8,128)S(1)}, f32[64,512]{1,0:T(8,128)}, u32[]{:S(2)}) copy-start(f32[64,512]{1,0:T(8,128)} %get-tuple-element.32) | copy-start | bytes 393220
  53.8 7.5 %collective-permute-start.5 = (f32[32,1024]{1,0:T(8,128)S(1)}, f32[32,1024]{1,0:T(8,128)S(1)}, u32[]{:S(2)}, u32[]{:S(2)}) collective-permute-start(f32[32,1024]{1,0:T(8,128)S(1)} %pad_maximum_fusion), channel_id=1, source_target_pairs={{0,8},{4,12},{8,0},{12,4},{16,24},{20,28},{24,16},{28,20},{1,9},{5... | collective-permute-start | bytes 393224 | tf_op jit(solution)/shard_map/ppermute | solution.py:25
  61.3 6.3 %collective-permute-start.6 = (bf16[10,8,256]{2,1,0:T(8,128)(2,1)}, bf16[10,8,256]{2,1,0:T(8,128)(2,1)S(1)}, u32[]{:S(2)}, u32[]{:S(2)}) collective-permute-start(bf16[10,8,256]{2,1,0:T(8,128)(2,1)} %get-tuple-element.42), channel_id=1, source_target_pairs={{0,1},{1,2},{2,3},{3,0},{4,5},{5,6},{6,7},{7,4},{8,9},{9,10},{10,1... | collective-permute-start | bytes 122888 | tf_op jit(solution)/shard_map/ppermute | solution.py:20
  61.4 6.4 %collective-permute-start.10 = (f32[16,1536]{1,0:T(8,128)S(1)}, f32[16,1536]{1,0:T(8,128)S(1)}, u32[]{:S(2)}, u32[]{:S(2)}) collective-permute-start(f32[16,1536]{1,0:T(8,128)S(1)} %constant_dynamic-update-slice_fusion), channel_id=1, source_target_pairs={{0,4},{4,0},{8,12},{12,8},{16,20},{20,16},{24,28},{28,24},{1,5},{5... | collective-permute-start | bytes 294920 | tf_op jit(solution)/shard_map/ppermute | solution.py:25
  61.5 6.2 %collective-permute-start.7 = (bf16[10,8,256]{2,1,0:T(8,128)(2,1)}, bf16[10,8,256]{2,1,0:T(8,128)(2,1)S(1)}, u32[]{:S(2)}, u32[]{:S(2)}) collective-permute-start(bf16[10,8,256]{2,1,0:T(8,128)(2,1)} %get-tuple-element.43), channel_id=1, source_target_pairs={{0,3},{1,0},{2,1},{3,2},{4,7},{5,4},{6,5},{7,6},{8,11},{9,8},{10,9... | collective-permute-start | bytes 122888 | tf_op jit(solution)/shard_map/ppermute | solution.py:20
  67.7 7.1 %copy-start.5 = (bf16[10,8,256]{2,1,0:T(8,128)(2,1)}, bf16[10,8,256]{2,1,0:T(8,128)(2,1)S(1)}, u32[]{:S(2)}) copy-start(bf16[10,8,256]{2,1,0:T(8,128)(2,1)S(1)} %collective-permute-done.6.after_ref) | copy-start | bytes 122884
  67.7 7.1 %copy-start.6 = (bf16[10,8,256]{2,1,0:T(8,128)(2,1)}, bf16[10,8,256]{2,1,0:T(8,128)(2,1)S(1)}, u32[]{:S(2)}) copy-start(bf16[10,8,256]{2,1,0:T(8,128)(2,1)S(1)} %collective-permute-done.7.before_ref) | copy-start | bytes 122884
  67.9 4.7 %collective-permute-start.11 = (f32[16,1536]{1,0:T(8,128)S(1)}, f32[16,1536]{1,0:T(8,128)S(1)}, u32[]{:S(2)}, u32[]{:S(2)}) collective-permute-start(f32[16,1536]{1,0:T(8,128)S(1)} %constant_dynamic-update-slice_fusion.4), channel_id=1, source_target_pairs={{0,1},{1,0},{2,3},{3,2},{4,5},{5,4},{6,7},{7,6},{8,9},{9,8},{10,11... | collective-permute-start | bytes 294920 | tf_op jit(solution)/shard_map/ppermute | solution.py:25
  69.1 5.6 %collective-permute-start.8 = (bf16[6,32,256]{2,1,0:T(8,128)(2,1)S(1)}, bf16[6,32,256]{2,1,0:T(8,128)(2,1)S(1)}, u32[]{:S(2)}, u32[]{:S(2)}) collective-permute-start(bf16[6,32,256]{2,1,0:T(8,128)(2,1)S(1)} %get-tuple-element.72), channel_id=1, source_target_pairs={{0,28},{4,0},{8,4},{12,8},{16,12},{20,16},{24,20},{28,24},{1,29},{... | collective-permute-start | bytes 294920 | tf_op jit(solution)/shard_map/ppermute | solution.py:20
  69.5 5.2 %collective-permute-start.9 = (bf16[6,32,256]{2,1,0:T(8,128)(2,1)S(1)}, bf16[6,32,256]{2,1,0:T(8,128)(2,1)S(1)}, u32[]{:S(2)}, u32[]{:S(2)}) collective-permute-start(bf16[6,32,256]{2,1,0:T(8,128)(2,1)S(1)} %get-tuple-element.71), channel_id=1, source_target_pairs={{0,4},{4,8},{8,12},{12,16},{16,20},{20,24},{24,28},{28,0},{1,5},{5... | collective-permute-start | bytes 294920 | tf_op jit(solution)/shard_map/ppermute | solution.py:20
  72.6 7.7 %copy-start = (f32[16,1536]{1,0:T(8,128)}, f32[16,1536]{1,0:T(8,128)S(1)}, u32[]{:S(2)}) copy-start(f32[16,1536]{1,0:T(8,128)S(1)} %add.66.mine_ref) | copy-start | bytes 294916
  72.6 7.7 %collective-permute-start.12 = (f32[16,1536]{1,0:T(8,128)S(1)}, f32[16,1536]{1,0:T(8,128)S(1)}, u32[]{:S(2)}, u32[]{:S(2)}) collective-permute-start(f32[16,1536]{1,0:T(8,128)S(1)} %add.66.mine_ref), channel_id=1, source_target_pairs={{0,2},{1,3},{2,0},{3,1},{4,6},{5,7},{6,4},{7,5},{8,10},{9,11},{10,... | collective-permute-start | bytes 294920 | tf_op jit(solution)/shard_map/ppermute | solution.py:25
  74.7 0.6 copy-start.3
  75.4 0.6 copy-start.4
  80.3 0.6 copy-start.2

commit v4 on v2

--- a/solution.py
+++ b/solution.py
@@ -117,6 +117,7 @@
     gpre_ref,
     keep_ref,
     give_ref,
+    conv_t_ref,
     split_ref,
     conv_ref,
     down_ref,
@@ -140,7 +141,9 @@
         gconv_t_ref[...] = jnp.zeros_like(gconv_t_ref)
         gdb_ref[...] = jnp.zeros_like(gdb_ref)
         sq_ref[...] = jnp.zeros_like(sq_ref)
-        conv_ref[:, : 16 * group] = (0.5 * conv_rows(conv_weight_ref, tap_ref)).astype(bf16)
+        conv = conv_rows(conv_weight_ref, tap_ref)
+        conv_t_ref[...] = jnp.transpose(conv).astype(bf16)
+        conv_ref[:, : 16 * group] = (0.5 * conv).astype(bf16)
         bias = 0.5 * row_of(conv_bias_ref, hidden)
         at = lax.broadcasted_iota(jnp.int32, bias.shape, 1)
         columns = jnp.zeros_like(bias)
@@ -268,17 +271,52 @@
         give_ref[:, 8 * hidden :] = small
 
 
+def merged(piece, group):
+    halves = [
+        piece[par * group : (par + 1) * group]
+        + pltpu.roll(piece[(2 + par) * group : (3 + par) * group], 1, 1)
+        for par in range(2)
+    ]
+    return jnp.concatenate(halves, axis=1)
+
+
+def sides_kernel(sizes, first_ref, last_ref, conv_t_ref, merge_ref, edge_t_ref, before_ref, after_ref):
+    channels, pairs = sizes
+    group = 4 * channels
+    span = 4 * group
+    found = []
+    for ref, dy in ((first_ref, 0), (last_ref, 1)):
+        weights = jnp.concatenate([conv_t_ref[(2 * dz + dy) * span : (2 * dz + dy + 1) * span] for dz in range(2)], axis=0)
+        found.append(dot(weights, jnp.concatenate([ref[pair] for pair in range(pairs)], axis=1)))
+    rows = []
+    for slot in range(pairs + 1):
+        outer = []
+        for value in found:
+            total = 0.0
+            for dz in range(2):
+                pair = slot - dz
+                if 0 <= pair < pairs:
+                    total = total + value[dz * span : (dz + 1) * span, pair * lanes : (pair + 1) * lanes]
+            outer.append(merged(total, group))
+        rows.append(jnp.concatenate(outer, axis=0))
+    for slot in range(pairs + 1):
+        sides = 0.0
+        for value in split_two(rows[slot]):
+            sides = sides + dot(dot(edge_t_ref[...], value).astype(bf16), merge_ref[...])
+        for par in range(2):
+            before_ref[2 * slot + par] = sides[par * 16 : par * 16 + 8].astype(bf16)
+            after_ref[2 * slot + par] = sides[par * 16 + 8 : par * 16 + 16].astype(bf16)
+
+
 def spread_kernel(sizes, *refs):
-    channels, count, half_rows, tile, opening = sizes
+    channels, half_rows, tile, plan = sizes
+    pairs, slots, taken, done, given = plan
     refs = list(refs)
-    gpre_ref, conv_weight_ref, tap_ref, merge_ref, row_t_ref, edge_t_ref = refs[:6]
-    if opening:
-        core_ref, before_ref, after_ref, open_ref, spread_ref, conv_t_ref = refs[6:]
-        at = 0
-    else:
-        open_ref, early_before_ref, early_after_ref = refs[6:9]
-        core_ref, before_ref, after_ref, spread_ref, conv_t_ref = refs[9:]
-        at = early_before_ref.shape[0]
+    gpre_ref, conv_t_ref, merge_ref, row_t_ref = refs[:4]
+    taken_refs = refs[4 : 4 + len(taken)]
+    core_ref = refs[4 + len(taken)]
+    given_refs = refs[5 + len(taken) : -1]
+    spread_ref = refs[-1]
     group = 4 * channels
     span = 4 * group
     row_count = 2 * half_rows
@@ -292,62 +330,49 @@
                 for dy in range(2):
                     first = (2 * dz + dy) * span
                     here = slice(part * tile + dy * lanes, (part + 1) * tile + dy * lanes)
-                    spread_ref[pair + dz, :, here] += spread[first : first + span]
+                    spread_ref[slots.index(pair + dz), :, here] += spread[first : first + span]
 
     def finish(slot):
-        rows = []
-        for row in range(half_rows + 1):
-            piece = spread_ref[slot, :, row * lanes : (row + 1) * lanes]
-            halves = [
-                piece[par * group : (par + 1) * group]
-                + pltpu.roll(piece[(2 + par) * group : (3 + par) * group], 1, 1)
-                for par in range(2)
-            ]
-            rows.append(jnp.concatenate(halves, axis=1))
-        core, sides = 0.0, 0.0
-        outer = jnp.concatenate([rows[0], rows[half_rows]], axis=0)
+        rows = [
+            merged(spread_ref[slots.index(slot), :, row * lanes : (row + 1) * lanes], group)
+            for row in range(half_rows + 1)
+        ]
+        core = 0.0
         for value in split_two(jnp.concatenate(rows, axis=0)):
             core = core + dot(dot(row_t_ref[...], value).astype(bf16), merge_ref[...])
-        for value in split_two(outer):
-            sides = sides + dot(dot(edge_t_ref[...], value).astype(bf16), merge_ref[...])
         for par in range(2):
-            before_ref[at + 2 * slot + par] = sides[par * 16 : par * 16 + 8].astype(bf16)
-            after_ref[at + 2 * slot + par] = sides[par * 16 + 8 : par * 16 + 16].astype(bf16)
             for ch in range(channels):
                 first = (par * channels + ch) * row_count
-                core_ref[2 * slot + par, ch] = core[first : first + row_count]
-
-    for pair in range(count):
-
-        @pl.when(step == pair)
+                core_ref[2 * done.index(slot) + par, ch] = core[first : first + row_count]
+
+    for k, pair in enumerate(pairs):
+
+        @pl.when(step == k)
         def _():
-            if pair == 0:
+            if k == 0:
                 spread_ref[...] = jnp.zeros_like(spread_ref)
-                conv_t_ref[...] = jnp.transpose(conv_rows(conv_weight_ref, tap_ref)).astype(bf16)
-                if not opening:
-                    spread_ref[0] = open_ref[...]
-                    before_ref[:at] = early_before_ref[...]
-                    after_ref[:at] = early_after_ref[...]
-            else:
-                finish(pair - 1)
+                for slot, ref in zip(taken, taken_refs, strict=True):
+                    spread_ref[slots.index(slot)] = ref[...]
+            for slot in done:
+                if all(later not in (slot - 1, slot) for later in pairs[k:]) and slot - 1 != pairs[-1]:
+                    if any(before in (slot - 1, slot) for before in pairs[k - 1 : k]):
+                        finish(slot)
             spread_out(pair)
-            if pair == count - 1:
-                finish(pair)
-                if opening:
-                    open_ref[...] = spread_ref[count]
-                else:
-                    finish(count)
-
-
-def join_kernel(
-    sizes, early_ref, late_ref, below_ref, above_ref, before_ref, after_ref, out_ref
-):
-    channels, depth, row_count = sizes
-    early = early_ref.shape[0]
+            if k == len(pairs) - 1:
+                for slot in done:
+                    if pair in (slot - 1, slot):
+                        finish(slot)
+                for slot, ref in zip(given, given_refs, strict=True):
+                    ref[...] = spread_ref[slots.index(slot)]
+
+
+def join_kernel(sizes, *refs):
+    channels, depth, row_count, places = sizes
+    below_ref, above_ref, before_ref, after_ref, out_ref = refs[-5:]
     for z in range(depth):
-        plane_ref = early_ref.at[z + 1] if z + 1 < early else late_ref.at[z + 1 - early]
+        which, at = places[z]
         for ch in range(channels):
-            value = plane_ref[ch]
+            value = refs[which][at, ch]
             if z == 0:
                 value = value + above_ref[ch].astype(f32)
             if z == depth - 1:
@@ -374,8 +399,9 @@
 
 def call(kernel, sizes, out_shape, *args, grid=None, in_specs=None, out_specs=None, scratch=(), flops=0, name):
     if grid is None:
-        in_specs = [pl.BlockSpec(memory_space=pltpu.VMEM)] * len(args)
-        out_specs = [pl.BlockSpec(memory_space=pltpu.VMEM)] * len(out_shape)
+        grid = (1,)
+        in_specs = [whole(a.shape) for a in args]
+        out_specs = [whole(o.shape) for o in out_shape]
     return pl.pallas_call(
         functools.partial(kernel, sizes),
         out_shape=out_shape,
@@ -389,7 +415,7 @@
             transcendentals=0,
         ),
         name=name,
-        **({} if grid is None else {"grid": grid}),
+        grid=grid,
     )(*args)
 
 
@@ -432,6 +458,7 @@
             jax.ShapeDtypeStruct((pairs, big, cells), bf16),
             jax.ShapeDtypeStruct((out_count // 2, big), f32),
             jax.ShapeDtypeStruct((out_count // 2, big + 2 * lanes), f32),
+            jax.ShapeDtypeStruct((win, big), bf16),
         ],
         *args,
         grid=(pairs,),
@@ -441,6 +468,7 @@
             pl.BlockSpec((1, big, cells), lambda z: (z, 0, 0)),
             whole((out_count // 2, big)),
             whole((out_count // 2, big + 2 * lanes)),
+            whole((win, big)),
         ],
         scratch=[
             pltpu.VMEM((pairs + 1, 16 * channels, cells + lanes), bf16),
@@ -460,33 +488,49 @@
     )
 
 
-def backward(grad_pre, first, count, conv_weight, fixed, shape, open_slot=None, early=()):
-    channels, depth, row_count, col_count = shape
+def sides(grad_pre, conv_t, fixed, shape):
+    channels, depth, _, col_count = shape
+    pairs, big, cells = grad_pre.shape
+    args = (grad_pre, grad_pre, conv_t, fixed["merge"], fixed["edge_t"])
+    out = jax.ShapeDtypeStruct((depth + 2, 8, col_count), bf16)
+    outer = [
+        pl.BlockSpec((pairs, big, lanes), lambda z: (0, 0, 0)),
+        pl.BlockSpec((pairs, big, lanes), lambda z: (0, 0, cells // lanes - 1)),
+    ]
+    return call(
+        sides_kernel,
+        (channels, pairs),
+        [out, out],
+        *args,
+        grid=(1,),
+        in_specs=outer + [whole(a.shape) for a in args[2:]],
+        out_specs=[whole(out.shape)] * 2,
+        flops=4 * pairs * big * lanes * conv_t.shape[0],
+        name="sides",
+    )
+
+
+def spread(grad_pre, conv_t, fixed, shape, plan, *taken):
+    channels, _, row_count, col_count = shape
     _, big, cells = grad_pre.shape
-    half_rows = row_count // 2
-    win = 64 * channels
-    opening = open_slot is None
-    args = (grad_pre, conv_weight, fixed["tap"], fixed["merge"], fixed["row_t"], fixed["edge_t"])
-    if not opening:
-        args += (open_slot, *early)
-    slots = count if opening else count + 1
-    sides = jax.ShapeDtypeStruct((2 * (first + slots), 8, col_count), bf16)
-    outs = [jax.ShapeDtypeStruct((2 * slots, channels, row_count, col_count), f32), sides, sides]
-    if opening:
-        outs.append(jax.ShapeDtypeStruct((16 * channels, cells + lanes), f32))
+    pairs, slots, _, done, given = plan
+    open_shape = (16 * channels, cells + lanes)
+    args = (grad_pre, conv_t, fixed["merge"], fixed["row_t"], *taken)
+    outs = [jax.ShapeDtypeStruct((2 * len(done), channels, row_count, col_count), f32)]
+    outs += [jax.ShapeDtypeStruct(open_shape, f32)] * len(given)
+    first = pairs[0]
+    stride = pairs[1] - first if len(pairs) > 1 else 1
     return call(
         spread_kernel,
-        (channels, count, half_rows, spread_tile, opening),
+        (channels, row_count // 2, spread_tile, plan),
         outs,
         *args,
-        grid=(count,),
-        in_specs=[pl.BlockSpec((1, big, cells), lambda z: (first + z, 0, 0))] + [whole(a.shape) for a in args[1:]],
+        grid=(len(pairs),),
+        in_specs=[pl.BlockSpec((1, big, cells), lambda z: (first + stride * z, 0, 0))]
+        + [whole(a.shape) for a in args[1:]],
         out_specs=[whole(o.shape) for o in outs],
-        scratch=[
-            pltpu.VMEM((count + 1, 16 * channels, cells + lanes), f32),
-            pltpu.VMEM((win, big), bf16),
-        ],
-        flops=2 * count * cells * big * win,
+        scratch=[pltpu.VMEM((len(slots), *open_shape), f32)],
+        flops=2 * len(pairs) * cells * big * conv_t.shape[0],
         name="spread",
     )
 
@@ -514,49 +558,41 @@
 
     before = shifted(side(row_count - 1), "gy", 1)
     after = shifted(side(0), "gy", -1)
-    out_field, grad_pre, own, packed = forward(
+    out_field, grad_pre, own, packed, conv_t = forward(
         fields, below, above, before, after, target,
         conv_weight, conv_bias, down_weight, down_bias, fixed, cell_total,
     )
+    pairs = depth // 2
+    shape = fields.shape
 
     def beside(value, count):
         return jnp.concatenate(jnp.split(value, value.shape[0] // count, axis=0), axis=1)
 
     me = lax.axis_index("gz")
-    bit = lax.axis_size("gz") // 2
     small = packed[:, big:]
-    parts, open_slot, early, core = 2, None, (), []
-    pairs = depth // 2
-    while True:
-        got = exchanged(packed, "gz", bit)
-        if len(core) < parts:
-            count = pairs // parts
-            found = backward(
-                grad_pre, len(core) * count, count, conv_weight, fixed, fields.shape, open_slot, early
-            )
-            core.append(found[0])
-            early = found[1:3]
-            open_slot = found[3] if len(core) < parts else None
-        count = own.shape[0]
-        own = own + got[:, :big]
-        pieces = jnp.split(got[:, big:], hidden // count, axis=1)
-        small = small + jnp.concatenate(pieces, axis=0)
-        if bit == 1:
-            break
-        bit //= 2
-        count //= 2
+
+    def added(own, small, got):
+        pieces = jnp.split(got[:, big:], hidden // own.shape[0], axis=1)
+        return own + got[:, :big], small + jnp.concatenate(pieces, axis=0)
+
+    def halved(own, small, bit):
+        count = own.shape[0] // 2
         upper = (me // bit) % 2
         give = lax.dynamic_slice_in_dim(own, (1 - upper) * count, count, 0)
         own = lax.dynamic_slice_in_dim(own, upper * count, count, 0)
-        packed = jnp.concatenate([give, beside(small, count)], axis=1)
-        if len(core) < parts:
-            packed, open_slot = lax.optimization_barrier((packed, open_slot))
-    packed = jnp.concatenate([own, beside(small, own.shape[0])], axis=1)
-    count = own.shape[0]
-    to_before, to_after = early
-
+        return own, jnp.concatenate([give, beside(small, count)], axis=1)
+
+    bit = lax.axis_size("gz") // 2
+    got = exchanged(packed, "gz", bit)
+    to_before, to_after = sides(grad_pre, conv_t, fixed, shape)
     from_before = shifted(to_after, "gy", 1)
     from_after = shifted(to_before, "gy", -1)
+    outer = ((0, pairs - 1), (0, 1, pairs - 1, pairs), (), (0, pairs), (1, pairs - 1))
+    outer_core, low_open, high_open = spread(grad_pre, conv_t, fixed, shape, outer)
+    own, small = added(own, small, got)
+    bit //= 2
+    own, packed = halved(own, small, bit)
+    packed, low_open = lax.optimization_barrier((packed, low_open))
 
     def plane(value, at):
         low = from_before[at, :channels, None].astype(f32)
@@ -564,19 +600,37 @@
         gap = jnp.zeros((channels, row_count - 2, col_count), f32)
         return (value + jnp.concatenate([low, gap, high], axis=1)).astype(bf16)
 
-    from_below = shifted(plane(core[-1][-1], depth + 1), "gz", 1)
-    from_above = shifted(plane(core[0][0], 0), "gz", -1)
+    got = exchanged(packed, "gz", bit)
+    from_below = shifted(plane(outer_core[3], depth + 1), "gz", 1)
+    from_above = shifted(plane(outer_core[0], 0), "gz", -1)
+    middle = pairs // 2
+    lower = (tuple(range(1, middle)), tuple(range(1, middle + 1)), (1,), tuple(range(1, middle)), (middle,))
+    lower_core, middle_open = spread(grad_pre, conv_t, fixed, shape, lower, low_open)
+    own, small = added(own, small, got)
+    while bit > 1:
+        bit //= 2
+        own, packed = halved(own, small, bit)
+        own, small = added(own, small, exchanged(packed, "gz", bit))
+    packed = jnp.concatenate([own, beside(small, own.shape[0])], axis=1)
+    count = own.shape[0]
+    packed, middle_open = lax.optimization_barrier((packed, middle_open))
 
     bit = 1
+    got = exchanged(packed, "gy", bit)
+    slots = tuple(range(middle, pairs))
+    upper = (tuple(range(middle, pairs - 1)), slots, (middle, pairs - 1), slots, ())
+    (upper_core,) = spread(grad_pre, conv_t, fixed, shape, upper, middle_open, high_open)
     while 2 * bit < lax.axis_size("gy"):
-        packed = packed + exchanged(packed, "gy", bit)
+        packed = packed + got
         bit *= 2
-    got = exchanged(packed, "gy", bit)
+        got = exchanged(packed, "gy", bit)
+    places = [(0, 1)] + [(1, at) for at in range(2 * middle - 2)]
+    places += [(2, at) for at in range(2 * (pairs - middle))] + [(0, 2)]
     (sensitivity,) = call(
         join_kernel,
-        (channels, depth, row_count),
-        [jax.ShapeDtypeStruct(fields.shape, f32)],
-        *core, from_above, from_below, from_after, from_before,
+        (channels, depth, row_count, tuple(places)),
+        [jax.ShapeDtypeStruct(shape, f32)],
+        outer_core, lower_core, upper_core, from_above, from_below, from_after, from_before,
         name="join",
     )
     conv, cbias, down, dbias, loss = call(

time: 83.2 us -> 87.2 us (1.048)
  Pallas kernels: 43.8 us -> 49.2 us
  other arithmetic: 2.11 us -> 1.09 us
    pallas_call x5 -> x7, Pallas kernels: 43.8 us -> 49.2 us  [call(): pl.pallas_call(functools.partial(kernel, sizes), out_shape=out_shape, in_...]
    ppermute x8, starting transfers between devices: 12 us -> 14.2 us  [shifted(): lax.ppermute(value, axis, [(i, (i + by) % count) for i in range(count)])]
    ppermute x8, waiting for transfers between devices: 8.6 us -> 6.52 us  [shifted(): lax.ppermute(value, axis, [(i, (i + by) % count) for i in range(count)])]
    ppermute x5, starting transfers between devices: 3.81 us -> 2.22 us  [exchanged(): return lax.ppermute(value, axis, [(i, i ^ bit) for i in range(count)])]
    ppermute x5, waiting for transfers between devices: 5.53 us -> 7.01 us  [exchanged(): return lax.ppermute(value, axis, [(i, i ^ bit) for i in range(count)])]
    convert_element_type x1, other arithmetic: 1.13 us -> 0.1 us  [plane(): return (value + jnp.concatenate([low, gap, high], axis=1)).astype(bf16)]
    unnamed x27 -> x29, local copies, waits for them, and re-layouts: 2.44 us -> 2.1 us
  transfers between devices with their start and end apart: 13 -> 13, of which waited for: 9 -> 6; matrix products, arithmetic and copies ran while one was open for 5% -> 4% of each run, Pallas kernels for 11% -> 25%
where the time goes in v4:
time: 87.2 us; the launch traced here: 86.9 us
  Pallas kernels  49.2 us (56%)
  starting transfers between devices  16.4 us (19%)
  waiting for transfers between devices  13.5 us (15%)
  local copies, waits for them, and re-layouts  5.69 us (7%)
  other arithmetic  1.09 us (1%)
  between operations  1 us (1%)
    pallas_call x7, Pallas kernels, call(): pl.pallas_call(functools.partial(kernel, sizes), out_shape=out_shape, in_...  49.2 us
    ppermute x8, starting transfers between devices, shifted(): lax.ppermute(value, axis, [(i, (i + by) % count) for i in range(count)])  14.2 us
    ppermute x5, waiting for transfers between devices, exchanged(): return lax.ppermute(value, axis, [(i, i ^ bit) for i in range(count)])  7.01 us
    ppermute x8, waiting for transfers between devices, shifted(): lax.ppermute(value, axis, [(i, (i + by) % count) for i in range(count)])  6.52 us
    ppermute x5, starting transfers between devices, exchanged(): return lax.ppermute(value, axis, [(i, i ^ bit) for i in range(count)])  2.22 us
    unnamed x29, local copies, waits for them, and re-layouts  2.1 us
  transfers between devices with their start and end apart: 13, of which 6 were waited for; matrix products, arithmetic and copies ran while one was open for 4% of the time, Pallas kernels for 25%

profile of v4, /device:TPU:0, one launch (start us, length us, event | category | flops | bytes accessed | tf_op | source)
XLA Modules:
  0.0 86.9 jit_solution(15024754884902112912)
XLA Ops:
  0.6 1.0 %fusion.8 = (bf16[6,1,32,256]{3,2,1,0:T(8,128)(2,1)S(1)}, bf16[6,1,32,256]{3,2,1,0:T(8,128)(2,1)S(1)}) fusion(bf16[6,8,32,256]{3,2,1,0:T(8,128)(2,1)} %field_ref.1), kind=kLoop, calls=%fused_computation.37 | loop fusion | bytes 393216 | tf_op jit(solution)/shard_map/slice | solution.py:552
  1.6 0.1 copy.40
  1.7 0.5 collective-permute-start
  2.2 0.1 copy.39
  2.2 3.0 %collective-permute-start.1 = (bf16[6,32,256]{2,0,1:T(8,128)(2,1)S(1)}, bf16[6,32,256]{2,0,1:T(8,128)(2,1)S(1)}, u32[]{:S(2)}, u32[]{:S(2)}) collective-permute-start(bf16[6,32,256]{2,0,1:T(8,128)(2,1)S(1)} %bitcast.44), channel_id=1, source_target_pairs={{0,28},{4,0},{8,4},{12,8},{16,12},{20,16},{24,20},{28,24},{1,29},{... | collective-permute-start | bytes 294920 | tf_op jit(solution)/shard_map/ppermute | solution.py:20
  5.2 1.1 %fusion.7 = (bf16[6,8,1,256]{3,2,1,0:T(2,128)(2,1)S(1)}, bf16[6,8,1,256]{3,2,1,0:T(2,128)(2,1)S(1)}) fusion(bf16[6,8,32,256]{3,2,1,0:T(8,128)(2,1)} %field_ref.1), kind=kLoop, calls=%fused_computation.36 | loop fusion | bytes 98304 | tf_op jit(solution)/shard_map/slice | solution.py:555
  6.3 1.4 %collective-permute-done = bf16[6,32,256]{2,0,1:T(8,128)(2,1)S(1)} collective-permute-done((bf16[6,32,256]{2,0,1:T(8,128)(2,1)S(1)}, bf16[6,32,256]{2,0,1:T(8,128)(2,1)S(1)}, u32[]{:S(2)}, u32[]{:S(2)}) %collective-permute-start) | collective-permute-done | bytes 98336 | tf_op jit(solution)/shard_map/ppermute | solution.py:20
  7.7 0.3 collective-permute-done.1
  8.0 4.1 %collective-permute-start.3 = (bf16[10,8,256]{2,1,0:T(8,128)(2,1)S(1)}, bf16[10,8,256]{2,1,0:T(8,128)(2,1)S(1)}, u32[]{:S(2)}, u32[]{:S(2)}) collective-permute-start(bf16[10,8,256]{2,1,0:T(8,128)(2,1)S(1)} %pad.8), channel_id=1, source_target_pairs={{0,3},{1,0},{2,1},{3,2},{4,7},{5,4},{6,5},{7,6},{8,11},{9,8},{10,9... | collective-permute-start | bytes 122888 | tf_op jit(solution)/shard_map/ppermute | solution.py:20
  12.2 0.1 collective-permute-start.2
  12.3 0.7 copy.25.below_ref
  12.9 0.7 copy.26.above_ref
  13.6 0.3 collective-permute-done.3.after_ref
  13.8 4.6 %collective-permute-done.2.before_ref = bf16[10,8,256]{2,1,0:T(8,128)(2,1)S(1)} collective-permute-done((bf16[10,8,256]{2,1,0:T(8,128)(2,1)S(1)}, bf16[10,8,256]{2,1,0:T(8,128)(2,1)S(1)}, u32[]{:S(2)}, u32[]{:S(2)}) %collective-permute-start.2) | collective-permute-done | bytes 40992 | tf_op jit(solution)/shard_map/ppermute | solution.py:20
  18.5 0.6 copy-done.9
  19.1 25.6 %forward.1 = (bf16[128,4,16,128]{3,2,1,0:T(8,128)(2,1)}, bf16[4,512,2048]{2,1,0:T(8,128)(2,1)}, f32[64,512]{1,0:T(8,128)}, f32[64,768]{1,0:T(8,128)}, bf16[384,512]{1,0:T(8,128)(2,1)}) custom-call(bf16[6,8,32,256]{3,2,1,0:T(8,128)(2,1)} %field_ref.1, bf16[6,32,256]{2,1,0:T(8,128)(2,1)} %copy.25.below_ref, bf16[6,32,256]{2,1,0:T(8,128)(2,1)} %copy.26.above_ref, ...), custom_call_target="tpu_custom_call" | custom-call | flops 8589934592 | bytes 16488448 | tf_op jit(solution)/shard_map/forward/pallas_call | solution.py:405
  44.7 1.6 %collective-permute-start.4 = (f32[64,768]{1,0:T(8,128)}, f32[64,768]{1,0:T(8,128)S(1)}, u32[]{:S(2)}, u32[]{:S(2)}) collective-permute-start(f32[64,768]{1,0:T(8,128)} %get-tuple-element.33), channel_id=1, source_target_pairs={{0,16},{4,20},{8,24},{12,28},{16,0},{20,4},{24,8},{28,12},{1,17},{... | collective-permute-start | bytes 589832 | tf_op jit(solution)/shard_map/ppermute | solution.py:25
  46.4 0.1 pad.13.clone
  46.4 3.1 %sides.1 = (bf16[10,8,256]{2,1,0:T(8,128)(2,1)}, bf16[10,8,256]{2,1,0:T(8,128)(2,1)}) custom-call(bf16[4,512,2048]{2,1,0:T(8,128)(2,1)} %get-tuple-element.29.refs_0_.first_ref.last_ref, bf16[4,512,2048]{2,1,0:T(8,128)(2,1)} %get-tuple-element.29.refs_0_.first_ref.last_ref, bf16[384,512]{1,0:T(8,128)(2,1)} %get-tuple-element.30.refs_1_.conv_t_ref, ...), custom_call_target="tpu_custom_call" | custom-call | flops 402653184 | bytes 17386496 | tf_op jit(solution)/shard_map/sides/pallas_call | solution.py:405
  49.5 0.0 collective-permute-start.7
  49.5 3.8 %collective-permute-start.8 = (bf16[10,8,256]{2,1,0:T(8,128)(2,1)}, bf16[10,8,256]{2,1,0:T(8,128)(2,1)S(1)}, u32[]{:S(2)}, u32[]{:S(2)}) collective-permute-start(bf16[10,8,256]{2,1,0:T(8,128)(2,1)} %get-tuple-element.42), channel_id=1, source_target_pairs={{0,3},{1,0},{2,1},{3,2},{4,7},{5,4},{6,5},{7,6},{8,11},{9,8},{10,9... | collective-permute-start | bytes 122888 | tf_op jit(solution)/shard_map/ppermute | solution.py:20
  53.3 6.4 %spread.3 = (f32[4,6,32,256]{3,2,1,0:T(8,128)}, f32[96,2176]{1,0:T(8,128)}, f32[96,2176]{1,0:T(8,128)}) custom-call(bf16[4,512,2048]{2,1,0:T(8,128)(2,1)} %get-tuple-element.29.refs_0_.first_ref.last_ref, bf16[384,512]{1,0:T(8,128)(2,1)} %get-tuple-element.30.refs_1_.conv_t_ref, bf16[256,256]{1,0:T(8,128)(2,1)} %constant.71.clone.refs_2_.merge_ref, ...), custom_call_target="tpu_custom_call" | custom-call | flops 1610612736 | bytes 11683840 | tf_op jit(solution)/shard_map/spread/pallas_call | solution.py:405
  59.7 0.0 collective-permute-done.4
  59.7 0.8 slice_add_fusion.2
  60.7 0.4 collective-permute-start.5
  61.0 0.0 collective-permute-done.7.refs_6_
  61.0 4.7 %collective-permute-done.5 = f32[32,1024]{1,0:T(8,128)S(1)} collective-permute-done((f32[32,1024]{1,0:T(8,128)S(1)}, f32[32,1024]{1,0:T(8,128)S(1)}, u32[]{:S(2)}, u32[]{:S(2)}) %collective-permute-start.5) | collective-permute-done | bytes 131104 | tf_op jit(solution)/shard_map/ppermute | solution.py:25
  65.8 0.1 collective-permute-start.6
  65.9 0.0 collective-permute-done.8.refs_5_
  65.9 0.0 copy-start.7
  66.0 4.5 %spread.4 = (f32[2,6,32,256]{3,2,1,0:T(8,128)}, f32[96,2176]{1,0:T(8,128)}) custom-call(bf16[4,512,2048]{2,1,0:T(8,128)(2,1)} %get-tuple-element.29.refs_0_.first_ref.last_ref, bf16[384,512]{1,0:T(8,128)(2,1)} %get-tuple-element.30.refs_1_.conv_t_ref, bf16[256,256]{1,0:T(8,128)(2,1)} %constant.71.clone.refs_2_.merge_ref, ...), custom_call_target="tpu_custom_call" | custom-call | flops 805306368 | bytes 11290624 | tf_op jit(solution)/shard_map/spread/pallas_call | solution.py:405
  70.4 0.0 copy-done.7
  70.5 0.0 collective-permute-done.6
  70.6 0.1 collective-permute-start.11
  70.7 0.1 fusion.1
  70.8 0.5 collective-permute-start.10
  71.3 2.2 %collective-permute-start.9 = (bf16[6,32,256]{2,1,0:T(8,128)(2,1)S(1)}, bf16[6,32,256]{2,1,0:T(8,128)(2,1)S(1)}, u32[]{:S(2)}, u32[]{:S(2)}) collective-permute-start(bf16[6,32,256]{2,1,0:T(8,128)(2,1)S(1)} %get-tuple-element.50), channel_id=1, source_target_pairs={{0,28},{4,0},{8,4},{12,8},{16,12},{20,16},{24,20},{28,24},{1,29},{... | collective-permute-start | bytes 294920 | tf_op jit(solution)/shard_map/ppermute | solution.py:20
  73.5 2.3 %collective-permute-done.11 = f32[16,1536]{1,0:T(8,128)S(1)} collective-permute-done((f32[16,1536]{1,0:T(8,128)S(1)}, f32[16,1536]{1,0:T(8,128)S(1)}, u32[]{:S(2)}, u32[]{:S(2)}) %collective-permute-start.11) | collective-permute-done | bytes 98336 | tf_op jit(solution)/shard_map/ppermute | solution.py:25
  75.8 0.1 collective-permute-start.12
  75.9 5.1 %spread.5.refs_2_ = f32[4,6,32,256]{3,2,1,0:T(8,128)} custom-call(bf16[4,512,2048]{2,1,0:T(8,128)(2,1)} %get-tuple-element.29.refs_0_.first_ref.last_ref, bf16[384,512]{1,0:T(8,128)(2,1)} %get-tuple-element.30.refs_1_.conv_t_ref, bf16[256,256]{1,0:T(8,128)(2,1)} %constant.71.clone.refs_2_.merge_ref, bf16[384,408]{1,0:T(8,128)(2,1)} %constant.73.clone.refs_3_, ...), custom_call_target="tpu_custom_call" | custom-call | flops 805306368 | bytes 11683840 | tf_op jit(solution)/shard_map/spread/pallas_call | solution.py:405
  81.1 0.0 collective-permute-done.10.refs_4_
  81.1 0.0 collective-permute-done.9.refs_3_
  81.1 0.6 copy-done.4
  81.7 0.1 copy-done.5
  81.8 2.9 %join.1 = f32[6,8,32,256]{3,2,1,0:T(8,128)} custom-call(f32[4,6,32,256]{3,2,1,0:T(8,128)} %get-tuple-element.31.refs_0_, f32[2,6,32,256]{3,2,1,0:T(8,128)} %get-tuple-element.36.refs_1_, f32[4,6,32,256]{3,2,1,0:T(8,128)} %spread.5.refs_2_, bf16[6,32,256]{2,1,0:T(8,128)(2,1)} %copy-done.5, bf16[6,32,256]{2,1,0:T(8,128)(2,1)} %copy-done.4, ...), custom_call_target="tpu_custom_call" | custom-call | bytes 3817472 | tf_op jit(solution)/shard_map/join/pallas_call | solution.py:405
  84.7 0.0 collective-permute-done.12.theirs_ref
  84.7 0.6 copy-done.3
  85.3 1.6 %last.1 = (f32[64,162]{1,0:T(8,128)}, f32[1,64]{1,0:T(1,128)}, f32[16,512]{1,0:T(8,128)}, f32[1,128]{1,0:T(1,128)}, f32[1,1]{1,0:T(1,128)}) custom-call(f32[16,1536]{1,0:T(8,128)} %copy-done.1, f32[16,1536]{1,0:T(8,128)} %copy-done.3), custom_call_target="tpu_custom_call" | custom-call | bytes 271620 | tf_op jit(solution)/shard_map/last/pallas_call | solution.py:405
  (48 shorter events, 0.3 us)
Async XLA Ops:
  1.7 6.0 %collective-permute-start = (bf16[6,32,256]{2,0,1:T(8,128)(2,1)S(1)}, bf16[6,32,256]{2,0,1:T(8,128)(2,1)S(1)}, u32[]{:S(2)}, u32[]{:S(2)}) collective-permute-start(bf16[6,32,256]{2,0,1:T(8,128)(2,1)S(1)} %bitcast.43), channel_id=1, source_target_pairs={{0,4},{4,8},{8,12},{12,16},{16,20},{20,24},{24,28},{28,0},{1,5},{5... | collective-permute-start | bytes 294920 | tf_op jit(solution)/shard_map/ppermute | solution.py:20
  2.2 5.7 %collective-permute-start.1 = (bf16[6,32,256]{2,0,1:T(8,128)(2,1)S(1)}, bf16[6,32,256]{2,0,1:T(8,128)(2,1)S(1)}, u32[]{:S(2)}, u32[]{:S(2)}) collective-permute-start(bf16[6,32,256]{2,0,1:T(8,128)(2,1)S(1)} %bitcast.44), channel_id=1, source_target_pairs={{0,28},{4,0},{8,4},{12,8},{16,12},{20,16},{24,20},{28,24},{1,29},{... | collective-permute-start | bytes 294920 | tf_op jit(solution)/shard_map/ppermute | solution.py:20
  8.0 5.8 %collective-permute-start.3 = (bf16[10,8,256]{2,1,0:T(8,128)(2,1)S(1)}, bf16[10,8,256]{2,1,0:T(8,128)(2,1)S(1)}, u32[]{:S(2)}, u32[]{:S(2)}) collective-permute-start(bf16[10,8,256]{2,1,0:T(8,128)(2,1)S(1)} %pad.8), channel_id=1, source_target_pairs={{0,3},{1,0},{2,1},{3,2},{4,7},{5,4},{6,5},{7,6},{8,11},{9,8},{10,9... | collective-permute-start | bytes 122888 | tf_op jit(solution)/shard_map/ppermute | solution.py:20
  12.2 6.3 %collective-permute-start.2 = (bf16[10,8,256]{2,1,0:T(8,128)(2,1)S(1)}, bf16[10,8,256]{2,1,0:T(8,128)(2,1)S(1)}, u32[]{:S(2)}, u32[]{:S(2)}) collective-permute-start(bf16[10,8,256]{2,1,0:T(8,128)(2,1)S(1)} %pad.7), channel_id=1, source_target_pairs={{0,1},{1,2},{2,3},{3,0},{4,5},{5,6},{6,7},{7,4},{8,9},{9,10},{10,1... | collective-permute-start | bytes 122888 | tf_op jit(solution)/shard_map/ppermute | solution.py:20
  13.8 4.6 %copy-start.8 = (bf16[10,8,256]{2,1,0:T(8,128)(2,1)}, bf16[10,8,256]{2,1,0:T(8,128)(2,1)S(1)}, u32[]{:S(2)}) copy-start(bf16[10,8,256]{2,1,0:T(8,128)(2,1)S(1)} %collective-permute-done.3.after_ref) | copy-start | bytes 122884
  18.5 0.6 copy-start.9
  44.7 15.0 %collective-permute-start.4 = (f32[64,768]{1,0:T(8,128)}, f32[64,768]{1,0:T(8,128)S(1)}, u32[]{:S(2)}, u32[]{:S(2)}) collective-permute-start(f32[64,768]{1,0:T(8,128)} %get-tuple-element.33), channel_id=1, source_target_pairs={{0,16},{4,20},{8,24},{12,28},{16,0},{20,4},{24,8},{28,12},{1,17},{... | collective-permute-start | bytes 589832 | tf_op jit(solution)/shard_map/ppermute | solution.py:25
  49.5 11.6 %collective-permute-start.7 = (bf16[10,8,256]{2,1,0:T(8,128)(2,1)}, bf16[10,8,256]{2,1,0:T(8,128)(2,1)S(1)}, u32[]{:S(2)}, u32[]{:S(2)}) collective-permute-start(bf16[10,8,256]{2,1,0:T(8,128)(2,1)} %get-tuple-element.41), channel_id=1, source_target_pairs={{0,1},{1,2},{2,3},{3,0},{4,5},{5,6},{6,7},{7,4},{8,9},{9,10},{10,1... | collective-permute-start | bytes 122888 | tf_op jit(solution)/shard_map/ppermute | solution.py:20
  49.5 11.1 %copy-start.2 = (f32[64,512]{1,0:T(8,128)S(1)}, f32[64,512]{1,0:T(8,128)}, u32[]{:S(2)}) copy-start(f32[64,512]{1,0:T(8,128)} %get-tuple-element.32) | copy-start | bytes 393220
  49.5 16.4 %collective-permute-start.8 = (bf16[10,8,256]{2,1,0:T(8,128)(2,1)}, bf16[10,8,256]{2,1,0:T(8,128)(2,1)S(1)}, u32[]{:S(2)}, u32[]{:S(2)}) collective-permute-start(bf16[10,8,256]{2,1,0:T(8,128)(2,1)} %get-tuple-element.42), channel_id=1, source_target_pairs={{0,3},{1,0},{2,1},{3,2},{4,7},{5,4},{6,5},{7,6},{8,11},{9,8},{10,9... | collective-permute-start | bytes 122888 | tf_op jit(solution)/shard_map/ppermute | solution.py:20
  60.7 5.0 %collective-permute-start.5 = (f32[32,1024]{1,0:T(8,128)S(1)}, f32[32,1024]{1,0:T(8,128)S(1)}, u32[]{:S(2)}, u32[]{:S(2)}) collective-permute-start(f32[32,1024]{1,0:T(8,128)S(1)} %pad_maximum_fusion), channel_id=1, source_target_pairs={{0,8},{4,12},{8,0},{12,4},{16,24},{20,28},{24,16},{28,20},{1,9},{5... | collective-permute-start | bytes 393224 | tf_op jit(solution)/shard_map/ppermute | solution.py:25
  61.0 9.4 %copy-start.6 = (bf16[10,8,256]{2,1,0:T(8,128)(2,1)}, bf16[10,8,256]{2,1,0:T(8,128)(2,1)S(1)}, u32[]{:S(2)}) copy-start(bf16[10,8,256]{2,1,0:T(8,128)(2,1)S(1)} %collective-permute-done.7.refs_6_) | copy-start | bytes 122884
  65.8 4.7 %collective-permute-start.6 = (f32[16,1536]{1,0:T(8,128)S(1)}, f32[16,1536]{1,0:T(8,128)S(1)}, u32[]{:S(2)}, u32[]{:S(2)}) collective-permute-start(f32[16,1536]{1,0:T(8,128)S(1)} %constant_dynamic-update-slice_fusion), channel_id=1, source_target_pairs={{0,4},{4,0},{8,12},{12,8},{16,20},{20,16},{24,28},{28,24},{1,5},{5... | collective-permute-start | bytes 294920 | tf_op jit(solution)/shard_map/ppermute | solution.py:25
  65.9 4.6 %copy-start.7 = (bf16[10,8,256]{2,1,0:T(8,128)(2,1)}, bf16[10,8,256]{2,1,0:T(8,128)(2,1)S(1)}, u32[]{:S(2)}) copy-start(bf16[10,8,256]{2,1,0:T(8,128)(2,1)S(1)} %collective-permute-done.8.refs_5_) | copy-start | bytes 122884
  66.0 4.7 %copy-start = (f32[4,6,32,256]{3,2,1,0:T(8,128)S(1)}, f32[4,6,32,256]{3,2,1,0:T(8,128)}, u32[]{:S(2)}) copy-start(f32[4,6,32,256]{3,2,1,0:T(8,128)} %get-tuple-element.31.refs_0_) | copy-start | bytes 2359300
  70.6 5.2 %collective-permute-start.11 = (f32[16,1536]{1,0:T(8,128)S(1)}, f32[16,1536]{1,0:T(8,128)S(1)}, u32[]{:S(2)}, u32[]{:S(2)}) collective-permute-start(f32[16,1536]{1,0:T(8,128)S(1)} %constant_dynamic-update-slice_fusion.4), channel_id=1, source_target_pairs={{0,1},{1,0},{2,3},{3,2},{4,5},{5,4},{6,7},{7,6},{8,9},{9,8},{10,11... | collective-permute-start | bytes 294920 | tf_op jit(solution)/shard_map/ppermute | solution.py:25
  70.8 10.3 %collective-permute-start.10 = (bf16[6,32,256]{2,1,0:T(8,128)(2,1)S(1)}, bf16[6,32,256]{2,1,0:T(8,128)(2,1)S(1)}, u32[]{:S(2)}, u32[]{:S(2)}) collective-permute-start(bf16[6,32,256]{2,1,0:T(8,128)(2,1)S(1)} %get-tuple-element.49), channel_id=1, source_target_pairs={{0,4},{4,8},{8,12},{12,16},{16,20},{20,24},{24,28},{28,0},{1,5},{5... | collective-permute-start | bytes 294920 | tf_op jit(solution)/shard_map/ppermute | solution.py:20
  71.3 9.8 %collective-permute-start.9 = (bf16[6,32,256]{2,1,0:T(8,128)(2,1)S(1)}, bf16[6,32,256]{2,1,0:T(8,128)(2,1)S(1)}, u32[]{:S(2)}, u32[]{:S(2)}) collective-permute-start(bf16[6,32,256]{2,1,0:T(8,128)(2,1)S(1)} %get-tuple-element.50), channel_id=1, source_target_pairs={{0,28},{4,0},{8,4},{12,8},{16,12},{20,16},{24,20},{28,24},{1,29},{... | collective-permute-start | bytes 294920 | tf_op jit(solution)/shard_map/ppermute | solution.py:20
  75.8 5.2 %copy-start.1 = (f32[16,1536]{1,0:T(8,128)}, f32[16,1536]{1,0:T(8,128)S(1)}, u32[]{:S(2)}) copy-start(f32[16,1536]{1,0:T(8,128)S(1)} %add.66.mine_ref) | copy-start | bytes 294916
  75.8 8.8 %collective-permute-start.12 = (f32[16,1536]{1,0:T(8,128)S(1)}, f32[16,1536]{1,0:T(8,128)S(1)}, u32[]{:S(2)}, u32[]{:S(2)}) collective-permute-start(f32[16,1536]{1,0:T(8,128)S(1)} %add.66.mine_ref), channel_id=1, source_target_pairs={{0,2},{1,3},{2,0},{3,1},{4,6},{5,7},{6,4},{7,5},{8,10},{9,11},{10,... | collective-permute-start | bytes 294920 | tf_op jit(solution)/shard_map/ppermute | solution.py:25
  81.1 0.6 copy-start.4
  81.1 0.7 copy-start.5
  84.7 0.6 copy-start.3

commit v5 on v4

--- a/solution.py
+++ b/solution.py
@@ -96,32 +96,79 @@
     return jnp.transpose(jnp.broadcast_to(ref[...], (lanes, count)))
 
 
-def forward_kernel(
+def prepare_kernel(
     sizes,
     field_ref,
     below_ref,
     above_ref,
+    conv_weight_ref,
+    conv_bias_ref,
+    down_weight_ref,
+    tap_ref,
+    order_ref,
+    col_ref,
+    row_ref,
+    split_ref,
+    conv_ref,
+    conv_t_ref,
+    down_ref,
+    down_t_ref,
+):
+    channels, pairs, half_rows, hidden = sizes
+    group = 4 * channels
+    conv = conv_rows(conv_weight_ref, tap_ref)
+    conv_t_ref[...] = jnp.transpose(conv).astype(bf16)
+    conv_ref[:, : 16 * group] = (0.5 * conv).astype(bf16)
+    bias = 0.5 * row_of(conv_bias_ref, hidden)
+    at = lax.broadcasted_iota(jnp.int32, bias.shape, 1)
+    columns = jnp.zeros_like(bias)
+    for k, piece in enumerate(split_three(bias)):
+        columns = jnp.where(at == k, piece.astype(f32), columns)
+    columns = jnp.concatenate([columns[:, :16]] * 8, axis=0)
+    conv_ref[:, 16 * group :] = columns.astype(bf16)
+    down = dot(down_weight_ref[...], order_ref[...])
+    down_ref[...] = down.astype(bf16)
+    down_t_ref[...] = jnp.transpose(down).astype(bf16)
+    for slot in range(pairs + 1):
+        lower = below_ref if slot == 0 else field_ref.at[:, 2 * slot - 1]
+        upper = above_ref if slot == pairs else field_ref.at[:, 2 * slot]
+        rows = [ref[ch] for ref in (lower, upper) for ch in range(channels)]
+        rows = dot(row_ref[...], jnp.concatenate(rows, axis=0)).astype(bf16)
+        rows = dot(rows, col_ref[...])
+        for row in range(half_rows + 1):
+            piece = rows[row * group : (row + 1) * group]
+            split_ref[slot, :, row * lanes : (row + 1) * lanes] = shifts_of(piece).astype(bf16)
+
+
+def shifts_of(piece):
+    piece = jnp.concatenate([piece[:, :lanes], piece[:, lanes:]], axis=0)
+    return jnp.concatenate([piece, pltpu.roll(piece, lanes - 1, 1)], axis=0)
+
+
+def forward_kernel(
+    sizes,
+    early_ref,
     before_ref,
     after_ref,
     target_ref,
-    conv_weight_ref,
-    conv_bias_ref,
-    down_weight_ref,
+    conv_ref,
+    conv_t_ref,
+    down_ref,
+    down_t_ref,
     down_bias_ref,
     tap_ref,
     order_ref,
     col_ref,
-    row_ref,
     edge_ref,
+    merge_ref,
+    edge_t_ref,
     out_ref,
     gpre_ref,
     keep_ref,
     give_ref,
-    conv_t_ref,
+    to_before_ref,
+    to_after_ref,
     split_ref,
-    conv_ref,
-    down_ref,
-    down_t_ref,
     gdown_t_ref,
     gconv_t_ref,
     gdb_ref,
@@ -129,6 +176,8 @@
     hid_ref,
     slope_ref,
     whole_ref,
+    outer_ref,
+    sem,
 ):
     channels, pairs, half_rows, hidden, out_count, tile, cell_total = sizes
     group = 4 * channels
@@ -137,41 +186,23 @@
 
     @pl.when(step == 0)
     def _():
+        copy = pltpu.make_async_copy(early_ref, split_ref, sem)
+        copy.start()
         gdown_t_ref[...] = jnp.zeros_like(gdown_t_ref)
         gconv_t_ref[...] = jnp.zeros_like(gconv_t_ref)
         gdb_ref[...] = jnp.zeros_like(gdb_ref)
         sq_ref[...] = jnp.zeros_like(sq_ref)
-        conv = conv_rows(conv_weight_ref, tap_ref)
-        conv_t_ref[...] = jnp.transpose(conv).astype(bf16)
-        conv_ref[:, : 16 * group] = (0.5 * conv).astype(bf16)
-        bias = 0.5 * row_of(conv_bias_ref, hidden)
-        at = lax.broadcasted_iota(jnp.int32, bias.shape, 1)
-        columns = jnp.zeros_like(bias)
-        for k, piece in enumerate(split_three(bias)):
-            columns = jnp.where(at == k, piece.astype(f32), columns)
-        columns = jnp.concatenate([columns[:, :16]] * 8, axis=0)
-        conv_ref[:, 16 * group :] = columns.astype(bf16)
-        down = dot(down_weight_ref[...], order_ref[...])
-        down_ref[...] = down.astype(bf16)
-        down_t_ref[...] = jnp.transpose(down).astype(bf16)
+        pieces = []
         for slot in range(pairs + 1):
-            lower = below_ref if slot == 0 else field_ref.at[:, 2 * slot - 1]
-            upper = above_ref if slot == pairs else field_ref.at[:, 2 * slot]
-            rows = [ref[ch] for ref in (lower, upper) for ch in range(channels)]
-            rows = dot(row_ref[...], jnp.concatenate(rows, axis=0)).astype(bf16)
-            rows = dot(rows, col_ref[...])
             sides = [ref[2 * slot + par].astype(f32) for par in range(2) for ref in (before_ref, after_ref)]
             sides = jnp.concatenate(sides, axis=0).astype(bf16)
             sides = dot(dot(edge_ref[...], sides).astype(bf16), col_ref[...])
-            for row in range(half_rows + 1):
-                piece = rows[row * group : (row + 1) * group]
-                if row == 0:
-                    piece = piece + sides[:group]
-                if row == half_rows:
-                    piece = piece + sides[group:]
-                piece = jnp.concatenate([piece[:, :lanes], piece[:, lanes:]], axis=0)
-                piece = jnp.concatenate([piece, pltpu.roll(piece, lanes - 1, 1)], axis=0)
-                split_ref[slot, :, row * lanes : (row + 1) * lanes] = piece.astype(bf16)
+            pieces.append((shifts_of(sides[:group]), shifts_of(sides[group:])))
+        copy.wait()
+        for slot in range(pairs + 1):
+            for piece, row in zip(pieces[slot], (0, half_rows), strict=True):
+                here = slice(row * lanes, (row + 1) * lanes)
+                split_ref[slot, :, here] = (split_ref[slot, :, here].astype(f32) + piece).astype(bf16)
 
     ones = jnp.ones((16, tile), bf16)
     down_bias = row_of(down_bias_ref, out_count)
@@ -239,6 +270,8 @@
                 second[k]()
             if k < len(first):
                 first[k]()
+    for side, at in enumerate((0, cells - lanes)):
+        outer_ref[side, step] = gpre_ref[0, :, at : at + lanes]
     outputs = [value for part in range(parts) for value in outputs[part]]
     out_ref[:, 0] = jnp.swapaxes(jnp.stack(outputs, axis=0), 0, 1).astype(bf16)
 
@@ -269,6 +302,7 @@
         keep_ref[...] = whole_ref[pl.ds(pl.multiple_of(upper * rows, rows), rows)]
         give_ref[:, : 8 * hidden] = whole_ref[pl.ds(pl.multiple_of((1 - upper) * rows, rows), rows)]
         give_ref[:, 8 * hidden :] = small
+        sides_of(channels, pairs, outer_ref, conv_t_ref, merge_ref, edge_t_ref, to_before_ref, to_after_ref)
 
 
 def merged(piece, group):
@@ -280,14 +314,14 @@
     return jnp.concatenate(halves, axis=1)
 
 
-def sides_kernel(sizes, first_ref, last_ref, conv_t_ref, merge_ref, edge_t_ref, before_ref, after_ref):
-    channels, pairs = sizes
+def sides_of(channels, pairs, outer_ref, conv_t_ref, merge_ref, edge_t_ref, before_ref, after_ref):
     group = 4 * channels
     span = 4 * group
     found = []
-    for ref, dy in ((first_ref, 0), (last_ref, 1)):
-        weights = jnp.concatenate([conv_t_ref[(2 * dz + dy) * span : (2 * dz + dy + 1) * span] for dz in range(2)], axis=0)
-        found.append(dot(weights, jnp.concatenate([ref[pair] for pair in range(pairs)], axis=1)))
+    for dy in range(2):
+        weights = [conv_t_ref[(2 * dz + dy) * span : (2 * dz + dy + 1) * span] for dz in range(2)]
+        values = [outer_ref[dy, pair] for pair in range(pairs)]
+        found.append(dot(jnp.concatenate(weights, axis=0), jnp.concatenate(values, axis=1)))
     rows = []
     for slot in range(pairs + 1):
         outer = []
@@ -438,18 +472,41 @@
     return {name: jnp.asarray(value, bf16) for name, value in names.items()}
 
 
-def forward(fields, below, above, before, after, target, conv_weight, conv_bias, down_weight, down_bias, fixed, cell_total):
-    channels, depth, row_count, col_count = fields.shape
+def prepare(fields, below, above, conv_weight, conv_bias, down_weight, fixed):
+    channels, depth, row_count, _ = fields.shape
     hidden, out_count = conv_weight.shape[0], down_weight.shape[0]
-    pairs, half_rows, half_cols = depth // 2, row_count // 2, col_count // 2
+    pairs, half_rows = depth // 2, row_count // 2
+    big, win = 8 * hidden, 64 * channels
+    return call(
+        prepare_kernel,
+        (channels, pairs, half_rows, hidden),
+        [
+            jax.ShapeDtypeStruct((pairs + 1, 16 * channels, (half_rows + 1) * lanes), bf16),
+            jax.ShapeDtypeStruct((big, win + 16), bf16),
+            jax.ShapeDtypeStruct((win, big), bf16),
+            jax.ShapeDtypeStruct((out_count, big), bf16),
+            jax.ShapeDtypeStruct((big, out_count), bf16),
+        ],
+        fields, below, above, conv_weight, conv_bias[None], down_weight,
+        fixed["tap"], fixed["order"], fixed["col"], fixed["row"],
+        flops=2 * fields.size * row_count * channels * 4,
+        name="prepare",
+    )
+
+
+def forward(early, before, after, target, conv, conv_t, down, down_t, down_bias, fixed, channels, cell_total):
+    out_count, pairs, half_rows, half_cols = target.shape
+    win, big = conv_t.shape
+    hidden = big // 8
     cells = half_rows * half_cols
-    big, win = 8 * hidden, 64 * channels
     args = (
-        fields, below, above, before, after, target,
-        conv_weight, conv_bias[None], down_weight, down_bias[None],
-        fixed["tap"], fixed["order"], fixed["col"], fixed["row"], fixed["edge"],
+        early, before, after, target, conv, conv_t, down, down_t, down_bias[None],
+        fixed["tap"], fixed["order"], fixed["col"], fixed["edge"], fixed["merge"], fixed["edge_t"],
     )
     slab = pl.BlockSpec((out_count, 1, half_rows, half_cols), lambda z: (0, z, 0, 0))
+    in_specs = [whole(a.shape) for a in args]
+    in_specs[0] = pl.BlockSpec(memory_space=pl.ANY)
+    in_specs[3] = slab
     return call(
         forward_kernel,
         (channels, pairs, half_rows, hidden, out_count, forward_tile, cell_total),
@@ -458,23 +515,22 @@
             jax.ShapeDtypeStruct((pairs, big, cells), bf16),
             jax.ShapeDtypeStruct((out_count // 2, big), f32),
             jax.ShapeDtypeStruct((out_count // 2, big + 2 * lanes), f32),
-            jax.ShapeDtypeStruct((win, big), bf16),
+            jax.ShapeDtypeStruct(before.shape, bf16),
+            jax.ShapeDtypeStruct(after.shape, bf16),
         ],
         *args,
         grid=(pairs,),
-        in_specs=[slab if i == 5 else whole(a.shape) for i, a in enumerate(args)],
+        in_specs=in_specs,
         out_specs=[
             slab,
             pl.BlockSpec((1, big, cells), lambda z: (z, 0, 0)),
             whole((out_count // 2, big)),
             whole((out_count // 2, big + 2 * lanes)),
-            whole((win, big)),
+            whole(before.shape),
+            whole(after.shape),
         ],
         scratch=[
-            pltpu.VMEM((pairs + 1, 16 * channels, cells + lanes), bf16),
-            pltpu.VMEM((big, win + 16), bf16),
-            pltpu.VMEM((out_count, big), bf16),
-            pltpu.VMEM((big, out_count), bf16),
+            pltpu.VMEM(early.shape, bf16),
             pltpu.VMEM((big, out_count), f32),
             pltpu.VMEM((win + 16, big), f32),
             pltpu.VMEM((out_count, lanes), f32),
@@ -482,31 +538,11 @@
             pltpu.VMEM((2, big, forward_tile), bf16),
             pltpu.VMEM((2, big, forward_tile), f32),
             pltpu.VMEM((out_count, big), f32),
+            pltpu.VMEM((2, pairs, big, lanes), bf16),
+            pltpu.SemaphoreType.DMA,
         ],
         flops=4 * pairs * cells * big * (win + out_count),
         name="forward",
-    )
-
-
-def sides(grad_pre, conv_t, fixed, shape):
-    channels, depth, _, col_count = shape
-    pairs, big, cells = grad_pre.shape
-    args = (grad_pre, grad_pre, conv_t, fixed["merge"], fixed["edge_t"])
-    out = jax.ShapeDtypeStruct((depth + 2, 8, col_count), bf16)
-    outer = [
-        pl.BlockSpec((pairs, big, lanes), lambda z: (0, 0, 0)),
-        pl.BlockSpec((pairs, big, lanes), lambda z: (0, 0, cells // lanes - 1)),
-    ]
-    return call(
-        sides_kernel,
-        (channels, pairs),
-        [out, out],
-        *args,
-        grid=(1,),
-        in_specs=outer + [whole(a.shape) for a in args[2:]],
-        out_specs=[whole(out.shape)] * 2,
-        flops=4 * pairs * big * lanes * conv_t.shape[0],
-        name="sides",
     )
 
 
@@ -558,9 +594,11 @@
 
     before = shifted(side(row_count - 1), "gy", 1)
     after = shifted(side(0), "gy", -1)
-    out_field, grad_pre, own, packed, conv_t = forward(
-        fields, below, above, before, after, target,
-        conv_weight, conv_bias, down_weight, down_bias, fixed, cell_total,
+    early, conv_big, conv_t, down_big, down_t = prepare(
+        fields, below, above, conv_weight, conv_bias, down_weight, fixed
+    )
+    out_field, grad_pre, own, packed, to_before, to_after = forward(
+        early, before, after, target, conv_big, conv_t, down_big, down_t, down_bias, fixed, channels, cell_total
     )
     pairs = depth // 2
     shape = fields.shape
@@ -584,7 +622,6 @@
 
     bit = lax.axis_size("gz") // 2
     got = exchanged(packed, "gz", bit)
-    to_before, to_after = sides(grad_pre, conv_t, fixed, shape)
     from_before = shifted(to_after, "gy", 1)
     from_after = shifted(to_before, "gy", -1)
     outer = ((0, pairs - 1), (0, 1, pairs - 1, pairs), (), (0, pairs), (1, pairs - 1))
@@ -607,6 +644,7 @@
     lower = (tuple(range(1, middle)), tuple(range(1, middle + 1)), (1,), tuple(range(1, middle)), (middle,))
     lower_core, middle_open = spread(grad_pre, conv_t, fixed, shape, lower, low_open)
     own, small = added(own, small, got)
+    own, small, middle_open = lax.optimization_barrier((own, small, middle_open))
     while bit > 1:
         bit //= 2
         own, packed = halved(own, small, bit)

time: 87.2 us -> 81.8 us (0.938)
  waiting for transfers between devices: 13.5 us -> 5.27 us
  Pallas kernels: 49.2 us -> 51.6 us
    ppermute x8, waiting for transfers between devices: 6.52 us -> 1.65 us  [shifted(): lax.ppermute(value, axis, [(i, (i + by) % count) for i in range(count)])]
    ppermute x5, waiting for transfers between devices: 7.01 us -> 3.62 us  [exchanged(): return lax.ppermute(value, axis, [(i, i ^ bit) for i in range(count)])]
    pallas_call x7, Pallas kernels: 49.2 us -> 51.6 us  [call(): pl.pallas_call(functools.partial(kernel, sizes), out_shape=out_shape, in_...]
  transfers between devices with their start and end apart: 13 -> 13, of which waited for: 6 -> 5; matrix products, arithmetic and copies ran while one was open for 4% -> 5% of each run, Pallas kernels for 25% -> 30%
where the time goes in v5:
time: 81.8 us; the launch traced here: 81.5 us
  Pallas kernels  51.6 us (63%)
  starting transfers between devices  16.8 us (21%)
  local copies, waits for them, and re-layouts  5.67 us (7%)
  waiting for transfers between devices  5.27 us (6%)
  other arithmetic  1.09 us (1%)
  between operations  1 us (1%)
    pallas_call x7, Pallas kernels, call(): pl.pallas_call(functools.partial(kernel, sizes), out_shape=out_shape, in_...  51.6 us
    ppermute x8, starting transfers between devices, shifted(): lax.ppermute(value, axis, [(i, (i + by) % count) for i in range(count)])  14.2 us
    ppermute x5, waiting for transfers between devices, exchanged(): return lax.ppermute(value, axis, [(i, i ^ bit) for i in range(count)])  3.62 us
    ppermute x5, starting transfers between devices, exchanged(): return lax.ppermute(value, axis, [(i, i ^ bit) for i in range(count)])  2.62 us
    unnamed x29, local copies, waits for them, and re-layouts  2.07 us
    ppermute x8, waiting for transfers between devices, shifted(): lax.ppermute(value, axis, [(i, (i + by) % count) for i in range(count)])  1.65 us
  transfers between devices with their start and end apart: 13, of which 5 were waited for; matrix products, arithmetic and copies ran while one was open for 5% of the time, Pallas kernels for 30%

profile of v5, /device:TPU:0, one launch (start us, length us, event | category | flops | bytes accessed | tf_op | source)
XLA Modules:
  0.0 81.5 jit_solution(17160824961391814569)
XLA Ops:
  0.6 1.0 %fusion.8 = (bf16[6,1,32,256]{3,2,1,0:T(8,128)(2,1)S(1)}, bf16[6,1,32,256]{3,2,1,0:T(8,128)(2,1)S(1)}) fusion(bf16[6,8,32,256]{3,2,1,0:T(8,128)(2,1)} %field_ref.1), kind=kLoop, calls=%fused_computation.37 | loop fusion | bytes 393216 | tf_op jit(solution)/shard_map/slice | solution.py:588
  1.6 0.1 copy.40
  1.7 0.5 collective-permute-start
  2.2 0.1 copy.39
  2.2 3.0 %collective-permute-start.1 = (bf16[6,32,256]{2,0,1:T(8,128)(2,1)S(1)}, bf16[6,32,256]{2,0,1:T(8,128)(2,1)S(1)}, u32[]{:S(2)}, u32[]{:S(2)}) collective-permute-start(bf16[6,32,256]{2,0,1:T(8,128)(2,1)S(1)} %bitcast.44), channel_id=1, source_target_pairs={{0,28},{4,0},{8,4},{12,8},{16,12},{20,16},{24,20},{28,24},{1,29},{... | collective-permute-start | bytes 294920 | tf_op jit(solution)/shard_map/ppermute | solution.py:20
  5.2 1.1 %fusion.7 = (bf16[6,8,1,256]{3,2,1,0:T(2,128)(2,1)S(1)}, bf16[6,8,1,256]{3,2,1,0:T(2,128)(2,1)S(1)}) fusion(bf16[6,8,32,256]{3,2,1,0:T(8,128)(2,1)} %field_ref.1), kind=kLoop, calls=%fused_computation.36 | loop fusion | bytes 98304 | tf_op jit(solution)/shard_map/slice | solution.py:591
  6.3 1.4 %collective-permute-done = bf16[6,32,256]{2,0,1:T(8,128)(2,1)S(1)} collective-permute-done((bf16[6,32,256]{2,0,1:T(8,128)(2,1)S(1)}, bf16[6,32,256]{2,0,1:T(8,128)(2,1)S(1)}, u32[]{:S(2)}, u32[]{:S(2)}) %collective-permute-start) | collective-permute-done | bytes 98336 | tf_op jit(solution)/shard_map/ppermute | solution.py:20
  7.7 0.3 collective-permute-done.1
  8.0 2.1 %collective-permute-start.2 = (bf16[10,8,256]{2,1,0:T(8,128)(2,1)S(1)}, bf16[10,8,256]{2,1,0:T(8,128)(2,1)S(1)}, u32[]{:S(2)}, u32[]{:S(2)}) collective-permute-start(bf16[10,8,256]{2,1,0:T(8,128)(2,1)S(1)} %pad.7), channel_id=1, source_target_pairs={{0,1},{1,2},{2,3},{3,0},{4,5},{5,6},{6,7},{7,4},{8,9},{9,10},{10,1... | collective-permute-start | bytes 122888 | tf_op jit(solution)/shard_map/ppermute | solution.py:20
  10.2 2.1 %collective-permute-start.3 = (bf16[10,8,256]{2,1,0:T(8,128)(2,1)S(1)}, bf16[10,8,256]{2,1,0:T(8,128)(2,1)S(1)}, u32[]{:S(2)}, u32[]{:S(2)}) collective-permute-start(bf16[10,8,256]{2,1,0:T(8,128)(2,1)S(1)} %pad.8), channel_id=1, source_target_pairs={{0,3},{1,0},{2,1},{3,2},{4,7},{5,4},{6,5},{7,6},{8,11},{9,8},{10,9... | collective-permute-start | bytes 122888 | tf_op jit(solution)/shard_map/ppermute | solution.py:20
  12.3 0.7 copy.23.below_ref
  12.9 0.7 copy.24.above_ref
  13.6 5.5 %prepare.1 = (bf16[5,96,2176]{2,1,0:T(8,128)(2,1)}, bf16[512,400]{1,0:T(8,128)(2,1)}, bf16[384,512]{1,0:T(8,128)(2,1)}, bf16[128,512]{1,0:T(8,128)(2,1)}, bf16[512,128]{1,0:T(8,128)(2,1)}) custom-call(bf16[6,8,32,256]{3,2,1,0:T(8,128)(2,1)} %field_ref.1, bf16[6,32,256]{2,1,0:T(8,128)(2,1)} %copy.23.below_ref, bf16[6,32,256]{2,1,0:T(8,128)(2,1)} %copy.24.above_ref, ...), custom_call_target="tpu_custom_call" | custom-call | flops 603979776 | bytes 6253056 | tf_op jit(solution)/shard_map/prepare/pallas_call | solution.py:439
  19.1 0.0 collective-permute-done.2.before_ref
  19.1 0.0 copy-start.8
  19.1 0.0 collective-permute-done.3.after_ref
  19.1 0.6 copy-done.8
  19.7 0.0 copy-done.9
  19.7 25.5 %forward.1 = (bf16[128,4,16,128]{3,2,1,0:T(8,128)(2,1)}, bf16[4,512,2048]{2,1,0:T(8,128)(2,1)}, f32[64,512]{1,0:T(8,128)}, f32[64,768]{1,0:T(8,128)}, bf16[10,8,...) custom-call(bf16[5,96,2176]{2,1,0:T(8,128)(2,1)} %get-tuple-element.35.early_ref, bf16[10,8,256]{2,1,0:T(8,128)(2,1)} %copy-done.8, ...), custom_call_target="tpu_custom_call" | custom-call | flops 8589934592 | bytes 18016768 | tf_op jit(solution)/shard_map/forward/pallas_call | solution.py:439
  45.3 2.3 %collective-permute-start.4 = (f32[64,768]{1,0:T(8,128)}, f32[64,768]{1,0:T(8,128)S(1)}, u32[]{:S(2)}, u32[]{:S(2)}) collective-permute-start(f32[64,768]{1,0:T(8,128)} %get-tuple-element.44), channel_id=1, source_target_pairs={{0,16},{4,20},{8,24},{12,28},{16,0},{20,4},{24,8},{28,12},{1,17},{... | collective-permute-start | bytes 589832 | tf_op jit(solution)/shard_map/ppermute | solution.py:25
  47.5 0.1 pad.13.clone
  47.6 3.8 %collective-permute-start.8 = (bf16[10,8,256]{2,1,0:T(8,128)(2,1)}, bf16[10,8,256]{2,1,0:T(8,128)(2,1)S(1)}, u32[]{:S(2)}, u32[]{:S(2)}) collective-permute-start(bf16[10,8,256]{2,1,0:T(8,128)(2,1)} %get-tuple-element.56), channel_id=1, source_target_pairs={{0,3},{1,0},{2,1},{3,2},{4,7},{5,4},{6,5},{7,6},{8,11},{9,8},{10,9... | collective-permute-start | bytes 122888 | tf_op jit(solution)/shard_map/ppermute | solution.py:20
  51.4 6.4 %spread.3 = (f32[4,6,32,256]{3,2,1,0:T(8,128)}, f32[96,2176]{1,0:T(8,128)}, f32[96,2176]{1,0:T(8,128)}) custom-call(bf16[4,512,2048]{2,1,0:T(8,128)(2,1)} %get-tuple-element.41.refs_0_, bf16[384,512]{1,0:T(8,128)(2,1)} %get-tuple-element.37.conv_t_ref.refs_1_, bf16[256,256]{1,0:T(8,128)(2,1)} %constant.71.clone.merge_ref.refs_2_, ...), custom_call_target="tpu_custom_call" | custom-call | flops 1610612736 | bytes 11683840 | tf_op jit(solution)/shard_map/spread/pallas_call | solution.py:439
  57.9 0.0 collective-permute-done.4
  57.9 0.8 %slice_add_fusion.2 = f32[64,256]{1,0:T(8,128)S(1)} fusion(f32[64,768]{1,0:T(8,128)S(1)} %collective-permute-done.4, f32[64,768]{1,0:T(8,128)} %get-tuple-element.44), kind=kLoop, calls=%fused_computation.9 | loop fusion | flops 16384 | bytes 196608 | tf_op jit(solution)/shard_map/add | solution.py:614
  58.8 0.1 collective-permute-start.5
  59.0 0.0 collective-permute-done.7.refs_6_
  59.0 4.5 %spread.4 = (f32[2,6,32,256]{3,2,1,0:T(8,128)}, f32[96,2176]{1,0:T(8,128)}) custom-call(bf16[4,512,2048]{2,1,0:T(8,128)(2,1)} %get-tuple-element.41.refs_0_, bf16[384,512]{1,0:T(8,128)(2,1)} %get-tuple-element.37.conv_t_ref.refs_1_, bf16[256,256]{1,0:T(8,128)(2,1)} %constant.71.clone.merge_ref.refs_2_, bf16[384,408]{1,0:T(8,128)(2,1)} %constant.73.clone.refs_3_, ...), custom_call_target="tpu_custom_call" | custom-call | flops 805306368 | bytes 11290624 | tf_op jit(solution)/shard_map/spread/pallas_call | solution.py:439
  63.4 0.4 collective-permute-done.5
  64.0 0.1 collective-permute-start.6
  64.0 0.0 collective-permute-done.8.refs_5_
  64.0 0.0 copy-start.7
  64.1 1.2 %collective-permute-done.6 = f32[16,1536]{1,0:T(8,128)S(1)} collective-permute-done((f32[16,1536]{1,0:T(8,128)S(1)}, f32[16,1536]{1,0:T(8,128)S(1)}, u32[]{:S(2)}, u32[]{:S(2)}) %collective-permute-start.6) | collective-permute-done | bytes 98336 | tf_op jit(solution)/shard_map/ppermute | solution.py:25
  65.4 0.1 collective-permute-start.11
  65.5 0.1 fusion.1
  65.6 0.2 collective-permute-start.10
  65.8 2.5 %collective-permute-start.9 = (bf16[6,32,256]{2,1,0:T(8,128)(2,1)S(1)}, bf16[6,32,256]{2,1,0:T(8,128)(2,1)S(1)}, u32[]{:S(2)}, u32[]{:S(2)}) collective-permute-start(bf16[6,32,256]{2,1,0:T(8,128)(2,1)S(1)} %get-tuple-element.64), channel_id=1, source_target_pairs={{0,28},{4,0},{8,4},{12,8},{16,12},{20,16},{24,20},{28,24},{1,29},{... | collective-permute-start | bytes 294920 | tf_op jit(solution)/shard_map/ppermute | solution.py:20
  68.3 2.0 %collective-permute-done.11 = f32[16,1536]{1,0:T(8,128)S(1)} collective-permute-done((f32[16,1536]{1,0:T(8,128)S(1)}, f32[16,1536]{1,0:T(8,128)S(1)}, u32[]{:S(2)}, u32[]{:S(2)}) %collective-permute-start.11) | collective-permute-done | bytes 98336 | tf_op jit(solution)/shard_map/ppermute | solution.py:25
  70.4 0.1 collective-permute-start.12
  70.4 5.1 %spread.5.refs_2_ = f32[4,6,32,256]{3,2,1,0:T(8,128)} custom-call(bf16[4,512,2048]{2,1,0:T(8,128)(2,1)} %get-tuple-element.41.refs_0_, bf16[384,512]{1,0:T(8,128)(2,1)} %get-tuple-element.37.conv_t_ref.refs_1_, bf16[256,256]{1,0:T(8,128)(2,1)} %constant.71.clone.merge_ref.refs_2_, bf16[384,408]{1,0:T(8,128)(2,1)} %constant.73.clone.refs_3_, ...), custom_call_target="tpu_custom_call" | custom-call | flops 805306368 | bytes 11683840 | tf_op jit(solution)/shard_map/spread/pallas_call | solution.py:439
  75.6 0.0 collective-permute-done.10.refs_4_
  75.6 0.0 collective-permute-done.9.refs_3_
  75.6 0.6 copy-done.4
  76.2 0.1 copy-done.5
  76.3 2.9 %join.1 = f32[6,8,32,256]{3,2,1,0:T(8,128)} custom-call(f32[4,6,32,256]{3,2,1,0:T(8,128)} %get-tuple-element.42.refs_0_, f32[2,6,32,256]{3,2,1,0:T(8,128)} %get-tuple-element.47.refs_1_, f32[4,6,32,256]{3,2,1,0:T(8,128)} %spread.5.refs_2_, bf16[6,32,256]{2,1,0:T(8,128)(2,1)} %copy-done.5, bf16[6,32,256]{2,1,0:T(8,128)(2,1)} %copy-done.4, ...), custom_call_target="tpu_custom_call" | custom-call | bytes 3817472 | tf_op jit(solution)/shard_map/join/pallas_call | solution.py:439
  79.2 0.0 collective-permute-done.12.theirs_ref
  79.2 0.6 copy-done.3
  79.8 1.6 %last.1 = (f32[64,162]{1,0:T(8,128)}, f32[1,64]{1,0:T(1,128)}, f32[16,512]{1,0:T(8,128)}, f32[1,128]{1,0:T(1,128)}, f32[1,1]{1,0:T(1,128)}) custom-call(f32[16,1536]{1,0:T(8,128)} %copy-done.1, f32[16,1536]{1,0:T(8,128)} %copy-done.3), custom_call_target="tpu_custom_call" | custom-call | bytes 271620 | tf_op jit(solution)/shard_map/last/pallas_call | solution.py:439
  (48 shorter events, 0.3 us)
Async XLA Ops:
  1.7 6.0 %collective-permute-start = (bf16[6,32,256]{2,0,1:T(8,128)(2,1)S(1)}, bf16[6,32,256]{2,0,1:T(8,128)(2,1)S(1)}, u32[]{:S(2)}, u32[]{:S(2)}) collective-permute-start(bf16[6,32,256]{2,0,1:T(8,128)(2,1)S(1)} %bitcast.43), channel_id=1, source_target_pairs={{0,4},{4,8},{8,12},{12,16},{16,20},{20,24},{24,28},{28,0},{1,5},{5... | collective-permute-start | bytes 294920 | tf_op jit(solution)/shard_map/ppermute | solution.py:20
  2.2 5.7 %collective-permute-start.1 = (bf16[6,32,256]{2,0,1:T(8,128)(2,1)S(1)}, bf16[6,32,256]{2,0,1:T(8,128)(2,1)S(1)}, u32[]{:S(2)}, u32[]{:S(2)}) collective-permute-start(bf16[6,32,256]{2,0,1:T(8,128)(2,1)S(1)} %bitcast.44), channel_id=1, source_target_pairs={{0,28},{4,0},{8,4},{12,8},{16,12},{20,16},{24,20},{28,24},{1,29},{... | collective-permute-start | bytes 294920 | tf_op jit(solution)/shard_map/ppermute | solution.py:20
  8.0 11.1 %collective-permute-start.2 = (bf16[10,8,256]{2,1,0:T(8,128)(2,1)S(1)}, bf16[10,8,256]{2,1,0:T(8,128)(2,1)S(1)}, u32[]{:S(2)}, u32[]{:S(2)}) collective-permute-start(bf16[10,8,256]{2,1,0:T(8,128)(2,1)S(1)} %pad.7), channel_id=1, source_target_pairs={{0,1},{1,2},{2,3},{3,0},{4,5},{5,6},{6,7},{7,4},{8,9},{9,10},{10,1... | collective-permute-start | bytes 122888 | tf_op jit(solution)/shard_map/ppermute | solution.py:20
  10.2 8.9 %collective-permute-start.3 = (bf16[10,8,256]{2,1,0:T(8,128)(2,1)S(1)}, bf16[10,8,256]{2,1,0:T(8,128)(2,1)S(1)}, u32[]{:S(2)}, u32[]{:S(2)}) collective-permute-start(bf16[10,8,256]{2,1,0:T(8,128)(2,1)S(1)} %pad.8), channel_id=1, source_target_pairs={{0,3},{1,0},{2,1},{3,2},{4,7},{5,4},{6,5},{7,6},{8,11},{9,8},{10,9... | collective-permute-start | bytes 122888 | tf_op jit(solution)/shard_map/ppermute | solution.py:20
  19.1 0.6 copy-start.8
  19.1 0.6 copy-start.9
  45.3 12.6 %collective-permute-start.4 = (f32[64,768]{1,0:T(8,128)}, f32[64,768]{1,0:T(8,128)S(1)}, u32[]{:S(2)}, u32[]{:S(2)}) collective-permute-start(f32[64,768]{1,0:T(8,128)} %get-tuple-element.44), channel_id=1, source_target_pairs={{0,16},{4,20},{8,24},{12,28},{16,0},{20,4},{24,8},{28,12},{1,17},{... | collective-permute-start | bytes 589832 | tf_op jit(solution)/shard_map/ppermute | solution.py:25
  47.6 11.4 %collective-permute-start.7 = (bf16[10,8,256]{2,1,0:T(8,128)(2,1)}, bf16[10,8,256]{2,1,0:T(8,128)(2,1)S(1)}, u32[]{:S(2)}, u32[]{:S(2)}) collective-permute-start(bf16[10,8,256]{2,1,0:T(8,128)(2,1)} %get-tuple-element.55), channel_id=1, source_target_pairs={{0,1},{1,2},{2,3},{3,0},{4,5},{5,6},{6,7},{7,4},{8,9},{9,10},{10,1... | collective-permute-start | bytes 122888 | tf_op jit(solution)/shard_map/ppermute | solution.py:20
  47.6 16.4 %collective-permute-start.8 = (bf16[10,8,256]{2,1,0:T(8,128)(2,1)}, bf16[10,8,256]{2,1,0:T(8,128)(2,1)S(1)}, u32[]{:S(2)}, u32[]{:S(2)}) collective-permute-start(bf16[10,8,256]{2,1,0:T(8,128)(2,1)} %get-tuple-element.56), channel_id=1, source_target_pairs={{0,3},{1,0},{2,1},{3,2},{4,7},{5,4},{6,5},{7,6},{8,11},{9,8},{10,9... | collective-permute-start | bytes 122888 | tf_op jit(solution)/shard_map/ppermute | solution.py:20
  51.4 7.3 %copy-start.2 = (f32[64,512]{1,0:T(8,128)S(1)}, f32[64,512]{1,0:T(8,128)}, u32[]{:S(2)}) copy-start(f32[64,512]{1,0:T(8,128)} %get-tuple-element.43) | copy-start | bytes 393220
  58.8 5.0 %collective-permute-start.5 = (f32[32,1024]{1,0:T(8,128)S(1)}, f32[32,1024]{1,0:T(8,128)S(1)}, u32[]{:S(2)}, u32[]{:S(2)}) collective-permute-start(f32[32,1024]{1,0:T(8,128)S(1)} %pad_maximum_fusion), channel_id=1, source_target_pairs={{0,8},{4,12},{8,0},{12,4},{16,24},{20,28},{24,16},{28,20},{1,9},{5... | collective-permute-start | bytes 393224 | tf_op jit(solution)/shard_map/ppermute | solution.py:25
  59.0 4.5 %copy-start.6 = (bf16[10,8,256]{2,1,0:T(8,128)(2,1)}, bf16[10,8,256]{2,1,0:T(8,128)(2,1)S(1)}, u32[]{:S(2)}) copy-start(bf16[10,8,256]{2,1,0:T(8,128)(2,1)S(1)} %collective-permute-done.7.refs_6_) | copy-start | bytes 122884
  59.0 6.5 %copy-start = (f32[4,6,32,256]{3,2,1,0:T(8,128)S(1)}, f32[4,6,32,256]{3,2,1,0:T(8,128)}, u32[]{:S(2)}) copy-start(f32[4,6,32,256]{3,2,1,0:T(8,128)} %get-tuple-element.42.refs_0_) | copy-start | bytes 2359300
  64.0 1.4 %collective-permute-start.6 = (f32[16,1536]{1,0:T(8,128)S(1)}, f32[16,1536]{1,0:T(8,128)S(1)}, u32[]{:S(2)}, u32[]{:S(2)}) collective-permute-start(f32[16,1536]{1,0:T(8,128)S(1)} %constant_dynamic-update-slice_fusion), channel_id=1, source_target_pairs={{0,4},{4,0},{8,12},{12,8},{16,20},{20,16},{24,28},{28,24},{1,5},{5... | collective-permute-start | bytes 294920 | tf_op jit(solution)/shard_map/ppermute | solution.py:25
  64.0 11.5 %copy-start.7 = (bf16[10,8,256]{2,1,0:T(8,128)(2,1)}, bf16[10,8,256]{2,1,0:T(8,128)(2,1)S(1)}, u32[]{:S(2)}) copy-start(bf16[10,8,256]{2,1,0:T(8,128)(2,1)S(1)} %collective-permute-done.8.refs_5_) | copy-start | bytes 122884
  65.4 4.9 %collective-permute-start.11 = (f32[16,1536]{1,0:T(8,128)S(1)}, f32[16,1536]{1,0:T(8,128)S(1)}, u32[]{:S(2)}, u32[]{:S(2)}) collective-permute-start(f32[16,1536]{1,0:T(8,128)S(1)} %constant_dynamic-update-slice_fusion.4), channel_id=1, source_target_pairs={{0,1},{1,0},{2,3},{3,2},{4,5},{5,4},{6,7},{7,6},{8,9},{9,8},{10,11... | collective-permute-start | bytes 294920 | tf_op jit(solution)/shard_map/ppermute | solution.py:25
  65.6 10.0 %collective-permute-start.10 = (bf16[6,32,256]{2,1,0:T(8,128)(2,1)S(1)}, bf16[6,32,256]{2,1,0:T(8,128)(2,1)S(1)}, u32[]{:S(2)}, u32[]{:S(2)}) collective-permute-start(bf16[6,32,256]{2,1,0:T(8,128)(2,1)S(1)} %get-tuple-element.63), channel_id=1, source_target_pairs={{0,4},{4,8},{8,12},{12,16},{16,20},{20,24},{24,28},{28,0},{1,5},{5... | collective-permute-start | bytes 294920 | tf_op jit(solution)/shard_map/ppermute | solution.py:20
  65.8 9.8 %collective-permute-start.9 = (bf16[6,32,256]{2,1,0:T(8,128)(2,1)S(1)}, bf16[6,32,256]{2,1,0:T(8,128)(2,1)S(1)}, u32[]{:S(2)}, u32[]{:S(2)}) collective-permute-start(bf16[6,32,256]{2,1,0:T(8,128)(2,1)S(1)} %get-tuple-element.64), channel_id=1, source_target_pairs={{0,28},{4,0},{8,4},{12,8},{16,12},{20,16},{24,20},{28,24},{1,29},{... | collective-permute-start | bytes 294920 | tf_op jit(solution)/shard_map/ppermute | solution.py:20
  70.3 5.2 %copy-start.1 = (f32[16,1536]{1,0:T(8,128)}, f32[16,1536]{1,0:T(8,128)S(1)}, u32[]{:S(2)}) copy-start(f32[16,1536]{1,0:T(8,128)S(1)} %add.66.mine_ref) | copy-start | bytes 294916
  70.4 8.8 %collective-permute-start.12 = (f32[16,1536]{1,0:T(8,128)S(1)}, f32[16,1536]{1,0:T(8,128)S(1)}, u32[]{:S(2)}, u32[]{:S(2)}) collective-permute-start(f32[16,1536]{1,0:T(8,128)S(1)} %add.66.mine_ref), channel_id=1, source_target_pairs={{0,2},{1,3},{2,0},{3,1},{4,6},{5,7},{6,4},{7,5},{8,10},{9,11},{10,... | collective-permute-start | bytes 294920 | tf_op jit(solution)/shard_map/ppermute | solution.py:25
  75.6 0.6 copy-start.4
  75.6 0.7 copy-start.5
  79.2 0.6 copy-start.3

commit v6 on v5

--- a/solution.py
+++ b/solution.py
@@ -96,39 +96,37 @@
     return jnp.transpose(jnp.broadcast_to(ref[...], (lanes, count)))
 
 
-def prepare_kernel(
+def weights_kernel(
     sizes,
-    field_ref,
-    below_ref,
-    above_ref,
     conv_weight_ref,
     conv_bias_ref,
     down_weight_ref,
     tap_ref,
     order_ref,
-    col_ref,
-    row_ref,
-    split_ref,
     conv_ref,
     conv_t_ref,
     down_ref,
     down_t_ref,
 ):
-    channels, pairs, half_rows, hidden = sizes
-    group = 4 * channels
+    hidden, win = sizes
     conv = conv_rows(conv_weight_ref, tap_ref)
     conv_t_ref[...] = jnp.transpose(conv).astype(bf16)
-    conv_ref[:, : 16 * group] = (0.5 * conv).astype(bf16)
+    conv_ref[:, :win] = (0.5 * conv).astype(bf16)
     bias = 0.5 * row_of(conv_bias_ref, hidden)
     at = lax.broadcasted_iota(jnp.int32, bias.shape, 1)
     columns = jnp.zeros_like(bias)
     for k, piece in enumerate(split_three(bias)):
         columns = jnp.where(at == k, piece.astype(f32), columns)
     columns = jnp.concatenate([columns[:, :16]] * 8, axis=0)
-    conv_ref[:, 16 * group :] = columns.astype(bf16)
+    conv_ref[:, win:] = columns.astype(bf16)
     down = dot(down_weight_ref[...], order_ref[...])
     down_ref[...] = down.astype(bf16)
     down_t_ref[...] = jnp.transpose(down).astype(bf16)
+
+
+def cells_kernel(sizes, field_ref, below_ref, above_ref, col_ref, row_ref, split_ref):
+    channels, pairs, half_rows = sizes
+    group = 4 * channels
     for slot in range(pairs + 1):
         lower = below_ref if slot == 0 else field_ref.at[:, 2 * slot - 1]
         upper = above_ref if slot == pairs else field_ref.at[:, 2 * slot]
@@ -156,8 +154,8 @@
     down_ref,
     down_t_ref,
     down_bias_ref,
-    tap_ref,
-    order_ref,
+    far_tap_ref,
+    far_order_ref,
     col_ref,
     edge_ref,
     merge_ref,
@@ -177,32 +175,57 @@
     slope_ref,
     whole_ref,
     outer_ref,
-    sem,
+    tap_ref,
+    order_ref,
+    sides_ref,
+    split_sem,
+    late_sem,
 ):
     channels, pairs, half_rows, hidden, out_count, tile, cell_total = sizes
     group = 4 * channels
     cells = half_rows * lanes
     step = pl.program_id(0)
 
+    def arrival(slot):
+        return pltpu.make_async_copy(early_ref.at[slot], split_ref.at[slot], split_sem.at[slot])
+
+    late = [
+        pltpu.make_async_copy(far_tap_ref, tap_ref, late_sem.at[0]),
+        pltpu.make_async_copy(far_order_ref, order_ref, late_sem.at[1]),
+    ]
+
+    def complete(slot):
+        arrival(slot).wait()
+        for side, row in enumerate((0, half_rows)):
+            here = slice(row * lanes, (row + 1) * lanes)
+            value = split_ref[slot, :, here].astype(f32) + sides_ref[slot, side]
+            split_ref[slot, :, here] = value.astype(bf16)
+
     @pl.when(step == 0)
     def _():
-        copy = pltpu.make_async_copy(early_ref, split_ref, sem)
-        copy.start()
+        for slot in range(pairs + 1):
+            arrival(slot).start()
+        for copy in late:
+            copy.start()
         gdown_t_ref[...] = jnp.zeros_like(gdown_t_ref)
         gconv_t_ref[...] = jnp.zeros_like(gconv_t_ref)
         gdb_ref[...] = jnp.zeros_like(gdb_ref)
         sq_ref[...] = jnp.zeros_like(sq_ref)
-        pieces = []
+        width = 2 * lanes
+        rows = []
         for slot in range(pairs + 1):
             sides = [ref[2 * slot + par].astype(f32) for par in range(2) for ref in (before_ref, after_ref)]
-            sides = jnp.concatenate(sides, axis=0).astype(bf16)
-            sides = dot(dot(edge_ref[...], sides).astype(bf16), col_ref[...])
-            pieces.append((shifts_of(sides[:group]), shifts_of(sides[group:])))
-        copy.wait()
+            rows.append(jnp.concatenate(sides, axis=0).astype(bf16))
+        rows = dot(edge_ref[...], jnp.concatenate(rows, axis=1)).astype(bf16)
+        rows = [rows[:, slot * width : (slot + 1) * width] for slot in range(pairs + 1)]
+        rows = dot(jnp.concatenate(rows, axis=0), col_ref[...])
         for slot in range(pairs + 1):
-            for piece, row in zip(pieces[slot], (0, half_rows), strict=True):
-                here = slice(row * lanes, (row + 1) * lanes)
-                split_ref[slot, :, here] = (split_ref[slot, :, here].astype(f32) + piece).astype(bf16)
+            for side in range(2):
+                first = (2 * slot + side) * group
+                sides_ref[slot, side] = shifts_of(rows[first : first + group])
+        complete(0)
+
+    complete(step + 1)
 
     ones = jnp.ones((16, tile), bf16)
     down_bias = row_of(down_bias_ref, out_count)
@@ -278,6 +301,8 @@
     @pl.when(step == pairs - 1)
     def _():
         taps = channels * 27
+        for copy in late:
+            copy.wait()
         folded = 0.0
         cb = jnp.zeros((hidden, 1), f32)
         gconv = jnp.transpose(gconv_t_ref[...])
@@ -333,24 +358,28 @@
                     total = total + value[dz * span : (dz + 1) * span, pair * lanes : (pair + 1) * lanes]
             outer.append(merged(total, group))
         rows.append(jnp.concatenate(outer, axis=0))
-    for slot in range(pairs + 1):
-        sides = 0.0
-        for value in split_two(rows[slot]):
-            sides = sides + dot(dot(edge_t_ref[...], value).astype(bf16), merge_ref[...])
-        for par in range(2):
-            before_ref[2 * slot + par] = sides[par * 16 : par * 16 + 8].astype(bf16)
-            after_ref[2 * slot + par] = sides[par * 16 + 8 : par * 16 + 16].astype(bf16)
+    width = 2 * lanes
+    sides = 0.0
+    for value in split_two(jnp.concatenate(rows, axis=1)):
+        value = dot(edge_t_ref[...], value).astype(bf16)
+        value = [value[:, slot * width : (slot + 1) * width] for slot in range(pairs + 1)]
+        sides = sides + dot(jnp.concatenate(value, axis=0), merge_ref[...])
+    for at in range(2 * pairs + 2):
+        before_ref[at] = sides[at * 16 : at * 16 + 8].astype(bf16)
+        after_ref[at] = sides[at * 16 + 8 : at * 16 + 16].astype(bf16)
 
 
 def spread_kernel(sizes, *refs):
-    channels, half_rows, tile, plan = sizes
+    channels, depth, half_rows, tile, plan = sizes
     pairs, slots, taken, done, given = plan
-    refs = list(refs)
     gpre_ref, conv_t_ref, merge_ref, row_t_ref = refs[:4]
-    taken_refs = refs[4 : 4 + len(taken)]
-    core_ref = refs[4 + len(taken)]
-    given_refs = refs[5 + len(taken) : -1]
+    rest = refs[4:-1]
     spread_ref = refs[-1]
+    if taken:
+        taken_refs = rest[: len(taken)]
+        outer_ref, below_ref, above_ref, before_ref, after_ref, out_ref = rest[len(taken) :]
+    else:
+        core_ref, *given_refs = rest
     group = 4 * channels
     span = 4 * group
     row_count = 2 * half_rows
@@ -365,6 +394,12 @@
                     first = (2 * dz + dy) * span
                     here = slice(part * tile + dy * lanes, (part + 1) * tile + dy * lanes)
                     spread_ref[slots.index(pair + dz), :, here] += spread[first : first + span]
+
+    def lay_out(at, ch, value):
+        z = at - 1
+        out_ref[ch, z] = value
+        out_ref[ch, z, 0:1] += after_ref[at, ch : ch + 1].astype(f32)
+        out_ref[ch, z, row_count - 1 : row_count] += before_ref[at, ch : ch + 1].astype(f32)
 
     def finish(slot):
         rows = [
@@ -377,43 +412,37 @@
         for par in range(2):
             for ch in range(channels):
                 first = (par * channels + ch) * row_count
-                core_ref[2 * done.index(slot) + par, ch] = core[first : first + row_count]
+                value = core[first : first + row_count]
+                if taken:
+                    lay_out(2 * slot + par, ch, value)
+                else:
+                    core_ref[2 * done.index(slot) + par, ch] = value
 
     for k, pair in enumerate(pairs):
 
         @pl.when(step == k)
         def _():
             if k == 0:
-                spread_ref[...] = jnp.zeros_like(spread_ref)
-                for slot, ref in zip(taken, taken_refs, strict=True):
-                    spread_ref[slots.index(slot)] = ref[...]
+                for slot in slots:
+                    if slot in taken:
+                        spread_ref[slots.index(slot)] = taken_refs[taken.index(slot)][...]
+                    else:
+                        spread_ref[slots.index(slot)] = jnp.zeros(spread_ref.shape[1:], f32)
+            if k == 0 and taken:
+                for ch in range(channels):
+                    lay_out(1, ch, outer_ref[1, ch] + above_ref[ch].astype(f32))
+                    lay_out(depth, ch, outer_ref[2, ch] + below_ref[ch].astype(f32))
             for slot in done:
-                if all(later not in (slot - 1, slot) for later in pairs[k:]) and slot - 1 != pairs[-1]:
-                    if any(before in (slot - 1, slot) for before in pairs[k - 1 : k]):
-                        finish(slot)
+                if k > 0 and pairs[k - 1] in (slot - 1, slot) and not set(pairs[k:]) & {slot - 1, slot}:
+                    finish(slot)
             spread_out(pair)
             if k == len(pairs) - 1:
                 for slot in done:
                     if pair in (slot - 1, slot):
                         finish(slot)
-                for slot, ref in zip(given, given_refs, strict=True):
-                    ref[...] = spread_ref[slots.index(slot)]
-
-
-def join_kernel(sizes, *refs):
-    channels, depth, row_count, places = sizes
-    below_ref, above_ref, before_ref, after_ref, out_ref = refs[-5:]
-    for z in range(depth):
-        which, at = places[z]
-        for ch in range(channels):
-            value = refs[which][at, ch]
-            if z == 0:
-                value = value + above_ref[ch].astype(f32)
-            if z == depth - 1:
-                value = value + below_ref[ch].astype(f32)
-            out_ref[ch, z] = value
-            out_ref[ch, z, 0:1] += after_ref[z + 1, ch : ch + 1].astype(f32)
-            out_ref[ch, z, row_count - 1 : row_count] += before_ref[z + 1, ch : ch + 1].astype(f32)
+                if not taken:
+                    for slot, ref in zip(given, given_refs, strict=True):
+                        ref[...] = spread_ref[slots.index(slot)]
 
 
 def last_kernel(sizes, mine_ref, theirs_ref, conv_out, cbias_out, down_out, dbias_out, loss_out):
@@ -472,26 +501,36 @@
     return {name: jnp.asarray(value, bf16) for name, value in names.items()}
 
 
-def prepare(fields, below, above, conv_weight, conv_bias, down_weight, fixed):
-    channels, depth, row_count, _ = fields.shape
+def weights(conv_weight, conv_bias, down_weight, fixed):
     hidden, out_count = conv_weight.shape[0], down_weight.shape[0]
-    pairs, half_rows = depth // 2, row_count // 2
-    big, win = 8 * hidden, 64 * channels
+    big, win = 8 * hidden, fixed["tap"].shape[2]
     return call(
-        prepare_kernel,
-        (channels, pairs, half_rows, hidden),
+        weights_kernel,
+        (hidden, win),
         [
-            jax.ShapeDtypeStruct((pairs + 1, 16 * channels, (half_rows + 1) * lanes), bf16),
             jax.ShapeDtypeStruct((big, win + 16), bf16),
             jax.ShapeDtypeStruct((win, big), bf16),
             jax.ShapeDtypeStruct((out_count, big), bf16),
             jax.ShapeDtypeStruct((big, out_count), bf16),
         ],
-        fields, below, above, conv_weight, conv_bias[None], down_weight,
-        fixed["tap"], fixed["order"], fixed["col"], fixed["row"],
+        conv_weight, conv_bias[None], down_weight, fixed["tap"], fixed["order"],
+        flops=2 * big * win * conv_weight.shape[1],
+        name="weights",
+    )
+
+
+def parity_cells(fields, below, above, fixed):
+    channels, depth, row_count, _ = fields.shape
+    pairs, half_rows = depth // 2, row_count // 2
+    (early,) = call(
+        cells_kernel,
+        (channels, pairs, half_rows),
+        [jax.ShapeDtypeStruct((pairs + 1, 16 * channels, (half_rows + 1) * lanes), bf16)],
+        fields, below, above, fixed["col"], fixed["row"],
         flops=2 * fields.size * row_count * channels * 4,
-        name="prepare",
-    )
+        name="cells",
+    )
+    return early
 
 
 def forward(early, before, after, target, conv, conv_t, down, down_t, down_bias, fixed, channels, cell_total):
@@ -505,7 +544,8 @@
     )
     slab = pl.BlockSpec((out_count, 1, half_rows, half_cols), lambda z: (0, z, 0, 0))
     in_specs = [whole(a.shape) for a in args]
-    in_specs[0] = pl.BlockSpec(memory_space=pl.ANY)
+    for i in (0, 9, 10):
+        in_specs[i] = pl.BlockSpec(memory_space=pl.ANY)
     in_specs[3] = slab
     return call(
         forward_kernel,
@@ -539,26 +579,33 @@
             pltpu.VMEM((2, big, forward_tile), f32),
             pltpu.VMEM((out_count, big), f32),
             pltpu.VMEM((2, pairs, big, lanes), bf16),
-            pltpu.SemaphoreType.DMA,
+            pltpu.VMEM(fixed["tap"].shape, bf16),
+            pltpu.VMEM(fixed["order"].shape, bf16),
+            pltpu.VMEM((pairs + 1, 2, 16 * channels, lanes), f32),
+            pltpu.SemaphoreType.DMA((pairs + 1,)),
+            pltpu.SemaphoreType.DMA((2,)),
         ],
         flops=4 * pairs * cells * big * (win + out_count),
         name="forward",
     )
 
 
-def spread(grad_pre, conv_t, fixed, shape, plan, *taken):
-    channels, _, row_count, col_count = shape
+def spread(grad_pre, conv_t, fixed, shape, plan, taken=(), beside=()):
+    channels, depth, row_count, col_count = shape
     _, big, cells = grad_pre.shape
     pairs, slots, _, done, given = plan
     open_shape = (16 * channels, cells + lanes)
-    args = (grad_pre, conv_t, fixed["merge"], fixed["row_t"], *taken)
-    outs = [jax.ShapeDtypeStruct((2 * len(done), channels, row_count, col_count), f32)]
+    args = (grad_pre, conv_t, fixed["merge"], fixed["row_t"], *taken, *beside)
+    if taken:
+        outs = [jax.ShapeDtypeStruct(shape, f32)]
+    else:
+        outs = [jax.ShapeDtypeStruct((2 * len(done), channels, row_count, col_count), f32)]
     outs += [jax.ShapeDtypeStruct(open_shape, f32)] * len(given)
     first = pairs[0]
     stride = pairs[1] - first if len(pairs) > 1 else 1
     return call(
         spread_kernel,
-        (channels, row_count // 2, spread_tile, plan),
+        (channels, depth, row_count // 2, spread_tile, plan),
         outs,
         *args,
         grid=(len(pairs),),
@@ -594,9 +641,8 @@
 
     before = shifted(side(row_count - 1), "gy", 1)
     after = shifted(side(0), "gy", -1)
-    early, conv_big, conv_t, down_big, down_t = prepare(
-        fields, below, above, conv_weight, conv_bias, down_weight, fixed
-    )
+    conv_big, conv_t, down_big, down_t = weights(conv_weight, conv_bias, down_weight, fixed)
+    early = parity_cells(fields, below, above, fixed)
     out_field, grad_pre, own, packed, to_before, to_after = forward(
         early, before, after, target, conv_big, conv_t, down_big, down_t, down_bias, fixed, channels, cell_total
     )
@@ -629,7 +675,6 @@
     own, small = added(own, small, got)
     bit //= 2
     own, packed = halved(own, small, bit)
-    packed, low_open = lax.optimization_barrier((packed, low_open))
 
     def plane(value, at):
         low = from_before[at, :channels, None].astype(f32)
@@ -640,36 +685,24 @@
     got = exchanged(packed, "gz", bit)
     from_below = shifted(plane(outer_core[3], depth + 1), "gz", 1)
     from_above = shifted(plane(outer_core[0], 0), "gz", -1)
-    middle = pairs // 2
-    lower = (tuple(range(1, middle)), tuple(range(1, middle + 1)), (1,), tuple(range(1, middle)), (middle,))
-    lower_core, middle_open = spread(grad_pre, conv_t, fixed, shape, lower, low_open)
     own, small = added(own, small, got)
-    own, small, middle_open = lax.optimization_barrier((own, small, middle_open))
     while bit > 1:
         bit //= 2
         own, packed = halved(own, small, bit)
         own, small = added(own, small, exchanged(packed, "gz", bit))
     packed = jnp.concatenate([own, beside(small, own.shape[0])], axis=1)
     count = own.shape[0]
-    packed, middle_open = lax.optimization_barrier((packed, middle_open))
 
     bit = 1
+    while 2 * bit < lax.axis_size("gy"):
+        packed = packed + exchanged(packed, "gy", bit)
+        bit *= 2
+    packed, low_open = lax.optimization_barrier((packed, low_open))
     got = exchanged(packed, "gy", bit)
-    slots = tuple(range(middle, pairs))
-    upper = (tuple(range(middle, pairs - 1)), slots, (middle, pairs - 1), slots, ())
-    (upper_core,) = spread(grad_pre, conv_t, fixed, shape, upper, middle_open, high_open)
-    while 2 * bit < lax.axis_size("gy"):
-        packed = packed + got
-        bit *= 2
-        got = exchanged(packed, "gy", bit)
-    places = [(0, 1)] + [(1, at) for at in range(2 * middle - 2)]
-    places += [(2, at) for at in range(2 * (pairs - middle))] + [(0, 2)]
-    (sensitivity,) = call(
-        join_kernel,
-        (channels, depth, row_count, tuple(places)),
-        [jax.ShapeDtypeStruct(shape, f32)],
-        outer_core, lower_core, upper_core, from_above, from_below, from_after, from_before,
-        name="join",
+    inner = tuple(range(1, pairs - 1)), tuple(range(1, pairs)), (1, pairs - 1), tuple(range(1, pairs)), ()
+    (sensitivity,) = spread(
+        grad_pre, conv_t, fixed, shape, inner, (low_open, high_open),
+        (outer_core, from_above, from_below, from_after, from_before),
     )
     conv, cbias, down, dbias, loss = call(
         last_kernel,

time: 81.8 us -> 81.2 us (level)
  waiting for transfers between devices: 5.27 us -> 9.69 us
  Pallas kernels: 51.6 us -> 47.7 us
  starting transfers between devices: 16.8 us -> 15.7 us
    ppermute x5, waiting for transfers between devices: 3.62 us -> 9.67 us  [exchanged(): return lax.ppermute(value, axis, [(i, i ^ bit) for i in range(count)])]
    pallas_call x7 -> x6, Pallas kernels: 51.6 us -> 47.7 us  [call(): pl.pallas_call(functools.partial(kernel, sizes), out_shape=out_shape, in_...]
    ppermute x8, starting transfers between devices: 14.2 us -> 10.6 us  [shifted(): lax.ppermute(value, axis, [(i, (i + by) % count) for i in range(count)])]
    ppermute x5, starting transfers between devices: 2.62 us -> 5.09 us  [exchanged(): return lax.ppermute(value, axis, [(i, i ^ bit) for i in range(count)])]
    ppermute x8, waiting for transfers between devices: 1.65 us -> 0.02 us  [shifted(): lax.ppermute(value, axis, [(i, (i + by) % count) for i in range(count)])]
  transfers between devices with their start and end apart: 13 -> 13, of which waited for: 5 -> 3; matrix products, arithmetic and copies ran while one was open for 5% -> 5% of each run, Pallas kernels for 30% -> 26%
where the time goes in v6:
time: 81.2 us; the launch traced here: 80.9 us
  Pallas kernels  47.7 us (59%)
  starting transfers between devices  15.7 us (19%)
  waiting for transfers between devices  9.69 us (12%)
  local copies, waits for them, and re-layouts  5.63 us (7%)
  other arithmetic  1.15 us (1%)
  between operations  0.99 us (1%)
    pallas_call x6, Pallas kernels, call(): pl.pallas_call(functools.partial(kernel, sizes), out_shape=out_shape, in_...  47.7 us
    ppermute x8, starting transfers between devices, shifted(): lax.ppermute(value, axis, [(i, (i + by) % count) for i in range(count)])  10.6 us
    ppermute x5, waiting for transfers between devices, exchanged(): return lax.ppermute(value, axis, [(i, i ^ bit) for i in range(count)])  9.67 us
    ppermute x5, starting transfers between devices, exchanged(): return lax.ppermute(value, axis, [(i, i ^ bit) for i in range(count)])  5.09 us
    unnamed x29, local copies, waits for them, and re-layouts  2.04 us
  transfers between devices with their start and end apart: 13, of which 3 were waited for; matrix products, arithmetic and copies ran while one was open for 5% of the time, Pallas kernels for 26%

profile of v6, /device:TPU:0, one launch (start us, length us, event | category | flops | bytes accessed | tf_op | source)
XLA Modules:
  0.0 80.9 jit_solution(10158869485960775923)
XLA Ops:
  0.6 1.0 %fusion.8 = (bf16[6,1,32,256]{3,2,1,0:T(8,128)(2,1)S(1)}, bf16[6,1,32,256]{3,2,1,0:T(8,128)(2,1)S(1)}) fusion(bf16[6,8,32,256]{3,2,1,0:T(8,128)(2,1)} %field_ref.1), kind=kLoop, calls=%fused_computation.37 | loop fusion | bytes 393216 | tf_op jit(solution)/shard_map/slice | solution.py:635
  1.6 0.1 copy.40
  1.7 0.5 collective-permute-start
  2.2 0.1 copy.39
  2.2 3.0 %collective-permute-start.1 = (bf16[6,32,256]{2,0,1:T(8,128)(2,1)S(1)}, bf16[6,32,256]{2,0,1:T(8,128)(2,1)S(1)}, u32[]{:S(2)}, u32[]{:S(2)}) collective-permute-start(bf16[6,32,256]{2,0,1:T(8,128)(2,1)S(1)} %bitcast.44), channel_id=1, source_target_pairs={{0,28},{4,0},{8,4},{12,8},{16,12},{20,16},{24,20},{28,24},{1,29},{... | collective-permute-start | bytes 294920 | tf_op jit(solution)/shard_map/ppermute | solution.py:20
  5.2 1.1 %fusion.7 = (bf16[6,8,1,256]{3,2,1,0:T(2,128)(2,1)S(1)}, bf16[6,8,1,256]{3,2,1,0:T(2,128)(2,1)S(1)}) fusion(bf16[6,8,32,256]{3,2,1,0:T(8,128)(2,1)} %field_ref.1), kind=kLoop, calls=%fused_computation.36 | loop fusion | bytes 98304 | tf_op jit(solution)/shard_map/slice | solution.py:638
  6.3 2.8 %weights.1 = (bf16[512,400]{1,0:T(8,128)(2,1)}, bf16[384,512]{1,0:T(8,128)(2,1)}, bf16[128,512]{1,0:T(8,128)(2,1)}, bf16[512,128]{1,0:T(8,128)(2,1)}) custom-call(bf16[64,162]{1,0:T(8,128)(2,1)} %conv_weight_ref.1, f32[1,64]{1,0:T(1,128)} %bitcast.45, bf16[128,512]{1,0:T(8,128)(2,1)} %down_weight_ref.1, ...), custom_call_target="tpu_custom_call" | custom-call | flops 63700992 | bytes 2736640 | tf_op jit(solution)/shard_map/weights/pallas_call | solution.py:468
  9.2 0.0 collective-permute-done.1
  9.2 0.0 collective-permute-done
  9.2 2.4 %collective-permute-start.2 = (bf16[10,8,256]{2,1,0:T(8,128)(2,1)S(1)}, bf16[10,8,256]{2,1,0:T(8,128)(2,1)S(1)}, u32[]{:S(2)}, u32[]{:S(2)}) collective-permute-start(bf16[10,8,256]{2,1,0:T(8,128)(2,1)S(1)} %pad.7), channel_id=1, source_target_pairs={{0,1},{1,2},{2,3},{3,0},{4,5},{5,6},{6,7},{7,4},{8,9},{9,10},{10,1... | collective-permute-start | bytes 122888 | tf_op jit(solution)/shard_map/ppermute | solution.py:20
  11.6 2.1 %collective-permute-start.3 = (bf16[10,8,256]{2,1,0:T(8,128)(2,1)S(1)}, bf16[10,8,256]{2,1,0:T(8,128)(2,1)S(1)}, u32[]{:S(2)}, u32[]{:S(2)}) collective-permute-start(bf16[10,8,256]{2,1,0:T(8,128)(2,1)S(1)} %pad.8), channel_id=1, source_target_pairs={{0,3},{1,0},{2,1},{3,2},{4,7},{5,4},{6,5},{7,6},{8,11},{9,8},{10,9... | collective-permute-start | bytes 122888 | tf_op jit(solution)/shard_map/ppermute | solution.py:20
  13.7 0.7 copy.23.below_ref
  14.4 0.7 copy.24.above_ref
  15.0 4.6 %cells.1.early_ref = bf16[5,96,2176]{2,1,0:T(8,128)(2,1)} custom-call(bf16[6,8,32,256]{3,2,1,0:T(8,128)(2,1)} %field_ref.1, bf16[6,32,256]{2,1,0:T(8,128)(2,1)} %copy.23.below_ref, bf16[6,32,256]{2,1,0:T(8,128)(2,1)} %copy.24.above_ref, bf16[256,256]{1,0:T(8,128)(2,1)} %constant.70.clone.col_ref, bf16[408,384]{1,0:T(8,128)(2,1)} %constant.72.clone.row_ref), custom_call_target="tpu_custom_call" | custom-call | flops 603979776 | bytes 3516416 | tf_op jit(solution)/shard_map/cells/pallas_call | solution.py:468
  19.7 0.0 collective-permute-done.2.before_ref
  19.7 0.0 collective-permute-done.3.after_ref
  19.7 0.0 copy-start.9
  19.7 0.6 copy-done.8
  20.3 0.0 copy-done.9
  20.3 24.7 %forward.1 = (bf16[128,4,16,128]{3,2,1,0:T(8,128)(2,1)}, bf16[4,512,2048]{2,1,0:T(8,128)(2,1)}, f32[64,512]{1,0:T(8,128)}, f32[64,768]{1,0:T(8,128)}, bf16[10,8,...) custom-call(bf16[5,96,2176]{2,1,0:T(8,128)(2,1)} %cells.1.early_ref, bf16[10,8,256]{2,1,0:T(8,128)(2,1)} %copy-done.8, ...), custom_call_target="tpu_custom_call" | custom-call | flops 8589934592 | bytes 18016768 | tf_op jit(solution)/shard_map/forward/pallas_call | solution.py:468
  45.0 1.8 %collective-permute-start.4 = (f32[64,768]{1,0:T(8,128)}, f32[64,768]{1,0:T(8,128)S(1)}, u32[]{:S(2)}, u32[]{:S(2)}) collective-permute-start(f32[64,768]{1,0:T(8,128)} %get-tuple-element.34), channel_id=1, source_target_pairs={{0,16},{4,20},{8,24},{12,28},{16,0},{20,4},{24,8},{28,12},{1,17},{... | collective-permute-start | bytes 589832 | tf_op jit(solution)/shard_map/ppermute | solution.py:25
  46.8 0.1 pad.13.clone
  46.9 1.8 %collective-permute-start.9 = (bf16[10,8,256]{2,1,0:T(8,128)(2,1)}, bf16[10,8,256]{2,1,0:T(8,128)(2,1)S(1)}, u32[]{:S(2)}, u32[]{:S(2)}) collective-permute-start(bf16[10,8,256]{2,1,0:T(8,128)(2,1)} %get-tuple-element.40), channel_id=1, source_target_pairs={{0,3},{1,0},{2,1},{3,2},{4,7},{5,4},{6,5},{7,6},{8,11},{9,8},{10,9... | collective-permute-start | bytes 122888 | tf_op jit(solution)/shard_map/ppermute | solution.py:20
  48.7 0.2 collective-permute-start.8
  48.9 6.4 %spread.2 = (f32[4,6,32,256]{3,2,1,0:T(8,128)}, f32[96,2176]{1,0:T(8,128)}, f32[96,2176]{1,0:T(8,128)}) custom-call(bf16[4,512,2048]{2,1,0:T(8,128)(2,1)} %get-tuple-element.32.refs_0_, bf16[384,512]{1,0:T(8,128)(2,1)} %get-tuple-element.28.conv_t_ref.refs_1_, bf16[256,256]{1,0:T(8,128)(2,1)} %constant.71.clone.merge_ref.refs_2_, ...), custom_call_target="tpu_custom_call" | custom-call | flops 1610612736 | bytes 11683840 | tf_op jit(solution)/shard_map/spread/pallas_call | solution.py:468
  55.4 0.0 collective-permute-done.4
  55.4 0.9 %slice_add_fusion.2 = f32[64,256]{1,0:T(8,128)S(1)} fusion(f32[64,768]{1,0:T(8,128)S(1)} %collective-permute-done.4, f32[64,768]{1,0:T(8,128)} %get-tuple-element.34), kind=kLoop, calls=%fused_computation.9 | loop fusion | flops 16384 | bytes 196608 | tf_op jit(solution)/shard_map/add | solution.py:660
  56.4 0.7 collective-permute-start.5
  57.0 0.0 collective-permute-done.9.refs_9_
  57.0 4.4 %collective-permute-done.5 = f32[32,1024]{1,0:T(8,128)S(1)} collective-permute-done((f32[32,1024]{1,0:T(8,128)S(1)}, f32[32,1024]{1,0:T(8,128)S(1)}, u32[]{:S(2)}, u32[]{:S(2)}) %collective-permute-start.5) | collective-permute-done | bytes 131104 | tf_op jit(solution)/shard_map/ppermute | solution.py:25
  61.5 0.1 collective-permute-start.6
  61.6 0.0 collective-permute-done.8.refs_10_
  61.7 1.2 %collective-permute-done.6 = f32[16,1536]{1,0:T(8,128)S(1)} collective-permute-done((f32[16,1536]{1,0:T(8,128)S(1)}, f32[16,1536]{1,0:T(8,128)S(1)}, u32[]{:S(2)}, u32[]{:S(2)}) %collective-permute-start.6) | collective-permute-done | bytes 98336 | tf_op jit(solution)/shard_map/ppermute | solution.py:25
  63.0 0.1 collective-permute-start.7
  63.1 0.1 fusion.1
  63.2 0.6 collective-permute-start.10
  63.8 0.0 collective-permute-start.11
  63.8 4.1 %collective-permute-done.7 = f32[16,1536]{1,0:T(8,128)S(1)} collective-permute-done((f32[16,1536]{1,0:T(8,128)S(1)}, f32[16,1536]{1,0:T(8,128)S(1)}, u32[]{:S(2)}, u32[]{:S(2)}) %collective-permute-start.7) | collective-permute-done | bytes 98336 | tf_op jit(solution)/shard_map/ppermute | solution.py:25
  67.9 0.0 copy-start.1
  67.9 2.5 %collective-permute-start.12 = (f32[16,1536]{1,0:T(8,128)S(1)}, f32[16,1536]{1,0:T(8,128)S(1)}, u32[]{:S(2)}, u32[]{:S(2)}) collective-permute-start(f32[16,1536]{1,0:T(8,128)S(1)} %add.64.mine_ref), channel_id=1, source_target_pairs={{0,2},{1,3},{2,0},{3,1},{4,6},{5,7},{6,4},{7,5},{8,10},{9,11},{10,... | collective-permute-start | bytes 294920 | tf_op jit(solution)/shard_map/ppermute | solution.py:25
  70.4 0.0 collective-permute-done.10.refs_7_
  70.4 0.0 collective-permute-done.11.refs_8_
  70.5 0.6 copy-done.4
  71.1 0.0 copy-done.5
  71.1 7.5 %spread.3 = f32[6,8,32,256]{3,2,1,0:T(8,128)} custom-call(bf16[4,512,2048]{2,1,0:T(8,128)(2,1)} %get-tuple-element.32.refs_0_, bf16[384,512]{1,0:T(8,128)(2,1)} %get-tuple-element.28.conv_t_ref.refs_1_, bf16[256,256]{1,0:T(8,128)(2,1)} %constant.71.clone.merge_ref.refs_2_, bf16[384,408]{1,0:T(8,128)(2,1)} %constant.73.clone.refs_3_, ...), custom_call_target="tpu_custom_call" | custom-call | flops 1610612736 | bytes 13535232 | tf_op jit(solution)/shard_map/spread/pallas_call | solution.py:468
  78.6 0.0 collective-permute-done.12.theirs_ref
  78.6 0.6 copy-done.3
  79.2 1.6 %last.1 = (f32[64,162]{1,0:T(8,128)}, f32[1,64]{1,0:T(1,128)}, f32[16,512]{1,0:T(8,128)}, f32[1,128]{1,0:T(1,128)}, f32[1,1]{1,0:T(1,128)}) custom-call(f32[16,1536]{1,0:T(8,128)} %copy-done.1, f32[16,1536]{1,0:T(8,128)} %copy-done.3), custom_call_target="tpu_custom_call" | custom-call | bytes 271620 | tf_op jit(solution)/shard_map/last/pallas_call | solution.py:468
  (47 shorter events, 0.3 us)
Async XLA Ops:
  1.7 7.5 %collective-permute-start = (bf16[6,32,256]{2,0,1:T(8,128)(2,1)S(1)}, bf16[6,32,256]{2,0,1:T(8,128)(2,1)S(1)}, u32[]{:S(2)}, u32[]{:S(2)}) collective-permute-start(bf16[6,32,256]{2,0,1:T(8,128)(2,1)S(1)} %bitcast.43), channel_id=1, source_target_pairs={{0,4},{4,8},{8,12},{12,16},{16,20},{20,24},{24,28},{28,0},{1,5},{5... | collective-permute-start | bytes 294920 | tf_op jit(solution)/shard_map/ppermute | solution.py:20
  2.2 6.9 %collective-permute-start.1 = (bf16[6,32,256]{2,0,1:T(8,128)(2,1)S(1)}, bf16[6,32,256]{2,0,1:T(8,128)(2,1)S(1)}, u32[]{:S(2)}, u32[]{:S(2)}) collective-permute-start(bf16[6,32,256]{2,0,1:T(8,128)(2,1)S(1)} %bitcast.44), channel_id=1, source_target_pairs={{0,28},{4,0},{8,4},{12,8},{16,12},{20,16},{24,20},{28,24},{1,29},{... | collective-permute-start | bytes 294920 | tf_op jit(solution)/shard_map/ppermute | solution.py:20
  9.2 10.5 %collective-permute-start.2 = (bf16[10,8,256]{2,1,0:T(8,128)(2,1)S(1)}, bf16[10,8,256]{2,1,0:T(8,128)(2,1)S(1)}, u32[]{:S(2)}, u32[]{:S(2)}) collective-permute-start(bf16[10,8,256]{2,1,0:T(8,128)(2,1)S(1)} %pad.7), channel_id=1, source_target_pairs={{0,1},{1,2},{2,3},{3,0},{4,5},{5,6},{6,7},{7,4},{8,9},{9,10},{10,1... | collective-permute-start | bytes 122888 | tf_op jit(solution)/shard_map/ppermute | solution.py:20
  11.6 8.1 %collective-permute-start.3 = (bf16[10,8,256]{2,1,0:T(8,128)(2,1)S(1)}, bf16[10,8,256]{2,1,0:T(8,128)(2,1)S(1)}, u32[]{:S(2)}, u32[]{:S(2)}) collective-permute-start(bf16[10,8,256]{2,1,0:T(8,128)(2,1)S(1)} %pad.8), channel_id=1, source_target_pairs={{0,3},{1,0},{2,1},{3,2},{4,7},{5,4},{6,5},{7,6},{8,11},{9,8},{10,9... | collective-permute-start | bytes 122888 | tf_op jit(solution)/shard_map/ppermute | solution.py:20
  19.7 0.6 copy-start.8
  19.7 0.6 copy-start.9
  45.0 10.3 %collective-permute-start.4 = (f32[64,768]{1,0:T(8,128)}, f32[64,768]{1,0:T(8,128)S(1)}, u32[]{:S(2)}, u32[]{:S(2)}) collective-permute-start(f32[64,768]{1,0:T(8,128)} %get-tuple-element.34), channel_id=1, source_target_pairs={{0,16},{4,20},{8,24},{12,28},{16,0},{20,4},{24,8},{28,12},{1,17},{... | collective-permute-start | bytes 589832 | tf_op jit(solution)/shard_map/ppermute | solution.py:25
  46.9 10.1 %collective-permute-start.9 = (bf16[10,8,256]{2,1,0:T(8,128)(2,1)}, bf16[10,8,256]{2,1,0:T(8,128)(2,1)S(1)}, u32[]{:S(2)}, u32[]{:S(2)}) collective-permute-start(bf16[10,8,256]{2,1,0:T(8,128)(2,1)} %get-tuple-element.40), channel_id=1, source_target_pairs={{0,3},{1,0},{2,1},{3,2},{4,7},{5,4},{6,5},{7,6},{8,11},{9,8},{10,9... | collective-permute-start | bytes 122888 | tf_op jit(solution)/shard_map/ppermute | solution.py:20
  48.7 12.9 %collective-permute-start.8 = (bf16[10,8,256]{2,1,0:T(8,128)(2,1)}, bf16[10,8,256]{2,1,0:T(8,128)(2,1)S(1)}, u32[]{:S(2)}, u32[]{:S(2)}) collective-permute-start(bf16[10,8,256]{2,1,0:T(8,128)(2,1)} %get-tuple-element.39), channel_id=1, source_target_pairs={{0,1},{1,2},{2,3},{3,0},{4,5},{5,6},{6,7},{7,4},{8,9},{9,10},{10,1... | collective-permute-start | bytes 122888 | tf_op jit(solution)/shard_map/ppermute | solution.py:20
  48.9 7.4 %copy-start.2 = (f32[64,512]{1,0:T(8,128)S(1)}, f32[64,512]{1,0:T(8,128)}, u32[]{:S(2)}) copy-start(f32[64,512]{1,0:T(8,128)} %get-tuple-element.33) | copy-start | bytes 393220
  55.4 7.7 %copy-start = (f32[4,6,32,256]{3,2,1,0:T(8,128)S(1)}, f32[4,6,32,256]{3,2,1,0:T(8,128)}, u32[]{:S(2)}) copy-start(f32[4,6,32,256]{3,2,1,0:T(8,128)} %get-tuple-element.38.refs_6_) | copy-start | bytes 2359300
  56.4 5.0 %collective-permute-start.5 = (f32[32,1024]{1,0:T(8,128)S(1)}, f32[32,1024]{1,0:T(8,128)S(1)}, u32[]{:S(2)}, u32[]{:S(2)}) collective-permute-start(f32[32,1024]{1,0:T(8,128)S(1)} %pad_maximum_fusion), channel_id=1, source_target_pairs={{0,8},{4,12},{8,0},{12,4},{16,24},{20,28},{24,16},{28,20},{1,9},{5... | collective-permute-start | bytes 393224 | tf_op jit(solution)/shard_map/ppermute | solution.py:25
  57.0 13.4 %copy-start.6 = (bf16[10,8,256]{2,1,0:T(8,128)(2,1)}, bf16[10,8,256]{2,1,0:T(8,128)(2,1)S(1)}, u32[]{:S(2)}) copy-start(bf16[10,8,256]{2,1,0:T(8,128)(2,1)S(1)} %collective-permute-done.9.refs_9_) | copy-start | bytes 122884
  61.5 1.4 %collective-permute-start.6 = (f32[16,1536]{1,0:T(8,128)S(1)}, f32[16,1536]{1,0:T(8,128)S(1)}, u32[]{:S(2)}, u32[]{:S(2)}) collective-permute-start(f32[16,1536]{1,0:T(8,128)S(1)} %constant_dynamic-update-slice_fusion), channel_id=1, source_target_pairs={{0,4},{4,0},{8,12},{12,8},{16,20},{20,16},{24,28},{28,24},{1,5},{5... | collective-permute-start | bytes 294920 | tf_op jit(solution)/shard_map/ppermute | solution.py:25
  61.6 8.8 %copy-start.7 = (bf16[10,8,256]{2,1,0:T(8,128)(2,1)}, bf16[10,8,256]{2,1,0:T(8,128)(2,1)S(1)}, u32[]{:S(2)}) copy-start(bf16[10,8,256]{2,1,0:T(8,128)(2,1)S(1)} %collective-permute-done.8.refs_10_) | copy-start | bytes 122884
  63.0 4.9 %collective-permute-start.7 = (f32[16,1536]{1,0:T(8,128)S(1)}, f32[16,1536]{1,0:T(8,128)S(1)}, u32[]{:S(2)}, u32[]{:S(2)}) collective-permute-start(f32[16,1536]{1,0:T(8,128)S(1)} %constant_dynamic-update-slice_fusion.4), channel_id=1, source_target_pairs={{0,1},{1,0},{2,3},{3,2},{4,5},{5,4},{6,7},{7,6},{8,9},{9,8},{10,11... | collective-permute-start | bytes 294920 | tf_op jit(solution)/shard_map/ppermute | solution.py:25
  63.2 7.2 %collective-permute-start.10 = (bf16[6,32,256]{2,1,0:T(8,128)(2,1)S(1)}, bf16[6,32,256]{2,1,0:T(8,128)(2,1)S(1)}, u32[]{:S(2)}, u32[]{:S(2)}) collective-permute-start(bf16[6,32,256]{2,1,0:T(8,128)(2,1)S(1)} %get-tuple-element.48), channel_id=1, source_target_pairs={{0,28},{4,0},{8,4},{12,8},{16,12},{20,16},{24,20},{28,24},{1,29},{... | collective-permute-start | bytes 294920 | tf_op jit(solution)/shard_map/ppermute | solution.py:20
  63.8 6.6 %collective-permute-start.11 = (bf16[6,32,256]{2,1,0:T(8,128)(2,1)S(1)}, bf16[6,32,256]{2,1,0:T(8,128)(2,1)S(1)}, u32[]{:S(2)}, u32[]{:S(2)}) collective-permute-start(bf16[6,32,256]{2,1,0:T(8,128)(2,1)S(1)} %get-tuple-element.47), channel_id=1, source_target_pairs={{0,4},{4,8},{8,12},{12,16},{16,20},{20,24},{24,28},{28,0},{1,5},{5... | collective-permute-start | bytes 294920 | tf_op jit(solution)/shard_map/ppermute | solution.py:20
  67.9 10.7 %copy-start.1 = (f32[16,1536]{1,0:T(8,128)}, f32[16,1536]{1,0:T(8,128)S(1)}, u32[]{:S(2)}) copy-start(f32[16,1536]{1,0:T(8,128)S(1)} %add.64.mine_ref) | copy-start | bytes 294916
  67.9 10.7 %collective-permute-start.12 = (f32[16,1536]{1,0:T(8,128)S(1)}, f32[16,1536]{1,0:T(8,128)S(1)}, u32[]{:S(2)}, u32[]{:S(2)}) collective-permute-start(f32[16,1536]{1,0:T(8,128)S(1)} %add.64.mine_ref), channel_id=1, source_target_pairs={{0,2},{1,3},{2,0},{3,1},{4,6},{5,7},{6,4},{7,5},{8,10},{9,11},{10,... | collective-permute-start | bytes 294920 | tf_op jit(solution)/shard_map/ppermute | solution.py:25
  70.4 0.6 copy-start.4
  70.4 0.7 copy-start.5
  78.6 0.6 copy-start.3

commit v7 on v6

--- a/solution.py
+++ b/solution.py
@@ -88,6 +88,12 @@
     return (high,) + split_two(value - high.astype(f32))
 
 
+def beside(value, count):
+    while value.shape[0] > count:
+        value = jnp.concatenate(jnp.split(value, 2, axis=0), axis=1)
+    return value
+
+
 def conv_rows(conv_ref, tap_ref):
     return jnp.concatenate([dot(conv_ref[...], tap_ref[cls]) for cls in range(8)], axis=0)
 
@@ -96,37 +102,44 @@
     return jnp.transpose(jnp.broadcast_to(ref[...], (lanes, count)))
 
 
-def weights_kernel(
+def planes_kernel(sizes, first_ref, last_ref, first_out, last_out):
+    first_out[...] = first_ref[:, 0]
+    last_out[...] = last_ref[:, 0]
+
+
+def prepare_kernel(
     sizes,
+    field_ref,
+    below_ref,
+    above_ref,
     conv_weight_ref,
     conv_bias_ref,
     down_weight_ref,
     tap_ref,
     order_ref,
+    col_ref,
+    row_ref,
+    split_ref,
     conv_ref,
     conv_t_ref,
     down_ref,
     down_t_ref,
 ):
-    hidden, win = sizes
+    channels, pairs, half_rows, hidden = sizes
+    group = 4 * channels
     conv = conv_rows(conv_weight_ref, tap_ref)
     conv_t_ref[...] = jnp.transpose(conv).astype(bf16)
-    conv_ref[:, :win] = (0.5 * conv).astype(bf16)
+    conv_ref[:, : 16 * group] = (0.5 * conv).astype(bf16)
     bias = 0.5 * row_of(conv_bias_ref, hidden)
     at = lax.broadcasted_iota(jnp.int32, bias.shape, 1)
     columns = jnp.zeros_like(bias)
     for k, piece in enumerate(split_three(bias)):
         columns = jnp.where(at == k, piece.astype(f32), columns)
     columns = jnp.concatenate([columns[:, :16]] * 8, axis=0)
-    conv_ref[:, win:] = columns.astype(bf16)
+    conv_ref[:, 16 * group :] = columns.astype(bf16)
     down = dot(down_weight_ref[...], order_ref[...])
     down_ref[...] = down.astype(bf16)
     down_t_ref[...] = jnp.transpose(down).astype(bf16)
-
-
-def cells_kernel(sizes, field_ref, below_ref, above_ref, col_ref, row_ref, split_ref):
-    channels, pairs, half_rows = sizes
-    group = 4 * channels
     for slot in range(pairs + 1):
         lower = below_ref if slot == 0 else field_ref.at[:, 2 * slot - 1]
         upper = above_ref if slot == pairs else field_ref.at[:, 2 * slot]
@@ -162,10 +175,13 @@
     edge_t_ref,
     out_ref,
     gpre_ref,
-    keep_ref,
-    give_ref,
     to_before_ref,
     to_after_ref,
+    *rest,
+):
+    channels, pairs, half_rows, hidden, out_count, tile, cell_total, groups = sizes
+    message_refs = rest[:groups]
+    (
     split_ref,
     gdown_t_ref,
     gconv_t_ref,
@@ -180,8 +196,7 @@
     sides_ref,
     split_sem,
     late_sem,
-):
-    channels, pairs, half_rows, hidden, out_count, tile, cell_total = sizes
+    ) = rest[groups:]
     group = 4 * channels
     cells = half_rows * lanes
     step = pl.program_id(0)
@@ -321,12 +336,14 @@
         pieces = jnp.concatenate(split_three(jnp.transpose(gdown_t_ref[...])), axis=0)
         pieces = dot_rows(pieces, order_ref[...])
         grad_down = pieces[:out_count] + (pieces[out_count : 2 * out_count] + pieces[2 * out_count :])
-        rows = out_count // 2
-        upper = lax.axis_index("gz") // (lax.axis_size("gz") // 2)
+        rows = out_count // len(message_refs)
+        small = beside(small, rows)
+        here = lax.axis_index("gz") // 2
         whole_ref[...] = grad_down / cell_total
-        keep_ref[...] = whole_ref[pl.ds(pl.multiple_of(upper * rows, rows), rows)]
-        give_ref[:, : 8 * hidden] = whole_ref[pl.ds(pl.multiple_of((1 - upper) * rows, rows), rows)]
-        give_ref[:, 8 * hidden :] = small
+        for far, ref in enumerate(message_refs):
+            first = pl.multiple_of((here ^ far) * rows, rows)
+            ref[:, : 8 * hidden] = whole_ref[pl.ds(first, rows)]
+            ref[:, 8 * hidden :] = small
         sides_of(channels, pairs, outer_ref, conv_t_ref, merge_ref, edge_t_ref, to_before_ref, to_after_ref)
 
 
@@ -445,13 +462,16 @@
                         ref[...] = spread_ref[slots.index(slot)]
 
 
-def last_kernel(sizes, mine_ref, theirs_ref, conv_out, cbias_out, down_out, dbias_out, loss_out):
+def last_kernel(sizes, *refs):
     hidden, taps, big = sizes
-    total = mine_ref[...] + theirs_ref[...]
+    conv_out, cbias_out, down_out, dbias_out, loss_out = refs[-5:]
+    total = refs[0][...]
+    for ref in refs[1:-5]:
+        total = total + ref[...]
     down_out[...] = total[:, :big]
-    small = jnp.concatenate(
-        [total[:, at : at + 2 * lanes] for at in range(big, total.shape[1], 2 * lanes)], axis=0
-    )
+    small = total[:, big:]
+    while small.shape[0] < hidden:
+        small = jnp.concatenate(jnp.split(small, 2, axis=1), axis=0)
     conv_out[...] = small[:, :taps]
     turned = jnp.transpose(small[:, lanes:])
     at = taps - lanes
@@ -501,39 +521,45 @@
     return {name: jnp.asarray(value, bf16) for name, value in names.items()}
 
 
-def weights(conv_weight, conv_bias, down_weight, fixed):
+def outer_planes(fields):
+    channels, depth, row_count, col_count = fields.shape
+    out = jax.ShapeDtypeStruct((channels, row_count, col_count), fields.dtype)
+    block = (channels, 1, row_count, col_count)
+    return call(
+        planes_kernel,
+        (),
+        [out, out],
+        fields, fields,
+        grid=(1,),
+        in_specs=[pl.BlockSpec(block, lambda z: (0, 0, 0, 0)), pl.BlockSpec(block, lambda z: (0, depth - 1, 0, 0))],
+        out_specs=[whole(out.shape)] * 2,
+        name="planes",
+    )
+
+
+def prepare(fields, below, above, conv_weight, conv_bias, down_weight, fixed):
+    channels, depth, row_count, _ = fields.shape
     hidden, out_count = conv_weight.shape[0], down_weight.shape[0]
-    big, win = 8 * hidden, fixed["tap"].shape[2]
+    pairs, half_rows = depth // 2, row_count // 2
+    big, win = 8 * hidden, 64 * channels
     return call(
-        weights_kernel,
-        (hidden, win),
+        prepare_kernel,
+        (channels, pairs, half_rows, hidden),
         [
+            jax.ShapeDtypeStruct((pairs + 1, 16 * channels, (half_rows + 1) * lanes), bf16),
             jax.ShapeDtypeStruct((big, win + 16), bf16),
             jax.ShapeDtypeStruct((win, big), bf16),
             jax.ShapeDtypeStruct((out_count, big), bf16),
             jax.ShapeDtypeStruct((big, out_count), bf16),
         ],
-        conv_weight, conv_bias[None], down_weight, fixed["tap"], fixed["order"],
-        flops=2 * big * win * conv_weight.shape[1],
-        name="weights",
-    )
-
-
-def parity_cells(fields, below, above, fixed):
-    channels, depth, row_count, _ = fields.shape
-    pairs, half_rows = depth // 2, row_count // 2
-    (early,) = call(
-        cells_kernel,
-        (channels, pairs, half_rows),
-        [jax.ShapeDtypeStruct((pairs + 1, 16 * channels, (half_rows + 1) * lanes), bf16)],
-        fields, below, above, fixed["col"], fixed["row"],
+        fields, below, above, conv_weight, conv_bias[None], down_weight,
+        fixed["tap"], fixed["order"], fixed["col"], fixed["row"],
         flops=2 * fields.size * row_count * channels * 4,
-        name="cells",
-    )
-    return early
-
-
-def forward(early, before, after, target, conv, conv_t, down, down_t, down_bias, fixed, channels, cell_total):
+        name="prepare",
+    )
+
+
+def forward(early, before, after, target, conv, conv_t, down, down_t, down_bias, fixed, channels, cell_total, groups):
     out_count, pairs, half_rows, half_cols = target.shape
     win, big = conv_t.shape
     hidden = big // 8
@@ -543,32 +569,32 @@
         fixed["tap"], fixed["order"], fixed["col"], fixed["edge"], fixed["merge"], fixed["edge_t"],
     )
     slab = pl.BlockSpec((out_count, 1, half_rows, half_cols), lambda z: (0, z, 0, 0))
+    rows = out_count // groups
+    message = jax.ShapeDtypeStruct((rows, big + 2 * lanes * hidden // rows), f32)
     in_specs = [whole(a.shape) for a in args]
     for i in (0, 9, 10):
         in_specs[i] = pl.BlockSpec(memory_space=pl.ANY)
     in_specs[3] = slab
     return call(
         forward_kernel,
-        (channels, pairs, half_rows, hidden, out_count, forward_tile, cell_total),
+        (channels, pairs, half_rows, hidden, out_count, forward_tile, cell_total, groups),
         [
             jax.ShapeDtypeStruct(target.shape, bf16),
             jax.ShapeDtypeStruct((pairs, big, cells), bf16),
-            jax.ShapeDtypeStruct((out_count // 2, big), f32),
-            jax.ShapeDtypeStruct((out_count // 2, big + 2 * lanes), f32),
             jax.ShapeDtypeStruct(before.shape, bf16),
             jax.ShapeDtypeStruct(after.shape, bf16),
-        ],
+        ]
+        + [message] * groups,
         *args,
         grid=(pairs,),
         in_specs=in_specs,
         out_specs=[
             slab,
             pl.BlockSpec((1, big, cells), lambda z: (z, 0, 0)),
-            whole((out_count // 2, big)),
-            whole((out_count // 2, big + 2 * lanes)),
             whole(before.shape),
             whole(after.shape),
-        ],
+        ]
+        + [whole(message.shape)] * groups,
         scratch=[
             pltpu.VMEM(early.shape, bf16),
             pltpu.VMEM((big, out_count), f32),
@@ -631,8 +657,9 @@
     cell_total = fields.size // channels // 8 * lax.axis_size("gz") * lax.axis_size("gy")
     fixed = constants(channels, row_count, col_count // 2, hidden)
 
-    below = shifted(fields[:, depth - 1], "gz", 1)
-    above = shifted(fields[:, 0], "gz", -1)
+    first_plane, last_plane = outer_planes(fields)
+    below = shifted(last_plane, "gz", 1)
+    above = shifted(first_plane, "gz", -1)
 
     def side(row):
         rows = [below[:, row][:, None], fields[:, :, row], above[:, row][:, None]]
@@ -641,40 +668,22 @@
 
     before = shifted(side(row_count - 1), "gy", 1)
     after = shifted(side(0), "gy", -1)
-    conv_big, conv_t, down_big, down_t = weights(conv_weight, conv_bias, down_weight, fixed)
-    early = parity_cells(fields, below, above, fixed)
-    out_field, grad_pre, own, packed, to_before, to_after = forward(
-        early, before, after, target, conv_big, conv_t, down_big, down_t, down_bias, fixed, channels, cell_total
+    early, conv_big, conv_t, down_big, down_t = prepare(
+        fields, below, above, conv_weight, conv_bias, down_weight, fixed
+    )
+    groups = lax.axis_size("gz") // 2
+    out_field, grad_pre, to_before, to_after, *messages = forward(
+        early, before, after, target, conv_big, conv_t, down_big, down_t, down_bias, fixed, channels, cell_total, groups
     )
     pairs = depth // 2
     shape = fields.shape
 
-    def beside(value, count):
-        return jnp.concatenate(jnp.split(value, value.shape[0] // count, axis=0), axis=1)
-
-    me = lax.axis_index("gz")
-    small = packed[:, big:]
-
-    def added(own, small, got):
-        pieces = jnp.split(got[:, big:], hidden // own.shape[0], axis=1)
-        return own + got[:, :big], small + jnp.concatenate(pieces, axis=0)
-
-    def halved(own, small, bit):
-        count = own.shape[0] // 2
-        upper = (me // bit) % 2
-        give = lax.dynamic_slice_in_dim(own, (1 - upper) * count, count, 0)
-        own = lax.dynamic_slice_in_dim(own, upper * count, count, 0)
-        return own, jnp.concatenate([give, beside(small, count)], axis=1)
-
-    bit = lax.axis_size("gz") // 2
-    got = exchanged(packed, "gz", bit)
+    got = [exchanged(message, "gz", 2 * far) for far, message in enumerate(messages) if far > 0]
     from_before = shifted(to_after, "gy", 1)
     from_after = shifted(to_before, "gy", -1)
     outer = ((0, pairs - 1), (0, 1, pairs - 1, pairs), (), (0, pairs), (1, pairs - 1))
     outer_core, low_open, high_open = spread(grad_pre, conv_t, fixed, shape, outer)
-    own, small = added(own, small, got)
-    bit //= 2
-    own, packed = halved(own, small, bit)
+    packed = sum(got, messages[0])
 
     def plane(value, at):
         low = from_before[at, :channels, None].astype(f32)
@@ -682,23 +691,17 @@
         gap = jnp.zeros((channels, row_count - 2, col_count), f32)
         return (value + jnp.concatenate([low, gap, high], axis=1)).astype(bf16)
 
-    got = exchanged(packed, "gz", bit)
     from_below = shifted(plane(outer_core[3], depth + 1), "gz", 1)
     from_above = shifted(plane(outer_core[0], 0), "gz", -1)
-    own, small = added(own, small, got)
-    while bit > 1:
-        bit //= 2
-        own, packed = halved(own, small, bit)
-        own, small = added(own, small, exchanged(packed, "gz", bit))
-    packed = jnp.concatenate([own, beside(small, own.shape[0])], axis=1)
-    count = own.shape[0]
-
-    bit = 1
-    while 2 * bit < lax.axis_size("gy"):
-        packed = packed + exchanged(packed, "gy", bit)
-        bit *= 2
+    count = packed.shape[0] // 2
+    core = lax.axis_index("gz") % 2
+    own, small = packed[:, :big], beside(packed[:, big:], count)
+    give = lax.dynamic_slice_in_dim(own, (1 - core) * count, count, 0)
+    own = lax.dynamic_slice_in_dim(own, core * count, count, 0)
+    packed = jnp.concatenate([own, small], axis=1) + exchanged(jnp.concatenate([give, small], axis=1), "gz", 1)
+
     packed, low_open = lax.optimization_barrier((packed, low_open))
-    got = exchanged(packed, "gy", bit)
+    got = [exchanged(packed, "gy", far) for far in range(1, lax.axis_size("gy"))]
     inner = tuple(range(1, pairs - 1)), tuple(range(1, pairs)), (1, pairs - 1), tuple(range(1, pairs)), ()
     (sensitivity,) = spread(
         grad_pre, conv_t, fixed, shape, inner, (low_open, high_open),
@@ -714,7 +717,7 @@
             jax.ShapeDtypeStruct((1, out_count), f32),
             jax.ShapeDtypeStruct((1, 1), f32),
         ],
-        packed, got,
+        packed, *got,
         name="last",
     )
     return out_field, sensitivity, conv, cbias[0], down, dbias[0], loss[0, 0]

time: 81.2 us -> 79.1 us (0.974)
  waiting for transfers between devices: 9.69 us -> 1.89 us
  starting transfers between devices: 15.7 us -> 20.1 us
  local copies, waits for them, and re-layouts: 5.63 us -> 7.04 us
    ppermute x5 -> x7, waiting for transfers between devices: 9.67 us -> 0.02 us  [exchanged(): return lax.ppermute(value, axis, [(i, i ^ bit) for i in range(count)])]
    ppermute x5 -> x7, starting transfers between devices: 5.09 us -> 8.07 us  [exchanged(): return lax.ppermute(value, axis, [(i, i ^ bit) for i in range(count)])]
    pallas_call x0 -> x2, local copies, waits for them, and re-layouts: none -> 1.9 us  [call(): pl.pallas_call(functools.partial(kernel, sizes), out_shape=out_shape, in_...]
    ppermute x8, waiting for transfers between devices: 0.02 us -> 1.87 us  [shifted(): lax.ppermute(value, axis, [(i, (i + by) % count) for i in range(count)])]
    ppermute x8, starting transfers between devices: 10.6 us -> 12 us  [shifted(): lax.ppermute(value, axis, [(i, (i + by) % count) for i in range(count)])]
    convert_element_type x1, other arithmetic: 0.1 us -> 1.13 us  [plane(): return (value + jnp.concatenate([low, gap, high], axis=1)).astype(bf16)]
    slice x1, local copies, waits for them, and re-layouts: 0.96 us -> 0.01 us  [on_device(): own, small = (packed[:, :big], beside(packed[:, big:], count))]
    add x6 -> x2, other arithmetic: 0.99 us -> 0.04 us  [the longest x1 0.03 us: on_device(): packed = sum(got, messages[0])]
  transfers between devices with their start and end apart: 13 -> 15, of which waited for: 3 -> 2; matrix products, arithmetic and copies ran while one was open for 5% -> 6% of each run, Pallas kernels for 26% -> 25%
where the time goes in v7:
time: 79.1 us; the launch traced here: 78.8 us
  Pallas kernels  47.6 us (60%)
  starting transfers between devices  20.1 us (25%)
  local copies, waits for them, and re-layouts  7.04 us (9%)
  waiting for transfers between devices  1.89 us (2%)
  other arithmetic  1.22 us (2%)
  between operations  0.95 us (1%)
    pallas_call x6, Pallas kernels, call(): pl.pallas_call(functools.partial(kernel, sizes), out_shape=out_shape, in_...  47.6 us
    ppermute x8, starting transfers between devices, shifted(): lax.ppermute(value, axis, [(i, (i + by) % count) for i in range(count)])  12 us
    ppermute x7, starting transfers between devices, exchanged(): return lax.ppermute(value, axis, [(i, i ^ bit) for i in range(count)])  8.07 us
    unnamed x22, local copies, waits for them, and re-layouts  2.52 us
    pallas_call x2, local copies, waits for them, and re-layouts, call(): pl.pallas_call(functools.partial(kernel, sizes), out_shape=out_shape, in_...  1.9 us
    ppermute x8, waiting for transfers between devices, shifted(): lax.ppermute(value, axis, [(i, (i + by) % count) for i in range(count)])  1.87 us
  transfers between devices with their start and end apart: 15, of which 2 were waited for; matrix products, arithmetic and copies ran while one was open for 6% of the time, Pallas kernels for 25%

profile of v7, /device:TPU:0, one launch (start us, length us, event | category | flops | bytes accessed | tf_op | source)
XLA Modules:
  0.0 78.8 jit_solution(14525662485850303672)
XLA Ops:
  0.6 1.6 %planes.1 = (bf16[6,32,256]{2,1,0:T(8,128)(2,1)}, bf16[6,32,256]{2,1,0:T(8,128)(2,1)}) custom-call(bf16[6,8,32,256]{3,2,1,0:T(8,128)(2,1)} %field_ref.1, bf16[6,8,32,256]{3,2,1,0:T(8,128)(2,1)} %field_ref.1), custom_call_target="tpu_custom_call" | custom-call | bytes 1769472 | tf_op jit(solution)/shard_map/planes/pallas_call | solution.py:488
  2.3 1.0 %copy.21 = bf16[6,32,256]{2,0,1:T(8,128)(2,1)S(1)} copy(bf16[6,32,256]{2,1,0:T(8,128)(2,1)} %get-tuple-element.32) | data formatting | bytes 196608 | tf_op jit(solution)/shard_map/planes/pallas_call | solution.py:488
  3.2 0.5 collective-permute-start
  3.7 1.0 %copy.22 = bf16[6,32,256]{2,0,1:T(8,128)(2,1)S(1)} copy(bf16[6,32,256]{2,1,0:T(8,128)(2,1)} %get-tuple-element.33) | data formatting | bytes 196608 | tf_op jit(solution)/shard_map/planes/pallas_call | solution.py:488
  4.7 2.9 %collective-permute-start.1 = (bf16[6,32,256]{2,0,1:T(8,128)(2,1)S(1)}, bf16[6,32,256]{2,0,1:T(8,128)(2,1)S(1)}, u32[]{:S(2)}, u32[]{:S(2)}) collective-permute-start(bf16[6,32,256]{2,0,1:T(8,128)(2,1)S(1)} %copy.22), channel_id=1, source_target_pairs={{0,28},{4,0},{8,4},{12,8},{16,12},{20,16},{24,20},{28,24},{1,29},{... | collective-permute-start | bytes 294920 | tf_op jit(solution)/shard_map/ppermute | solution.py:20
  7.6 1.1 %fusion.7 = (bf16[6,8,1,256]{3,2,1,0:T(2,128)(2,1)S(1)}, bf16[6,8,1,256]{3,2,1,0:T(2,128)(2,1)S(1)}) fusion(bf16[6,8,32,256]{3,2,1,0:T(8,128)(2,1)} %field_ref.1), kind=kLoop, calls=%fused_computation.24 | loop fusion | bytes 98304 | tf_op jit(solution)/shard_map/slice | solution.py:665
  8.8 0.1 pad.13.clone
  8.9 1.3 %collective-permute-done.1 = bf16[6,32,256]{2,0,1:T(8,128)(2,1)S(1)} collective-permute-done((bf16[6,32,256]{2,0,1:T(8,128)(2,1)S(1)}, bf16[6,32,256]{2,0,1:T(8,128)(2,1)S(1)}, u32[]{:S(2)}, u32[]{:S(2)}) %collective-permute-start.1) | collective-permute-done | bytes 98336 | tf_op jit(solution)/shard_map/ppermute | solution.py:20
  10.2 0.0 collective-permute-done
  10.2 2.4 %collective-permute-start.2 = (bf16[10,8,256]{2,1,0:T(8,128)(2,1)S(1)}, bf16[10,8,256]{2,1,0:T(8,128)(2,1)S(1)}, u32[]{:S(2)}, u32[]{:S(2)}) collective-permute-start(bf16[10,8,256]{2,1,0:T(8,128)(2,1)S(1)} %pad.7), channel_id=1, source_target_pairs={{0,1},{1,2},{2,3},{3,0},{4,5},{5,6},{6,7},{7,4},{8,9},{9,10},{10,1... | collective-permute-start | bytes 122888 | tf_op jit(solution)/shard_map/ppermute | solution.py:20
  12.6 2.1 %collective-permute-start.3 = (bf16[10,8,256]{2,1,0:T(8,128)(2,1)S(1)}, bf16[10,8,256]{2,1,0:T(8,128)(2,1)S(1)}, u32[]{:S(2)}, u32[]{:S(2)}) collective-permute-start(bf16[10,8,256]{2,1,0:T(8,128)(2,1)S(1)} %pad.8), channel_id=1, source_target_pairs={{0,3},{1,0},{2,1},{3,2},{4,7},{5,4},{6,5},{7,6},{8,11},{9,8},{10,9... | collective-permute-start | bytes 122888 | tf_op jit(solution)/shard_map/ppermute | solution.py:20
  14.7 0.7 copy.23.below_ref
  15.4 0.7 copy.24.above_ref
  16.0 5.5 %prepare.1 = (bf16[5,96,2176]{2,1,0:T(8,128)(2,1)}, bf16[512,400]{1,0:T(8,128)(2,1)}, bf16[384,512]{1,0:T(8,128)(2,1)}, bf16[128,512]{1,0:T(8,128)(2,1)}, bf16[512,128]{1,0:T(8,128)(2,1)}) custom-call(bf16[6,8,32,256]{3,2,1,0:T(8,128)(2,1)} %field_ref.1, bf16[6,32,256]{2,1,0:T(8,128)(2,1)} %copy.23.below_ref, bf16[6,32,256]{2,1,0:T(8,128)(2,1)} %copy.24.above_ref, ...), custom_call_target="tpu_custom_call" | custom-call | flops 603979776 | bytes 6253056 | tf_op jit(solution)/shard_map/prepare/pallas_call | solution.py:488
  21.5 0.0 collective-permute-done.2.before_ref
  21.5 0.0 copy-start.9
  21.5 0.0 collective-permute-done.3.after_ref
  21.5 0.6 copy-done.9
  22.1 0.0 copy-done.10
  22.2 24.8 %forward.1 = (bf16[128,4,16,128]{3,2,1,0:T(8,128)(2,1)}, bf16[4,512,2048]{2,1,0:T(8,128)(2,1)}, bf16[10,8,256]{2,1,0:T(8,128)(2,1)}, bf16[10,8,256]{2,1,0:T(8,12...) custom-call(bf16[5,96,2176]{2,1,0:T(8,128)(2,1)} %get-tuple-element.34.early_ref, ...), custom_call_target="tpu_custom_call" | custom-call | flops 8589934592 | bytes 18213376 | tf_op jit(solution)/shard_map/forward/pallas_call | solution.py:488
  46.9 1.8 %collective-permute-start.6 = (f32[32,1024]{1,0:T(8,128)}, f32[32,1024]{1,0:T(8,128)S(1)}, u32[]{:S(2)}, u32[]{:S(2)}) collective-permute-start(f32[32,1024]{1,0:T(8,128)} %get-tuple-element.44), channel_id=1, source_target_pairs={{0,24},{4,28},{8,16},{12,20},{16,8},{20,12},{24,0},{28,4},{1,25},{... | collective-permute-start | bytes 393224 | tf_op jit(solution)/shard_map/ppermute | solution.py:25
  48.8 0.5 collective-permute-start.5
  49.3 1.2 %collective-permute-start.4 = (f32[32,1024]{1,0:T(8,128)}, f32[32,1024]{1,0:T(8,128)S(1)}, u32[]{:S(2)}, u32[]{:S(2)}) collective-permute-start(f32[32,1024]{1,0:T(8,128)} %get-tuple-element.42), channel_id=1, source_target_pairs={{0,8},{4,12},{8,0},{12,4},{16,24},{20,28},{24,16},{28,20},{1,9},{5... | collective-permute-start | bytes 393224 | tf_op jit(solution)/shard_map/ppermute | solution.py:25
  50.5 2.0 %collective-permute-start.9 = (bf16[10,8,256]{2,1,0:T(8,128)(2,1)}, bf16[10,8,256]{2,1,0:T(8,128)(2,1)S(1)}, u32[]{:S(2)}, u32[]{:S(2)}) collective-permute-start(bf16[10,8,256]{2,1,0:T(8,128)(2,1)} %get-tuple-element.50), channel_id=1, source_target_pairs={{0,3},{1,0},{2,1},{3,2},{4,7},{5,4},{6,5},{7,6},{8,11},{9,8},{10,9... | collective-permute-start | bytes 122888 | tf_op jit(solution)/shard_map/ppermute | solution.py:20
  52.5 0.1 collective-permute-start.8
  52.5 6.4 %spread.2 = (f32[4,6,32,256]{3,2,1,0:T(8,128)}, f32[96,2176]{1,0:T(8,128)}, f32[96,2176]{1,0:T(8,128)}) custom-call(bf16[4,512,2048]{2,1,0:T(8,128)(2,1)} %get-tuple-element.40.refs_0_, bf16[384,512]{1,0:T(8,128)(2,1)} %get-tuple-element.36.conv_t_ref.refs_1_, bf16[256,256]{1,0:T(8,128)(2,1)} %constant.46.clone.merge_ref.refs_2_, ...), custom_call_target="tpu_custom_call" | custom-call | flops 1610612736 | bytes 11683840 | tf_op jit(solution)/shard_map/spread/pallas_call | solution.py:488
  59.0 0.0 collective-permute-done.9.refs_9_
  59.0 0.0 collective-permute-done.8.refs_10_
  59.1 0.0 collective-permute-done.6
  59.1 0.0 collective-permute-done.5
  59.1 0.0 collective-permute-done.4
  59.2 0.1 collective-permute-start.7
  59.3 1.1 %fusion.1 = (bf16[6,32,256]{2,1,0:T(8,128)(2,1)S(1)}, bf16[6,32,256]{2,1,0:T(8,128)(2,1)S(1)}) fusion(f32[6,1,256]{2,1,0:T(1,128)S(1)} %copy.30, f32[6,1,256]{2,1,0:T(1,128)S(1)} %copy.29, f32[4,6,32,256]{3,2,1,0:T(8,128)} %get-tuple-element.48.refs_6_, f32[32]{0:T(128)S(1)} %pad.13.clone, f32[6,1,256]{2,1,0:T(1,128)S(1)} %copy.28, f32[6,1,256]{2,1,0:T(1,128)S(1)} %copy.27), kind=kLoop, calls=%fused_computation.3 | loop fusion | flops 393216 | bytes 614528 | tf_op jit(solution)/shard_map/convert_element_type | solution.py:692
  60.4 2.1 %collective-permute-start.10 = (bf16[6,32,256]{2,1,0:T(8,128)(2,1)S(1)}, bf16[6,32,256]{2,1,0:T(8,128)(2,1)S(1)}, u32[]{:S(2)}, u32[]{:S(2)}) collective-permute-start(bf16[6,32,256]{2,1,0:T(8,128)(2,1)S(1)} %get-tuple-element.58), channel_id=1, source_target_pairs={{0,28},{4,0},{8,4},{12,8},{16,12},{20,16},{24,20},{28,24},{1,29},{... | collective-permute-start | bytes 294920 | tf_op jit(solution)/shard_map/ppermute | solution.py:20
  62.5 0.0 collective-permute-start.11
  62.5 0.0 collective-permute-done.7
  62.5 0.1 collective-permute-start.12
  62.6 4.1 %collective-permute-start.13 = (f32[16,1536]{1,0:T(8,128)S(1)}, f32[16,1536]{1,0:T(8,128)S(1)}, u32[]{:S(2)}, u32[]{:S(2)}) collective-permute-start(f32[16,1536]{1,0:T(8,128)S(1)} %fusion.2.refs_0_), channel_id=1, source_target_pairs={{0,2},{1,3},{2,0},{3,1},{4,6},{5,7},{6,4},{7,5},{8,10},{9,11},{10,... | collective-permute-start | bytes 294920 | tf_op jit(solution)/shard_map/ppermute | solution.py:25
  66.8 0.2 collective-permute-start.14
  67.0 0.6 collective-permute-done.11.refs_8_
  67.6 0.0 copy-done.5
  67.6 0.6 copy-done.6
  68.2 7.5 %spread.3 = f32[6,8,32,256]{3,2,1,0:T(8,128)} custom-call(bf16[4,512,2048]{2,1,0:T(8,128)(2,1)} %get-tuple-element.40.refs_0_, bf16[384,512]{1,0:T(8,128)(2,1)} %get-tuple-element.36.conv_t_ref.refs_1_, bf16[256,256]{1,0:T(8,128)(2,1)} %constant.46.clone.merge_ref.refs_2_, bf16[384,408]{1,0:T(8,128)(2,1)} %constant.48.clone.refs_3_, ...), custom_call_target="tpu_custom_call" | custom-call | flops 1610612736 | bytes 13535232 | tf_op jit(solution)/shard_map/spread/pallas_call | solution.py:488
  75.7 0.0 collective-permute-done.12.refs_1_
  75.7 0.6 copy-done.2
  76.3 0.0 copy-done.3
  76.4 0.6 copy-done.4
  77.0 1.8 %last.1 = (f32[64,162]{1,0:T(8,128)}, f32[1,64]{1,0:T(1,128)}, f32[16,512]{1,0:T(8,128)}, f32[1,128]{1,0:T(1,128)}, f32[1,1]{1,0:T(1,128)}) custom-call(f32[16,1536]{1,0:T(8,128)} %copy-done, f32[16,1536]{1,0:T(8,128)} %copy-done.2, f32[16,1536]{1,0:T(8,128)} %copy-done.3, f32[16,1536]{1,0:T(8,128)} %copy-done.4), custom_call_target="tpu_custom_call" | custom-call | bytes 468228 | tf_op jit(solution)/shard_map/last/pallas_call | solution.py:488
  (37 shorter events, 0.2 us)
Async XLA Ops:
  3.2 6.9 %collective-permute-start = (bf16[6,32,256]{2,0,1:T(8,128)(2,1)S(1)}, bf16[6,32,256]{2,0,1:T(8,128)(2,1)S(1)}, u32[]{:S(2)}, u32[]{:S(2)}) collective-permute-start(bf16[6,32,256]{2,0,1:T(8,128)(2,1)S(1)} %copy.21), channel_id=1, source_target_pairs={{0,4},{4,8},{8,12},{12,16},{16,20},{20,24},{24,28},{28,0},{1,5},{5... | collective-permute-start | bytes 294920 | tf_op jit(solution)/shard_map/ppermute | solution.py:20
  4.7 5.5 %collective-permute-start.1 = (bf16[6,32,256]{2,0,1:T(8,128)(2,1)S(1)}, bf16[6,32,256]{2,0,1:T(8,128)(2,1)S(1)}, u32[]{:S(2)}, u32[]{:S(2)}) collective-permute-start(bf16[6,32,256]{2,0,1:T(8,128)(2,1)S(1)} %copy.22), channel_id=1, source_target_pairs={{0,28},{4,0},{8,4},{12,8},{16,12},{20,16},{24,20},{28,24},{1,29},{... | collective-permute-start | bytes 294920 | tf_op jit(solution)/shard_map/ppermute | solution.py:20
  10.2 11.3 %collective-permute-start.2 = (bf16[10,8,256]{2,1,0:T(8,128)(2,1)S(1)}, bf16[10,8,256]{2,1,0:T(8,128)(2,1)S(1)}, u32[]{:S(2)}, u32[]{:S(2)}) collective-permute-start(bf16[10,8,256]{2,1,0:T(8,128)(2,1)S(1)} %pad.7), channel_id=1, source_target_pairs={{0,1},{1,2},{2,3},{3,0},{4,5},{5,6},{6,7},{7,4},{8,9},{9,10},{10,1... | collective-permute-start | bytes 122888 | tf_op jit(solution)/shard_map/ppermute | solution.py:20
  12.6 8.9 %collective-permute-start.3 = (bf16[10,8,256]{2,1,0:T(8,128)(2,1)S(1)}, bf16[10,8,256]{2,1,0:T(8,128)(2,1)S(1)}, u32[]{:S(2)}, u32[]{:S(2)}) collective-permute-start(bf16[10,8,256]{2,1,0:T(8,128)(2,1)S(1)} %pad.8), channel_id=1, source_target_pairs={{0,3},{1,0},{2,1},{3,2},{4,7},{5,4},{6,5},{7,6},{8,11},{9,8},{10,9... | collective-permute-start | bytes 122888 | tf_op jit(solution)/shard_map/ppermute | solution.py:20
  21.5 0.6 copy-start.9
  21.5 0.6 copy-start.10
  46.9 12.1 %collective-permute-start.6 = (f32[32,1024]{1,0:T(8,128)}, f32[32,1024]{1,0:T(8,128)S(1)}, u32[]{:S(2)}, u32[]{:S(2)}) collective-permute-start(f32[32,1024]{1,0:T(8,128)} %get-tuple-element.44), channel_id=1, source_target_pairs={{0,24},{4,28},{8,16},{12,20},{16,8},{20,12},{24,0},{28,4},{1,25},{... | collective-permute-start | bytes 393224 | tf_op jit(solution)/shard_map/ppermute | solution.py:25
  48.8 10.3 %collective-permute-start.5 = (f32[32,1024]{1,0:T(8,128)}, f32[32,1024]{1,0:T(8,128)S(1)}, u32[]{:S(2)}, u32[]{:S(2)}) collective-permute-start(f32[32,1024]{1,0:T(8,128)} %get-tuple-element.43), channel_id=1, source_target_pairs={{0,16},{4,20},{8,24},{12,28},{16,0},{20,4},{24,8},{28,12},{1,17},{... | collective-permute-start | bytes 393224 | tf_op jit(solution)/shard_map/ppermute | solution.py:25
  49.3 9.8 %collective-permute-start.4 = (f32[32,1024]{1,0:T(8,128)}, f32[32,1024]{1,0:T(8,128)S(1)}, u32[]{:S(2)}, u32[]{:S(2)}) collective-permute-start(f32[32,1024]{1,0:T(8,128)} %get-tuple-element.42), channel_id=1, source_target_pairs={{0,8},{4,12},{8,0},{12,4},{16,24},{20,28},{24,16},{28,20},{1,9},{5... | collective-permute-start | bytes 393224 | tf_op jit(solution)/shard_map/ppermute | solution.py:25
  50.5 8.5 %collective-permute-start.9 = (bf16[10,8,256]{2,1,0:T(8,128)(2,1)}, bf16[10,8,256]{2,1,0:T(8,128)(2,1)S(1)}, u32[]{:S(2)}, u32[]{:S(2)}) collective-permute-start(bf16[10,8,256]{2,1,0:T(8,128)(2,1)} %get-tuple-element.50), channel_id=1, source_target_pairs={{0,3},{1,0},{2,1},{3,2},{4,7},{5,4},{6,5},{7,6},{8,11},{9,8},{10,9... | collective-permute-start | bytes 122888 | tf_op jit(solution)/shard_map/ppermute | solution.py:20
  52.5 6.5 %collective-permute-start.8 = (bf16[10,8,256]{2,1,0:T(8,128)(2,1)}, bf16[10,8,256]{2,1,0:T(8,128)(2,1)S(1)}, u32[]{:S(2)}, u32[]{:S(2)}) collective-permute-start(bf16[10,8,256]{2,1,0:T(8,128)(2,1)} %get-tuple-element.49), channel_id=1, source_target_pairs={{0,1},{1,2},{2,3},{3,0},{4,5},{5,6},{6,7},{7,4},{8,9},{9,10},{10,1... | collective-permute-start | bytes 122888 | tf_op jit(solution)/shard_map/ppermute | solution.py:20
  52.5 6.6 %copy-start.1 = (f32[32,1024]{1,0:T(8,128)S(1)}, f32[32,1024]{1,0:T(8,128)}, u32[]{:S(2)}) copy-start(f32[32,1024]{1,0:T(8,128)} %get-tuple-element.41) | copy-start | bytes 393220
  59.0 8.6 %copy-start.7 = (bf16[10,8,256]{2,1,0:T(8,128)(2,1)}, bf16[10,8,256]{2,1,0:T(8,128)(2,1)S(1)}, u32[]{:S(2)}) copy-start(bf16[10,8,256]{2,1,0:T(8,128)(2,1)S(1)} %collective-permute-done.9.refs_9_) | copy-start | bytes 122884
  59.0 8.6 %copy-start.8 = (bf16[10,8,256]{2,1,0:T(8,128)(2,1)}, bf16[10,8,256]{2,1,0:T(8,128)(2,1)S(1)}, u32[]{:S(2)}) copy-start(bf16[10,8,256]{2,1,0:T(8,128)(2,1)S(1)} %collective-permute-done.8.refs_10_) | copy-start | bytes 122884
  59.2 3.3 %collective-permute-start.7 = (f32[16,1536]{1,0:T(8,128)S(1)}, f32[16,1536]{1,0:T(8,128)S(1)}, u32[]{:S(2)}, u32[]{:S(2)}) collective-permute-start(f32[16,1536]{1,0:T(8,128)S(1)} %pad_maximum_fusion), channel_id=1, source_target_pairs={{0,4},{4,0},{8,12},{12,8},{16,20},{20,16},{24,28},{28,24},{1,5},{5... | collective-permute-start | bytes 294920 | tf_op jit(solution)/shard_map/ppermute | solution.py:25
  60.4 6.6 %collective-permute-start.10 = (bf16[6,32,256]{2,1,0:T(8,128)(2,1)S(1)}, bf16[6,32,256]{2,1,0:T(8,128)(2,1)S(1)}, u32[]{:S(2)}, u32[]{:S(2)}) collective-permute-start(bf16[6,32,256]{2,1,0:T(8,128)(2,1)S(1)} %get-tuple-element.58), channel_id=1, source_target_pairs={{0,28},{4,0},{8,4},{12,8},{16,12},{20,16},{24,20},{28,24},{1,29},{... | collective-permute-start | bytes 294920 | tf_op jit(solution)/shard_map/ppermute | solution.py:20
  62.5 5.1 %collective-permute-start.11 = (bf16[6,32,256]{2,1,0:T(8,128)(2,1)S(1)}, bf16[6,32,256]{2,1,0:T(8,128)(2,1)S(1)}, u32[]{:S(2)}, u32[]{:S(2)}) collective-permute-start(bf16[6,32,256]{2,1,0:T(8,128)(2,1)S(1)} %get-tuple-element.57), channel_id=1, source_target_pairs={{0,4},{4,8},{8,12},{12,16},{16,20},{20,24},{24,28},{28,0},{1,5},{5... | collective-permute-start | bytes 294920 | tf_op jit(solution)/shard_map/ppermute | solution.py:20
  62.5 13.2 %copy-start = (f32[16,1536]{1,0:T(8,128)}, f32[16,1536]{1,0:T(8,128)S(1)}, u32[]{:S(2)}) copy-start(f32[16,1536]{1,0:T(8,128)S(1)} %fusion.2.refs_0_) | copy-start | bytes 294916
  62.5 13.2 %collective-permute-start.12 = (f32[16,1536]{1,0:T(8,128)S(1)}, f32[16,1536]{1,0:T(8,128)S(1)}, u32[]{:S(2)}, u32[]{:S(2)}) collective-permute-start(f32[16,1536]{1,0:T(8,128)S(1)} %fusion.2.refs_0_), channel_id=1, source_target_pairs={{0,1},{1,0},{2,3},{3,2},{4,5},{5,4},{6,7},{7,6},{8,9},{9,8},{10,11... | collective-permute-start | bytes 294920 | tf_op jit(solution)/shard_map/ppermute | solution.py:25
  62.6 13.1 %collective-permute-start.13 = (f32[16,1536]{1,0:T(8,128)S(1)}, f32[16,1536]{1,0:T(8,128)S(1)}, u32[]{:S(2)}, u32[]{:S(2)}) collective-permute-start(f32[16,1536]{1,0:T(8,128)S(1)} %fusion.2.refs_0_), channel_id=1, source_target_pairs={{0,2},{1,3},{2,0},{3,1},{4,6},{5,7},{6,4},{7,5},{8,10},{9,11},{10,... | collective-permute-start | bytes 294920 | tf_op jit(solution)/shard_map/ppermute | solution.py:25
  66.8 9.0 %collective-permute-start.14 = (f32[16,1536]{1,0:T(8,128)S(1)}, f32[16,1536]{1,0:T(8,128)S(1)}, u32[]{:S(2)}, u32[]{:S(2)}) collective-permute-start(f32[16,1536]{1,0:T(8,128)S(1)} %fusion.2.refs_0_), channel_id=1, source_target_pairs={{0,3},{1,2},{2,1},{3,0},{4,7},{5,6},{6,5},{7,4},{8,11},{9,10},{10,... | collective-permute-start | bytes 294920 | tf_op jit(solution)/shard_map/ppermute | solution.py:25
  67.0 0.6 copy-start.5
  67.6 0.6 copy-start.6
  75.7 0.6 copy-start.2
  75.7 0.6 copy-start.3
  76.4 0.6 copy-start.4

commit v8 on v7

--- a/solution.py
+++ b/solution.py
@@ -102,9 +102,33 @@
     return jnp.transpose(jnp.broadcast_to(ref[...], (lanes, count)))
 
 
-def planes_kernel(sizes, first_ref, last_ref, first_out, last_out):
-    first_out[...] = first_ref[:, 0]
-    last_out[...] = last_ref[:, 0]
+def fetched(pairs_of_refs, sems):
+    copies = [pltpu.make_async_copy(*refs, sems.at[i]) for i, refs in enumerate(pairs_of_refs)]
+    for copy in copies:
+        copy.start()
+    for copy in copies:
+        copy.wait()
+
+
+def rows_kernel(
+    sizes, low_ref, high_ref, far_below_ref, far_above_ref, first_out, last_out, below_ref, above_ref, sems
+):
+    channels, depth = sizes
+    fetched([(far_below_ref, below_ref), (far_above_ref, above_ref)], sems)
+    for ref, at, out in ((low_ref, 0, first_out), (high_ref, -1, last_out)):
+        for z in range(depth + 2):
+            rows = []
+            for ch in range(channels):
+                if z == 0:
+                    value = below_ref[ch]
+                elif z == depth + 1:
+                    value = above_ref[ch]
+                else:
+                    value = ref[ch, z - 1]
+                value = value.astype(f32)
+                rows.append(value[:1] if at == 0 else value[value.shape[0] - 1 :])
+            rows.append(jnp.zeros((8 - channels, rows[0].shape[1]), f32))
+            out[z] = jnp.concatenate(rows, axis=0).astype(bf16)
 
 
 def prepare_kernel(
@@ -159,8 +183,8 @@
 def forward_kernel(
     sizes,
     early_ref,
-    before_ref,
-    after_ref,
+    far_before_ref,
+    far_after_ref,
     target_ref,
     conv_ref,
     conv_t_ref,
@@ -194,6 +218,8 @@
     tap_ref,
     order_ref,
     sides_ref,
+    before_ref,
+    after_ref,
     split_sem,
     late_sem,
     ) = rest[groups:]
@@ -218,6 +244,12 @@
 
     @pl.when(step == 0)
     def _():
+        sides = [
+            pltpu.make_async_copy(far_before_ref, before_ref, late_sem.at[2]),
+            pltpu.make_async_copy(far_after_ref, after_ref, late_sem.at[3]),
+        ]
+        for copy in sides:
+            copy.start()
         for slot in range(pairs + 1):
             arrival(slot).start()
         for copy in late:
@@ -228,6 +260,8 @@
         sq_ref[...] = jnp.zeros_like(sq_ref)
         width = 2 * lanes
         rows = []
+        for copy in sides:
+            copy.wait()
         for slot in range(pairs + 1):
             sides = [ref[2 * slot + par].astype(f32) for par in range(2) for ref in (before_ref, after_ref)]
             rows.append(jnp.concatenate(sides, axis=0).astype(bf16))
@@ -393,8 +427,11 @@
     rest = refs[4:-1]
     spread_ref = refs[-1]
     if taken:
+        rest, spread_ref = refs[4:-6], refs[-6]
         taken_refs = rest[: len(taken)]
-        outer_ref, below_ref, above_ref, before_ref, after_ref, out_ref = rest[len(taken) :]
+        outer_ref, *far_refs, out_ref = rest[len(taken) :]
+        near_refs, sems = refs[-5:-1], refs[-1]
+        below_ref, above_ref, before_ref, after_ref = near_refs
     else:
         core_ref, *given_refs = rest
     group = 4 * channels
@@ -446,6 +483,7 @@
                     else:
                         spread_ref[slots.index(slot)] = jnp.zeros(spread_ref.shape[1:], f32)
             if k == 0 and taken:
+                fetched(list(zip(far_refs, near_refs, strict=True)), sems)
                 for ch in range(channels):
                     lay_out(1, ch, outer_ref[1, ch] + above_ref[ch].astype(f32))
                     lay_out(depth, ch, outer_ref[2, ch] + below_ref[ch].astype(f32))
@@ -463,11 +501,12 @@
 
 
 def last_kernel(sizes, *refs):
-    hidden, taps, big = sizes
-    conv_out, cbias_out, down_out, dbias_out, loss_out = refs[-5:]
-    total = refs[0][...]
-    for ref in refs[1:-5]:
-        total = total + ref[...]
+    hidden, taps, big, parts = sizes
+    conv_out, cbias_out, down_out, dbias_out, loss_out, here_ref, sems = refs[parts:]
+    fetched([(ref, here_ref.at[i]) for i, ref in enumerate(refs[:parts])], sems)
+    total = here_ref[0]
+    for i in range(1, parts):
+        total = total + here_ref[i]
     down_out[...] = total[:, :big]
     small = total[:, big:]
     while small.shape[0] < hidden:
@@ -480,7 +519,7 @@
     loss_out[...] = jnp.sum(turned[at + 3 : at + 4] + turned[at + 4 : at + 5], axis=1, keepdims=True)
 
 
-def call(kernel, sizes, out_shape, *args, grid=None, in_specs=None, out_specs=None, scratch=(), flops=0, name):
+def call(kernel, sizes, out_shape, *args, grid=None, in_specs=None, out_specs=None, scratch=(), flops=0, vmem=16, name):
     if grid is None:
         grid = (1,)
         in_specs = [whole(a.shape) for a in args]
@@ -491,7 +530,7 @@
         in_specs=in_specs,
         out_specs=out_specs,
         scratch_shapes=scratch,
-        compiler_params=pltpu.CompilerParams(vmem_limit_bytes=56 * 1024 * 1024),
+        compiler_params=pltpu.CompilerParams(vmem_limit_bytes=vmem * 1024 * 1024),
         cost_estimate=pl.CostEstimate(
             flops=flops,
             bytes_accessed=sum(a.size * a.dtype.itemsize for a in (*args, *out_shape)),
@@ -521,19 +560,26 @@
     return {name: jnp.asarray(value, bf16) for name, value in names.items()}
 
 
-def outer_planes(fields):
+def outer_rows(fields, below, above):
     channels, depth, row_count, col_count = fields.shape
-    out = jax.ShapeDtypeStruct((channels, row_count, col_count), fields.dtype)
-    block = (channels, 1, row_count, col_count)
+    out = jax.ShapeDtypeStruct((depth + 2, 8, col_count), fields.dtype)
+    block = (channels, depth, 16, col_count)
+    beside = pl.BlockSpec(memory_space=pl.ANY)
     return call(
-        planes_kernel,
-        (),
+        rows_kernel,
+        (channels, depth),
         [out, out],
-        fields, fields,
+        fields, fields, below, above,
         grid=(1,),
-        in_specs=[pl.BlockSpec(block, lambda z: (0, 0, 0, 0)), pl.BlockSpec(block, lambda z: (0, depth - 1, 0, 0))],
+        in_specs=[
+            pl.BlockSpec(block, lambda z: (0, 0, 0, 0)),
+            pl.BlockSpec(block, lambda z: (0, 0, row_count // 16 - 1, 0)),
+            beside,
+            beside,
+        ],
         out_specs=[whole(out.shape)] * 2,
-        name="planes",
+        scratch=[pltpu.VMEM(below.shape, bf16), pltpu.VMEM(above.shape, bf16), pltpu.SemaphoreType.DMA((2,))],
+        name="rows",
     )
 
 
@@ -573,6 +619,8 @@
     message = jax.ShapeDtypeStruct((rows, big + 2 * lanes * hidden // rows), f32)
     in_specs = [whole(a.shape) for a in args]
     for i in (0, 9, 10):
+        in_specs[i] = pl.BlockSpec(memory_space=pl.ANY)
+    for i in (1, 2):
         in_specs[i] = pl.BlockSpec(memory_space=pl.ANY)
     in_specs[3] = slab
     return call(
@@ -608,10 +656,13 @@
             pltpu.VMEM(fixed["tap"].shape, bf16),
             pltpu.VMEM(fixed["order"].shape, bf16),
             pltpu.VMEM((pairs + 1, 2, 16 * channels, lanes), f32),
+            pltpu.VMEM(before.shape, bf16),
+            pltpu.VMEM(after.shape, bf16),
             pltpu.SemaphoreType.DMA((pairs + 1,)),
-            pltpu.SemaphoreType.DMA((2,)),
+            pltpu.SemaphoreType.DMA((4,)),
         ],
         flops=4 * pairs * cells * big * (win + out_count),
+        vmem=40,
         name="forward",
     )
 
@@ -636,10 +687,14 @@
         *args,
         grid=(len(pairs),),
         in_specs=[pl.BlockSpec((1, big, cells), lambda z: (first + stride * z, 0, 0))]
-        + [whole(a.shape) for a in args[1:]],
+        + [whole(a.shape) for a in args[1 : len(args) - len(beside[1:])]]
+        + [pl.BlockSpec(memory_space=pl.ANY) for _ in beside[1:]],
         out_specs=[whole(o.shape) for o in outs],
-        scratch=[pltpu.VMEM((len(slots), *open_shape), f32)],
+        scratch=[pltpu.VMEM((len(slots), *open_shape), f32)]
+        + [pltpu.VMEM(a.shape, a.dtype) for a in beside[1:]]
+        + ([pltpu.SemaphoreType.DMA((len(beside) - 1,))] if beside else []),
         flops=2 * len(pairs) * cells * big * conv_t.shape[0],
+        vmem=32,
         name="spread",
     )
 
@@ -657,17 +712,11 @@
     cell_total = fields.size // channels // 8 * lax.axis_size("gz") * lax.axis_size("gy")
     fixed = constants(channels, row_count, col_count // 2, hidden)
 
-    first_plane, last_plane = outer_planes(fields)
-    below = shifted(last_plane, "gz", 1)
-    above = shifted(first_plane, "gz", -1)
-
-    def side(row):
-        rows = [below[:, row][:, None], fields[:, :, row], above[:, row][:, None]]
-        rows = jnp.concatenate(rows, axis=1).transpose(1, 0, 2)
-        return jnp.pad(rows, ((0, 0), (0, 8 - channels), (0, 0)))
-
-    before = shifted(side(row_count - 1), "gy", 1)
-    after = shifted(side(0), "gy", -1)
+    below = shifted(fields[:, depth - 1], "gz", 1)
+    above = shifted(fields[:, 0], "gz", -1)
+    first_rows, last_rows = outer_rows(fields, below, above)
+    before = shifted(last_rows, "gy", 1)
+    after = shifted(first_rows, "gy", -1)
     early, conv_big, conv_t, down_big, down_t = prepare(
         fields, below, above, conv_weight, conv_bias, down_weight, fixed
     )
@@ -709,7 +758,7 @@
     )
     conv, cbias, down, dbias, loss = call(
         last_kernel,
-        (hidden, taps, big),
+        (hidden, taps, big, 1 + len(got)),
         [
             jax.ShapeDtypeStruct((hidden, taps), f32),
             jax.ShapeDtypeStruct((1, hidden), f32),
@@ -718,6 +767,10 @@
             jax.ShapeDtypeStruct((1, 1), f32),
         ],
         packed, *got,
+        grid=(1,),
+        in_specs=[pl.BlockSpec(memory_space=pl.ANY)] * (1 + len(got)),
+        out_specs=[pl.BlockSpec(memory_space=pltpu.VMEM)] * 5,
+        scratch=[pltpu.VMEM((1 + len(got), *packed.shape), f32), pltpu.SemaphoreType.DMA((1 + len(got),))],
         name="last",
     )
     return out_field, sensitivity, conv, cbias[0], down, dbias[0], loss[0, 0]

time: 79.1 us -> 70 us (0.88)
  Pallas kernels: 47.6 us -> 36.5 us
  waiting for transfers between devices: 1.89 us -> 4.66 us
  other arithmetic: 1.22 us -> 0.17 us
    pallas_call x6, Pallas kernels: 47.6 us -> 36.5 us  [call(): pl.pallas_call(functools.partial(kernel, sizes), out_shape=out_shape, in_...]
    unnamed x22 -> x32, local copies, waits for them, and re-layouts: 2.52 us -> 6.23 us
    pallas_call x2 -> x0, local copies, waits for them, and re-layouts: 1.9 us -> none  [call(): pl.pallas_call(functools.partial(kernel, sizes), out_shape=out_shape, in_...]
    ppermute x7, waiting for transfers between devices: 0.02 us -> 1.67 us  [exchanged(): return lax.ppermute(value, axis, [(i, i ^ bit) for i in range(count)])]
    ppermute x2 -> x0, local copies, waits for them, and re-layouts: 1.32 us -> none  [shifted(): lax.ppermute(value, axis, [(i, (i + by) % count) for i in range(count)])]
    ppermute x8, waiting for transfers between devices: 1.87 us -> 2.99 us  [shifted(): lax.ppermute(value, axis, [(i, (i + by) % count) for i in range(count)])]
    slice x3 -> x0, local copies, waits for them, and re-layouts: 1.11 us -> none  [side(): rows = [below[:, row][:, None], fields[:, :, row], above[:, row][:, None]]]
    convert_element_type x1, other arithmetic: 1.13 us -> 0.1 us  [plane(): return (value + jnp.concatenate([low, gap, high], axis=1)).astype(bf16)]
  transfers between devices with their start and end apart: 15 -> 15, of which waited for: 2 -> 3; matrix products, arithmetic and copies ran while one was open for 6% -> 0% of each run, Pallas kernels for 25% -> 15%
where the time goes in v8:
time: 70 us; the launch traced here: 69.7 us
  Pallas kernels  36.5 us (52%)
  starting transfers between devices  19.9 us (28%)
  local copies, waits for them, and re-layouts  7.37 us (11%)
  waiting for transfers between devices  4.66 us (7%)
  between operations  1.12 us (2%)
    pallas_call x6, Pallas kernels, call(): pl.pallas_call(functools.partial(kernel, sizes), out_shape=out_shape, in_...  36.5 us
    ppermute x8, starting transfers between devices, shifted(): lax.ppermute(value, axis, [(i, (i + by) % count) for i in range(count)])  11.8 us
    ppermute x7, starting transfers between devices, exchanged(): return lax.ppermute(value, axis, [(i, i ^ bit) for i in range(count)])  8.11 us
    unnamed x32, local copies, waits for them, and re-layouts  6.23 us
    ppermute x8, waiting for transfers between devices, shifted(): lax.ppermute(value, axis, [(i, (i + by) % count) for i in range(count)])  2.99 us
    ppermute x7, waiting for transfers between devices, exchanged(): return lax.ppermute(value, axis, [(i, i ^ bit) for i in range(count)])  1.67 us
  transfers between devices with their start and end apart: 15, of which 3 were waited for; matrix products, arithmetic and copies ran while one was open for 0% of the time, Pallas kernels for 15%

profile of v8, /device:TPU:0, one launch (start us, length us, event | category | flops | bytes accessed | tf_op | source)
XLA Modules:
  0.0 69.7 jit_solution(10088677070162916770)
XLA Ops:
  0.6 0.0 copy-start.6
  0.6 0.0 copy-start.11
  0.7 1.0 %slice_bitcast_fusion = (bf16[6,32,256]{2,1,0:T(8,128)(2,1)S(1)}, bf16[6,32,256]{2,1,0:T(8,128)(2,1)S(1)}) fusion(bf16[6,8,32,256]{3,2,1,0:T(8,128)(2,1)} %high_ref.1), kind=kLoop, calls=%fused_computation.10 | loop fusion | bytes 393216 | tf_op jit(solution)/shard_map/squeeze | solution.py:716
  1.7 0.5 collective-permute-start
  2.2 2.9 %collective-permute-start.1 = (bf16[6,32,256]{2,1,0:T(8,128)(2,1)S(1)}, bf16[6,32,256]{2,1,0:T(8,128)(2,1)S(1)}, u32[]{:S(2)}, u32[]{:S(2)}) collective-permute-start(bf16[6,32,256]{2,1,0:T(8,128)(2,1)S(1)} %get-tuple-element.59), channel_id=1, source_target_pairs={{0,28},{4,0},{8,4},{12,8},{16,12},{20,16},{24,20},{28,24},{1,29},{... | collective-permute-start | bytes 294920 | tf_op jit(solution)/shard_map/ppermute | solution.py:20
  5.1 0.1 pad.4.clone
  5.2 2.2 %collective-permute-done.below_ref.far_below_ref = bf16[6,32,256]{2,1,0:T(8,128)(2,1)S(1)} collective-permute-done((bf16[6,32,256]{2,1,0:T(8,128)(2,1)S(1)}, bf16[6,32,256]{2,1,0:T(8,128)(2,1)S(1)}, u32[]{:S(2)}, u32[]{:S(2)}) %collective-permute-start) | collective-permute-done | bytes 98336 | tf_op jit(solution)/shard_map/ppermute | solution.py:20
  7.4 0.0 collective-permute-done.1.above_ref.far_above_ref
  7.4 1.1 %copy-done.1 = bf16[6,8,32,256]{3,2,1,0:T(8,128)(2,1)S(1)} copy-done((bf16[6,8,32,256]{3,2,1,0:T(8,128)(2,1)S(1)}, bf16[6,8,32,256]{3,2,1,0:T(8,128)(2,1)}, u32[]{:S(2)}) %copy-start.1) | copy-done | bytes 786456
  8.5 0.0 copy-start.15
  8.5 0.4 rows.1
  8.9 2.4 %collective-permute-start.2 = (bf16[10,8,256]{2,1,0:T(8,128)(2,1)S(1)}, bf16[10,8,256]{2,1,0:T(8,128)(2,1)S(1)}, u32[]{:S(2)}, u32[]{:S(2)}) collective-permute-start(bf16[10,8,256]{2,1,0:T(8,128)(2,1)S(1)} %get-tuple-element.33), channel_id=1, source_target_pairs={{0,1},{1,2},{2,3},{3,0},{4,5},{5,6},{6,7},{7,4},{8,9},{9,10},{10,1... | collective-permute-start | bytes 122888 | tf_op jit(solution)/shard_map/ppermute | solution.py:20
  11.3 2.1 %collective-permute-start.3 = (bf16[10,8,256]{2,1,0:T(8,128)(2,1)S(1)}, bf16[10,8,256]{2,1,0:T(8,128)(2,1)S(1)}, u32[]{:S(2)}, u32[]{:S(2)}) collective-permute-start(bf16[10,8,256]{2,1,0:T(8,128)(2,1)S(1)} %get-tuple-element.34), channel_id=1, source_target_pairs={{0,3},{1,0},{2,1},{3,2},{4,7},{5,4},{6,5},{7,6},{8,11},{9,8},{10,9... | collective-permute-start | bytes 122888 | tf_op jit(solution)/shard_map/ppermute | solution.py:20
  13.4 0.0 copy-start.8
  13.4 0.9 %copy-done.8 = bf16[256,256]{1,0:T(8,128)(2,1)S(1)} copy-done((bf16[256,256]{1,0:T(8,128)(2,1)S(1)}, bf16[256,256]{1,0:T(8,128)(2,1)}, u32[]{:S(2)}) %copy-start.8) | copy-done | bytes 131096
  14.3 0.8 %copy-done.10 = bf16[64,162]{1,0:T(8,128)(2,1)S(1)} copy-done((bf16[64,162]{1,0:T(8,128)(2,1)S(1)}, bf16[64,162]{1,0:T(8,128)(2,1)}, u32[]{:S(2)}) %copy-start.10) | copy-done | bytes 20760
  15.1 2.2 %prepare.1 = (bf16[5,96,2176]{2,1,0:T(8,128)(2,1)S(1)}, bf16[512,400]{1,0:T(8,128)(2,1)S(1)}, bf16[384,512]{1,0:T(8,128)(2,1)S(1)}, bf16[128,512]{1,0:T(8,128)(2,1)S(1)}, bf16[512,128]{1,0:T(8,128)(2,1)S(1)}) custom-call(bf16[6,8,32,256]{3,2,1,0:T(8,128)(2,1)S(1)} %copy-done.1, bf16[6,32,256]{2,1,0:T(8,128)(2,1)S(1)} %collective-permute-done.below_ref.far_below_ref, ...), custom_call_target="tpu_custom_call" | custom-call | flops 603979776 | bytes 6253056 | tf_op jit(solution)/shard_map/prepare/pallas_call | solution.py:527
  17.3 0.0 collective-permute-done.2.far_before_ref
  17.3 0.0 collective-permute-done.3.far_after_ref
  17.4 0.0 copy-start.2
  17.4 24.2 %forward.1 = (bf16[128,4,16,128]{3,2,1,0:T(8,128)(2,1)}, bf16[4,512,2048]{2,1,0:T(8,128)(2,1)}, bf16[10,8,256]{2,1,0:T(8,128)(2,1)S(1)}, bf16[10,8,256]{2,1,0:T(...) custom-call(bf16[5,96,2176]{2,1,0:T(8,128)(2,1)S(1)} %get-tuple-elem, ...), custom_call_target="tpu_custom_call" | custom-call | flops 8589934592 | bytes 18213376 | tf_op jit(solution)/shard_map/forward/pallas_call | solution.py:527
  41.6 1.8 %collective-permute-start.6 = (f32[32,1024]{1,0:T(8,128)S(1)}, f32[32,1024]{1,0:T(8,128)S(1)}, u32[]{:S(2)}, u32[]{:S(2)}) collective-permute-start(f32[32,1024]{1,0:T(8,128)S(1)} %get-tuple-element.44), channel_id=1, source_target_pairs={{0,24},{4,28},{8,16},{12,20},{16,8},{20,12},{24,0},{28,4},{1,25},{... | collective-permute-start | bytes 393224 | tf_op jit(solution)/shard_map/ppermute | solution.py:25
  43.4 0.6 collective-permute-start.5
  43.9 1.2 %collective-permute-start.4 = (f32[32,1024]{1,0:T(8,128)S(1)}, f32[32,1024]{1,0:T(8,128)S(1)}, u32[]{:S(2)}, u32[]{:S(2)}) collective-permute-start(f32[32,1024]{1,0:T(8,128)S(1)} %get-tuple-element.42), channel_id=1, source_target_pairs={{0,8},{4,12},{8,0},{12,4},{16,24},{20,28},{24,16},{28,20},{1,9},{5... | collective-permute-start | bytes 393224 | tf_op jit(solution)/shard_map/ppermute | solution.py:25
  45.2 2.2 %collective-permute-start.9 = (bf16[10,8,256]{2,1,0:T(8,128)(2,1)S(1)}, bf16[10,8,256]{2,1,0:T(8,128)(2,1)S(1)}, u32[]{:S(2)}, u32[]{:S(2)}) collective-permute-start(bf16[10,8,256]{2,1,0:T(8,128)(2,1)S(1)} %get-tuple-element.50), channel_id=1, source_target_pairs={{0,3},{1,0},{2,1},{3,2},{4,7},{5,4},{6,5},{7,6},{8,11},{9,8},{10,9... | collective-permute-start | bytes 122888 | tf_op jit(solution)/shard_map/ppermute | solution.py:20
  47.4 0.0 collective-permute-start.8
  47.4 3.4 %copy-done = bf16[4,512,2048]{2,1,0:T(8,128)(2,1)S(1)} copy-done((bf16[4,512,2048]{2,1,0:T(8,128)(2,1)S(1)}, bf16[4,512,2048]{2,1,0:T(8,128)(2,1)}, u32[]{:S(2)}) %copy-start) | copy-done | bytes 8388632
  50.8 3.1 %spread.2 = (f32[4,6,32,256]{3,2,1,0:T(8,128)S(1)}, f32[96,2176]{1,0:T(8,128)S(1)}, f32[96,2176]{1,0:T(8,128)S(1)}) custom-call(bf16[4,512,2048]{2,1,0:T(8,128)(2,1)S(1)} %copy-done, bf16[384,512]{1,0:T(8,128)(2,1)S(1)} %get-tuple-element.36.conv_t_ref.refs_1_, bf16[256,256]{1,0:T(8,128)(2,1)S(1)} %copy-done.4, bf16[384,408]{1,0:T(8,128)(2,1)S(1)} %copy-done.2), custom_call_target="tpu_custom_call" | custom-call | flops 1610612736 | bytes 11683840 | tf_op jit(solution)/shard_map/spread/pallas_call | solution.py:527
  53.9 0.0 collective-permute-done.9.refs_9_
  54.0 0.0 collective-permute-done.8.refs_10_
  54.0 0.0 collective-permute-done.6
  54.0 0.0 collective-permute-done.5
  54.1 0.0 collective-permute-done.4
  54.2 0.1 collective-permute-start.7
  54.2 0.1 fusion.1
  54.3 1.6 %collective-permute-start.10 = (bf16[6,32,256]{2,1,0:T(8,128)(2,1)S(1)}, bf16[6,32,256]{2,1,0:T(8,128)(2,1)S(1)}, u32[]{:S(2)}, u32[]{:S(2)}) collective-permute-start(bf16[6,32,256]{2,1,0:T(8,128)(2,1)S(1)} %get-tuple-element.58), channel_id=1, source_target_pairs={{0,28},{4,0},{8,4},{12,8},{16,12},{20,16},{24,20},{28,24},{1,29},{... | collective-permute-start | bytes 294920 | tf_op jit(solution)/shard_map/ppermute | solution.py:20
  56.0 0.0 collective-permute-start.11
  56.0 0.0 collective-permute-done.7
  56.0 0.1 collective-permute-start.12
  56.1 4.4 %collective-permute-start.13 = (f32[16,1536]{1,0:T(8,128)S(1)}, f32[16,1536]{1,0:T(8,128)S(1)}, u32[]{:S(2)}, u32[]{:S(2)}) collective-permute-start(f32[16,1536]{1,0:T(8,128)S(1)} %fusion.2.refs_0_), channel_id=1, source_target_pairs={{0,2},{1,3},{2,0},{3,1},{4,6},{5,7},{6,4},{7,5},{8,10},{9,11},{10,... | collective-permute-start | bytes 294920 | tf_op jit(solution)/shard_map/ppermute | solution.py:25
  60.5 0.0 collective-permute-start.14
  60.5 0.0 collective-permute-done.10.refs_7_
  60.5 0.8 %collective-permute-done.11.refs_8_ = bf16[6,32,256]{2,1,0:T(8,128)(2,1)S(1)} collective-permute-done((bf16[6,32,256]{2,1,0:T(8,128)(2,1)S(1)}, bf16[6,32,256]{2,1,0:T(8,128)(2,1)S(1)}, u32[]{:S(2)}, u32[]{:S(2)}) %collective-permute-start.11) | collective-permute-done | bytes 98336 | tf_op jit(solution)/shard_map/ppermute | solution.py:20
  61.3 5.3 %spread.3 = f32[6,8,32,256]{3,2,1,0:T(8,128)} custom-call(bf16[4,512,2048]{2,1,0:T(8,128)(2,1)S(1)} %copy-done, bf16[384,512]{1,0:T(8,128)(2,1)S(1)} %get-tuple-element.36.conv_t_ref.refs_1_, bf16[256,256]{1,0:T(8,128)(2,1)S(1)} %copy-done.4, bf16[384,408]{1,0:T(8,128)(2,1)S(1)} %copy-done.2, f32[96,2176]{1,0:T(8,128)S(1)} %get-tuple-element.46.refs_4_, ...), custom_call_target="tpu_custom_call" | custom-call | flops 1610612736 | bytes 13535232 | tf_op jit(solution)/shard_map/spread/pallas_call | solution.py:527
  66.6 0.0 collective-permute-done.12.refs_1_
  66.7 1.7 %collective-permute-done.13.refs_2_ = f32[16,1536]{1,0:T(8,128)S(1)} collective-permute-done((f32[16,1536]{1,0:T(8,128)S(1)}, f32[16,1536]{1,0:T(8,128)S(1)}, u32[]{:S(2)}, u32[]{:S(2)}) %collective-permute-start.13) | collective-permute-done | bytes 98336 | tf_op jit(solution)/shard_map/ppermute | solution.py:25
  68.3 0.0 collective-permute-done.14.refs_3_
  68.3 1.3 %last.1 = (f32[64,162]{1,0:T(8,128)}, f32[1,64]{1,0:T(1,128)}, f32[16,512]{1,0:T(8,128)}, f32[1,128]{1,0:T(1,128)}, f32[1,1]{1,0:T(1,128)}) custom-call(f32[16,1536]{1,0:T(8,128)S(1)} %fusion.2.refs_0_, f32[16,1536]{1,0:T(8,128)S(1)} %collective-permute-done.12.refs_1_, f32[16,1536]{1,0:T(8,128)S(1)} %collective-permute-done.13.refs_2_, ...), custom_call_target="tpu_custom_call" | custom-call | bytes 468228 | tf_op jit(solution)/shard_map/last/pallas_call | solution.py:527
  (35 shorter events, 0.2 us)
Async XLA Ops:
  0.6 12.8 %copy-start.6 = (bf16[408,384]{1,0:T(8,128)(2,1)S(1)}, bf16[408,384]{1,0:T(8,128)(2,1)}, u32[]{:S(2)}) copy-start(bf16[408,384]{1,0:T(8,128)(2,1)} %constant.45.clone.row_ref) | copy-start | bytes 940036
  0.6 12.8 %copy-start.11 = (f32[64]{0:T(128)S(1)}, f32[64]{0:T(128)}, u32[]{:S(2)}) copy-start(f32[64]{0:T(128)} %param.17) | copy-start | bytes 772
  0.7 12.8 %copy-start.7 = (bf16[128,512]{1,0:T(8,128)(2,1)S(1)}, bf16[128,512]{1,0:T(8,128)(2,1)}, u32[]{:S(2)}) copy-start(bf16[128,512]{1,0:T(8,128)(2,1)} %down_weight_ref.1) | copy-start | bytes 393220
  1.7 5.7 %collective-permute-start = (bf16[6,32,256]{2,1,0:T(8,128)(2,1)S(1)}, bf16[6,32,256]{2,1,0:T(8,128)(2,1)S(1)}, u32[]{:S(2)}, u32[]{:S(2)}) collective-permute-start(bf16[6,32,256]{2,1,0:T(8,128)(2,1)S(1)} %get-tuple-element.60), channel_id=1, source_target_pairs={{0,4},{4,8},{8,12},{12,16},{16,20},{20,24},{24,28},{28,0},{1,5},{5... | collective-permute-start | bytes 294920 | tf_op jit(solution)/shard_map/ppermute | solution.py:20
  2.2 5.2 %collective-permute-start.1 = (bf16[6,32,256]{2,1,0:T(8,128)(2,1)S(1)}, bf16[6,32,256]{2,1,0:T(8,128)(2,1)S(1)}, u32[]{:S(2)}, u32[]{:S(2)}) collective-permute-start(bf16[6,32,256]{2,1,0:T(8,128)(2,1)S(1)} %get-tuple-element.59), channel_id=1, source_target_pairs={{0,28},{4,0},{8,4},{12,8},{16,12},{20,16},{24,20},{28,24},{1,29},{... | collective-permute-start | bytes 294920 | tf_op jit(solution)/shard_map/ppermute | solution.py:20
  5.1 12.2 %copy-start.13 = (f32[128]{0:T(128)S(1)}, f32[128]{0:T(128)}, u32[]{:S(2)}) copy-start(f32[128]{0:T(128)} %param.19) | copy-start | bytes 1540
  7.4 1.1 %copy-start.1 = (bf16[6,8,32,256]{3,2,1,0:T(8,128)(2,1)S(1)}, bf16[6,8,32,256]{3,2,1,0:T(8,128)(2,1)}, u32[]{:S(2)}) copy-start(bf16[6,8,32,256]{3,2,1,0:T(8,128)(2,1)} %high_ref.1) | copy-start | bytes 2359300
  8.5 4.9 %copy-start.3 = (bf16[8,162,384]{2,1,0:T(8,128)(2,1)S(1)}, bf16[8,162,384]{2,1,0:T(8,128)(2,1)}, u32[]{:S(2)}) copy-start(bf16[8,162,384]{2,1,0:T(8,128)(2,1)} %constant.49.clone.tap_ref.far_tap_ref) | copy-start | bytes 2985988
  8.5 4.9 %copy-start.5 = (bf16[512,512]{1,0:T(8,128)(2,1)S(1)}, bf16[512,512]{1,0:T(8,128)(2,1)}, u32[]{:S(2)}) copy-start(bf16[512,512]{1,0:T(8,128)(2,1)} %constant.50.clone.order_ref.far_order_ref) | copy-start | bytes 1572868
  8.5 8.8 %copy-start.4 = (bf16[256,256]{1,0:T(8,128)(2,1)S(1)}, bf16[256,256]{1,0:T(8,128)(2,1)}, u32[]{:S(2)}) copy-start(bf16[256,256]{1,0:T(8,128)(2,1)} %constant.44.clone.merge_ref.refs_2_) | copy-start | bytes 393220
  8.5 8.9 %copy-start.14 = (bf16[48,32]{1,0:T(8,128)(2,1)S(1)}, bf16[48,32]{1,0:T(8,128)(2,1)}, u32[]{:S(2)}) copy-start(bf16[48,32]{1,0:T(8,128)(2,1)} %constant.47.clone.edge_ref) | copy-start | bytes 9220
  8.5 8.9 %copy-start.15 = (bf16[32,48]{1,0:T(8,128)(2,1)S(1)}, bf16[32,48]{1,0:T(8,128)(2,1)}, u32[]{:S(2)}) copy-start(bf16[32,48]{1,0:T(8,128)(2,1)} %constant.48.clone.edge_t_ref) | copy-start | bytes 9220
  8.9 8.4 %collective-permute-start.2 = (bf16[10,8,256]{2,1,0:T(8,128)(2,1)S(1)}, bf16[10,8,256]{2,1,0:T(8,128)(2,1)S(1)}, u32[]{:S(2)}, u32[]{:S(2)}) collective-permute-start(bf16[10,8,256]{2,1,0:T(8,128)(2,1)S(1)} %get-tuple-element.33), channel_id=1, source_target_pairs={{0,1},{1,2},{2,3},{3,0},{4,5},{5,6},{6,7},{7,4},{8,9},{9,10},{10,1... | collective-permute-start | bytes 122888 | tf_op jit(solution)/shard_map/ppermute | solution.py:20
  11.3 6.0 %collective-permute-start.3 = (bf16[10,8,256]{2,1,0:T(8,128)(2,1)S(1)}, bf16[10,8,256]{2,1,0:T(8,128)(2,1)S(1)}, u32[]{:S(2)}, u32[]{:S(2)}) collective-permute-start(bf16[10,8,256]{2,1,0:T(8,128)(2,1)S(1)} %get-tuple-element.34), channel_id=1, source_target_pairs={{0,3},{1,0},{2,1},{3,2},{4,7},{5,4},{6,5},{7,6},{8,11},{9,8},{10,9... | collective-permute-start | bytes 122888 | tf_op jit(solution)/shard_map/ppermute | solution.py:20
  13.4 0.9 %copy-start.8 = (bf16[256,256]{1,0:T(8,128)(2,1)S(1)}, bf16[256,256]{1,0:T(8,128)(2,1)}, u32[]{:S(2)}) copy-start(bf16[256,256]{1,0:T(8,128)(2,1)} %constant.43.clone.col_ref) | copy-start | bytes 393220
  14.3 0.8 %copy-start.10 = (bf16[64,162]{1,0:T(8,128)(2,1)S(1)}, bf16[64,162]{1,0:T(8,128)(2,1)}, u32[]{:S(2)}) copy-start(bf16[64,162]{1,0:T(8,128)(2,1)} %conv_weight_ref.1) | copy-start | bytes 62212
  15.1 2.3 %copy-start.9 = (bf16[256,256]{1,0:T(8,128)(2,1)S(1)}, bf16[256,256]{1,0:T(8,128)(2,1)}, u32[]{:S(2)}) copy-start(bf16[256,256]{1,0:T(8,128)(2,1)} %constant.43.clone.col_ref) | copy-start | bytes 393220
  15.1 2.3 %copy-start.12 = (bf16[128,4,16,128]{3,2,1,0:T(8,128)(2,1)S(1)}, bf16[128,4,16,128]{3,2,1,0:T(8,128)(2,1)}, u32[]{:S(2)}) copy-start(bf16[128,4,16,128]{3,2,1,0:T(8,128)(2,1)} %target_ref.1) | copy-start | bytes 6291460
  17.4 30.0 %copy-start.2 = (bf16[384,408]{1,0:T(8,128)(2,1)S(1)}, bf16[384,408]{1,0:T(8,128)(2,1)}, u32[]{:S(2)}) copy-start(bf16[384,408]{1,0:T(8,128)(2,1)} %constant.46.clone.refs_3_) | copy-start | bytes 940036
  41.6 12.4 %collective-permute-start.6 = (f32[32,1024]{1,0:T(8,128)S(1)}, f32[32,1024]{1,0:T(8,128)S(1)}, u32[]{:S(2)}, u32[]{:S(2)}) collective-permute-start(f32[32,1024]{1,0:T(8,128)S(1)} %get-tuple-element.44), channel_id=1, source_target_pairs={{0,24},{4,28},{8,16},{12,20},{16,8},{20,12},{24,0},{28,4},{1,25},{... | collective-permute-start | bytes 393224 | tf_op jit(solution)/shard_map/ppermute | solution.py:25
  43.4 10.7 %collective-permute-start.5 = (f32[32,1024]{1,0:T(8,128)S(1)}, f32[32,1024]{1,0:T(8,128)S(1)}, u32[]{:S(2)}, u32[]{:S(2)}) collective-permute-start(f32[32,1024]{1,0:T(8,128)S(1)} %get-tuple-element.43), channel_id=1, source_target_pairs={{0,16},{4,20},{8,24},{12,28},{16,0},{20,4},{24,8},{28,12},{1,17},{... | collective-permute-start | bytes 393224 | tf_op jit(solution)/shard_map/ppermute | solution.py:25
  43.9 10.1 %collective-permute-start.4 = (f32[32,1024]{1,0:T(8,128)S(1)}, f32[32,1024]{1,0:T(8,128)S(1)}, u32[]{:S(2)}, u32[]{:S(2)}) collective-permute-start(f32[32,1024]{1,0:T(8,128)S(1)} %get-tuple-element.42), channel_id=1, source_target_pairs={{0,8},{4,12},{8,0},{12,4},{16,24},{20,28},{24,16},{28,20},{1,9},{5... | collective-permute-start | bytes 393224 | tf_op jit(solution)/shard_map/ppermute | solution.py:25
  45.2 8.7 %collective-permute-start.9 = (bf16[10,8,256]{2,1,0:T(8,128)(2,1)S(1)}, bf16[10,8,256]{2,1,0:T(8,128)(2,1)S(1)}, u32[]{:S(2)}, u32[]{:S(2)}) collective-permute-start(bf16[10,8,256]{2,1,0:T(8,128)(2,1)S(1)} %get-tuple-element.50), channel_id=1, source_target_pairs={{0,3},{1,0},{2,1},{3,2},{4,7},{5,4},{6,5},{7,6},{8,11},{9,8},{10,9... | collective-permute-start | bytes 122888 | tf_op jit(solution)/shard_map/ppermute | solution.py:20
  47.4 6.6 %collective-permute-start.8 = (bf16[10,8,256]{2,1,0:T(8,128)(2,1)S(1)}, bf16[10,8,256]{2,1,0:T(8,128)(2,1)S(1)}, u32[]{:S(2)}, u32[]{:S(2)}) collective-permute-start(bf16[10,8,256]{2,1,0:T(8,128)(2,1)S(1)} %get-tuple-element.49), channel_id=1, source_target_pairs={{0,1},{1,2},{2,3},{3,0},{4,5},{5,6},{6,7},{7,4},{8,9},{9,10},{10,1... | collective-permute-start | bytes 122888 | tf_op jit(solution)/shard_map/ppermute | solution.py:20
  47.4 3.4 %copy-start = (bf16[4,512,2048]{2,1,0:T(8,128)(2,1)S(1)}, bf16[4,512,2048]{2,1,0:T(8,128)(2,1)}, u32[]{:S(2)}) copy-start(bf16[4,512,2048]{2,1,0:T(8,128)(2,1)} %get-tuple-element.40.refs_0_) | copy-start | bytes 25165828
  54.2 1.8 %collective-permute-start.7 = (f32[16,1536]{1,0:T(8,128)S(1)}, f32[16,1536]{1,0:T(8,128)S(1)}, u32[]{:S(2)}, u32[]{:S(2)}) collective-permute-start(f32[16,1536]{1,0:T(8,128)S(1)} %pad_maximum_fusion), channel_id=1, source_target_pairs={{0,4},{4,0},{8,12},{12,8},{16,20},{20,16},{24,28},{28,24},{1,5},{5... | collective-permute-start | bytes 294920 | tf_op jit(solution)/shard_map/ppermute | solution.py:25
  54.3 6.1 %collective-permute-start.10 = (bf16[6,32,256]{2,1,0:T(8,128)(2,1)S(1)}, bf16[6,32,256]{2,1,0:T(8,128)(2,1)S(1)}, u32[]{:S(2)}, u32[]{:S(2)}) collective-permute-start(bf16[6,32,256]{2,1,0:T(8,128)(2,1)S(1)} %get-tuple-element.58), channel_id=1, source_target_pairs={{0,28},{4,0},{8,4},{12,8},{16,12},{20,16},{24,20},{28,24},{1,29},{... | collective-permute-start | bytes 294920 | tf_op jit(solution)/shard_map/ppermute | solution.py:20
  56.0 5.3 %collective-permute-start.11 = (bf16[6,32,256]{2,1,0:T(8,128)(2,1)S(1)}, bf16[6,32,256]{2,1,0:T(8,128)(2,1)S(1)}, u32[]{:S(2)}, u32[]{:S(2)}) collective-permute-start(bf16[6,32,256]{2,1,0:T(8,128)(2,1)S(1)} %get-tuple-element.57), channel_id=1, source_target_pairs={{0,4},{4,8},{8,12},{12,16},{16,20},{20,24},{24,28},{28,0},{1,5},{5... | collective-permute-start | bytes 294920 | tf_op jit(solution)/shard_map/ppermute | solution.py:20
  56.0 10.6 %collective-permute-start.12 = (f32[16,1536]{1,0:T(8,128)S(1)}, f32[16,1536]{1,0:T(8,128)S(1)}, u32[]{:S(2)}, u32[]{:S(2)}) collective-permute-start(f32[16,1536]{1,0:T(8,128)S(1)} %fusion.2.refs_0_), channel_id=1, source_target_pairs={{0,1},{1,0},{2,3},{3,2},{4,5},{5,4},{6,7},{7,6},{8,9},{9,8},{10,11... | collective-permute-start | bytes 294920 | tf_op jit(solution)/shard_map/ppermute | solution.py:25
  56.1 12.2 %collective-permute-start.13 = (f32[16,1536]{1,0:T(8,128)S(1)}, f32[16,1536]{1,0:T(8,128)S(1)}, u32[]{:S(2)}, u32[]{:S(2)}) collective-permute-start(f32[16,1536]{1,0:T(8,128)S(1)} %fusion.2.refs_0_), channel_id=1, source_target_pairs={{0,2},{1,3},{2,0},{3,1},{4,6},{5,7},{6,4},{7,5},{8,10},{9,11},{10,... | collective-permute-start | bytes 294920 | tf_op jit(solution)/shard_map/ppermute | solution.py:25
  60.5 7.8 %collective-permute-start.14 = (f32[16,1536]{1,0:T(8,128)S(1)}, f32[16,1536]{1,0:T(8,128)S(1)}, u32[]{:S(2)}, u32[]{:S(2)}) collective-permute-start(f32[16,1536]{1,0:T(8,128)S(1)} %fusion.2.refs_0_), channel_id=1, source_target_pairs={{0,3},{1,2},{2,1},{3,0},{4,7},{5,6},{6,5},{7,4},{8,11},{9,10},{10,... | collective-permute-start | bytes 294920 | tf_op jit(solution)/shard_map/ppermute | solution.py:25

commit v9 on v8

--- a/solution.py
+++ b/solution.py
@@ -662,7 +662,7 @@
             pltpu.SemaphoreType.DMA((4,)),
         ],
         flops=4 * pairs * cells * big * (win + out_count),
-        vmem=40,
+        vmem=36,
         name="forward",
     )
 
@@ -694,7 +694,7 @@
         + [pltpu.VMEM(a.shape, a.dtype) for a in beside[1:]]
         + ([pltpu.SemaphoreType.DMA((len(beside) - 1,))] if beside else []),
         flops=2 * len(pairs) * cells * big * conv_t.shape[0],
-        vmem=32,
+        vmem=20,
         name="spread",
     )
 

time: 70 us -> 67.2 us (0.960)
  local copies, waits for them, and re-layouts: 7.37 us -> 3.99 us
  waiting for transfers between devices: 4.66 us -> 5.98 us
  Pallas kernels: 36.5 us -> 35.8 us
    unnamed x32 -> x30, local copies, waits for them, and re-layouts: 6.23 us -> 2.85 us
    ppermute x8, waiting for transfers between devices: 2.99 us -> 5.5 us  [shifted(): lax.ppermute(value, axis, [(i, (i + by) % count) for i in range(count)])]
    ppermute x7, waiting for transfers between devices: 1.67 us -> 0.48 us  [exchanged(): return lax.ppermute(value, axis, [(i, i ^ bit) for i in range(count)])]
  transfers between devices with their start and end apart: 15 -> 15, of which waited for: 3 -> 4; matrix products, arithmetic and copies ran while one was open for 0% -> 0% of each run, Pallas kernels for 15% -> 16%
where the time goes in v9:
time: 67.2 us; the launch traced here: 66.9 us
  Pallas kernels  35.8 us (53%)
  starting transfers between devices  19.9 us (30%)
  waiting for transfers between devices  5.98 us (9%)
  local copies, waits for them, and re-layouts  3.99 us (6%)
  between operations  1.11 us (2%)
    pallas_call x6, Pallas kernels, call(): pl.pallas_call(functools.partial(kernel, sizes), out_shape=out_shape, in_...  35.8 us
    ppermute x8, starting transfers between devices, shifted(): lax.ppermute(value, axis, [(i, (i + by) % count) for i in range(count)])  11.8 us
    ppermute x7, starting transfers between devices, exchanged(): return lax.ppermute(value, axis, [(i, i ^ bit) for i in range(count)])  8.08 us
    ppermute x8, waiting for transfers between devices, shifted(): lax.ppermute(value, axis, [(i, (i + by) % count) for i in range(count)])  5.5 us
    unnamed x30, local copies, waits for them, and re-layouts  2.85 us
  transfers between devices with their start and end apart: 15, of which 4 were waited for; matrix products, arithmetic and copies ran while one was open for 0% of the time, Pallas kernels for 16%

profile of v9, /device:TPU:0, one launch (start us, length us, event | category | flops | bytes accessed | tf_op | source)
XLA Modules:
  0.0 66.9 jit_solution(3588321517941286229)
XLA Ops:
  0.6 0.0 copy-start.5
  0.7 1.0 %slice_bitcast_fusion = (bf16[6,32,256]{2,1,0:T(8,128)(2,1)S(1)}, bf16[6,32,256]{2,1,0:T(8,128)(2,1)S(1)}) fusion(bf16[6,8,32,256]{3,2,1,0:T(8,128)(2,1)} %high_ref.1), kind=kLoop, calls=%fused_computation.10 | loop fusion | bytes 393216 | tf_op jit(solution)/shard_map/squeeze | solution.py:716
  1.7 0.5 collective-permute-start
  2.2 2.9 %collective-permute-start.1 = (bf16[6,32,256]{2,1,0:T(8,128)(2,1)S(1)}, bf16[6,32,256]{2,1,0:T(8,128)(2,1)S(1)}, u32[]{:S(2)}, u32[]{:S(2)}) collective-permute-start(bf16[6,32,256]{2,1,0:T(8,128)(2,1)S(1)} %get-tuple-element.59), channel_id=1, source_target_pairs={{0,28},{4,0},{8,4},{12,8},{16,12},{20,16},{24,20},{28,24},{1,29},{... | collective-permute-start | bytes 294920 | tf_op jit(solution)/shard_map/ppermute | solution.py:20
  5.1 0.1 pad.4.clone
  5.2 2.2 %collective-permute-done.below_ref.far_below_ref = bf16[6,32,256]{2,1,0:T(8,128)(2,1)S(1)} collective-permute-done((bf16[6,32,256]{2,1,0:T(8,128)(2,1)S(1)}, bf16[6,32,256]{2,1,0:T(8,128)(2,1)S(1)}, u32[]{:S(2)}, u32[]{:S(2)}) %collective-permute-start) | collective-permute-done | bytes 98336 | tf_op jit(solution)/shard_map/ppermute | solution.py:20
  7.4 0.0 collective-permute-done.1.above_ref.far_above_ref
  7.4 1.1 %copy-done = bf16[6,8,32,256]{3,2,1,0:T(8,128)(2,1)S(1)} copy-done((bf16[6,8,32,256]{3,2,1,0:T(8,128)(2,1)S(1)}, bf16[6,8,32,256]{3,2,1,0:T(8,128)(2,1)}, u32[]{:S(2)}) %copy-start) | copy-done | bytes 786456
  8.5 0.0 copy-start.14
  8.5 0.4 rows.1
  8.9 2.4 %collective-permute-start.2 = (bf16[10,8,256]{2,1,0:T(8,128)(2,1)S(1)}, bf16[10,8,256]{2,1,0:T(8,128)(2,1)S(1)}, u32[]{:S(2)}, u32[]{:S(2)}) collective-permute-start(bf16[10,8,256]{2,1,0:T(8,128)(2,1)S(1)} %get-tuple-element.33), channel_id=1, source_target_pairs={{0,1},{1,2},{2,3},{3,0},{4,5},{5,6},{6,7},{7,4},{8,9},{9,10},{10,1... | collective-permute-start | bytes 122888 | tf_op jit(solution)/shard_map/ppermute | solution.py:20
  11.3 2.1 %collective-permute-start.3 = (bf16[10,8,256]{2,1,0:T(8,128)(2,1)S(1)}, bf16[10,8,256]{2,1,0:T(8,128)(2,1)S(1)}, u32[]{:S(2)}, u32[]{:S(2)}) collective-permute-start(bf16[10,8,256]{2,1,0:T(8,128)(2,1)S(1)} %get-tuple-element.34), channel_id=1, source_target_pairs={{0,3},{1,0},{2,1},{3,2},{4,7},{5,4},{6,5},{7,6},{8,11},{9,8},{10,9... | collective-permute-start | bytes 122888 | tf_op jit(solution)/shard_map/ppermute | solution.py:20
  13.4 0.0 copy-done.10
  13.4 0.0 copy-done.2
  13.4 0.0 copy-start.7
  13.4 0.9 %copy-done.7 = bf16[256,256]{1,0:T(8,128)(2,1)S(1)} copy-done((bf16[256,256]{1,0:T(8,128)(2,1)S(1)}, bf16[256,256]{1,0:T(8,128)(2,1)}, u32[]{:S(2)}) %copy-start.7) | copy-done | bytes 131096
  14.3 0.8 %copy-done.9 = bf16[64,162]{1,0:T(8,128)(2,1)S(1)} copy-done((bf16[64,162]{1,0:T(8,128)(2,1)S(1)}, bf16[64,162]{1,0:T(8,128)(2,1)}, u32[]{:S(2)}) %copy-start.9) | copy-done | bytes 20760
  15.1 2.2 %prepare.1 = (bf16[5,96,2176]{2,1,0:T(8,128)(2,1)S(1)}, bf16[512,400]{1,0:T(8,128)(2,1)S(1)}, bf16[384,512]{1,0:T(8,128)(2,1)S(1)}, bf16[128,512]{1,0:T(8,128)(2,1)S(1)}, bf16[512,128]{1,0:T(8,128)(2,1)S(1)}) custom-call(bf16[6,8,32,256]{3,2,1,0:T(8,128)(2,1)S(1)} %copy-done, bf16[6,32,256]{2,1,0:T(8,128)(2,1)S(1)} %collective-permute-done.below_ref.far_below_ref, ...), custom_call_target="tpu_custom_call" | custom-call | flops 603979776 | bytes 6253056 | tf_op jit(solution)/shard_map/prepare/pallas_call | solution.py:527
  17.3 0.0 collective-permute-done.2.far_before_ref
  17.3 0.0 collective-permute-done.3.far_after_ref
  17.4 0.0 copy-start.1
  17.4 23.5 %forward.1 = (bf16[128,4,16,128]{3,2,1,0:T(8,128)(2,1)}, bf16[4,512,2048]{2,1,0:T(8,128)(2,1)S(1)}, bf16[10,8,256]{2,1,0:T(8,128)(2,1)S(1)}, bf16[10,8,256]{2,1,...) custom-call(bf16[5,96,2176]{2,1,0:T(8,128)(2,1)S(1)} %get-tuple-elem, ...), custom_call_target="tpu_custom_call" | custom-call | flops 8589934592 | bytes 18213376 | tf_op jit(solution)/shard_map/forward/pallas_call | solution.py:527
  40.9 1.8 %collective-permute-start.6 = (f32[32,1024]{1,0:T(8,128)S(1)}, f32[32,1024]{1,0:T(8,128)S(1)}, u32[]{:S(2)}, u32[]{:S(2)}) collective-permute-start(f32[32,1024]{1,0:T(8,128)S(1)} %get-tuple-element.44), channel_id=1, source_target_pairs={{0,24},{4,28},{8,16},{12,20},{16,8},{20,12},{24,0},{28,4},{1,25},{... | collective-permute-start | bytes 393224 | tf_op jit(solution)/shard_map/ppermute | solution.py:25
  42.7 0.6 collective-permute-start.5
  43.3 1.2 %collective-permute-start.4 = (f32[32,1024]{1,0:T(8,128)S(1)}, f32[32,1024]{1,0:T(8,128)S(1)}, u32[]{:S(2)}, u32[]{:S(2)}) collective-permute-start(f32[32,1024]{1,0:T(8,128)S(1)} %get-tuple-element.42), channel_id=1, source_target_pairs={{0,8},{4,12},{8,0},{12,4},{16,24},{20,28},{24,16},{28,20},{1,9},{5... | collective-permute-start | bytes 393224 | tf_op jit(solution)/shard_map/ppermute | solution.py:25
  44.5 2.2 %collective-permute-start.9 = (bf16[10,8,256]{2,1,0:T(8,128)(2,1)S(1)}, bf16[10,8,256]{2,1,0:T(8,128)(2,1)S(1)}, u32[]{:S(2)}, u32[]{:S(2)}) collective-permute-start(bf16[10,8,256]{2,1,0:T(8,128)(2,1)S(1)} %get-tuple-element.50), channel_id=1, source_target_pairs={{0,3},{1,0},{2,1},{3,2},{4,7},{5,4},{6,5},{7,6},{8,11},{9,8},{10,9... | collective-permute-start | bytes 122888 | tf_op jit(solution)/shard_map/ppermute | solution.py:20
  46.7 0.0 collective-permute-start.8
  46.7 3.1 %spread.2 = (f32[4,6,32,256]{3,2,1,0:T(8,128)S(1)}, f32[96,2176]{1,0:T(8,128)S(1)}, f32[96,2176]{1,0:T(8,128)S(1)}) custom-call(bf16[4,512,2048]{2,1,0:T(8,128)(2,1)S(1)} %get-tuple-element.40.refs_0_, bf16[384,512]{1,0:T(8,128)(2,1)S(1)} %get-tuple-element.36.conv_t_ref.refs_1_, bf16[256,256]{1,0:T(8,128)(2,1)S(1)} %copy-done.3, bf16[384,408]{1,0:T(8,128)(2,1)S(1)} %copy-done.1), custom_call_target="tpu_custom_call" | custom-call | flops 1610612736 | bytes 11683840 | tf_op jit(solution)/shard_map/spread/pallas_call | solution.py:527
  49.9 0.0 collective-permute-done.9.refs_9_
  49.9 2.6 %collective-permute-done.8.refs_10_ = bf16[10,8,256]{2,1,0:T(8,128)(2,1)S(1)} collective-permute-done((bf16[10,8,256]{2,1,0:T(8,128)(2,1)S(1)}, bf16[10,8,256]{2,1,0:T(8,128)(2,1)S(1)}, u32[]{:S(2)}, u32[]{:S(2)}) %collective-permute-start.8) | collective-permute-done | bytes 40992 | tf_op jit(solution)/shard_map/ppermute | solution.py:20
  52.6 0.0 collective-permute-done.6
  52.6 0.0 collective-permute-done.5
  52.6 0.0 collective-permute-done.4
  52.7 0.1 collective-permute-start.7
  52.8 0.1 fusion.1
  52.9 1.6 %collective-permute-start.10 = (bf16[6,32,256]{2,1,0:T(8,128)(2,1)S(1)}, bf16[6,32,256]{2,1,0:T(8,128)(2,1)S(1)}, u32[]{:S(2)}, u32[]{:S(2)}) collective-permute-start(bf16[6,32,256]{2,1,0:T(8,128)(2,1)S(1)} %get-tuple-element.58), channel_id=1, source_target_pairs={{0,28},{4,0},{8,4},{12,8},{16,12},{20,16},{24,20},{28,24},{1,29},{... | collective-permute-start | bytes 294920 | tf_op jit(solution)/shard_map/ppermute | solution.py:20
  54.5 0.0 collective-permute-start.11
  54.5 0.0 collective-permute-done.7
  54.5 0.1 collective-permute-start.12
  54.6 1.8 %collective-permute-start.13 = (f32[16,1536]{1,0:T(8,128)S(1)}, f32[16,1536]{1,0:T(8,128)S(1)}, u32[]{:S(2)}, u32[]{:S(2)}) collective-permute-start(f32[16,1536]{1,0:T(8,128)S(1)} %fusion.2.refs_0_), channel_id=1, source_target_pairs={{0,2},{1,3},{2,0},{3,1},{4,6},{5,7},{6,4},{7,5},{8,10},{9,11},{10,... | collective-permute-start | bytes 294920 | tf_op jit(solution)/shard_map/ppermute | solution.py:25
  56.4 2.6 %collective-permute-start.14 = (f32[16,1536]{1,0:T(8,128)S(1)}, f32[16,1536]{1,0:T(8,128)S(1)}, u32[]{:S(2)}, u32[]{:S(2)}) collective-permute-start(f32[16,1536]{1,0:T(8,128)S(1)} %fusion.2.refs_0_), channel_id=1, source_target_pairs={{0,3},{1,2},{2,1},{3,0},{4,7},{5,6},{6,5},{7,4},{8,11},{9,10},{10,... | collective-permute-start | bytes 294920 | tf_op jit(solution)/shard_map/ppermute | solution.py:25
  59.0 0.0 collective-permute-done.10.refs_7_
  59.0 0.7 %collective-permute-done.11.refs_8_ = bf16[6,32,256]{2,1,0:T(8,128)(2,1)S(1)} collective-permute-done((bf16[6,32,256]{2,1,0:T(8,128)(2,1)S(1)}, bf16[6,32,256]{2,1,0:T(8,128)(2,1)S(1)}, u32[]{:S(2)}, u32[]{:S(2)}) %collective-permute-start.11) | collective-permute-done | bytes 98336 | tf_op jit(solution)/shard_map/ppermute | solution.py:20
  59.7 5.3 %spread.3 = f32[6,8,32,256]{3,2,1,0:T(8,128)} custom-call(bf16[4,512,2048]{2,1,0:T(8,128)(2,1)S(1)} %get-tuple-element.40.refs_0_, bf16[384,512]{1,0:T(8,128)(2,1)S(1)} %get-tuple-element.36.conv_t_ref.refs_1_, bf16[256,256]{1,0:T(8,128)(2,1)S(1)} %copy-done.3, bf16[384,408]{1,0:T(8,128)(2,1)S(1)} %copy-done.1, f32[96,2176]{1,0:T(8,128)S(1)} %get-tuple-element.46.refs_4_, ...), custom_call_target="tpu_custom_call" | custom-call | flops 1610612736 | bytes 13535232 | tf_op jit(solution)/shard_map/spread/pallas_call | solution.py:527
  65.0 0.0 collective-permute-done.12.refs_1_
  65.0 0.5 collective-permute-done.13.refs_2_
  65.5 0.0 collective-permute-done.14.refs_3_
  65.5 1.3 %last.1 = (f32[64,162]{1,0:T(8,128)}, f32[1,64]{1,0:T(1,128)}, f32[16,512]{1,0:T(8,128)}, f32[1,128]{1,0:T(1,128)}, f32[1,1]{1,0:T(1,128)}) custom-call(f32[16,1536]{1,0:T(8,128)S(1)} %fusion.2.refs_0_, f32[16,1536]{1,0:T(8,128)S(1)} %collective-permute-done.12.refs_1_, f32[16,1536]{1,0:T(8,128)S(1)} %collective-permute-done.13.refs_2_, ...), custom_call_target="tpu_custom_call" | custom-call | bytes 468228 | tf_op jit(solution)/shard_map/last/pallas_call | solution.py:527
  (33 shorter events, 0.2 us)
Async XLA Ops:
  0.6 12.8 %copy-start.5 = (bf16[408,384]{1,0:T(8,128)(2,1)S(1)}, bf16[408,384]{1,0:T(8,128)(2,1)}, u32[]{:S(2)}) copy-start(bf16[408,384]{1,0:T(8,128)(2,1)} %constant.45.clone.row_ref) | copy-start | bytes 940036
  0.6 12.8 %copy-start.10 = (f32[64]{0:T(128)S(1)}, f32[64]{0:T(128)}, u32[]{:S(2)}) copy-start(f32[64]{0:T(128)} %param.17) | copy-start | bytes 772
  0.7 12.8 %copy-start.6 = (bf16[128,512]{1,0:T(8,128)(2,1)S(1)}, bf16[128,512]{1,0:T(8,128)(2,1)}, u32[]{:S(2)}) copy-start(bf16[128,512]{1,0:T(8,128)(2,1)} %down_weight_ref.1) | copy-start | bytes 393220
  1.7 5.7 %collective-permute-start = (bf16[6,32,256]{2,1,0:T(8,128)(2,1)S(1)}, bf16[6,32,256]{2,1,0:T(8,128)(2,1)S(1)}, u32[]{:S(2)}, u32[]{:S(2)}) collective-permute-start(bf16[6,32,256]{2,1,0:T(8,128)(2,1)S(1)} %get-tuple-element.60), channel_id=1, source_target_pairs={{0,4},{4,8},{8,12},{12,16},{16,20},{20,24},{24,28},{28,0},{1,5},{5... | collective-permute-start | bytes 294920 | tf_op jit(solution)/shard_map/ppermute | solution.py:20
  2.2 5.2 %collective-permute-start.1 = (bf16[6,32,256]{2,1,0:T(8,128)(2,1)S(1)}, bf16[6,32,256]{2,1,0:T(8,128)(2,1)S(1)}, u32[]{:S(2)}, u32[]{:S(2)}) collective-permute-start(bf16[6,32,256]{2,1,0:T(8,128)(2,1)S(1)} %get-tuple-element.59), channel_id=1, source_target_pairs={{0,28},{4,0},{8,4},{12,8},{16,12},{20,16},{24,20},{28,24},{1,29},{... | collective-permute-start | bytes 294920 | tf_op jit(solution)/shard_map/ppermute | solution.py:20
  5.1 12.2 %copy-start.12 = (f32[128]{0:T(128)S(1)}, f32[128]{0:T(128)}, u32[]{:S(2)}) copy-start(f32[128]{0:T(128)} %param.19) | copy-start | bytes 1540
  7.4 1.1 %copy-start = (bf16[6,8,32,256]{3,2,1,0:T(8,128)(2,1)S(1)}, bf16[6,8,32,256]{3,2,1,0:T(8,128)(2,1)}, u32[]{:S(2)}) copy-start(bf16[6,8,32,256]{3,2,1,0:T(8,128)(2,1)} %high_ref.1) | copy-start | bytes 2359300
  8.5 4.9 %copy-start.2 = (bf16[8,162,384]{2,1,0:T(8,128)(2,1)S(1)}, bf16[8,162,384]{2,1,0:T(8,128)(2,1)}, u32[]{:S(2)}) copy-start(bf16[8,162,384]{2,1,0:T(8,128)(2,1)} %constant.49.clone.tap_ref.far_tap_ref) | copy-start | bytes 2985988
  8.5 4.9 %copy-start.4 = (bf16[512,512]{1,0:T(8,128)(2,1)S(1)}, bf16[512,512]{1,0:T(8,128)(2,1)}, u32[]{:S(2)}) copy-start(bf16[512,512]{1,0:T(8,128)(2,1)} %constant.50.clone.order_ref.far_order_ref) | copy-start | bytes 1572868
  8.5 8.8 %copy-start.3 = (bf16[256,256]{1,0:T(8,128)(2,1)S(1)}, bf16[256,256]{1,0:T(8,128)(2,1)}, u32[]{:S(2)}) copy-start(bf16[256,256]{1,0:T(8,128)(2,1)} %constant.44.clone.merge_ref.refs_2_) | copy-start | bytes 393220
  8.5 8.9 %copy-start.13 = (bf16[48,32]{1,0:T(8,128)(2,1)S(1)}, bf16[48,32]{1,0:T(8,128)(2,1)}, u32[]{:S(2)}) copy-start(bf16[48,32]{1,0:T(8,128)(2,1)} %constant.47.clone.edge_ref) | copy-start | bytes 9220
  8.5 8.9 %copy-start.14 = (bf16[32,48]{1,0:T(8,128)(2,1)S(1)}, bf16[32,48]{1,0:T(8,128)(2,1)}, u32[]{:S(2)}) copy-start(bf16[32,48]{1,0:T(8,128)(2,1)} %constant.48.clone.edge_t_ref) | copy-start | bytes 9220
  8.9 8.4 %collective-permute-start.2 = (bf16[10,8,256]{2,1,0:T(8,128)(2,1)S(1)}, bf16[10,8,256]{2,1,0:T(8,128)(2,1)S(1)}, u32[]{:S(2)}, u32[]{:S(2)}) collective-permute-start(bf16[10,8,256]{2,1,0:T(8,128)(2,1)S(1)} %get-tuple-element.33), channel_id=1, source_target_pairs={{0,1},{1,2},{2,3},{3,0},{4,5},{5,6},{6,7},{7,4},{8,9},{9,10},{10,1... | collective-permute-start | bytes 122888 | tf_op jit(solution)/shard_map/ppermute | solution.py:20
  11.3 6.0 %collective-permute-start.3 = (bf16[10,8,256]{2,1,0:T(8,128)(2,1)S(1)}, bf16[10,8,256]{2,1,0:T(8,128)(2,1)S(1)}, u32[]{:S(2)}, u32[]{:S(2)}) collective-permute-start(bf16[10,8,256]{2,1,0:T(8,128)(2,1)S(1)} %get-tuple-element.34), channel_id=1, source_target_pairs={{0,3},{1,0},{2,1},{3,2},{4,7},{5,4},{6,5},{7,6},{8,11},{9,8},{10,9... | collective-permute-start | bytes 122888 | tf_op jit(solution)/shard_map/ppermute | solution.py:20
  13.4 0.9 %copy-start.7 = (bf16[256,256]{1,0:T(8,128)(2,1)S(1)}, bf16[256,256]{1,0:T(8,128)(2,1)}, u32[]{:S(2)}) copy-start(bf16[256,256]{1,0:T(8,128)(2,1)} %constant.43.clone.col_ref) | copy-start | bytes 393220
  14.3 0.8 %copy-start.9 = (bf16[64,162]{1,0:T(8,128)(2,1)S(1)}, bf16[64,162]{1,0:T(8,128)(2,1)}, u32[]{:S(2)}) copy-start(bf16[64,162]{1,0:T(8,128)(2,1)} %conv_weight_ref.1) | copy-start | bytes 62212
  15.1 2.3 %copy-start.8 = (bf16[256,256]{1,0:T(8,128)(2,1)S(1)}, bf16[256,256]{1,0:T(8,128)(2,1)}, u32[]{:S(2)}) copy-start(bf16[256,256]{1,0:T(8,128)(2,1)} %constant.43.clone.col_ref) | copy-start | bytes 393220
  15.1 2.3 %copy-start.11 = (bf16[128,4,16,128]{3,2,1,0:T(8,128)(2,1)S(1)}, bf16[128,4,16,128]{3,2,1,0:T(8,128)(2,1)}, u32[]{:S(2)}) copy-start(bf16[128,4,16,128]{3,2,1,0:T(8,128)(2,1)} %target_ref.1) | copy-start | bytes 6291460
  17.4 29.3 %copy-start.1 = (bf16[384,408]{1,0:T(8,128)(2,1)S(1)}, bf16[384,408]{1,0:T(8,128)(2,1)}, u32[]{:S(2)}) copy-start(bf16[384,408]{1,0:T(8,128)(2,1)} %constant.46.clone.refs_3_) | copy-start | bytes 940036
  40.9 11.7 %collective-permute-start.6 = (f32[32,1024]{1,0:T(8,128)S(1)}, f32[32,1024]{1,0:T(8,128)S(1)}, u32[]{:S(2)}, u32[]{:S(2)}) collective-permute-start(f32[32,1024]{1,0:T(8,128)S(1)} %get-tuple-element.44), channel_id=1, source_target_pairs={{0,24},{4,28},{8,16},{12,20},{16,8},{20,12},{24,0},{28,4},{1,25},{... | collective-permute-start | bytes 393224 | tf_op jit(solution)/shard_map/ppermute | solution.py:25
  42.7 9.9 %collective-permute-start.5 = (f32[32,1024]{1,0:T(8,128)S(1)}, f32[32,1024]{1,0:T(8,128)S(1)}, u32[]{:S(2)}, u32[]{:S(2)}) collective-permute-start(f32[32,1024]{1,0:T(8,128)S(1)} %get-tuple-element.43), channel_id=1, source_target_pairs={{0,16},{4,20},{8,24},{12,28},{16,0},{20,4},{24,8},{28,12},{1,17},{... | collective-permute-start | bytes 393224 | tf_op jit(solution)/shard_map/ppermute | solution.py:25
  43.3 9.3 %collective-permute-start.4 = (f32[32,1024]{1,0:T(8,128)S(1)}, f32[32,1024]{1,0:T(8,128)S(1)}, u32[]{:S(2)}, u32[]{:S(2)}) collective-permute-start(f32[32,1024]{1,0:T(8,128)S(1)} %get-tuple-element.42), channel_id=1, source_target_pairs={{0,8},{4,12},{8,0},{12,4},{16,24},{20,28},{24,16},{28,20},{1,9},{5... | collective-permute-start | bytes 393224 | tf_op jit(solution)/shard_map/ppermute | solution.py:25
  44.5 5.4 %collective-permute-start.9 = (bf16[10,8,256]{2,1,0:T(8,128)(2,1)S(1)}, bf16[10,8,256]{2,1,0:T(8,128)(2,1)S(1)}, u32[]{:S(2)}, u32[]{:S(2)}) collective-permute-start(bf16[10,8,256]{2,1,0:T(8,128)(2,1)S(1)} %get-tuple-element.50), channel_id=1, source_target_pairs={{0,3},{1,0},{2,1},{3,2},{4,7},{5,4},{6,5},{7,6},{8,11},{9,8},{10,9... | collective-permute-start | bytes 122888 | tf_op jit(solution)/shard_map/ppermute | solution.py:20
  46.7 5.8 %collective-permute-start.8 = (bf16[10,8,256]{2,1,0:T(8,128)(2,1)S(1)}, bf16[10,8,256]{2,1,0:T(8,128)(2,1)S(1)}, u32[]{:S(2)}, u32[]{:S(2)}) collective-permute-start(bf16[10,8,256]{2,1,0:T(8,128)(2,1)S(1)} %get-tuple-element.49), channel_id=1, source_target_pairs={{0,1},{1,2},{2,3},{3,0},{4,5},{5,6},{6,7},{7,4},{8,9},{9,10},{10,1... | collective-permute-start | bytes 122888 | tf_op jit(solution)/shard_map/ppermute | solution.py:20
  52.7 1.8 %collective-permute-start.7 = (f32[16,1536]{1,0:T(8,128)S(1)}, f32[16,1536]{1,0:T(8,128)S(1)}, u32[]{:S(2)}, u32[]{:S(2)}) collective-permute-start(f32[16,1536]{1,0:T(8,128)S(1)} %pad_maximum_fusion), channel_id=1, source_target_pairs={{0,4},{4,0},{8,12},{12,8},{16,20},{20,16},{24,28},{28,24},{1,5},{5... | collective-permute-start | bytes 294920 | tf_op jit(solution)/shard_map/ppermute | solution.py:25
  52.9 6.1 %collective-permute-start.10 = (bf16[6,32,256]{2,1,0:T(8,128)(2,1)S(1)}, bf16[6,32,256]{2,1,0:T(8,128)(2,1)S(1)}, u32[]{:S(2)}, u32[]{:S(2)}) collective-permute-start(bf16[6,32,256]{2,1,0:T(8,128)(2,1)S(1)} %get-tuple-element.58), channel_id=1, source_target_pairs={{0,28},{4,0},{8,4},{12,8},{16,12},{20,16},{24,20},{28,24},{1,29},{... | collective-permute-start | bytes 294920 | tf_op jit(solution)/shard_map/ppermute | solution.py:20
  54.5 5.2 %collective-permute-start.11 = (bf16[6,32,256]{2,1,0:T(8,128)(2,1)S(1)}, bf16[6,32,256]{2,1,0:T(8,128)(2,1)S(1)}, u32[]{:S(2)}, u32[]{:S(2)}) collective-permute-start(bf16[6,32,256]{2,1,0:T(8,128)(2,1)S(1)} %get-tuple-element.57), channel_id=1, source_target_pairs={{0,4},{4,8},{8,12},{12,16},{16,20},{20,24},{24,28},{28,0},{1,5},{5... | collective-permute-start | bytes 294920 | tf_op jit(solution)/shard_map/ppermute | solution.py:20
  54.5 10.5 %collective-permute-start.12 = (f32[16,1536]{1,0:T(8,128)S(1)}, f32[16,1536]{1,0:T(8,128)S(1)}, u32[]{:S(2)}, u32[]{:S(2)}) collective-permute-start(f32[16,1536]{1,0:T(8,128)S(1)} %fusion.2.refs_0_), channel_id=1, source_target_pairs={{0,1},{1,0},{2,3},{3,2},{4,5},{5,4},{6,7},{7,6},{8,9},{9,8},{10,11... | collective-permute-start | bytes 294920 | tf_op jit(solution)/shard_map/ppermute | solution.py:25
  54.6 10.9 %collective-permute-start.13 = (f32[16,1536]{1,0:T(8,128)S(1)}, f32[16,1536]{1,0:T(8,128)S(1)}, u32[]{:S(2)}, u32[]{:S(2)}) collective-permute-start(f32[16,1536]{1,0:T(8,128)S(1)} %fusion.2.refs_0_), channel_id=1, source_target_pairs={{0,2},{1,3},{2,0},{3,1},{4,6},{5,7},{6,4},{7,5},{8,10},{9,11},{10,... | collective-permute-start | bytes 294920 | tf_op jit(solution)/shard_map/ppermute | solution.py:25
  56.4 9.1 %collective-permute-start.14 = (f32[16,1536]{1,0:T(8,128)S(1)}, f32[16,1536]{1,0:T(8,128)S(1)}, u32[]{:S(2)}, u32[]{:S(2)}) collective-permute-start(f32[16,1536]{1,0:T(8,128)S(1)} %fusion.2.refs_0_), channel_id=1, source_target_pairs={{0,3},{1,2},{2,1},{3,0},{4,7},{5,6},{6,5},{7,4},{8,11},{9,10},{10,... | collective-permute-start | bytes 294920 | tf_op jit(solution)/shard_map/ppermute | solution.py:25

commit v10 on v9

--- a/solution.py
+++ b/solution.py
@@ -110,23 +110,24 @@
         copy.wait()
 
 
-def rows_kernel(
-    sizes, low_ref, high_ref, far_below_ref, far_above_ref, first_out, last_out, below_ref, above_ref, sems
-):
+def rows_kernel(sizes, low_ref, high_ref, first_out, last_out):
     channels, depth = sizes
-    fetched([(far_below_ref, below_ref), (far_above_ref, above_ref)], sems)
-    for ref, at, out in ((low_ref, 0, first_out), (high_ref, -1, last_out)):
-        for z in range(depth + 2):
-            rows = []
-            for ch in range(channels):
-                if z == 0:
-                    value = below_ref[ch]
-                elif z == depth + 1:
-                    value = above_ref[ch]
-                else:
-                    value = ref[ch, z - 1]
-                value = value.astype(f32)
-                rows.append(value[:1] if at == 0 else value[value.shape[0] - 1 :])
+    for ref, at, out in ((low_ref, 0, first_out), (high_ref, 15, last_out)):
+        for z in range(depth):
+            rows = [ref[ch, z].astype(f32)[at : at + 1] for ch in range(channels)]
+            rows.append(jnp.zeros((8 - channels, rows[0].shape[1]), f32))
+            out[z] = jnp.concatenate(rows, axis=0).astype(bf16)
+
+
+def more_rows_kernel(sizes, *refs):
+    channels, depth = sizes
+    first_out, last_out, first_ref, last_ref, below_ref, above_ref, sems = refs[4:]
+    fetched(list(zip(refs[:4], (first_ref, last_ref, below_ref, above_ref), strict=True)), sems)
+    count = below_ref.shape[1]
+    for ref, at, out in ((first_ref, 0, first_out), (last_ref, count - 1, last_out)):
+        out[1 : depth + 1] = ref[...]
+        for z, plane_ref in ((0, below_ref), (depth + 1, above_ref)):
+            rows = [plane_ref[ch].astype(f32)[at : at + 1] for ch in range(channels)]
             rows.append(jnp.zeros((8 - channels, rows[0].shape[1]), f32))
             out[z] = jnp.concatenate(rows, axis=0).astype(bf16)
 
@@ -560,26 +561,39 @@
     return {name: jnp.asarray(value, bf16) for name, value in names.items()}
 
 
-def outer_rows(fields, below, above):
+def outer_rows(fields):
     channels, depth, row_count, col_count = fields.shape
-    out = jax.ShapeDtypeStruct((depth + 2, 8, col_count), fields.dtype)
+    out = jax.ShapeDtypeStruct((depth, 8, col_count), fields.dtype)
     block = (channels, depth, 16, col_count)
-    beside = pl.BlockSpec(memory_space=pl.ANY)
     return call(
         rows_kernel,
         (channels, depth),
         [out, out],
-        fields, fields, below, above,
+        fields, fields,
         grid=(1,),
         in_specs=[
             pl.BlockSpec(block, lambda z: (0, 0, 0, 0)),
             pl.BlockSpec(block, lambda z: (0, 0, row_count // 16 - 1, 0)),
-            beside,
-            beside,
         ],
         out_specs=[whole(out.shape)] * 2,
-        scratch=[pltpu.VMEM(below.shape, bf16), pltpu.VMEM(above.shape, bf16), pltpu.SemaphoreType.DMA((2,))],
         name="rows",
+    )
+
+
+def more_rows(first_rows, last_rows, below, above):
+    depth, _, col_count = first_rows.shape
+    out = jax.ShapeDtypeStruct((depth + 2, 8, col_count), first_rows.dtype)
+    args = (first_rows, last_rows, below, above)
+    return call(
+        more_rows_kernel,
+        (below.shape[0], depth),
+        [out, out],
+        *args,
+        grid=(1,),
+        in_specs=[pl.BlockSpec(memory_space=pl.ANY)] * 4,
+        out_specs=[whole(out.shape)] * 2,
+        scratch=[pltpu.VMEM(a.shape, a.dtype) for a in args] + [pltpu.SemaphoreType.DMA((4,))],
+        name="more_rows",
     )
 
 
@@ -714,7 +728,7 @@
 
     below = shifted(fields[:, depth - 1], "gz", 1)
     above = shifted(fields[:, 0], "gz", -1)
-    first_rows, last_rows = outer_rows(fields, below, above)
+    first_rows, last_rows = more_rows(*outer_rows(fields), below, above)
     before = shifted(last_rows, "gy", 1)
     after = shifted(first_rows, "gy", -1)
     early, conv_big, conv_t, down_big, down_t = prepare(
@@ -727,9 +741,10 @@
     pairs = depth // 2
     shape = fields.shape
 
-    got = [exchanged(message, "gz", 2 * far) for far, message in enumerate(messages) if far > 0]
     from_before = shifted(to_after, "gy", 1)
     from_after = shifted(to_before, "gy", -1)
+    got = [exchanged(message, "gz", 2 * far) for far, message in enumerate(messages) if far > 0]
+    from_before, from_after, *got = lax.optimization_barrier((from_before, from_after, *got))
     outer = ((0, pairs - 1), (0, 1, pairs - 1, pairs), (), (0, pairs), (1, pairs - 1))
     outer_core, low_open, high_open = spread(grad_pre, conv_t, fixed, shape, outer)
     packed = sum(got, messages[0])

time: 67.2 us -> 69.2 us (1.030)
  starting transfers between devices: 19.9 us -> 21.4 us
  local copies, waits for them, and re-layouts: 3.99 us -> 5.17 us
  waiting for transfers between devices: 5.98 us -> 5.19 us
    ppermute x8, waiting for transfers between devices: 5.5 us -> 1.36 us  [shifted(): lax.ppermute(value, axis, [(i, (i + by) % count) for i in range(count)])]
    ppermute x7, waiting for transfers between devices: 0.48 us -> 3.83 us  [exchanged(): return lax.ppermute(value, axis, [(i, i ^ bit) for i in range(count)])]
    ppermute x8, starting transfers between devices: 11.8 us -> 13.3 us  [shifted(): lax.ppermute(value, axis, [(i, (i + by) % count) for i in range(count)])]
    unnamed x30 -> x34, local copies, waits for them, and re-layouts: 2.85 us -> 4.04 us
    pallas_call x6 -> x7, Pallas kernels: 35.8 us -> 35.9 us  [call(): pl.pallas_call(functools.partial(kernel, sizes), out_shape=out_shape, in_...]
where the time goes in v10:
time: 69.2 us; the launch traced here: 68.9 us
  Pallas kernels  35.9 us (52%)
  starting transfers between devices  21.4 us (31%)
  waiting for transfers between devices  5.19 us (8%)
  local copies, waits for them, and re-layouts  5.17 us (7%)
  between operations  1.14 us (2%)
    pallas_call x7, Pallas kernels, call(): pl.pallas_call(functools.partial(kernel, sizes), out_shape=out_shape, in_...  35.9 us
    ppermute x8, starting transfers between devices, shifted(): lax.ppermute(value, axis, [(i, (i + by) % count) for i in range(count)])  13.3 us
    ppermute x7, starting transfers between devices, exchanged(): return lax.ppermute(value, axis, [(i, i ^ bit) for i in range(count)])  8.11 us
    unnamed x34, local copies, waits for them, and re-layouts  4.04 us
    ppermute x7, waiting for transfers between devices, exchanged(): return lax.ppermute(value, axis, [(i, i ^ bit) for i in range(count)])  3.83 us
  transfers between devices with their start and end apart: 15, of which 4 were waited for; matrix products, arithmetic and copies ran while one was open for 0% of the time, Pallas kernels for 16%

profile of v10, /device:TPU:0, one launch (start us, length us, event | category | flops | bytes accessed | tf_op | source)
XLA Modules:
  0.0 68.9 jit_solution(6934228418564558145)
XLA Ops:
  0.6 0.0 copy-start.7
  0.7 0.0 copy-start.15
  0.7 0.0 copy-start.16
  0.7 1.0 %slice_bitcast_fusion = (bf16[6,32,256]{2,1,0:T(8,128)(2,1)S(1)}, bf16[6,32,256]{2,1,0:T(8,128)(2,1)S(1)}) fusion(bf16[6,8,32,256]{3,2,1,0:T(8,128)(2,1)} %high_ref.1), kind=kLoop, calls=%fused_computation.10 | loop fusion | bytes 393216 | tf_op jit(solution)/shard_map/squeeze | solution.py:730
  1.7 0.5 collective-permute-start
  2.2 3.0 %collective-permute-start.1 = (bf16[6,32,256]{2,1,0:T(8,128)(2,1)S(1)}, bf16[6,32,256]{2,1,0:T(8,128)(2,1)S(1)}, u32[]{:S(2)}, u32[]{:S(2)}) collective-permute-start(bf16[6,32,256]{2,1,0:T(8,128)(2,1)S(1)} %get-tuple-element.73), channel_id=1, source_target_pairs={{0,28},{4,0},{8,4},{12,8},{16,12},{20,16},{24,20},{28,24},{1,29},{... | collective-permute-start | bytes 294920 | tf_op jit(solution)/shard_map/ppermute | solution.py:20
  5.2 1.1 %copy-done = bf16[6,8,32,256]{3,2,1,0:T(8,128)(2,1)S(1)} copy-done((bf16[6,8,32,256]{3,2,1,0:T(8,128)(2,1)S(1)}, bf16[6,8,32,256]{3,2,1,0:T(8,128)(2,1)}, u32[]{:S(2)}) %copy-start) | copy-done | bytes 786456
  6.3 0.1 rows.1
  6.4 0.0 copy-start.4
  6.4 0.1 pad.4.clone
  6.5 0.9 %collective-permute-done.below_ref.refs_2_ = bf16[6,32,256]{2,1,0:T(8,128)(2,1)S(1)} collective-permute-done((bf16[6,32,256]{2,1,0:T(8,128)(2,1)S(1)}, bf16[6,32,256]{2,1,0:T(8,128)(2,1)S(1)}, u32[]{:S(2)}, u32[]{:S(2)}) %collective-permute-start) | collective-permute-done | bytes 98336 | tf_op jit(solution)/shard_map/ppermute | solution.py:20
  7.4 0.0 collective-permute-done.1.above_ref.refs_3_
  7.4 0.4 more_rows.1
  7.8 2.4 %collective-permute-start.2 = (bf16[10,8,256]{2,1,0:T(8,128)(2,1)S(1)}, bf16[10,8,256]{2,1,0:T(8,128)(2,1)S(1)}, u32[]{:S(2)}, u32[]{:S(2)}) collective-permute-start(bf16[10,8,256]{2,1,0:T(8,128)(2,1)S(1)} %get-tuple-element.42), channel_id=1, source_target_pairs={{0,1},{1,2},{2,3},{3,0},{4,5},{5,6},{6,7},{7,4},{8,9},{9,10},{10,1... | collective-permute-start | bytes 122888 | tf_op jit(solution)/shard_map/ppermute | solution.py:20
  10.2 2.1 %collective-permute-start.3 = (bf16[10,8,256]{2,1,0:T(8,128)(2,1)S(1)}, bf16[10,8,256]{2,1,0:T(8,128)(2,1)S(1)}, u32[]{:S(2)}, u32[]{:S(2)}) collective-permute-start(bf16[10,8,256]{2,1,0:T(8,128)(2,1)S(1)} %get-tuple-element.43), channel_id=1, source_target_pairs={{0,3},{1,0},{2,1},{3,2},{4,7},{5,4},{6,5},{7,6},{8,11},{9,8},{10,9... | collective-permute-start | bytes 122888 | tf_op jit(solution)/shard_map/ppermute | solution.py:20
  12.3 0.0 copy-start.5
  12.3 1.0 %copy-done.5 = bf16[512,512]{1,0:T(8,128)(2,1)S(1)} copy-done((bf16[512,512]{1,0:T(8,128)(2,1)S(1)}, bf16[512,512]{1,0:T(8,128)(2,1)}, u32[]{:S(2)}) %copy-start.5) | copy-done | bytes 524312
  13.3 0.9 %copy-done.8 = bf16[128,512]{1,0:T(8,128)(2,1)S(1)} copy-done((bf16[128,512]{1,0:T(8,128)(2,1)S(1)}, bf16[128,512]{1,0:T(8,128)(2,1)}, u32[]{:S(2)}) %copy-start.8) | copy-done | bytes 131096
  14.2 0.9 %copy-done.9 = bf16[256,256]{1,0:T(8,128)(2,1)S(1)} copy-done((bf16[256,256]{1,0:T(8,128)(2,1)S(1)}, bf16[256,256]{1,0:T(8,128)(2,1)}, u32[]{:S(2)}) %copy-start.9) | copy-done | bytes 131096
  15.1 2.2 %prepare.1 = (bf16[5,96,2176]{2,1,0:T(8,128)(2,1)S(1)}, bf16[512,400]{1,0:T(8,128)(2,1)S(1)}, bf16[384,512]{1,0:T(8,128)(2,1)S(1)}, bf16[128,512]{1,0:T(8,128)(2,1)S(1)}, bf16[512,128]{1,0:T(8,128)(2,1)S(1)}) custom-call(bf16[6,8,32,256]{3,2,1,0:T(8,128)(2,1)S(1)} %copy-done.1, bf16[6,32,256]{2,1,0:T(8,128)(2,1)S(1)} %collective-permute-done.below_ref.refs_2_, ...), custom_call_target="tpu_custom_call" | custom-call | flops 603979776 | bytes 6253056 | tf_op jit(solution)/shard_map/prepare/pallas_call | solution.py:528
  17.4 0.0 collective-permute-done.2.far_before_ref
  17.4 0.0 collective-permute-done.3.far_after_ref
  17.4 0.0 copy-start.2
  17.5 23.5 %forward.1 = (bf16[128,4,16,128]{3,2,1,0:T(8,128)(2,1)}, bf16[4,512,2048]{2,1,0:T(8,128)(2,1)S(1)}, bf16[10,8,256]{2,1,0:T(8,128)(2,1)S(1)}, bf16[10,8,256]{2,1,...) custom-call(bf16[5,96,2176]{2,1,0:T(8,128)(2,1)S(1)} %get-tuple-elem, ...), custom_call_target="tpu_custom_call" | custom-call | flops 8589934592 | bytes 18213376 | tf_op jit(solution)/shard_map/forward/pallas_call | solution.py:528
  41.0 0.1 collective-permute-start.4
  41.0 3.8 %collective-permute-start.5 = (bf16[10,8,256]{2,1,0:T(8,128)(2,1)S(1)}, bf16[10,8,256]{2,1,0:T(8,128)(2,1)S(1)}, u32[]{:S(2)}, u32[]{:S(2)}) collective-permute-start(bf16[10,8,256]{2,1,0:T(8,128)(2,1)S(1)} %get-tuple-element.52), channel_id=1, source_target_pairs={{0,3},{1,0},{2,1},{3,2},{4,7},{5,4},{6,5},{7,6},{8,11},{9,8},{10,9... | collective-permute-start | bytes 122888 | tf_op jit(solution)/shard_map/ppermute | solution.py:20
  44.9 0.8 %collective-permute-start.6 = (f32[32,1024]{1,0:T(8,128)S(1)}, f32[32,1024]{1,0:T(8,128)S(1)}, u32[]{:S(2)}, u32[]{:S(2)}) collective-permute-start(f32[32,1024]{1,0:T(8,128)S(1)} %get-tuple-element.53), channel_id=1, source_target_pairs={{0,8},{4,12},{8,0},{12,4},{16,24},{20,28},{24,16},{28,20},{1,9},{5... | collective-permute-start | bytes 393224 | tf_op jit(solution)/shard_map/ppermute | solution.py:25
  45.6 1.5 %collective-permute-start.7 = (f32[32,1024]{1,0:T(8,128)S(1)}, f32[32,1024]{1,0:T(8,128)S(1)}, u32[]{:S(2)}, u32[]{:S(2)}) collective-permute-start(f32[32,1024]{1,0:T(8,128)S(1)} %get-tuple-element.54), channel_id=1, source_target_pairs={{0,16},{4,20},{8,24},{12,28},{16,0},{20,4},{24,8},{28,12},{1,17},{... | collective-permute-start | bytes 393224 | tf_op jit(solution)/shard_map/ppermute | solution.py:25
  47.1 1.2 %collective-permute-start.8 = (f32[32,1024]{1,0:T(8,128)S(1)}, f32[32,1024]{1,0:T(8,128)S(1)}, u32[]{:S(2)}, u32[]{:S(2)}) collective-permute-start(f32[32,1024]{1,0:T(8,128)S(1)} %get-tuple-element.55), channel_id=1, source_target_pairs={{0,24},{4,28},{8,16},{12,20},{16,8},{20,12},{24,0},{28,4},{1,25},{... | collective-permute-start | bytes 393224 | tf_op jit(solution)/shard_map/ppermute | solution.py:25
  48.4 3.1 %spread.2 = (f32[4,6,32,256]{3,2,1,0:T(8,128)S(1)}, f32[96,2176]{1,0:T(8,128)S(1)}, f32[96,2176]{1,0:T(8,128)S(1)}) custom-call(bf16[4,512,2048]{2,1,0:T(8,128)(2,1)S(1)} %get-tuple-element.49.refs_0_, bf16[384,512]{1,0:T(8,128)(2,1)S(1)} %get-tuple-element.45.conv_t_ref.refs_1_, bf16[256,256]{1,0:T(8,128)(2,1)S(1)} %copy-done.4, bf16[384,408]{1,0:T(8,128)(2,1)S(1)} %copy-done.2), custom_call_target="tpu_custom_call" | custom-call | flops 1610612736 | bytes 11683840 | tf_op jit(solution)/shard_map/spread/pallas_call | solution.py:528
  51.5 0.0 collective-permute-done.5.refs_9_
  51.5 0.0 collective-permute-done.6
  51.5 3.1 %collective-permute-done.7 = f32[32,1024]{1,0:T(8,128)S(1)} collective-permute-done((f32[32,1024]{1,0:T(8,128)S(1)}, f32[32,1024]{1,0:T(8,128)S(1)}, u32[]{:S(2)}, u32[]{:S(2)}) %collective-permute-start.7) | collective-permute-done | bytes 131104 | tf_op jit(solution)/shard_map/ppermute | solution.py:25
  54.6 0.0 collective-permute-done.8
  54.7 0.2 collective-permute-start.9
  55.0 0.1 fusion.1
  55.1 1.4 %collective-permute-start.10 = (bf16[6,32,256]{2,1,0:T(8,128)(2,1)S(1)}, bf16[6,32,256]{2,1,0:T(8,128)(2,1)S(1)}, u32[]{:S(2)}, u32[]{:S(2)}) collective-permute-start(bf16[6,32,256]{2,1,0:T(8,128)(2,1)S(1)} %get-tuple-element.72), channel_id=1, source_target_pairs={{0,28},{4,0},{8,4},{12,8},{16,12},{20,16},{24,20},{28,24},{1,29},{... | collective-permute-start | bytes 294920 | tf_op jit(solution)/shard_map/ppermute | solution.py:20
  56.5 0.0 collective-permute-start.11
  56.5 0.0 collective-permute-done.9
  56.5 0.1 collective-permute-start.12
  56.6 0.6 collective-permute-start.13
  57.2 3.8 %collective-permute-start.14 = (f32[16,1536]{1,0:T(8,128)S(1)}, f32[16,1536]{1,0:T(8,128)S(1)}, u32[]{:S(2)}, u32[]{:S(2)}) collective-permute-start(f32[16,1536]{1,0:T(8,128)S(1)} %fusion.2.refs_0_), channel_id=1, source_target_pairs={{0,3},{1,2},{2,1},{3,0},{4,7},{5,6},{6,5},{7,4},{8,11},{9,10},{10,... | collective-permute-start | bytes 294920 | tf_op jit(solution)/shard_map/ppermute | solution.py:25
  61.0 0.0 collective-permute-done.10.refs_7_
  61.0 0.5 collective-permute-done.11.refs_8_
  61.5 5.3 %spread.3 = f32[6,8,32,256]{3,2,1,0:T(8,128)} custom-call(bf16[4,512,2048]{2,1,0:T(8,128)(2,1)S(1)} %get-tuple-element.49.refs_0_, bf16[384,512]{1,0:T(8,128)(2,1)S(1)} %get-tuple-element.45.conv_t_ref.refs_1_, bf16[256,256]{1,0:T(8,128)(2,1)S(1)} %copy-done.4, bf16[384,408]{1,0:T(8,128)(2,1)S(1)} %copy-done.2, f32[96,2176]{1,0:T(8,128)S(1)} %get-tuple-element.60.refs_4_, ...), custom_call_target="tpu_custom_call" | custom-call | flops 1610612736 | bytes 13535232 | tf_op jit(solution)/shard_map/spread/pallas_call | solution.py:528
  66.8 0.0 collective-permute-done.12.refs_1_
  66.8 0.7 %collective-permute-done.13.refs_2_ = f32[16,1536]{1,0:T(8,128)S(1)} collective-permute-done((f32[16,1536]{1,0:T(8,128)S(1)}, f32[16,1536]{1,0:T(8,128)S(1)}, u32[]{:S(2)}, u32[]{:S(2)}) %collective-permute-start.13) | collective-permute-done | bytes 98336 | tf_op jit(solution)/shard_map/ppermute | solution.py:25
  67.5 1.3 %last.1 = (f32[64,162]{1,0:T(8,128)}, f32[1,64]{1,0:T(1,128)}, f32[16,512]{1,0:T(8,128)}, f32[1,128]{1,0:T(1,128)}, f32[1,1]{1,0:T(1,128)}) custom-call(f32[16,1536]{1,0:T(8,128)S(1)} %fusion.2.refs_0_, f32[16,1536]{1,0:T(8,128)S(1)} %collective-permute-done.12.refs_1_, f32[16,1536]{1,0:T(8,128)S(1)} %collective-permute-done.13.refs_2_, ...), custom_call_target="tpu_custom_call" | custom-call | bytes 468228 | tf_op jit(solution)/shard_map/last/pallas_call | solution.py:528
  (37 shorter events, 0.2 us)
Async XLA Ops:
  0.6 11.6 %copy-start.7 = (bf16[408,384]{1,0:T(8,128)(2,1)S(1)}, bf16[408,384]{1,0:T(8,128)(2,1)}, u32[]{:S(2)}) copy-start(bf16[408,384]{1,0:T(8,128)(2,1)} %constant.45.clone.row_ref) | copy-start | bytes 940036
  0.6 11.6 %copy-start.11 = (bf16[64,162]{1,0:T(8,128)(2,1)S(1)}, bf16[64,162]{1,0:T(8,128)(2,1)}, u32[]{:S(2)}) copy-start(bf16[64,162]{1,0:T(8,128)(2,1)} %conv_weight_ref.1) | copy-start | bytes 62212
  0.7 11.6 %copy-start.12 = (f32[64]{0:T(128)S(1)}, f32[64]{0:T(128)}, u32[]{:S(2)}) copy-start(f32[64]{0:T(128)} %param.17) | copy-start | bytes 772
  0.7 16.7 %copy-start.15 = (bf16[48,32]{1,0:T(8,128)(2,1)S(1)}, bf16[48,32]{1,0:T(8,128)(2,1)}, u32[]{:S(2)}) copy-start(bf16[48,32]{1,0:T(8,128)(2,1)} %constant.47.clone.edge_ref) | copy-start | bytes 9220
  0.7 16.7 %copy-start.16 = (bf16[32,48]{1,0:T(8,128)(2,1)S(1)}, bf16[32,48]{1,0:T(8,128)(2,1)}, u32[]{:S(2)}) copy-start(bf16[32,48]{1,0:T(8,128)(2,1)} %constant.48.clone.edge_t_ref) | copy-start | bytes 9220
  1.7 5.7 %collective-permute-start = (bf16[6,32,256]{2,1,0:T(8,128)(2,1)S(1)}, bf16[6,32,256]{2,1,0:T(8,128)(2,1)S(1)}, u32[]{:S(2)}, u32[]{:S(2)}) collective-permute-start(bf16[6,32,256]{2,1,0:T(8,128)(2,1)S(1)} %get-tuple-element.74), channel_id=1, source_target_pairs={{0,4},{4,8},{8,12},{12,16},{16,20},{20,24},{24,28},{28,0},{1,5},{5... | collective-permute-start | bytes 294920 | tf_op jit(solution)/shard_map/ppermute | solution.py:20
  2.2 15.2 %copy-start.14 = (f32[128]{0:T(128)S(1)}, f32[128]{0:T(128)}, u32[]{:S(2)}) copy-start(f32[128]{0:T(128)} %param.19) | copy-start | bytes 1540
  2.2 5.2 %collective-permute-start.1 = (bf16[6,32,256]{2,1,0:T(8,128)(2,1)S(1)}, bf16[6,32,256]{2,1,0:T(8,128)(2,1)S(1)}, u32[]{:S(2)}, u32[]{:S(2)}) collective-permute-start(bf16[6,32,256]{2,1,0:T(8,128)(2,1)S(1)} %get-tuple-element.73), channel_id=1, source_target_pairs={{0,28},{4,0},{8,4},{12,8},{16,12},{20,16},{24,20},{28,24},{1,29},{... | collective-permute-start | bytes 294920 | tf_op jit(solution)/shard_map/ppermute | solution.py:20
  5.2 1.1 %copy-start = (bf16[6,8,32,256]{3,2,1,0:T(8,128)(2,1)S(1)}, bf16[6,8,32,256]{3,2,1,0:T(8,128)(2,1)}, u32[]{:S(2)}) copy-start(bf16[6,8,32,256]{3,2,1,0:T(8,128)(2,1)} %high_ref.1) | copy-start | bytes 2359300
  6.3 6.0 %copy-start.1 = (bf16[6,8,32,256]{3,2,1,0:T(8,128)(2,1)S(1)}, bf16[6,8,32,256]{3,2,1,0:T(8,128)(2,1)}, u32[]{:S(2)}) copy-start(bf16[6,8,32,256]{3,2,1,0:T(8,128)(2,1)} %high_ref.1) | copy-start | bytes 2359300
  6.3 6.0 %copy-start.3 = (bf16[8,162,384]{2,1,0:T(8,128)(2,1)S(1)}, bf16[8,162,384]{2,1,0:T(8,128)(2,1)}, u32[]{:S(2)}) copy-start(bf16[8,162,384]{2,1,0:T(8,128)(2,1)} %constant.49.clone.tap_ref.far_tap_ref) | copy-start | bytes 2985988
  6.4 11.0 %copy-start.4 = (bf16[256,256]{1,0:T(8,128)(2,1)S(1)}, bf16[256,256]{1,0:T(8,128)(2,1)}, u32[]{:S(2)}) copy-start(bf16[256,256]{1,0:T(8,128)(2,1)} %constant.44.clone.merge_ref.refs_2_) | copy-start | bytes 393220
  7.8 9.6 %collective-permute-start.2 = (bf16[10,8,256]{2,1,0:T(8,128)(2,1)S(1)}, bf16[10,8,256]{2,1,0:T(8,128)(2,1)S(1)}, u32[]{:S(2)}, u32[]{:S(2)}) collective-permute-start(bf16[10,8,256]{2,1,0:T(8,128)(2,1)S(1)} %get-tuple-element.42), channel_id=1, source_target_pairs={{0,1},{1,2},{2,3},{3,0},{4,5},{5,6},{6,7},{7,4},{8,9},{9,10},{10,1... | collective-permute-start | bytes 122888 | tf_op jit(solution)/shard_map/ppermute | solution.py:20
  10.2 7.2 %collective-permute-start.3 = (bf16[10,8,256]{2,1,0:T(8,128)(2,1)S(1)}, bf16[10,8,256]{2,1,0:T(8,128)(2,1)S(1)}, u32[]{:S(2)}, u32[]{:S(2)}) collective-permute-start(bf16[10,8,256]{2,1,0:T(8,128)(2,1)S(1)} %get-tuple-element.43), channel_id=1, source_target_pairs={{0,3},{1,0},{2,1},{3,2},{4,7},{5,4},{6,5},{7,6},{8,11},{9,8},{10,9... | collective-permute-start | bytes 122888 | tf_op jit(solution)/shard_map/ppermute | solution.py:20
  12.3 1.0 %copy-start.5 = (bf16[512,512]{1,0:T(8,128)(2,1)S(1)}, bf16[512,512]{1,0:T(8,128)(2,1)}, u32[]{:S(2)}) copy-start(bf16[512,512]{1,0:T(8,128)(2,1)} %constant.50.clone.order_ref.far_order_ref) | copy-start | bytes 1572868
  13.3 0.9 %copy-start.8 = (bf16[128,512]{1,0:T(8,128)(2,1)S(1)}, bf16[128,512]{1,0:T(8,128)(2,1)}, u32[]{:S(2)}) copy-start(bf16[128,512]{1,0:T(8,128)(2,1)} %down_weight_ref.1) | copy-start | bytes 393220
  14.2 0.9 %copy-start.9 = (bf16[256,256]{1,0:T(8,128)(2,1)S(1)}, bf16[256,256]{1,0:T(8,128)(2,1)}, u32[]{:S(2)}) copy-start(bf16[256,256]{1,0:T(8,128)(2,1)} %constant.43.clone.col_ref) | copy-start | bytes 393220
  15.1 2.3 %copy-start.6 = (bf16[512,512]{1,0:T(8,128)(2,1)S(1)}, bf16[512,512]{1,0:T(8,128)(2,1)}, u32[]{:S(2)}) copy-start(bf16[512,512]{1,0:T(8,128)(2,1)} %constant.50.clone.order_ref.far_order_ref) | copy-start | bytes 1572868
  15.1 2.3 %copy-start.10 = (bf16[256,256]{1,0:T(8,128)(2,1)S(1)}, bf16[256,256]{1,0:T(8,128)(2,1)}, u32[]{:S(2)}) copy-start(bf16[256,256]{1,0:T(8,128)(2,1)} %constant.43.clone.col_ref) | copy-start | bytes 393220
  15.1 2.3 %copy-start.13 = (bf16[128,4,16,128]{3,2,1,0:T(8,128)(2,1)S(1)}, bf16[128,4,16,128]{3,2,1,0:T(8,128)(2,1)}, u32[]{:S(2)}) copy-start(bf16[128,4,16,128]{3,2,1,0:T(8,128)(2,1)} %target_ref.1) | copy-start | bytes 6291460
  17.4 30.9 %copy-start.2 = (bf16[384,408]{1,0:T(8,128)(2,1)S(1)}, bf16[384,408]{1,0:T(8,128)(2,1)}, u32[]{:S(2)}) copy-start(bf16[384,408]{1,0:T(8,128)(2,1)} %constant.46.clone.refs_3_) | copy-start | bytes 940036
  41.0 10.5 %collective-permute-start.4 = (bf16[10,8,256]{2,1,0:T(8,128)(2,1)S(1)}, bf16[10,8,256]{2,1,0:T(8,128)(2,1)S(1)}, u32[]{:S(2)}, u32[]{:S(2)}) collective-permute-start(bf16[10,8,256]{2,1,0:T(8,128)(2,1)S(1)} %get-tuple-element.51), channel_id=1, source_target_pairs={{0,1},{1,2},{2,3},{3,0},{4,5},{5,6},{6,7},{7,4},{8,9},{9,10},{10,1... | collective-permute-start | bytes 122888 | tf_op jit(solution)/shard_map/ppermute | solution.py:20
  41.0 10.5 %collective-permute-start.5 = (bf16[10,8,256]{2,1,0:T(8,128)(2,1)S(1)}, bf16[10,8,256]{2,1,0:T(8,128)(2,1)S(1)}, u32[]{:S(2)}, u32[]{:S(2)}) collective-permute-start(bf16[10,8,256]{2,1,0:T(8,128)(2,1)S(1)} %get-tuple-element.52), channel_id=1, source_target_pairs={{0,3},{1,0},{2,1},{3,2},{4,7},{5,4},{6,5},{7,6},{8,11},{9,8},{10,9... | collective-permute-start | bytes 122888 | tf_op jit(solution)/shard_map/ppermute | solution.py:20
  44.9 6.6 %collective-permute-start.6 = (f32[32,1024]{1,0:T(8,128)S(1)}, f32[32,1024]{1,0:T(8,128)S(1)}, u32[]{:S(2)}, u32[]{:S(2)}) collective-permute-start(f32[32,1024]{1,0:T(8,128)S(1)} %get-tuple-element.53), channel_id=1, source_target_pairs={{0,8},{4,12},{8,0},{12,4},{16,24},{20,28},{24,16},{28,20},{1,9},{5... | collective-permute-start | bytes 393224 | tf_op jit(solution)/shard_map/ppermute | solution.py:25
  45.6 9.0 %collective-permute-start.7 = (f32[32,1024]{1,0:T(8,128)S(1)}, f32[32,1024]{1,0:T(8,128)S(1)}, u32[]{:S(2)}, u32[]{:S(2)}) collective-permute-start(f32[32,1024]{1,0:T(8,128)S(1)} %get-tuple-element.54), channel_id=1, source_target_pairs={{0,16},{4,20},{8,24},{12,28},{16,0},{20,4},{24,8},{28,12},{1,17},{... | collective-permute-start | bytes 393224 | tf_op jit(solution)/shard_map/ppermute | solution.py:25
  47.1 7.5 %collective-permute-start.8 = (f32[32,1024]{1,0:T(8,128)S(1)}, f32[32,1024]{1,0:T(8,128)S(1)}, u32[]{:S(2)}, u32[]{:S(2)}) collective-permute-start(f32[32,1024]{1,0:T(8,128)S(1)} %get-tuple-element.55), channel_id=1, source_target_pairs={{0,24},{4,28},{8,16},{12,20},{16,8},{20,12},{24,0},{28,4},{1,25},{... | collective-permute-start | bytes 393224 | tf_op jit(solution)/shard_map/ppermute | solution.py:25
  54.7 1.8 %collective-permute-start.9 = (f32[16,1536]{1,0:T(8,128)S(1)}, f32[16,1536]{1,0:T(8,128)S(1)}, u32[]{:S(2)}, u32[]{:S(2)}) collective-permute-start(f32[16,1536]{1,0:T(8,128)S(1)} %pad_maximum_fusion), channel_id=1, source_target_pairs={{0,4},{4,0},{8,12},{12,8},{16,20},{20,16},{24,28},{28,24},{1,5},{5... | collective-permute-start | bytes 294920 | tf_op jit(solution)/shard_map/ppermute | solution.py:25
  55.1 5.9 %collective-permute-start.10 = (bf16[6,32,256]{2,1,0:T(8,128)(2,1)S(1)}, bf16[6,32,256]{2,1,0:T(8,128)(2,1)S(1)}, u32[]{:S(2)}, u32[]{:S(2)}) collective-permute-start(bf16[6,32,256]{2,1,0:T(8,128)(2,1)S(1)} %get-tuple-element.72), channel_id=1, source_target_pairs={{0,28},{4,0},{8,4},{12,8},{16,12},{20,16},{24,20},{28,24},{1,29},{... | collective-permute-start | bytes 294920 | tf_op jit(solution)/shard_map/ppermute | solution.py:20
  56.5 4.9 %collective-permute-start.11 = (bf16[6,32,256]{2,1,0:T(8,128)(2,1)S(1)}, bf16[6,32,256]{2,1,0:T(8,128)(2,1)S(1)}, u32[]{:S(2)}, u32[]{:S(2)}) collective-permute-start(bf16[6,32,256]{2,1,0:T(8,128)(2,1)S(1)} %get-tuple-element.71), channel_id=1, source_target_pairs={{0,4},{4,8},{8,12},{12,16},{16,20},{20,24},{24,28},{28,0},{1,5},{5... | collective-permute-start | bytes 294920 | tf_op jit(solution)/shard_map/ppermute | solution.py:20
  56.5 10.3 %collective-permute-start.12 = (f32[16,1536]{1,0:T(8,128)S(1)}, f32[16,1536]{1,0:T(8,128)S(1)}, u32[]{:S(2)}, u32[]{:S(2)}) collective-permute-start(f32[16,1536]{1,0:T(8,128)S(1)} %fusion.2.refs_0_), channel_id=1, source_target_pairs={{0,1},{1,0},{2,3},{3,2},{4,5},{5,4},{6,7},{7,6},{8,9},{9,8},{10,11... | collective-permute-start | bytes 294920 | tf_op jit(solution)/shard_map/ppermute | solution.py:25
  56.6 10.9 %collective-permute-start.13 = (f32[16,1536]{1,0:T(8,128)S(1)}, f32[16,1536]{1,0:T(8,128)S(1)}, u32[]{:S(2)}, u32[]{:S(2)}) collective-permute-start(f32[16,1536]{1,0:T(8,128)S(1)} %fusion.2.refs_0_), channel_id=1, source_target_pairs={{0,2},{1,3},{2,0},{3,1},{4,6},{5,7},{6,4},{7,5},{8,10},{9,11},{10,... | collective-permute-start | bytes 294920 | tf_op jit(solution)/shard_map/ppermute | solution.py:25
  57.2 10.3 %collective-permute-start.14 = (f32[16,1536]{1,0:T(8,128)S(1)}, f32[16,1536]{1,0:T(8,128)S(1)}, u32[]{:S(2)}, u32[]{:S(2)}) collective-permute-start(f32[16,1536]{1,0:T(8,128)S(1)} %fusion.2.refs_0_), channel_id=1, source_target_pairs={{0,3},{1,2},{2,1},{3,0},{4,7},{5,6},{6,5},{7,4},{8,11},{9,10},{10,... | collective-permute-start | bytes 294920 | tf_op jit(solution)/shard_map/ppermute | solution.py:25

commit v11 on v10

--- a/solution.py
+++ b/solution.py
@@ -25,12 +25,13 @@
     return lax.ppermute(value, axis, [(i, i ^ bit) for i in range(count)])
 
 
-def column_merge(half_cols):
-    merge = np.zeros((2 * half_cols, 2 * half_cols), np.float32)
-    for par in range(2):
-        for col in range(half_cols):
-            merge[par * half_cols + col, (2 * col + par - 1) % (2 * half_cols)] = 1
-    return merge
+def merge_table(width, turned=False):
+    place = lax.broadcasted_iota(jnp.int32, (width, width), 1 if turned else 0)
+    found = lax.broadcasted_iota(jnp.int32, (width, width), 0 if turned else 1)
+    half = width // 2
+    at = jnp.where(place < half, 2 * place - 1, 2 * (place - half))
+    at = jnp.where(at < 0, width - 1, at)
+    return jnp.where(found == at, 1.0, 0.0).astype(bf16)
 
 
 def row_spread(channels, row_count):
@@ -142,7 +143,6 @@
     down_weight_ref,
     tap_ref,
     order_ref,
-    col_ref,
     row_ref,
     split_ref,
     conv_ref,
@@ -170,7 +170,7 @@
         upper = above_ref if slot == pairs else field_ref.at[:, 2 * slot]
         rows = [ref[ch] for ref in (lower, upper) for ch in range(channels)]
         rows = dot(row_ref[...], jnp.concatenate(rows, axis=0)).astype(bf16)
-        rows = dot(rows, col_ref[...])
+        rows = dot(rows, merge_table(2 * lanes, turned=True))
         for row in range(half_rows + 1):
             piece = rows[row * group : (row + 1) * group]
             split_ref[slot, :, row * lanes : (row + 1) * lanes] = shifts_of(piece).astype(bf16)
@@ -194,9 +194,7 @@
     down_bias_ref,
     far_tap_ref,
     far_order_ref,
-    col_ref,
     edge_ref,
-    merge_ref,
     edge_t_ref,
     out_ref,
     gpre_ref,
@@ -268,7 +266,7 @@
             rows.append(jnp.concatenate(sides, axis=0).astype(bf16))
         rows = dot(edge_ref[...], jnp.concatenate(rows, axis=1)).astype(bf16)
         rows = [rows[:, slot * width : (slot + 1) * width] for slot in range(pairs + 1)]
-        rows = dot(jnp.concatenate(rows, axis=0), col_ref[...])
+        rows = dot(jnp.concatenate(rows, axis=0), merge_table(2 * lanes, turned=True))
         for slot in range(pairs + 1):
             for side in range(2):
                 first = (2 * slot + side) * group
@@ -379,7 +377,7 @@
             first = pl.multiple_of((here ^ far) * rows, rows)
             ref[:, : 8 * hidden] = whole_ref[pl.ds(first, rows)]
             ref[:, 8 * hidden :] = small
-        sides_of(channels, pairs, outer_ref, conv_t_ref, merge_ref, edge_t_ref, to_before_ref, to_after_ref)
+        sides_of(channels, pairs, outer_ref, conv_t_ref, edge_t_ref, to_before_ref, to_after_ref)
 
 
 def merged(piece, group):
@@ -391,7 +389,7 @@
     return jnp.concatenate(halves, axis=1)
 
 
-def sides_of(channels, pairs, outer_ref, conv_t_ref, merge_ref, edge_t_ref, before_ref, after_ref):
+def sides_of(channels, pairs, outer_ref, conv_t_ref, edge_t_ref, before_ref, after_ref):
     group = 4 * channels
     span = 4 * group
     found = []
@@ -415,7 +413,7 @@
     for value in split_two(jnp.concatenate(rows, axis=1)):
         value = dot(edge_t_ref[...], value).astype(bf16)
         value = [value[:, slot * width : (slot + 1) * width] for slot in range(pairs + 1)]
-        sides = sides + dot(jnp.concatenate(value, axis=0), merge_ref[...])
+        sides = sides + dot(jnp.concatenate(value, axis=0), merge_table(2 * lanes))
     for at in range(2 * pairs + 2):
         before_ref[at] = sides[at * 16 : at * 16 + 8].astype(bf16)
         after_ref[at] = sides[at * 16 + 8 : at * 16 + 16].astype(bf16)
@@ -424,11 +422,11 @@
 def spread_kernel(sizes, *refs):
     channels, depth, half_rows, tile, plan = sizes
     pairs, slots, taken, done, given = plan
-    gpre_ref, conv_t_ref, merge_ref, row_t_ref = refs[:4]
-    rest = refs[4:-1]
+    gpre_ref, conv_t_ref, row_t_ref = refs[:3]
+    rest = refs[3:-1]
     spread_ref = refs[-1]
     if taken:
-        rest, spread_ref = refs[4:-6], refs[-6]
+        rest, spread_ref = refs[3:-6], refs[-6]
         taken_refs = rest[: len(taken)]
         outer_ref, *far_refs, out_ref = rest[len(taken) :]
         near_refs, sems = refs[-5:-1], refs[-1]
@@ -463,7 +461,7 @@
         ]
         core = 0.0
         for value in split_two(jnp.concatenate(rows, axis=0)):
-            core = core + dot(dot(row_t_ref[...], value).astype(bf16), merge_ref[...])
+            core = core + dot(dot(row_t_ref[...], value).astype(bf16), merge_table(2 * lanes))
         for par in range(2):
             for ch in range(channels):
                 first = (par * channels + ch) * row_count
@@ -546,11 +544,9 @@
     return pl.BlockSpec(tuple(shape), lambda z: (0,) * len(shape))
 
 
-def constants(channels, row_count, half_cols, hidden):
+def constants(channels, row_count, hidden):
     core, edge = row_spread(channels, row_count)
     names = {
-        "col": column_merge(half_cols).T,
-        "merge": column_merge(half_cols),
         "row": core,
         "row_t": core.T,
         "edge": edge,
@@ -613,7 +609,7 @@
             jax.ShapeDtypeStruct((big, out_count), bf16),
         ],
         fields, below, above, conv_weight, conv_bias[None], down_weight,
-        fixed["tap"], fixed["order"], fixed["col"], fixed["row"],
+        fixed["tap"], fixed["order"], fixed["row"],
         flops=2 * fields.size * row_count * channels * 4,
         name="prepare",
     )
@@ -626,7 +622,7 @@
     cells = half_rows * half_cols
     args = (
         early, before, after, target, conv, conv_t, down, down_t, down_bias[None],
-        fixed["tap"], fixed["order"], fixed["col"], fixed["edge"], fixed["merge"], fixed["edge_t"],
+        fixed["tap"], fixed["order"], fixed["edge"], fixed["edge_t"],
     )
     slab = pl.BlockSpec((out_count, 1, half_rows, half_cols), lambda z: (0, z, 0, 0))
     rows = out_count // groups
@@ -686,7 +682,7 @@
     _, big, cells = grad_pre.shape
     pairs, slots, _, done, given = plan
     open_shape = (16 * channels, cells + lanes)
-    args = (grad_pre, conv_t, fixed["merge"], fixed["row_t"], *taken, *beside)
+    args = (grad_pre, conv_t, fixed["row_t"], *taken, *beside)
     if taken:
         outs = [jax.ShapeDtypeStruct(shape, f32)]
     else:
@@ -724,7 +720,7 @@
     taps = channels * 27
     big = 8 * hidden
     cell_total = fields.size // channels // 8 * lax.axis_size("gz") * lax.axis_size("gy")
-    fixed = constants(channels, row_count, col_count // 2, hidden)
+    fixed = constants(channels, row_count, hidden)
 
     below = shifted(fields[:, depth - 1], "gz", 1)
     above = shifted(fields[:, 0], "gz", -1)
@@ -741,10 +737,9 @@
     pairs = depth // 2
     shape = fields.shape
 
+    got = [exchanged(message, "gz", 2 * far) for far, message in enumerate(messages) if far > 0]
     from_before = shifted(to_after, "gy", 1)
     from_after = shifted(to_before, "gy", -1)
-    got = [exchanged(message, "gz", 2 * far) for far, message in enumerate(messages) if far > 0]
-    from_before, from_after, *got = lax.optimization_barrier((from_before, from_after, *got))
     outer = ((0, pairs - 1), (0, 1, pairs - 1, pairs), (), (0, pairs), (1, pairs - 1))
     outer_core, low_open, high_open = spread(grad_pre, conv_t, fixed, shape, outer)
     packed = sum(got, messages[0])

time: 69.2 us -> 65.9 us (0.952)
  starting transfers between devices: 21.4 us -> 19.7 us
  local copies, waits for them, and re-layouts: 5.17 us -> 4.26 us
    ppermute x7, waiting for transfers between devices: 3.83 us -> 0.23 us  [exchanged(): return lax.ppermute(value, axis, [(i, i ^ bit) for i in range(count)])]
    ppermute x8, waiting for transfers between devices: 1.36 us -> 4.32 us  [shifted(): lax.ppermute(value, axis, [(i, (i + by) % count) for i in range(count)])]
    ppermute x8, starting transfers between devices: 13.3 us -> 11.6 us  [shifted(): lax.ppermute(value, axis, [(i, (i + by) % count) for i in range(count)])]
    unnamed x34 -> x28, local copies, waits for them, and re-layouts: 4.04 us -> 3.12 us
where the time goes in v11:
time: 65.9 us; the launch traced here: 65.7 us
  Pallas kernels  35.9 us (54%)
  starting transfers between devices  19.7 us (30%)
  waiting for transfers between devices  4.56 us (7%)
  local copies, waits for them, and re-layouts  4.26 us (6%)
  between operations  1.14 us (2%)
    pallas_call x7, Pallas kernels, call(): pl.pallas_call(functools.partial(kernel, sizes), out_shape=out_shape, in_...  35.9 us
    ppermute x8, starting transfers between devices, shifted(): lax.ppermute(value, axis, [(i, (i + by) % count) for i in range(count)])  11.6 us
    ppermute x7, starting transfers between devices, exchanged(): return lax.ppermute(value, axis, [(i, i ^ bit) for i in range(count)])  8.08 us
    ppermute x8, waiting for transfers between devices, shifted(): lax.ppermute(value, axis, [(i, (i + by) % count) for i in range(count)])  4.32 us
    unnamed x28, local copies, waits for them, and re-layouts  3.12 us
  transfers between devices with their start and end apart: 15, of which 4 were waited for; matrix products, arithmetic and copies ran while one was open for 0% of the time, Pallas kernels for 16%

profile of v11, /device:TPU:0, one launch (start us, length us, event | category | flops | bytes accessed | tf_op | source)
XLA Modules:
  0.0 65.7 jit_solution(10089056339109949612)
XLA Ops:
  0.6 0.0 copy-start.6
  0.7 1.0 %slice_bitcast_fusion = (bf16[6,32,256]{2,1,0:T(8,128)(2,1)S(1)}, bf16[6,32,256]{2,1,0:T(8,128)(2,1)S(1)}) fusion(bf16[6,8,32,256]{3,2,1,0:T(8,128)(2,1)} %high_ref.1), kind=kLoop, calls=%fused_computation.10 | loop fusion | bytes 393216 | tf_op jit(solution)/shard_map/squeeze | solution.py:726
  1.7 0.5 collective-permute-start
  2.2 2.9 %collective-permute-start.1 = (bf16[6,32,256]{2,1,0:T(8,128)(2,1)S(1)}, bf16[6,32,256]{2,1,0:T(8,128)(2,1)S(1)}, u32[]{:S(2)}, u32[]{:S(2)}) collective-permute-start(bf16[6,32,256]{2,1,0:T(8,128)(2,1)S(1)} %get-tuple-element.63), channel_id=1, source_target_pairs={{0,28},{4,0},{8,4},{12,8},{16,12},{20,16},{24,20},{28,24},{1,29},{... | collective-permute-start | bytes 294920 | tf_op jit(solution)/shard_map/ppermute | solution.py:20
  5.1 1.1 %copy-done = bf16[6,8,32,256]{3,2,1,0:T(8,128)(2,1)S(1)} copy-done((bf16[6,8,32,256]{3,2,1,0:T(8,128)(2,1)S(1)}, bf16[6,8,32,256]{3,2,1,0:T(8,128)(2,1)}, u32[]{:S(2)}) %copy-start) | copy-done | bytes 786456
  6.3 0.0 copy-start.13
  6.3 0.1 rows.1
  6.4 0.1 pad.4.clone
  6.5 0.9 %collective-permute-done.below_ref.refs_2_ = bf16[6,32,256]{2,1,0:T(8,128)(2,1)S(1)} collective-permute-done((bf16[6,32,256]{2,1,0:T(8,128)(2,1)S(1)}, bf16[6,32,256]{2,1,0:T(8,128)(2,1)S(1)}, u32[]{:S(2)}, u32[]{:S(2)}) %collective-permute-start) | collective-permute-done | bytes 98336 | tf_op jit(solution)/shard_map/ppermute | solution.py:20
  7.4 0.0 collective-permute-done.1.above_ref.refs_3_
  7.4 0.4 more_rows.1
  7.8 2.4 %collective-permute-start.2 = (bf16[10,8,256]{2,1,0:T(8,128)(2,1)S(1)}, bf16[10,8,256]{2,1,0:T(8,128)(2,1)S(1)}, u32[]{:S(2)}, u32[]{:S(2)}) collective-permute-start(bf16[10,8,256]{2,1,0:T(8,128)(2,1)S(1)} %get-tuple-element.37), channel_id=1, source_target_pairs={{0,1},{1,2},{2,3},{3,0},{4,5},{5,6},{6,7},{7,4},{8,9},{9,10},{10,1... | collective-permute-start | bytes 122888 | tf_op jit(solution)/shard_map/ppermute | solution.py:20
  10.1 2.1 %collective-permute-start.3 = (bf16[10,8,256]{2,1,0:T(8,128)(2,1)S(1)}, bf16[10,8,256]{2,1,0:T(8,128)(2,1)S(1)}, u32[]{:S(2)}, u32[]{:S(2)}) collective-permute-start(bf16[10,8,256]{2,1,0:T(8,128)(2,1)S(1)} %get-tuple-element.38), channel_id=1, source_target_pairs={{0,3},{1,0},{2,1},{3,2},{4,7},{5,4},{6,5},{7,6},{8,11},{9,8},{10,9... | collective-permute-start | bytes 122888 | tf_op jit(solution)/shard_map/ppermute | solution.py:20
  12.2 0.0 copy-start.4
  12.3 1.0 %copy-done.4 = bf16[512,512]{1,0:T(8,128)(2,1)S(1)} copy-done((bf16[512,512]{1,0:T(8,128)(2,1)S(1)}, bf16[512,512]{1,0:T(8,128)(2,1)}, u32[]{:S(2)}) %copy-start.4) | copy-done | bytes 524312
  13.3 0.9 %copy-done.7 = bf16[128,512]{1,0:T(8,128)(2,1)S(1)} copy-done((bf16[128,512]{1,0:T(8,128)(2,1)S(1)}, bf16[128,512]{1,0:T(8,128)(2,1)}, u32[]{:S(2)}) %copy-start.7) | copy-done | bytes 131096
  14.2 2.2 %prepare.1 = (bf16[5,96,2176]{2,1,0:T(8,128)(2,1)S(1)}, bf16[512,400]{1,0:T(8,128)(2,1)S(1)}, bf16[384,512]{1,0:T(8,128)(2,1)S(1)}, bf16[128,512]{1,0:T(8,128)(2,1)S(1)}, bf16[512,128]{1,0:T(8,128)(2,1)S(1)}) custom-call(bf16[6,8,32,256]{3,2,1,0:T(8,128)(2,1)S(1)} %copy-done.1, bf16[6,32,256]{2,1,0:T(8,128)(2,1)S(1)} %collective-permute-done.below_ref.refs_2_, ...), custom_call_target="tpu_custom_call" | custom-call | flops 603979776 | bytes 6121984 | tf_op jit(solution)/shard_map/prepare/pallas_call | solution.py:526
  16.4 0.0 collective-permute-done.2.far_before_ref
  16.4 0.0 collective-permute-done.3.far_after_ref
  16.5 0.0 copy-start.2
  16.5 23.5 %forward.1 = (bf16[128,4,16,128]{3,2,1,0:T(8,128)(2,1)}, bf16[4,512,2048]{2,1,0:T(8,128)(2,1)S(1)}, bf16[10,8,256]{2,1,0:T(8,128)(2,1)S(1)}, bf16[10,8,256]{2,1,...) custom-call(bf16[5,96,2176]{2,1,0:T(8,128)(2,1)S(1)} %get-tuple-elem, ...), custom_call_target="tpu_custom_call" | custom-call | flops 8589934592 | bytes 17951232 | tf_op jit(solution)/shard_map/forward/pallas_call | solution.py:526
  40.0 1.8 %collective-permute-start.6 = (f32[32,1024]{1,0:T(8,128)S(1)}, f32[32,1024]{1,0:T(8,128)S(1)}, u32[]{:S(2)}, u32[]{:S(2)}) collective-permute-start(f32[32,1024]{1,0:T(8,128)S(1)} %get-tuple-element.48), channel_id=1, source_target_pairs={{0,24},{4,28},{8,16},{12,20},{16,8},{20,12},{24,0},{28,4},{1,25},{... | collective-permute-start | bytes 393224 | tf_op jit(solution)/shard_map/ppermute | solution.py:25
  41.8 0.5 collective-permute-start.5
  42.3 1.2 %collective-permute-start.4 = (f32[32,1024]{1,0:T(8,128)S(1)}, f32[32,1024]{1,0:T(8,128)S(1)}, u32[]{:S(2)}, u32[]{:S(2)}) collective-permute-start(f32[32,1024]{1,0:T(8,128)S(1)} %get-tuple-element.46), channel_id=1, source_target_pairs={{0,8},{4,12},{8,0},{12,4},{16,24},{20,28},{24,16},{28,20},{1,9},{5... | collective-permute-start | bytes 393224 | tf_op jit(solution)/shard_map/ppermute | solution.py:25
  43.6 2.0 %collective-permute-start.9 = (bf16[10,8,256]{2,1,0:T(8,128)(2,1)S(1)}, bf16[10,8,256]{2,1,0:T(8,128)(2,1)S(1)}, u32[]{:S(2)}, u32[]{:S(2)}) collective-permute-start(bf16[10,8,256]{2,1,0:T(8,128)(2,1)S(1)} %get-tuple-element.54), channel_id=1, source_target_pairs={{0,3},{1,0},{2,1},{3,2},{4,7},{5,4},{6,5},{7,6},{8,11},{9,8},{10,9... | collective-permute-start | bytes 122888 | tf_op jit(solution)/shard_map/ppermute | solution.py:20
  45.5 0.1 collective-permute-start.8
  45.6 0.0 copy-done.2
  45.6 3.1 %spread.2 = (f32[4,6,32,256]{3,2,1,0:T(8,128)S(1)}, f32[96,2176]{1,0:T(8,128)S(1)}, f32[96,2176]{1,0:T(8,128)S(1)}) custom-call(bf16[4,512,2048]{2,1,0:T(8,128)(2,1)S(1)} %get-tuple-element.44.refs_0_, bf16[384,512]{1,0:T(8,128)(2,1)S(1)} %get-tuple-element.40.conv_t_ref.refs_1_, bf16[384,408]{1,0:T(8,128)(2,1)S(1)} %copy-done.2), custom_call_target="tpu_custom_call" | custom-call | flops 1610612736 | bytes 11552768 | tf_op jit(solution)/shard_map/spread/pallas_call | solution.py:526
  48.7 0.0 collective-permute-done.9.refs_8_
  48.7 2.6 %collective-permute-done.8.refs_9_ = bf16[10,8,256]{2,1,0:T(8,128)(2,1)S(1)} collective-permute-done((bf16[10,8,256]{2,1,0:T(8,128)(2,1)S(1)}, bf16[10,8,256]{2,1,0:T(8,128)(2,1)S(1)}, u32[]{:S(2)}, u32[]{:S(2)}) %collective-permute-start.8) | collective-permute-done | bytes 40992 | tf_op jit(solution)/shard_map/ppermute | solution.py:20
  51.4 0.0 collective-permute-done.6
  51.4 0.0 collective-permute-done.5
  51.4 0.0 collective-permute-done.4
  51.5 0.1 collective-permute-start.7
  51.6 0.1 fusion.1
  51.7 1.7 %collective-permute-start.10 = (bf16[6,32,256]{2,1,0:T(8,128)(2,1)S(1)}, bf16[6,32,256]{2,1,0:T(8,128)(2,1)S(1)}, u32[]{:S(2)}, u32[]{:S(2)}) collective-permute-start(bf16[6,32,256]{2,1,0:T(8,128)(2,1)S(1)} %get-tuple-element.62), channel_id=1, source_target_pairs={{0,28},{4,0},{8,4},{12,8},{16,12},{20,16},{24,20},{28,24},{1,29},{... | collective-permute-start | bytes 294920 | tf_op jit(solution)/shard_map/ppermute | solution.py:20
  53.4 0.0 collective-permute-start.11
  53.4 0.0 collective-permute-done.7
  53.4 0.1 collective-permute-start.12
  53.5 1.8 %collective-permute-start.13 = (f32[16,1536]{1,0:T(8,128)S(1)}, f32[16,1536]{1,0:T(8,128)S(1)}, u32[]{:S(2)}, u32[]{:S(2)}) collective-permute-start(f32[16,1536]{1,0:T(8,128)S(1)} %fusion.2.refs_0_), channel_id=1, source_target_pairs={{0,2},{1,3},{2,0},{3,1},{4,6},{5,7},{6,4},{7,5},{8,10},{9,11},{10,... | collective-permute-start | bytes 294920 | tf_op jit(solution)/shard_map/ppermute | solution.py:25
  55.2 2.6 %collective-permute-start.14 = (f32[16,1536]{1,0:T(8,128)S(1)}, f32[16,1536]{1,0:T(8,128)S(1)}, u32[]{:S(2)}, u32[]{:S(2)}) collective-permute-start(f32[16,1536]{1,0:T(8,128)S(1)} %fusion.2.refs_0_), channel_id=1, source_target_pairs={{0,3},{1,2},{2,1},{3,0},{4,7},{5,6},{6,5},{7,4},{8,11},{9,10},{10,... | collective-permute-start | bytes 294920 | tf_op jit(solution)/shard_map/ppermute | solution.py:25
  57.9 0.0 collective-permute-done.10.refs_6_
  57.9 0.9 %collective-permute-done.11.refs_7_ = bf16[6,32,256]{2,1,0:T(8,128)(2,1)S(1)} collective-permute-done((bf16[6,32,256]{2,1,0:T(8,128)(2,1)S(1)}, bf16[6,32,256]{2,1,0:T(8,128)(2,1)S(1)}, u32[]{:S(2)}, u32[]{:S(2)}) %collective-permute-start.11) | collective-permute-done | bytes 98336 | tf_op jit(solution)/shard_map/ppermute | solution.py:20
  58.7 5.3 %spread.3 = f32[6,8,32,256]{3,2,1,0:T(8,128)} custom-call(bf16[4,512,2048]{2,1,0:T(8,128)(2,1)S(1)} %get-tuple-element.44.refs_0_, bf16[384,512]{1,0:T(8,128)(2,1)S(1)} %get-tuple-element.40.conv_t_ref.refs_1_, bf16[384,408]{1,0:T(8,128)(2,1)S(1)} %copy-done.2, f32[96,2176]{1,0:T(8,128)S(1)} %get-tuple-element.50.refs_3_, ...), custom_call_target="tpu_custom_call" | custom-call | flops 1610612736 | bytes 13404160 | tf_op jit(solution)/shard_map/spread/pallas_call | solution.py:526
  64.0 0.0 collective-permute-done.12.refs_1_
  64.1 0.2 collective-permute-done.13.refs_2_
  64.3 0.0 collective-permute-done.14.refs_3_
  64.3 1.3 %last.1 = (f32[64,162]{1,0:T(8,128)}, f32[1,64]{1,0:T(1,128)}, f32[16,512]{1,0:T(8,128)}, f32[1,128]{1,0:T(1,128)}, f32[1,1]{1,0:T(1,128)}) custom-call(f32[16,1536]{1,0:T(8,128)S(1)} %fusion.2.refs_0_, f32[16,1536]{1,0:T(8,128)S(1)} %collective-permute-done.12.refs_1_, f32[16,1536]{1,0:T(8,128)S(1)} %collective-permute-done.13.refs_2_, ...), custom_call_target="tpu_custom_call" | custom-call | bytes 468228 | tf_op jit(solution)/shard_map/last/pallas_call | solution.py:526
  (32 shorter events, 0.2 us)
Async XLA Ops:
  0.6 11.6 %copy-start.6 = (bf16[408,384]{1,0:T(8,128)(2,1)S(1)}, bf16[408,384]{1,0:T(8,128)(2,1)}, u32[]{:S(2)}) copy-start(bf16[408,384]{1,0:T(8,128)(2,1)} %constant.39.clone.row_ref) | copy-start | bytes 940036
  0.6 11.6 %copy-start.8 = (bf16[64,162]{1,0:T(8,128)(2,1)S(1)}, bf16[64,162]{1,0:T(8,128)(2,1)}, u32[]{:S(2)}) copy-start(bf16[64,162]{1,0:T(8,128)(2,1)} %conv_weight_ref.1) | copy-start | bytes 62212
  0.7 11.6 %copy-start.9 = (f32[64]{0:T(128)S(1)}, f32[64]{0:T(128)}, u32[]{:S(2)}) copy-start(f32[64]{0:T(128)} %param.15) | copy-start | bytes 772
  1.7 5.7 %collective-permute-start = (bf16[6,32,256]{2,1,0:T(8,128)(2,1)S(1)}, bf16[6,32,256]{2,1,0:T(8,128)(2,1)S(1)}, u32[]{:S(2)}, u32[]{:S(2)}) collective-permute-start(bf16[6,32,256]{2,1,0:T(8,128)(2,1)S(1)} %get-tuple-element.64), channel_id=1, source_target_pairs={{0,4},{4,8},{8,12},{12,16},{16,20},{20,24},{24,28},{28,0},{1,5},{5... | collective-permute-start | bytes 294920 | tf_op jit(solution)/shard_map/ppermute | solution.py:20
  2.2 5.2 %collective-permute-start.1 = (bf16[6,32,256]{2,1,0:T(8,128)(2,1)S(1)}, bf16[6,32,256]{2,1,0:T(8,128)(2,1)S(1)}, u32[]{:S(2)}, u32[]{:S(2)}) collective-permute-start(bf16[6,32,256]{2,1,0:T(8,128)(2,1)S(1)} %get-tuple-element.63), channel_id=1, source_target_pairs={{0,28},{4,0},{8,4},{12,8},{16,12},{20,16},{24,20},{28,24},{1,29},{... | collective-permute-start | bytes 294920 | tf_op jit(solution)/shard_map/ppermute | solution.py:20
  5.1 1.1 %copy-start = (bf16[6,8,32,256]{3,2,1,0:T(8,128)(2,1)S(1)}, bf16[6,8,32,256]{3,2,1,0:T(8,128)(2,1)}, u32[]{:S(2)}) copy-start(bf16[6,8,32,256]{3,2,1,0:T(8,128)(2,1)} %high_ref.1) | copy-start | bytes 2359300
  6.3 6.0 %copy-start.1 = (bf16[6,8,32,256]{3,2,1,0:T(8,128)(2,1)S(1)}, bf16[6,8,32,256]{3,2,1,0:T(8,128)(2,1)}, u32[]{:S(2)}) copy-start(bf16[6,8,32,256]{3,2,1,0:T(8,128)(2,1)} %high_ref.1) | copy-start | bytes 2359300
  6.3 6.0 %copy-start.3 = (bf16[8,162,384]{2,1,0:T(8,128)(2,1)S(1)}, bf16[8,162,384]{2,1,0:T(8,128)(2,1)}, u32[]{:S(2)}) copy-start(bf16[8,162,384]{2,1,0:T(8,128)(2,1)} %constant.43.clone.tap_ref.far_tap_ref) | copy-start | bytes 2985988
  6.3 10.2 %copy-start.11 = (f32[128]{0:T(128)S(1)}, f32[128]{0:T(128)}, u32[]{:S(2)}) copy-start(f32[128]{0:T(128)} %param.17) | copy-start | bytes 1540
  6.3 10.2 %copy-start.12 = (bf16[48,32]{1,0:T(8,128)(2,1)S(1)}, bf16[48,32]{1,0:T(8,128)(2,1)}, u32[]{:S(2)}) copy-start(bf16[48,32]{1,0:T(8,128)(2,1)} %constant.41.clone.edge_ref) | copy-start | bytes 9220
  6.3 10.2 %copy-start.13 = (bf16[32,48]{1,0:T(8,128)(2,1)S(1)}, bf16[32,48]{1,0:T(8,128)(2,1)}, u32[]{:S(2)}) copy-start(bf16[32,48]{1,0:T(8,128)(2,1)} %constant.42.clone.edge_t_ref) | copy-start | bytes 9220
  7.8 8.7 %collective-permute-start.2 = (bf16[10,8,256]{2,1,0:T(8,128)(2,1)S(1)}, bf16[10,8,256]{2,1,0:T(8,128)(2,1)S(1)}, u32[]{:S(2)}, u32[]{:S(2)}) collective-permute-start(bf16[10,8,256]{2,1,0:T(8,128)(2,1)S(1)} %get-tuple-element.37), channel_id=1, source_target_pairs={{0,1},{1,2},{2,3},{3,0},{4,5},{5,6},{6,7},{7,4},{8,9},{9,10},{10,1... | collective-permute-start | bytes 122888 | tf_op jit(solution)/shard_map/ppermute | solution.py:20
  10.1 6.3 %collective-permute-start.3 = (bf16[10,8,256]{2,1,0:T(8,128)(2,1)S(1)}, bf16[10,8,256]{2,1,0:T(8,128)(2,1)S(1)}, u32[]{:S(2)}, u32[]{:S(2)}) collective-permute-start(bf16[10,8,256]{2,1,0:T(8,128)(2,1)S(1)} %get-tuple-element.38), channel_id=1, source_target_pairs={{0,3},{1,0},{2,1},{3,2},{4,7},{5,4},{6,5},{7,6},{8,11},{9,8},{10,9... | collective-permute-start | bytes 122888 | tf_op jit(solution)/shard_map/ppermute | solution.py:20
  12.2 1.0 %copy-start.4 = (bf16[512,512]{1,0:T(8,128)(2,1)S(1)}, bf16[512,512]{1,0:T(8,128)(2,1)}, u32[]{:S(2)}) copy-start(bf16[512,512]{1,0:T(8,128)(2,1)} %constant.44.clone.order_ref.far_order_ref) | copy-start | bytes 1572868
  13.3 0.9 %copy-start.7 = (bf16[128,512]{1,0:T(8,128)(2,1)S(1)}, bf16[128,512]{1,0:T(8,128)(2,1)}, u32[]{:S(2)}) copy-start(bf16[128,512]{1,0:T(8,128)(2,1)} %down_weight_ref.1) | copy-start | bytes 393220
  14.2 2.3 %copy-start.5 = (bf16[512,512]{1,0:T(8,128)(2,1)S(1)}, bf16[512,512]{1,0:T(8,128)(2,1)}, u32[]{:S(2)}) copy-start(bf16[512,512]{1,0:T(8,128)(2,1)} %constant.44.clone.order_ref.far_order_ref) | copy-start | bytes 1572868
  14.2 2.3 %copy-start.10 = (bf16[128,4,16,128]{3,2,1,0:T(8,128)(2,1)S(1)}, bf16[128,4,16,128]{3,2,1,0:T(8,128)(2,1)}, u32[]{:S(2)}) copy-start(bf16[128,4,16,128]{3,2,1,0:T(8,128)(2,1)} %target_ref.1) | copy-start | bytes 6291460
  16.5 29.1 %copy-start.2 = (bf16[384,408]{1,0:T(8,128)(2,1)S(1)}, bf16[384,408]{1,0:T(8,128)(2,1)}, u32[]{:S(2)}) copy-start(bf16[384,408]{1,0:T(8,128)(2,1)} %constant.40.clone.refs_2_) | copy-start | bytes 940036
  40.0 11.4 %collective-permute-start.6 = (f32[32,1024]{1,0:T(8,128)S(1)}, f32[32,1024]{1,0:T(8,128)S(1)}, u32[]{:S(2)}, u32[]{:S(2)}) collective-permute-start(f32[32,1024]{1,0:T(8,128)S(1)} %get-tuple-element.48), channel_id=1, source_target_pairs={{0,24},{4,28},{8,16},{12,20},{16,8},{20,12},{24,0},{28,4},{1,25},{... | collective-permute-start | bytes 393224 | tf_op jit(solution)/shard_map/ppermute | solution.py:25
  41.8 9.6 %collective-permute-start.5 = (f32[32,1024]{1,0:T(8,128)S(1)}, f32[32,1024]{1,0:T(8,128)S(1)}, u32[]{:S(2)}, u32[]{:S(2)}) collective-permute-start(f32[32,1024]{1,0:T(8,128)S(1)} %get-tuple-element.47), channel_id=1, source_target_pairs={{0,16},{4,20},{8,24},{12,28},{16,0},{20,4},{24,8},{28,12},{1,17},{... | collective-permute-start | bytes 393224 | tf_op jit(solution)/shard_map/ppermute | solution.py:25
  42.3 9.1 %collective-permute-start.4 = (f32[32,1024]{1,0:T(8,128)S(1)}, f32[32,1024]{1,0:T(8,128)S(1)}, u32[]{:S(2)}, u32[]{:S(2)}) collective-permute-start(f32[32,1024]{1,0:T(8,128)S(1)} %get-tuple-element.46), channel_id=1, source_target_pairs={{0,8},{4,12},{8,0},{12,4},{16,24},{20,28},{24,16},{28,20},{1,9},{5... | collective-permute-start | bytes 393224 | tf_op jit(solution)/shard_map/ppermute | solution.py:25
  43.6 5.2 %collective-permute-start.9 = (bf16[10,8,256]{2,1,0:T(8,128)(2,1)S(1)}, bf16[10,8,256]{2,1,0:T(8,128)(2,1)S(1)}, u32[]{:S(2)}, u32[]{:S(2)}) collective-permute-start(bf16[10,8,256]{2,1,0:T(8,128)(2,1)S(1)} %get-tuple-element.54), channel_id=1, source_target_pairs={{0,3},{1,0},{2,1},{3,2},{4,7},{5,4},{6,5},{7,6},{8,11},{9,8},{10,9... | collective-permute-start | bytes 122888 | tf_op jit(solution)/shard_map/ppermute | solution.py:20
  45.5 5.8 %collective-permute-start.8 = (bf16[10,8,256]{2,1,0:T(8,128)(2,1)S(1)}, bf16[10,8,256]{2,1,0:T(8,128)(2,1)S(1)}, u32[]{:S(2)}, u32[]{:S(2)}) collective-permute-start(bf16[10,8,256]{2,1,0:T(8,128)(2,1)S(1)} %get-tuple-element.53), channel_id=1, source_target_pairs={{0,1},{1,2},{2,3},{3,0},{4,5},{5,6},{6,7},{7,4},{8,9},{9,10},{10,1... | collective-permute-start | bytes 122888 | tf_op jit(solution)/shard_map/ppermute | solution.py:20
  51.5 1.9 %collective-permute-start.7 = (f32[16,1536]{1,0:T(8,128)S(1)}, f32[16,1536]{1,0:T(8,128)S(1)}, u32[]{:S(2)}, u32[]{:S(2)}) collective-permute-start(f32[16,1536]{1,0:T(8,128)S(1)} %pad_maximum_fusion), channel_id=1, source_target_pairs={{0,4},{4,0},{8,12},{12,8},{16,20},{20,16},{24,28},{28,24},{1,5},{5... | collective-permute-start | bytes 294920 | tf_op jit(solution)/shard_map/ppermute | solution.py:25
  51.7 6.2 %collective-permute-start.10 = (bf16[6,32,256]{2,1,0:T(8,128)(2,1)S(1)}, bf16[6,32,256]{2,1,0:T(8,128)(2,1)S(1)}, u32[]{:S(2)}, u32[]{:S(2)}) collective-permute-start(bf16[6,32,256]{2,1,0:T(8,128)(2,1)S(1)} %get-tuple-element.62), channel_id=1, source_target_pairs={{0,28},{4,0},{8,4},{12,8},{16,12},{20,16},{24,20},{28,24},{1,29},{... | collective-permute-start | bytes 294920 | tf_op jit(solution)/shard_map/ppermute | solution.py:20
  53.4 5.3 %collective-permute-start.11 = (bf16[6,32,256]{2,1,0:T(8,128)(2,1)S(1)}, bf16[6,32,256]{2,1,0:T(8,128)(2,1)S(1)}, u32[]{:S(2)}, u32[]{:S(2)}) collective-permute-start(bf16[6,32,256]{2,1,0:T(8,128)(2,1)S(1)} %get-tuple-element.61), channel_id=1, source_target_pairs={{0,4},{4,8},{8,12},{12,16},{16,20},{20,24},{24,28},{28,0},{1,5},{5... | collective-permute-start | bytes 294920 | tf_op jit(solution)/shard_map/ppermute | solution.py:20
  53.4 10.7 %collective-permute-start.12 = (f32[16,1536]{1,0:T(8,128)S(1)}, f32[16,1536]{1,0:T(8,128)S(1)}, u32[]{:S(2)}, u32[]{:S(2)}) collective-permute-start(f32[16,1536]{1,0:T(8,128)S(1)} %fusion.2.refs_0_), channel_id=1, source_target_pairs={{0,1},{1,0},{2,3},{3,2},{4,5},{5,4},{6,7},{7,6},{8,9},{9,8},{10,11... | collective-permute-start | bytes 294920 | tf_op jit(solution)/shard_map/ppermute | solution.py:25
  53.5 10.8 %collective-permute-start.13 = (f32[16,1536]{1,0:T(8,128)S(1)}, f32[16,1536]{1,0:T(8,128)S(1)}, u32[]{:S(2)}, u32[]{:S(2)}) collective-permute-start(f32[16,1536]{1,0:T(8,128)S(1)} %fusion.2.refs_0_), channel_id=1, source_target_pairs={{0,2},{1,3},{2,0},{3,1},{4,6},{5,7},{6,4},{7,5},{8,10},{9,11},{10,... | collective-permute-start | bytes 294920 | tf_op jit(solution)/shard_map/ppermute | solution.py:25
  55.2 9.0 %collective-permute-start.14 = (f32[16,1536]{1,0:T(8,128)S(1)}, f32[16,1536]{1,0:T(8,128)S(1)}, u32[]{:S(2)}, u32[]{:S(2)}) collective-permute-start(f32[16,1536]{1,0:T(8,128)S(1)} %fusion.2.refs_0_), channel_id=1, source_target_pairs={{0,3},{1,2},{2,1},{3,0},{4,7},{5,6},{6,5},{7,4},{8,11},{9,10},{10,... | collective-permute-start | bytes 294920 | tf_op jit(solution)/shard_map/ppermute | solution.py:25

commit v12 on v11

--- a/solution.py
+++ b/solution.py
@@ -485,7 +485,9 @@
                 fetched(list(zip(far_refs, near_refs, strict=True)), sems)
                 for ch in range(channels):
                     lay_out(1, ch, outer_ref[1, ch] + above_ref[ch].astype(f32))
-                    lay_out(depth, ch, outer_ref[2, ch] + below_ref[ch].astype(f32))
+                    lay_out(2, ch, outer_ref[2, ch])
+                    lay_out(3, ch, outer_ref[3, ch])
+                    lay_out(depth, ch, outer_ref[4, ch] + below_ref[ch].astype(f32))
             for slot in done:
                 if k > 0 and pairs[k - 1] in (slot - 1, slot) and not set(pairs[k:]) & {slot - 1, slot}:
                     finish(slot)
@@ -688,15 +690,20 @@
     else:
         outs = [jax.ShapeDtypeStruct((2 * len(done), channels, row_count, col_count), f32)]
     outs += [jax.ShapeDtypeStruct(open_shape, f32)] * len(given)
-    first = pairs[0]
-    stride = pairs[1] - first if len(pairs) > 1 else 1
+
+    def block_of(z):
+        at = pairs[0]
+        for k, pair in enumerate(pairs[1:]):
+            at = jnp.where(z == k + 1, pair, at)
+        return at, 0, 0
+
     return call(
         spread_kernel,
         (channels, depth, row_count // 2, spread_tile, plan),
         outs,
         *args,
         grid=(len(pairs),),
-        in_specs=[pl.BlockSpec((1, big, cells), lambda z: (first + stride * z, 0, 0))]
+        in_specs=[pl.BlockSpec((1, big, cells), block_of)]
         + [whole(a.shape) for a in args[1 : len(args) - len(beside[1:])]]
         + [pl.BlockSpec(memory_space=pl.ANY) for _ in beside[1:]],
         out_specs=[whole(o.shape) for o in outs],
@@ -740,7 +747,7 @@
     got = [exchanged(message, "gz", 2 * far) for far, message in enumerate(messages) if far > 0]
     from_before = shifted(to_after, "gy", 1)
     from_after = shifted(to_before, "gy", -1)
-    outer = ((0, pairs - 1), (0, 1, pairs - 1, pairs), (), (0, pairs), (1, pairs - 1))
+    outer = ((0, pairs - 1, 1), (0, 1, 2, pairs - 1, pairs), (), (0, 1, pairs), (2, pairs - 1))
     outer_core, low_open, high_open = spread(grad_pre, conv_t, fixed, shape, outer)
     packed = sum(got, messages[0])
 
@@ -750,7 +757,7 @@
         gap = jnp.zeros((channels, row_count - 2, col_count), f32)
         return (value + jnp.concatenate([low, gap, high], axis=1)).astype(bf16)
 
-    from_below = shifted(plane(outer_core[3], depth + 1), "gz", 1)
+    from_below = shifted(plane(outer_core[5], depth + 1), "gz", 1)
     from_above = shifted(plane(outer_core[0], 0), "gz", -1)
     count = packed.shape[0] // 2
     core = lax.axis_index("gz") % 2
@@ -761,7 +768,7 @@
 
     packed, low_open = lax.optimization_barrier((packed, low_open))
     got = [exchanged(packed, "gy", far) for far in range(1, lax.axis_size("gy"))]
-    inner = tuple(range(1, pairs - 1)), tuple(range(1, pairs)), (1, pairs - 1), tuple(range(1, pairs)), ()
+    inner = tuple(range(2, pairs - 1)), tuple(range(2, pairs)), (2, pairs - 1), tuple(range(2, pairs)), ()
     (sensitivity,) = spread(
         grad_pre, conv_t, fixed, shape, inner, (low_open, high_open),
         (outer_core, from_above, from_below, from_after, from_before),

time: 65.9 us -> 66.3 us (level)
    ppermute x7, waiting for transfers between devices: 0.23 us -> 2.3 us  [exchanged(): return lax.ppermute(value, axis, [(i, i ^ bit) for i in range(count)])]
    ppermute x8, waiting for transfers between devices: 4.32 us -> 2.72 us  [shifted(): lax.ppermute(value, axis, [(i, (i + by) % count) for i in range(count)])]
where the time goes in v12:
time: 66.3 us; the launch traced here: 66.1 us
  Pallas kernels  35.8 us (54%)
  starting transfers between devices  19.7 us (30%)
  waiting for transfers between devices  5.02 us (8%)
  local copies, waits for them, and re-layouts  4.26 us (6%)
  between operations  1.14 us (2%)
    pallas_call x7, Pallas kernels, call(): pl.pallas_call(functools.partial(kernel, sizes), out_shape=out_shape, in_...  35.8 us
    ppermute x8, starting transfers between devices, shifted(): lax.ppermute(value, axis, [(i, (i + by) % count) for i in range(count)])  11.6 us
    ppermute x7, starting transfers between devices, exchanged(): return lax.ppermute(value, axis, [(i, i ^ bit) for i in range(count)])  8.08 us
    unnamed x28, local copies, waits for them, and re-layouts  3.12 us
    ppermute x8, waiting for transfers between devices, shifted(): lax.ppermute(value, axis, [(i, (i + by) % count) for i in range(count)])  2.72 us
    ppermute x7, waiting for transfers between devices, exchanged(): return lax.ppermute(value, axis, [(i, i ^ bit) for i in range(count)])  2.3 us
  transfers between devices with their start and end apart: 15, of which 4 were waited for; matrix products, arithmetic and copies ran while one was open for 0% of the time, Pallas kernels for 16%

profile of v12, /device:TPU:0, one launch (start us, length us, event | category | flops | bytes accessed | tf_op | source)
XLA Modules:
  0.0 66.1 jit_solution(550783431253427350)
XLA Ops:
  0.6 0.0 copy-start.6
  0.7 1.0 %slice_bitcast_fusion = (bf16[6,32,256]{2,1,0:T(8,128)(2,1)S(1)}, bf16[6,32,256]{2,1,0:T(8,128)(2,1)S(1)}) fusion(bf16[6,8,32,256]{3,2,1,0:T(8,128)(2,1)} %high_ref.1), kind=kLoop, calls=%fused_computation.10 | loop fusion | bytes 393216 | tf_op jit(solution)/shard_map/squeeze | solution.py:733
  1.7 0.5 collective-permute-start
  2.2 2.9 %collective-permute-start.1 = (bf16[6,32,256]{2,1,0:T(8,128)(2,1)S(1)}, bf16[6,32,256]{2,1,0:T(8,128)(2,1)S(1)}, u32[]{:S(2)}, u32[]{:S(2)}) collective-permute-start(bf16[6,32,256]{2,1,0:T(8,128)(2,1)S(1)} %get-tuple-element.63), channel_id=1, source_target_pairs={{0,28},{4,0},{8,4},{12,8},{16,12},{20,16},{24,20},{28,24},{1,29},{... | collective-permute-start | bytes 294920 | tf_op jit(solution)/shard_map/ppermute | solution.py:20
  5.1 1.1 %copy-done = bf16[6,8,32,256]{3,2,1,0:T(8,128)(2,1)S(1)} copy-done((bf16[6,8,32,256]{3,2,1,0:T(8,128)(2,1)S(1)}, bf16[6,8,32,256]{3,2,1,0:T(8,128)(2,1)}, u32[]{:S(2)}) %copy-start) | copy-done | bytes 786456
  6.3 0.0 copy-start.13
  6.3 0.1 rows.1
  6.4 0.1 pad.4.clone
  6.5 0.9 %collective-permute-done.below_ref.refs_2_ = bf16[6,32,256]{2,1,0:T(8,128)(2,1)S(1)} collective-permute-done((bf16[6,32,256]{2,1,0:T(8,128)(2,1)S(1)}, bf16[6,32,256]{2,1,0:T(8,128)(2,1)S(1)}, u32[]{:S(2)}, u32[]{:S(2)}) %collective-permute-start) | collective-permute-done | bytes 98336 | tf_op jit(solution)/shard_map/ppermute | solution.py:20
  7.4 0.0 collective-permute-done.1.above_ref.refs_3_
  7.4 0.4 more_rows.1
  7.8 2.4 %collective-permute-start.2 = (bf16[10,8,256]{2,1,0:T(8,128)(2,1)S(1)}, bf16[10,8,256]{2,1,0:T(8,128)(2,1)S(1)}, u32[]{:S(2)}, u32[]{:S(2)}) collective-permute-start(bf16[10,8,256]{2,1,0:T(8,128)(2,1)S(1)} %get-tuple-element.37), channel_id=1, source_target_pairs={{0,1},{1,2},{2,3},{3,0},{4,5},{5,6},{6,7},{7,4},{8,9},{9,10},{10,1... | collective-permute-start | bytes 122888 | tf_op jit(solution)/shard_map/ppermute | solution.py:20
  10.1 2.1 %collective-permute-start.3 = (bf16[10,8,256]{2,1,0:T(8,128)(2,1)S(1)}, bf16[10,8,256]{2,1,0:T(8,128)(2,1)S(1)}, u32[]{:S(2)}, u32[]{:S(2)}) collective-permute-start(bf16[10,8,256]{2,1,0:T(8,128)(2,1)S(1)} %get-tuple-element.38), channel_id=1, source_target_pairs={{0,3},{1,0},{2,1},{3,2},{4,7},{5,4},{6,5},{7,6},{8,11},{9,8},{10,9... | collective-permute-start | bytes 122888 | tf_op jit(solution)/shard_map/ppermute | solution.py:20
  12.2 0.0 copy-start.4
  12.3 1.0 %copy-done.4 = bf16[512,512]{1,0:T(8,128)(2,1)S(1)} copy-done((bf16[512,512]{1,0:T(8,128)(2,1)S(1)}, bf16[512,512]{1,0:T(8,128)(2,1)}, u32[]{:S(2)}) %copy-start.4) | copy-done | bytes 524312
  13.3 0.9 %copy-done.7 = bf16[128,512]{1,0:T(8,128)(2,1)S(1)} copy-done((bf16[128,512]{1,0:T(8,128)(2,1)S(1)}, bf16[128,512]{1,0:T(8,128)(2,1)}, u32[]{:S(2)}) %copy-start.7) | copy-done | bytes 131096
  14.2 2.2 %prepare.1 = (bf16[5,96,2176]{2,1,0:T(8,128)(2,1)S(1)}, bf16[512,400]{1,0:T(8,128)(2,1)S(1)}, bf16[384,512]{1,0:T(8,128)(2,1)S(1)}, bf16[128,512]{1,0:T(8,128)(2,1)S(1)}, bf16[512,128]{1,0:T(8,128)(2,1)S(1)}) custom-call(bf16[6,8,32,256]{3,2,1,0:T(8,128)(2,1)S(1)} %copy-done.1, bf16[6,32,256]{2,1,0:T(8,128)(2,1)S(1)} %collective-permute-done.below_ref.refs_2_, ...), custom_call_target="tpu_custom_call" | custom-call | flops 603979776 | bytes 6121984 | tf_op jit(solution)/shard_map/prepare/pallas_call | solution.py:528
  16.4 0.0 collective-permute-done.2.far_before_ref
  16.4 0.0 collective-permute-done.3.far_after_ref
  16.5 0.0 copy-start.2
  16.5 23.5 %forward.1 = (bf16[128,4,16,128]{3,2,1,0:T(8,128)(2,1)}, bf16[4,512,2048]{2,1,0:T(8,128)(2,1)S(1)}, bf16[10,8,256]{2,1,0:T(8,128)(2,1)S(1)}, bf16[10,8,256]{2,1,...) custom-call(bf16[5,96,2176]{2,1,0:T(8,128)(2,1)S(1)} %get-tuple-elem, ...), custom_call_target="tpu_custom_call" | custom-call | flops 8589934592 | bytes 17951232 | tf_op jit(solution)/shard_map/forward/pallas_call | solution.py:528
  40.0 1.8 %collective-permute-start.6 = (f32[32,1024]{1,0:T(8,128)S(1)}, f32[32,1024]{1,0:T(8,128)S(1)}, u32[]{:S(2)}, u32[]{:S(2)}) collective-permute-start(f32[32,1024]{1,0:T(8,128)S(1)} %get-tuple-element.48), channel_id=1, source_target_pairs={{0,24},{4,28},{8,16},{12,20},{16,8},{20,12},{24,0},{28,4},{1,25},{... | collective-permute-start | bytes 393224 | tf_op jit(solution)/shard_map/ppermute | solution.py:25
  41.8 0.5 collective-permute-start.5
  42.3 1.2 %collective-permute-start.4 = (f32[32,1024]{1,0:T(8,128)S(1)}, f32[32,1024]{1,0:T(8,128)S(1)}, u32[]{:S(2)}, u32[]{:S(2)}) collective-permute-start(f32[32,1024]{1,0:T(8,128)S(1)} %get-tuple-element.46), channel_id=1, source_target_pairs={{0,8},{4,12},{8,0},{12,4},{16,24},{20,28},{24,16},{28,20},{1,9},{5... | collective-permute-start | bytes 393224 | tf_op jit(solution)/shard_map/ppermute | solution.py:25
  43.6 2.0 %collective-permute-start.9 = (bf16[10,8,256]{2,1,0:T(8,128)(2,1)S(1)}, bf16[10,8,256]{2,1,0:T(8,128)(2,1)S(1)}, u32[]{:S(2)}, u32[]{:S(2)}) collective-permute-start(bf16[10,8,256]{2,1,0:T(8,128)(2,1)S(1)} %get-tuple-element.54), channel_id=1, source_target_pairs={{0,3},{1,0},{2,1},{3,2},{4,7},{5,4},{6,5},{7,6},{8,11},{9,8},{10,9... | collective-permute-start | bytes 122888 | tf_op jit(solution)/shard_map/ppermute | solution.py:20
  45.5 0.1 collective-permute-start.8
  45.6 0.0 copy-done.2
  45.6 4.7 %spread.2 = (f32[6,6,32,256]{3,2,1,0:T(8,128)S(1)}, f32[96,2176]{1,0:T(8,128)S(1)}, f32[96,2176]{1,0:T(8,128)S(1)}) custom-call(bf16[4,512,2048]{2,1,0:T(8,128)(2,1)S(1)} %get-tuple-element.44.refs_0_, bf16[384,512]{1,0:T(8,128)(2,1)S(1)} %get-tuple-element.40.conv_t_ref.refs_1_, bf16[384,408]{1,0:T(8,128)(2,1)S(1)} %copy-done.2), custom_call_target="tpu_custom_call" | custom-call | flops 2415919104 | bytes 11945984 | tf_op jit(solution)/shard_map/spread/pallas_call | solution.py:528
  50.3 0.0 collective-permute-done.9.refs_8_
  50.3 1.0 %collective-permute-done.8.refs_9_ = bf16[10,8,256]{2,1,0:T(8,128)(2,1)S(1)} collective-permute-done((bf16[10,8,256]{2,1,0:T(8,128)(2,1)S(1)}, bf16[10,8,256]{2,1,0:T(8,128)(2,1)S(1)}, u32[]{:S(2)}, u32[]{:S(2)}) %collective-permute-start.8) | collective-permute-done | bytes 40992 | tf_op jit(solution)/shard_map/ppermute | solution.py:20
  51.4 0.0 collective-permute-done.6
  51.4 0.0 collective-permute-done.5
  51.4 0.0 collective-permute-done.4
  51.5 0.1 collective-permute-start.7
  51.6 0.1 fusion.1
  51.7 1.7 %collective-permute-start.10 = (bf16[6,32,256]{2,1,0:T(8,128)(2,1)S(1)}, bf16[6,32,256]{2,1,0:T(8,128)(2,1)S(1)}, u32[]{:S(2)}, u32[]{:S(2)}) collective-permute-start(bf16[6,32,256]{2,1,0:T(8,128)(2,1)S(1)} %get-tuple-element.62), channel_id=1, source_target_pairs={{0,28},{4,0},{8,4},{12,8},{16,12},{20,16},{24,20},{28,24},{1,29},{... | collective-permute-start | bytes 294920 | tf_op jit(solution)/shard_map/ppermute | solution.py:20
  53.4 0.0 collective-permute-start.11
  53.4 0.0 collective-permute-done.7
  53.4 0.1 collective-permute-start.12
  53.5 3.4 %collective-permute-start.13 = (f32[16,1536]{1,0:T(8,128)S(1)}, f32[16,1536]{1,0:T(8,128)S(1)}, u32[]{:S(2)}, u32[]{:S(2)}) collective-permute-start(f32[16,1536]{1,0:T(8,128)S(1)} %fusion.2.refs_0_), channel_id=1, source_target_pairs={{0,2},{1,3},{2,0},{3,1},{4,6},{5,7},{6,4},{7,5},{8,10},{9,11},{10,... | collective-permute-start | bytes 294920 | tf_op jit(solution)/shard_map/ppermute | solution.py:25
  56.8 1.0 %collective-permute-start.14 = (f32[16,1536]{1,0:T(8,128)S(1)}, f32[16,1536]{1,0:T(8,128)S(1)}, u32[]{:S(2)}, u32[]{:S(2)}) collective-permute-start(f32[16,1536]{1,0:T(8,128)S(1)} %fusion.2.refs_0_), channel_id=1, source_target_pairs={{0,3},{1,2},{2,1},{3,0},{4,7},{5,6},{6,5},{7,4},{8,11},{9,10},{10,... | collective-permute-start | bytes 294920 | tf_op jit(solution)/shard_map/ppermute | solution.py:25
  57.9 0.0 collective-permute-done.10.refs_6_
  57.9 0.9 %collective-permute-done.11.refs_7_ = bf16[6,32,256]{2,1,0:T(8,128)(2,1)S(1)} collective-permute-done((bf16[6,32,256]{2,1,0:T(8,128)(2,1)S(1)}, bf16[6,32,256]{2,1,0:T(8,128)(2,1)S(1)}, u32[]{:S(2)}, u32[]{:S(2)}) %collective-permute-start.11) | collective-permute-done | bytes 98336 | tf_op jit(solution)/shard_map/ppermute | solution.py:20
  58.7 3.6 %spread.3 = f32[6,8,32,256]{3,2,1,0:T(8,128)} custom-call(bf16[4,512,2048]{2,1,0:T(8,128)(2,1)S(1)} %get-tuple-element.44.refs_0_, bf16[384,512]{1,0:T(8,128)(2,1)S(1)} %get-tuple-element.40.conv_t_ref.refs_1_, bf16[384,408]{1,0:T(8,128)(2,1)S(1)} %copy-done.2, f32[96,2176]{1,0:T(8,128)S(1)} %get-tuple-element.50.refs_3_, ...), custom_call_target="tpu_custom_call" | custom-call | flops 805306368 | bytes 13797376 | tf_op jit(solution)/shard_map/spread/pallas_call | solution.py:528
  62.3 0.0 collective-permute-done.12.refs_1_
  62.4 2.3 %collective-permute-done.13.refs_2_ = f32[16,1536]{1,0:T(8,128)S(1)} collective-permute-done((f32[16,1536]{1,0:T(8,128)S(1)}, f32[16,1536]{1,0:T(8,128)S(1)}, u32[]{:S(2)}, u32[]{:S(2)}) %collective-permute-start.13) | collective-permute-done | bytes 98336 | tf_op jit(solution)/shard_map/ppermute | solution.py:25
  64.6 0.0 collective-permute-done.14.refs_3_
  64.6 1.3 %last.1 = (f32[64,162]{1,0:T(8,128)}, f32[1,64]{1,0:T(1,128)}, f32[16,512]{1,0:T(8,128)}, f32[1,128]{1,0:T(1,128)}, f32[1,1]{1,0:T(1,128)}) custom-call(f32[16,1536]{1,0:T(8,128)S(1)} %fusion.2.refs_0_, f32[16,1536]{1,0:T(8,128)S(1)} %collective-permute-done.12.refs_1_, f32[16,1536]{1,0:T(8,128)S(1)} %collective-permute-done.13.refs_2_, ...), custom_call_target="tpu_custom_call" | custom-call | bytes 468228 | tf_op jit(solution)/shard_map/last/pallas_call | solution.py:528
  (32 shorter events, 0.2 us)
Async XLA Ops:
  0.6 11.6 %copy-start.6 = (bf16[408,384]{1,0:T(8,128)(2,1)S(1)}, bf16[408,384]{1,0:T(8,128)(2,1)}, u32[]{:S(2)}) copy-start(bf16[408,384]{1,0:T(8,128)(2,1)} %constant.39.clone.row_ref) | copy-start | bytes 940036
  0.6 11.6 %copy-start.8 = (bf16[64,162]{1,0:T(8,128)(2,1)S(1)}, bf16[64,162]{1,0:T(8,128)(2,1)}, u32[]{:S(2)}) copy-start(bf16[64,162]{1,0:T(8,128)(2,1)} %conv_weight_ref.1) | copy-start | bytes 62212
  0.7 11.6 %copy-start.9 = (f32[64]{0:T(128)S(1)}, f32[64]{0:T(128)}, u32[]{:S(2)}) copy-start(f32[64]{0:T(128)} %param.15) | copy-start | bytes 772
  1.7 5.7 %collective-permute-start = (bf16[6,32,256]{2,1,0:T(8,128)(2,1)S(1)}, bf16[6,32,256]{2,1,0:T(8,128)(2,1)S(1)}, u32[]{:S(2)}, u32[]{:S(2)}) collective-permute-start(bf16[6,32,256]{2,1,0:T(8,128)(2,1)S(1)} %get-tuple-element.64), channel_id=1, source_target_pairs={{0,4},{4,8},{8,12},{12,16},{16,20},{20,24},{24,28},{28,0},{1,5},{5... | collective-permute-start | bytes 294920 | tf_op jit(solution)/shard_map/ppermute | solution.py:20
  2.2 5.2 %collective-permute-start.1 = (bf16[6,32,256]{2,1,0:T(8,128)(2,1)S(1)}, bf16[6,32,256]{2,1,0:T(8,128)(2,1)S(1)}, u32[]{:S(2)}, u32[]{:S(2)}) collective-permute-start(bf16[6,32,256]{2,1,0:T(8,128)(2,1)S(1)} %get-tuple-element.63), channel_id=1, source_target_pairs={{0,28},{4,0},{8,4},{12,8},{16,12},{20,16},{24,20},{28,24},{1,29},{... | collective-permute-start | bytes 294920 | tf_op jit(solution)/shard_map/ppermute | solution.py:20
  5.1 1.1 %copy-start = (bf16[6,8,32,256]{3,2,1,0:T(8,128)(2,1)S(1)}, bf16[6,8,32,256]{3,2,1,0:T(8,128)(2,1)}, u32[]{:S(2)}) copy-start(bf16[6,8,32,256]{3,2,1,0:T(8,128)(2,1)} %high_ref.1) | copy-start | bytes 2359300
  6.3 6.0 %copy-start.1 = (bf16[6,8,32,256]{3,2,1,0:T(8,128)(2,1)S(1)}, bf16[6,8,32,256]{3,2,1,0:T(8,128)(2,1)}, u32[]{:S(2)}) copy-start(bf16[6,8,32,256]{3,2,1,0:T(8,128)(2,1)} %high_ref.1) | copy-start | bytes 2359300
  6.3 6.0 %copy-start.3 = (bf16[8,162,384]{2,1,0:T(8,128)(2,1)S(1)}, bf16[8,162,384]{2,1,0:T(8,128)(2,1)}, u32[]{:S(2)}) copy-start(bf16[8,162,384]{2,1,0:T(8,128)(2,1)} %constant.43.clone.tap_ref.far_tap_ref) | copy-start | bytes 2985988
  6.3 10.2 %copy-start.11 = (f32[128]{0:T(128)S(1)}, f32[128]{0:T(128)}, u32[]{:S(2)}) copy-start(f32[128]{0:T(128)} %param.17) | copy-start | bytes 1540
  6.3 10.2 %copy-start.12 = (bf16[48,32]{1,0:T(8,128)(2,1)S(1)}, bf16[48,32]{1,0:T(8,128)(2,1)}, u32[]{:S(2)}) copy-start(bf16[48,32]{1,0:T(8,128)(2,1)} %constant.41.clone.edge_ref) | copy-start | bytes 9220
  6.3 10.2 %copy-start.13 = (bf16[32,48]{1,0:T(8,128)(2,1)S(1)}, bf16[32,48]{1,0:T(8,128)(2,1)}, u32[]{:S(2)}) copy-start(bf16[32,48]{1,0:T(8,128)(2,1)} %constant.42.clone.edge_t_ref) | copy-start | bytes 9220
  7.8 8.7 %collective-permute-start.2 = (bf16[10,8,256]{2,1,0:T(8,128)(2,1)S(1)}, bf16[10,8,256]{2,1,0:T(8,128)(2,1)S(1)}, u32[]{:S(2)}, u32[]{:S(2)}) collective-permute-start(bf16[10,8,256]{2,1,0:T(8,128)(2,1)S(1)} %get-tuple-element.37), channel_id=1, source_target_pairs={{0,1},{1,2},{2,3},{3,0},{4,5},{5,6},{6,7},{7,4},{8,9},{9,10},{10,1... | collective-permute-start | bytes 122888 | tf_op jit(solution)/shard_map/ppermute | solution.py:20
  10.1 6.3 %collective-permute-start.3 = (bf16[10,8,256]{2,1,0:T(8,128)(2,1)S(1)}, bf16[10,8,256]{2,1,0:T(8,128)(2,1)S(1)}, u32[]{:S(2)}, u32[]{:S(2)}) collective-permute-start(bf16[10,8,256]{2,1,0:T(8,128)(2,1)S(1)} %get-tuple-element.38), channel_id=1, source_target_pairs={{0,3},{1,0},{2,1},{3,2},{4,7},{5,4},{6,5},{7,6},{8,11},{9,8},{10,9... | collective-permute-start | bytes 122888 | tf_op jit(solution)/shard_map/ppermute | solution.py:20
  12.2 1.0 %copy-start.4 = (bf16[512,512]{1,0:T(8,128)(2,1)S(1)}, bf16[512,512]{1,0:T(8,128)(2,1)}, u32[]{:S(2)}) copy-start(bf16[512,512]{1,0:T(8,128)(2,1)} %constant.44.clone.order_ref.far_order_ref) | copy-start | bytes 1572868
  13.3 0.9 %copy-start.7 = (bf16[128,512]{1,0:T(8,128)(2,1)S(1)}, bf16[128,512]{1,0:T(8,128)(2,1)}, u32[]{:S(2)}) copy-start(bf16[128,512]{1,0:T(8,128)(2,1)} %down_weight_ref.1) | copy-start | bytes 393220
  14.2 2.3 %copy-start.5 = (bf16[512,512]{1,0:T(8,128)(2,1)S(1)}, bf16[512,512]{1,0:T(8,128)(2,1)}, u32[]{:S(2)}) copy-start(bf16[512,512]{1,0:T(8,128)(2,1)} %constant.44.clone.order_ref.far_order_ref) | copy-start | bytes 1572868
  14.2 2.3 %copy-start.10 = (bf16[128,4,16,128]{3,2,1,0:T(8,128)(2,1)S(1)}, bf16[128,4,16,128]{3,2,1,0:T(8,128)(2,1)}, u32[]{:S(2)}) copy-start(bf16[128,4,16,128]{3,2,1,0:T(8,128)(2,1)} %target_ref.1) | copy-start | bytes 6291460
  16.5 29.1 %copy-start.2 = (bf16[384,408]{1,0:T(8,128)(2,1)S(1)}, bf16[384,408]{1,0:T(8,128)(2,1)}, u32[]{:S(2)}) copy-start(bf16[384,408]{1,0:T(8,128)(2,1)} %constant.40.clone.refs_2_) | copy-start | bytes 940036
  40.0 11.4 %collective-permute-start.6 = (f32[32,1024]{1,0:T(8,128)S(1)}, f32[32,1024]{1,0:T(8,128)S(1)}, u32[]{:S(2)}, u32[]{:S(2)}) collective-permute-start(f32[32,1024]{1,0:T(8,128)S(1)} %get-tuple-element.48), channel_id=1, source_target_pairs={{0,24},{4,28},{8,16},{12,20},{16,8},{20,12},{24,0},{28,4},{1,25},{... | collective-permute-start | bytes 393224 | tf_op jit(solution)/shard_map/ppermute | solution.py:25
  41.8 9.6 %collective-permute-start.5 = (f32[32,1024]{1,0:T(8,128)S(1)}, f32[32,1024]{1,0:T(8,128)S(1)}, u32[]{:S(2)}, u32[]{:S(2)}) collective-permute-start(f32[32,1024]{1,0:T(8,128)S(1)} %get-tuple-element.47), channel_id=1, source_target_pairs={{0,16},{4,20},{8,24},{12,28},{16,0},{20,4},{24,8},{28,12},{1,17},{... | collective-permute-start | bytes 393224 | tf_op jit(solution)/shard_map/ppermute | solution.py:25
  42.3 9.1 %collective-permute-start.4 = (f32[32,1024]{1,0:T(8,128)S(1)}, f32[32,1024]{1,0:T(8,128)S(1)}, u32[]{:S(2)}, u32[]{:S(2)}) collective-permute-start(f32[32,1024]{1,0:T(8,128)S(1)} %get-tuple-element.46), channel_id=1, source_target_pairs={{0,8},{4,12},{8,0},{12,4},{16,24},{20,28},{24,16},{28,20},{1,9},{5... | collective-permute-start | bytes 393224 | tf_op jit(solution)/shard_map/ppermute | solution.py:25
  43.6 6.8 %collective-permute-start.9 = (bf16[10,8,256]{2,1,0:T(8,128)(2,1)S(1)}, bf16[10,8,256]{2,1,0:T(8,128)(2,1)S(1)}, u32[]{:S(2)}, u32[]{:S(2)}) collective-permute-start(bf16[10,8,256]{2,1,0:T(8,128)(2,1)S(1)} %get-tuple-element.54), channel_id=1, source_target_pairs={{0,3},{1,0},{2,1},{3,2},{4,7},{5,4},{6,5},{7,6},{8,11},{9,8},{10,9... | collective-permute-start | bytes 122888 | tf_op jit(solution)/shard_map/ppermute | solution.py:20
  45.5 5.8 %collective-permute-start.8 = (bf16[10,8,256]{2,1,0:T(8,128)(2,1)S(1)}, bf16[10,8,256]{2,1,0:T(8,128)(2,1)S(1)}, u32[]{:S(2)}, u32[]{:S(2)}) collective-permute-start(bf16[10,8,256]{2,1,0:T(8,128)(2,1)S(1)} %get-tuple-element.53), channel_id=1, source_target_pairs={{0,1},{1,2},{2,3},{3,0},{4,5},{5,6},{6,7},{7,4},{8,9},{9,10},{10,1... | collective-permute-start | bytes 122888 | tf_op jit(solution)/shard_map/ppermute | solution.py:20
  51.5 1.9 %collective-permute-start.7 = (f32[16,1536]{1,0:T(8,128)S(1)}, f32[16,1536]{1,0:T(8,128)S(1)}, u32[]{:S(2)}, u32[]{:S(2)}) collective-permute-start(f32[16,1536]{1,0:T(8,128)S(1)} %pad_maximum_fusion), channel_id=1, source_target_pairs={{0,4},{4,0},{8,12},{12,8},{16,20},{20,16},{24,28},{28,24},{1,5},{5... | collective-permute-start | bytes 294920 | tf_op jit(solution)/shard_map/ppermute | solution.py:25
  51.7 6.2 %collective-permute-start.10 = (bf16[6,32,256]{2,1,0:T(8,128)(2,1)S(1)}, bf16[6,32,256]{2,1,0:T(8,128)(2,1)S(1)}, u32[]{:S(2)}, u32[]{:S(2)}) collective-permute-start(bf16[6,32,256]{2,1,0:T(8,128)(2,1)S(1)} %get-tuple-element.62), channel_id=1, source_target_pairs={{0,28},{4,0},{8,4},{12,8},{16,12},{20,16},{24,20},{28,24},{1,29},{... | collective-permute-start | bytes 294920 | tf_op jit(solution)/shard_map/ppermute | solution.py:20
  53.4 5.3 %collective-permute-start.11 = (bf16[6,32,256]{2,1,0:T(8,128)(2,1)S(1)}, bf16[6,32,256]{2,1,0:T(8,128)(2,1)S(1)}, u32[]{:S(2)}, u32[]{:S(2)}) collective-permute-start(bf16[6,32,256]{2,1,0:T(8,128)(2,1)S(1)} %get-tuple-element.61), channel_id=1, source_target_pairs={{0,4},{4,8},{8,12},{12,16},{16,20},{20,24},{24,28},{28,0},{1,5},{5... | collective-permute-start | bytes 294920 | tf_op jit(solution)/shard_map/ppermute | solution.py:20
  53.4 9.0 %collective-permute-start.12 = (f32[16,1536]{1,0:T(8,128)S(1)}, f32[16,1536]{1,0:T(8,128)S(1)}, u32[]{:S(2)}, u32[]{:S(2)}) collective-permute-start(f32[16,1536]{1,0:T(8,128)S(1)} %fusion.2.refs_0_), channel_id=1, source_target_pairs={{0,1},{1,0},{2,3},{3,2},{4,5},{5,4},{6,7},{7,6},{8,9},{9,8},{10,11... | collective-permute-start | bytes 294920 | tf_op jit(solution)/shard_map/ppermute | solution.py:25
  53.5 11.2 %collective-permute-start.13 = (f32[16,1536]{1,0:T(8,128)S(1)}, f32[16,1536]{1,0:T(8,128)S(1)}, u32[]{:S(2)}, u32[]{:S(2)}) collective-permute-start(f32[16,1536]{1,0:T(8,128)S(1)} %fusion.2.refs_0_), channel_id=1, source_target_pairs={{0,2},{1,3},{2,0},{3,1},{4,6},{5,7},{6,4},{7,5},{8,10},{9,11},{10,... | collective-permute-start | bytes 294920 | tf_op jit(solution)/shard_map/ppermute | solution.py:25
  56.8 7.8 %collective-permute-start.14 = (f32[16,1536]{1,0:T(8,128)S(1)}, f32[16,1536]{1,0:T(8,128)S(1)}, u32[]{:S(2)}, u32[]{:S(2)}) collective-permute-start(f32[16,1536]{1,0:T(8,128)S(1)} %fusion.2.refs_0_), channel_id=1, source_target_pairs={{0,3},{1,2},{2,1},{3,0},{4,7},{5,6},{6,5},{7,4},{8,11},{9,10},{10,... | collective-permute-start | bytes 294920 | tf_op jit(solution)/shard_map/ppermute | solution.py:25
